TPU v7x, 32 devices: a whole 2x2x4 slice. The times are simulated.
32 devices in a mesh: dp: 4 (over z), mp: 4 (over y, x), grid: 2 (over core).
Axes of the slice: x: 2, y: 2, z: 4, core: 2. Of those that a mesh axis runs over, the one named last changes fastest.
Arguments:
- tokens: bfloat16 [12608, 1024], P(('dp', 'grid')), may hold values from -6 to 6
- cotangent: bfloat16 [12608, 1024], P(('dp', 'grid')), may hold values from -6 to 6
- w_qkv: bfloat16 [1024, 3, 1024], P('grid', None, 'mp'), may hold values from -0.1875 to 0.1875
- qv_bias: bfloat16 [2, 1024], P('grid', 'mp'), may hold values from -1.75 to 1.75
- w_proj: bfloat16 [1024, 1024], P('mp', 'grid'), may hold values from -0.75 to 0.75
- proj_bias: bfloat16 [1024], P('grid'), may hold values from -1.75 to 1.75
- norm_gains: bfloat16 [2, 1024], P(None, 'grid'), may hold values from 0.099609375 to 1.8984375
- norm_shifts: bfloat16 [2, 1024], P(None, 'grid'), may hold values from -1.75 to 1.75
- w_router: bfloat16 [1024, 16], P('grid'), may hold values from -0.125 to 0.125
- expert_shift: bfloat16 [16, 1024], P(None, 'grid'), may hold values from -12 to 12
- w_first: bfloat16 [16, 1024, 4096], P(('dp', 'mp'), 'grid'), may hold values from -0.1875 to 0.1875
- w_second: bfloat16 [16, 4096, 1024], P(('dp', 'mp'), None, 'grid'), may hold values from -1.5 to 1.5
- first_bias: bfloat16 [16, 4096], P(('dp', 'mp'), 'grid'), may hold values from -1.25 to 1.25
- routes: int32 [12608, 2], P(('dp', 'grid')), may hold values from 0 to 15, all different within a row; in each aligned block of 1576 rows (0 to 1575, 1576 to 3151, ...) at most 315 rows name the same one
- priority: int32 [12608, 2], P(('dp', 'grid')), may hold values from 0 to 3151, as said below
Outputs:
- block_out: bfloat16 [12608, 1024], P(('dp', 'grid'))
- grad_tokens: float32 [12608, 1024], P(('dp', 'grid'))
- grad_w_qkv: float32 [1024, 3, 1024], P('grid', None, 'mp')
- grad_qv_bias: float32 [2, 1024], P('grid', 'mp')
- grad_w_proj: float32 [1024, 1024], P('mp', 'grid')
- grad_proj_bias: float32 [1024], P('grid')
- grad_norm_gains: float32 [2, 1024], P(None, 'grid')
- grad_norm_shifts: float32 [2, 1024], P(None, 'grid')
- grad_router: float32 [1024, 16], P('grid')
- grad_expert_shift: float32 [16, 1024], P(None, 'grid')
- grad_first: float32 [16, 1024, 4096], P(('dp', 'mp'), 'grid')
- grad_second: float32 [16, 4096, 1024], P(('dp', 'mp'), None, 'grid')
- grad_first_bias: float32 [16, 4096], P(('dp', 'mp'), 'grid')
- keep_mask: int32 [12608, 2], P(('dp', 'grid'))
Inputs may be any that keep to these rules, and one draw needn't show every extreme that they name: `routes`: each row names two different experts. Within each aligned block of 1576 rows (the rows of one device) no expert is named by more than 315 rows, a bound that some block reaches. `priority`: within each aligned block of 1576 rows the 3152 entries are a permutation of 0 to 3151.
All inputs are finite; a program needn't handle non-finite values.
Results may differ from a plain program's by a relative error of at most 0.02.
Values may be sent and summed in bfloat16 or wider, within the bound.
No kernel may reach another device: no remote copies, remote signals or barrier semaphores. Data moves between devices by JAX's collectives and lax.ppermute only.
A program may use at most 320 MiB of HBM per device.

v0:
```python
import jax
import jax.numpy as jnp
from jax import lax
from jax.sharding import PartitionSpec as P

HEAD = 64
IMG_LEN = 197
EXP_DEV = 4


def entering(part, axis, combine, identity):
    place = lax.axis_index(axis)
    gathered = lax.all_gather(part, axis)
    state = jnp.zeros_like(part) + jnp.asarray(identity, part.dtype)

    def one(turn, state):
        return combine(state, lax.dynamic_index_in_dim(gathered, turn, 0, False))

    return lax.fori_loop(0, place, one, state)


def gelu_tanh(values):
    return (
        0.5
        * values
        * (1.0 + jnp.tanh(0.7978845608028654 * (values + 0.044715 * values * values * values)))
    )


def norm_parts(values):
    centred = values - jnp.mean(values, axis=-1, keepdims=True)
    inv_std = lax.rsqrt(jnp.mean(centred * centred, axis=-1, keepdims=True) + 1e-06)
    return (centred * inv_std, inv_std)


def norm_back(grad_norm, gain, normed, inv_std):
    scaled = grad_norm * gain
    return inv_std * (
        scaled
        - jnp.mean(scaled, axis=-1, keepdims=True)
        - normed * jnp.mean(scaled * normed, axis=-1, keepdims=True)
    )


def head_scores(queries, keyset, score_scale):
    return (
        jnp.einsum("iqhd,ikhd->ihqk", queries, keyset, preferred_element_type=jnp.float32)
        * score_scale
    )


def local(
    tokens,
    cotangent,
    w_qkv,
    qv_bias,
    w_proj,
    proj_bias,
    norm_gains,
    norm_shifts,
    w_router,
    expert_shift,
    w_first,
    w_second,
    first_bias,
    routes,
    priority,
):
    gathered = (
        lax.all_gather(w_qkv, "grid", axis=0, tiled=True),
        lax.all_gather(qv_bias, "grid", axis=0, tiled=True),
        lax.all_gather(w_proj, "grid", axis=1, tiled=True),
        lax.all_gather(proj_bias, "grid", axis=0, tiled=True),
        lax.all_gather(norm_gains, "grid", axis=1, tiled=True),
        lax.all_gather(norm_shifts, "grid", axis=1, tiled=True),
        lax.all_gather(w_router, "grid", axis=0, tiled=True),
        lax.all_gather(expert_shift, "grid", axis=1, tiled=True),
        lax.all_gather(w_first, "grid", axis=1, tiled=True),
        lax.all_gather(w_second, "grid", axis=2, tiled=True),
        lax.all_gather(first_bias, "grid", axis=1, tiled=True),
    )
    (
        qkv_full,
        qv_full,
        proj_full,
        pshift_full,
        gain_full,
        shift_full,
        router_full,
        eshift_full,
        first_full,
        second_full,
        fbias_full,
    ) = gathered
    rows_dev = tokens.shape[0]
    model_width = tokens.shape[1]
    local_width = w_proj.shape[0]
    head_count = local_width // HEAD
    images = rows_dev // IMG_LEN
    experts_all = w_router.shape[1]
    source_count = experts_all // EXP_DEV
    quarters = lax.axis_size("mp") // EXP_DEV
    mine = lax.axis_index("mp") // quarters
    slot_count = 16 * rows_dev // (5 * experts_all)
    capacity = (9 * rows_dev + 4 * EXP_DEV - 1) // (4 * EXP_DEV)
    score_scale = HEAD ** (-0.5)
    gain_rows = gain_full.astype(jnp.float32)
    shift_rows = shift_full.astype(jnp.float32)
    residual = tokens.astype(jnp.float32)
    normed_one, inv_one = norm_parts(residual)
    hidden_one = (normed_one * gain_rows[0] + shift_rows[0]).astype(jnp.bfloat16)
    qkv_rows = jnp.einsum("td,dcf->tcf", hidden_one, qkv_full, preferred_element_type=jnp.float32)
    qv_rows = qv_full.astype(jnp.float32)
    qkv_rows = (
        qkv_rows + jnp.stack([qv_rows[0], jnp.zeros_like(qv_rows[0]), qv_rows[1]])[None]
    ).astype(jnp.bfloat16)
    split_heads = qkv_rows.reshape(images, IMG_LEN, 3, head_count, HEAD)
    queries = split_heads[:, :, 0]
    keyset = split_heads[:, :, 1]
    valset = split_heads[:, :, 2]
    scores = head_scores(queries, keyset, score_scale)
    row_top = jnp.max(scores, axis=-1, keepdims=True)
    log_total = row_top + jnp.log(jnp.sum(jnp.exp(scores - row_top), axis=-1, keepdims=True))
    probs_low = jnp.exp(scores - log_total).astype(jnp.bfloat16)
    head_mix = jnp.einsum("ihqk,ikhd->iqhd", probs_low, valset, preferred_element_type=jnp.float32)
    head_mix = head_mix.reshape(rows_dev, local_width).astype(jnp.bfloat16)
    branch = lax.psum(jnp.dot(head_mix, proj_full, preferred_element_type=jnp.float32), "mp")
    after_attn = residual + branch + pshift_full.astype(jnp.float32)
    normed_two, inv_two = norm_parts(after_attn)
    hidden_two = (normed_two * gain_rows[1] + shift_rows[1]).astype(jnp.bfloat16)
    logits = jnp.dot(hidden_two, router_full, preferred_element_type=jnp.float32)
    exp_vals = jnp.exp(logits - jnp.max(logits, axis=-1, keepdims=True))
    router_probs = exp_vals / jnp.sum(exp_vals, axis=-1, keepdims=True)
    expert_ids = jnp.arange(experts_all, dtype=jnp.int32)
    route_hot = (routes[:, :, None] == expert_ids[None, None, :]).astype(jnp.float32)
    gates = jnp.sum(route_hot * router_probs[:, None, :], axis=-1)
    chosen = routes.reshape(-1)
    rank_flat = priority.reshape(-1)
    pair_hot = (chosen[:, None] == expert_ids[None, :]).astype(jnp.bfloat16)
    earlier = (rank_flat[None, :] < rank_flat[:, None]).astype(jnp.bfloat16)
    before = jnp.dot(earlier, pair_hot, preferred_element_type=jnp.float32)
    pair_float = pair_hot.astype(jnp.float32)
    local_place = jnp.sum(before * pair_float, axis=1).astype(jnp.int32)
    counts = jnp.sum(pair_float, axis=0).astype(jnp.int32)
    offsets = entering(counts, "dp", lambda first, second: first + second, jnp.zeros_like(counts))
    offset_pair = jnp.sum(pair_hot.astype(jnp.int32) * offsets[None, :], axis=1)
    kept_pair = offset_pair + local_place < capacity
    keep_float = kept_pair.astype(jnp.float32).reshape(rows_dev, 2)
    mine_pair = (chosen % EXP_DEV == mine).astype(jnp.float32).reshape(rows_dev, 2)
    slot_index = local_place * experts_all + chosen
    return_index = local_place * source_count + chosen // EXP_DEV
    token_index = jnp.arange(2 * rows_dev, dtype=jnp.int32) // 2
    target = jnp.where(kept_pair, slot_index, slot_count * experts_all)
    slot_token = (
        jnp.full((slot_count * experts_all,), rows_dev, jnp.int32)
        .at[target]
        .set(token_index, mode="drop")
    )
    own_token = lax.dynamic_index_in_dim(
        slot_token.reshape(slot_count, source_count, EXP_DEV), mine, 2, keepdims=False
    )
    padded_two = jnp.concatenate([hidden_two, jnp.zeros((1, model_width), jnp.bfloat16)], axis=0)
    outgoing = jnp.take(padded_two, own_token, axis=0)
    incoming = lax.all_to_all(outgoing, "dp", split_axis=1, concat_axis=0, tiled=True)
    pre_act = (
        jnp.einsum("rxd,xdf->rxf", incoming, first_full, preferred_element_type=jnp.float32)
        + fbias_full.astype(jnp.float32)[None]
    )
    active = gelu_tanh(pre_act).astype(jnp.bfloat16)
    produced = jnp.einsum(
        "rxf,xfd->rxd", active, second_full, preferred_element_type=jnp.float32
    ).astype(jnp.bfloat16)
    returned = lax.all_to_all(produced, "dp", split_axis=0, concat_axis=1, tiled=True)
    returned_flat = returned.reshape(slot_count * source_count, model_width)
    pair_out = (
        jnp.take(returned_flat, return_index, axis=0)
        .reshape(rows_dev, 2, model_width)
        .astype(jnp.float32)
    )
    pair_out = pair_out * mine_pair[:, :, None]
    weight = gates * keep_float
    expert_part = jnp.sum(weight[:, :, None] * pair_out, axis=1)
    expert_sum = lax.psum(expert_part.astype(jnp.bfloat16), "mp").astype(jnp.float32)
    eshift_rows = eshift_full.astype(jnp.float32)
    mix_weight = jnp.sum(weight[:, :, None] * route_hot, axis=1)
    expert_sum = expert_sum + jnp.dot(mix_weight, eshift_rows, precision=lax.Precision.HIGHEST)
    block_out = (after_attn + expert_sum).astype(jnp.bfloat16)
    grad_out = cotangent.astype(jnp.float32)
    grad_pair = jnp.sum(grad_out[:, None, :] * pair_out, axis=-1) * keep_float
    shift_dots = jnp.einsum("td,ed->te", cotangent, eshift_full, preferred_element_type=jnp.float32)
    gate_local = jnp.sum(route_hot * shift_dots[:, None, :], axis=-1) * keep_float
    grad_eshift = jnp.einsum("te,td->ed", mix_weight, grad_out, precision=lax.Precision.HIGHEST)
    slot_weight = (
        jnp.zeros((slot_count * experts_all,), jnp.float32)
        .at[target]
        .set(weight.reshape(-1), mode="drop")
    )
    own_weight = lax.dynamic_index_in_dim(
        slot_weight.reshape(slot_count, source_count, EXP_DEV), mine, 2, keepdims=False
    )
    padded_grad = jnp.concatenate([grad_out, jnp.zeros((1, model_width), jnp.float32)], axis=0)
    grad_slots = (jnp.take(padded_grad, own_token, axis=0) * own_weight[:, :, None]).astype(
        jnp.bfloat16
    )
    grad_in = lax.all_to_all(grad_slots, "dp", split_axis=1, concat_axis=0, tiled=True)
    grad_active = jnp.einsum(
        "rxd,xfd->rxf", grad_in, second_full, preferred_element_type=jnp.float32
    )
    gelu_out, gelu_pull = jax.vjp(gelu_tanh, pre_act)
    grad_pre = gelu_pull(grad_active)[0].astype(jnp.bfloat16)
    grad_second = jnp.einsum("rxf,rxd->xfd", active, grad_in, preferred_element_type=jnp.float32)
    grad_first = jnp.einsum("rxd,rxf->xdf", incoming, grad_pre, preferred_element_type=jnp.float32)
    grad_fbias = jnp.sum(grad_pre.astype(jnp.float32), axis=0)
    grad_rows = jnp.einsum(
        "rxf,xdf->rxd", grad_pre, first_full, preferred_element_type=jnp.float32
    ).astype(jnp.bfloat16)
    grad_back = lax.all_to_all(grad_rows, "dp", split_axis=0, concat_axis=1, tiled=True)
    grad_flat = grad_back.reshape(slot_count * source_count, model_width)
    grad_pairs = (
        jnp.take(grad_flat, return_index, axis=0)
        .reshape(rows_dev, 2, model_width)
        .astype(jnp.float32)
    )
    grad_disp = jnp.sum(grad_pairs * (keep_float * mine_pair)[:, :, None], axis=1)
    grad_two, gate_part = lax.psum((grad_disp, grad_pair), "mp")
    grad_gate = gate_part + gate_local
    grad_probs = jnp.sum(grad_gate[:, :, None] * route_hot, axis=1)
    grad_logits = (
        router_probs * (grad_probs - jnp.sum(router_probs * grad_probs, axis=-1, keepdims=True))
    ).astype(jnp.bfloat16)
    grad_two = grad_two + jnp.einsum(
        "te,de->td", grad_logits, router_full, preferred_element_type=jnp.float32
    )
    grad_router = jnp.einsum(
        "td,te->de", hidden_two, grad_logits, preferred_element_type=jnp.float32
    )
    gain_two = jnp.sum(grad_two * normed_two, axis=0)
    shift_two = jnp.sum(grad_two, axis=0)
    grad_after = grad_out + norm_back(grad_two, gain_rows[1], normed_two, inv_two)
    grad_branch = grad_after.astype(jnp.bfloat16)
    grad_pshift = jnp.sum(grad_branch.astype(jnp.float32), axis=0)
    grad_proj = jnp.einsum("tf,td->fd", head_mix, grad_branch, preferred_element_type=jnp.float32)
    grad_mix = jnp.einsum(
        "td,fd->tf", grad_branch, proj_full, preferred_element_type=jnp.float32
    ).astype(jnp.bfloat16)
    grad_mix = grad_mix.reshape(images, IMG_LEN, head_count, HEAD)
    att_soft = jnp.exp(head_scores(queries, keyset, score_scale) - log_total)
    soft_low = att_soft.astype(jnp.bfloat16)
    grad_att = jnp.einsum("iqhd,ikhd->ihqk", grad_mix, valset, preferred_element_type=jnp.float32)
    grad_val = jnp.einsum("ihqk,iqhd->ikhd", soft_low, grad_mix, preferred_element_type=jnp.float32)
    row_delta = jnp.sum(att_soft * grad_att, axis=-1, keepdims=True)
    grad_scores = (att_soft * (grad_att - row_delta)).astype(jnp.bfloat16)
    grad_query = (
        jnp.einsum("ihqk,ikhd->iqhd", grad_scores, keyset, preferred_element_type=jnp.float32)
        * score_scale
    )
    grad_key = (
        jnp.einsum("ihqk,iqhd->ikhd", grad_scores, queries, preferred_element_type=jnp.float32)
        * score_scale
    )
    grad_qkv = (
        jnp.stack([grad_query, grad_key, grad_val], axis=2)
        .reshape(rows_dev, 3, local_width)
        .astype(jnp.bfloat16)
    )
    qkv_sums = jnp.sum(grad_qkv.astype(jnp.float32), axis=0)
    grad_qv = jnp.stack([qkv_sums[0], qkv_sums[2]])
    grad_qkv_w = jnp.einsum("td,tcf->dcf", hidden_one, grad_qkv, preferred_element_type=jnp.float32)
    grad_one = jnp.einsum("tcf,dcf->td", grad_qkv, qkv_full, preferred_element_type=jnp.float32)
    grad_one = lax.psum(grad_one.astype(jnp.bfloat16), "mp").astype(jnp.float32)
    gain_one = jnp.sum(grad_one * normed_one, axis=0)
    shift_one = jnp.sum(grad_one, axis=0)
    grad_tokens = grad_after + norm_back(grad_one, gain_rows[0], normed_one, inv_one)
    grad_gains = jnp.stack([gain_one, gain_two])
    grad_shifts = jnp.stack([shift_one, shift_two])
    scattered = (
        lax.psum_scatter(
            grad_qkv_w.astype(jnp.bfloat16), "grid", scatter_dimension=0, tiled=True
        ).astype(jnp.float32),
        lax.psum_scatter(
            grad_qv.astype(jnp.bfloat16), "grid", scatter_dimension=0, tiled=True
        ).astype(jnp.float32),
        lax.psum_scatter(
            grad_proj.astype(jnp.bfloat16), "grid", scatter_dimension=1, tiled=True
        ).astype(jnp.float32),
        lax.psum_scatter(
            grad_pshift.astype(jnp.bfloat16), "grid", scatter_dimension=0, tiled=True
        ).astype(jnp.float32),
        lax.psum_scatter(
            grad_gains.astype(jnp.bfloat16), "grid", scatter_dimension=1, tiled=True
        ).astype(jnp.float32),
        lax.psum_scatter(
            grad_shifts.astype(jnp.bfloat16), "grid", scatter_dimension=1, tiled=True
        ).astype(jnp.float32),
        lax.psum_scatter(
            grad_router.astype(jnp.bfloat16), "grid", scatter_dimension=0, tiled=True
        ).astype(jnp.float32),
        lax.psum_scatter(
            grad_eshift.astype(jnp.bfloat16), "grid", scatter_dimension=1, tiled=True
        ).astype(jnp.float32),
        lax.psum_scatter(
            grad_first.astype(jnp.bfloat16), "grid", scatter_dimension=1, tiled=True
        ).astype(jnp.float32),
        lax.psum_scatter(
            grad_second.astype(jnp.bfloat16), "grid", scatter_dimension=2, tiled=True
        ).astype(jnp.float32),
        lax.psum_scatter(
            grad_fbias.astype(jnp.bfloat16), "grid", scatter_dimension=1, tiled=True
        ).astype(jnp.float32),
    )
    (
        part_qkv,
        part_qv,
        part_proj,
        part_pshift,
        part_gains,
        part_shifts,
        part_router,
        part_eshift,
        part_first,
        part_second,
        part_fbias,
    ) = scattered
    dense = (
        lax.psum(part_qkv.astype(jnp.bfloat16), "dp").astype(jnp.float32),
        lax.psum(part_qv.astype(jnp.bfloat16), "dp").astype(jnp.float32),
        lax.psum(part_proj.astype(jnp.bfloat16), "dp").astype(jnp.float32),
        lax.psum(part_pshift.astype(jnp.bfloat16), "dp").astype(jnp.float32),
        lax.psum(part_gains.astype(jnp.bfloat16), "dp").astype(jnp.float32),
        lax.psum(part_shifts.astype(jnp.bfloat16), "dp").astype(jnp.float32),
        lax.psum(part_router.astype(jnp.bfloat16), "dp").astype(jnp.float32),
        lax.psum(part_eshift.astype(jnp.bfloat16), "dp").astype(jnp.float32),
    )
    return (
        block_out,
        grad_tokens,
        dense[0],
        dense[1],
        dense[2],
        dense[3],
        dense[4],
        dense[5],
        dense[6],
        dense[7],
        part_first,
        part_second,
        part_fbias,
        kept_pair.reshape(rows_dev, 2).astype(jnp.int32),
    )


def solution(mesh):
    return jax.shard_map(
        local,
        mesh=mesh,
        in_specs=(
            P(("dp", "grid"), None),
            P(("dp", "grid"), None),
            P("grid", None, "mp"),
            P("grid", "mp"),
            P("mp", "grid"),
            P("grid"),
            P(None, "grid"),
            P(None, "grid"),
            P("grid", None),
            P(None, "grid"),
            P(("dp", "mp"), "grid", None),
            P(("dp", "mp"), None, "grid"),
            P(("dp", "mp"), "grid"),
            P(("dp", "grid"), None),
            P(("dp", "grid"), None),
        ),
        out_specs=(
            P(("dp", "grid"), None),
            P(("dp", "grid"), None),
            P("grid", None, "mp"),
            P("grid", "mp"),
            P("mp", "grid"),
            P("grid"),
            P(None, "grid"),
            P(None, "grid"),
            P("grid", None),
            P(None, "grid"),
            P(("dp", "mp"), "grid", None),
            P(("dp", "mp"), None, "grid"),
            P(("dp", "mp"), "grid"),
            P(("dp", "grid"), None),
        ),
        check_vma=False,
    )
```

profile of v0, /device:TPU:0, one launch (start us, length us, event | category | flops | bytes accessed | tf_op | source)
XLA Modules:
  0.0 1297.7 jit_solution(14602248771961361483)
XLA Ops:
  94.4 107.9 %all-reduce.14.cloned.1.call-done = f32[1576,1024]{1,0:T(8,128)} async-done(((f32[1576,1024]{1,0:T(8,128)}), f32[1576,1024]{1,0:T(8,128)}) %all-reduce.14.cloned.1.call-update) | async-done | bytes 6455312 | tf_op jit(solution)/shard_map/psum | solution.py:127
  213.6 15.9 %scatter_custom_fusion.1 = f32[5040]{0:T(1024)S(1)} fusion(s32[3152]{0:T(1024)S(1)} %fusion.106, f32[3152]{0:T(1024)S(1)} %get-tuple-element.130, f32[]{:T(128)} %constant.145.clone.1), kind=kCustom, calls=%fused_computation.169 | custom fusion | bytes 20164 | tf_op jit(solution)/shard_map/scatter | solution.py:196
  229.5 15.9 %scatter_custom_fusion = s32[5040]{0:T(1024)S(1)} fusion(s32[3152]{0:T(1024)S(1)} %fusion.106, s32[3152]{0:T(1024)S(1)} %add_select_fusion.1, s32[]{:T(128)} %constant.153.clone.1), kind=kCustom, calls=%fused_computation.171 | custom fusion | bytes 20164 | tf_op jit(solution)/shard_map/scatter | solution.py:157
  298.6 44.2 %all-to-all-done.2 = bf16[315,4,1024]{2,0,1:T(8,128)(2,1)} async-done(((bf16[315,4,1024]{2,0,1:T(8,128)(2,1)}), bf16[315,4,1024]{2,0,1:T(8,128)(2,1)}, u32[]{:S(2)}, u32[]{:S(2)}) %all-to-all-start.2) | async-done | bytes 2580512 | tf_op jit(solution)/shard_map/all_to_all | solution.py:205
  352.2 53.2 %all-to-all-done = bf16[315,4,1024]{2,0,1:T(8,128)(2,1)S(1)} async-done(((bf16[315,4,1024]{2,0,1:T(8,128)(2,1)}), bf16[315,4,1024]{2,0,1:T(8,128)(2,1)S(1)}, u32[]{:S(2)}, u32[]{:S(2)}) %all-to-all-start) | async-done | bytes 2580512 | tf_op jit(solution)/shard_map/all_to_all | solution.py:164
  407.6 18.5 %fusion.25 = f32[1260,4096]{1,0:T(8,128)} fusion(bf16[1260,1024]{1,0:T(8,128)(2,1)} %reshape.292, bf16[1,1024,4096]{2,1,0:T(8,128)(2,1)} %all-gather.9.cloned.1.call-done), kind=kOutput, calls=%fused_computation.46 | convolution fusion | flops 10569646080 | bytes 31612928 | tf_op jit(solution)/shard_map/rxd,xdf->rxf/dot_general | solution.py:166
  426.1 32.5 %fusion.131 = (bf16[4096]{0:T(1024)(128)(2,1)}, bf16[1260,1,4096]{2,0,1:T(8,128)(2,1)}) fusion(bf16[1260,1024]{1,0:T(8,128)(2,1)S(1)} %copy-done.30, bf16[1,4096,1024]{2,1,0:T(8,128)(2,1)} %all-gather.11.cloned.1.call-done, f32[4096]{0:T(1024)S(1)} %bitcast.260, f32[1260,4096]{1,0:T(8,128)} %fusion.25), kind=kOutput, calls=%fused_computation.216 | convolution fusion | flops 10703826944 | bytes 41959424 | tf_op jit(solution)/shard_map/rxd,xfd->rxf/dot_general | solution.py:206
  458.6 14.5 %fusion.63 = bf16[1260,1,1024]{2,0,1:T(8,128)(2,1)} fusion(bf16[1,1024,4096]{2,1,0:T(8,128)(2,1)S(1)} %copy-done.83, bf16[1260,1,4096]{2,0,1:T(8,128)(2,1)} %get-tuple-element.159), kind=kOutput, calls=%fused_computation.93 | convolution fusion | flops 10570936320 | bytes 21291008 | tf_op jit(solution)/shard_map/rxf,xdf->rxd/dot_general | solution.py:214
  486.7 20.6 %fusion.68 = bf16[1260,1,1024]{2,0,1:T(8,128)(2,1)} fusion(bf16[1,4096,1024]{2,1,0:T(8,128)(2,1)} %all-gather.11.cloned.1.call-done, f32[1260,4096]{1,0:T(8,128)} %fusion.25, f32[4096]{0:T(1024)S(1)} %bitcast.261), kind=kOutput, calls=%fused_computation.94 | convolution fusion | flops 10622545920 | bytes 31629312 | tf_op jit(solution)/shard_map/rxf,xfd->rxd/dot_general | solution.py:170
  515.7 29.1 %all-to-all-done.3 = bf16[4,2,161280]{2,1,0:T(2,128)(2,1)} async-done(((bf16[4,2,161280]{2,1,0:T(2,128)(2,1)}), bf16[4,2,161280]{2,1,0:T(2,128)(2,1)}, u32[]{:S(2)}, u32[]{:S(2)}) %all-to-all-start.3) | async-done | bytes 2580512 | tf_op jit(solution)/shard_map/all_to_all | solution.py:217
  556.7 16.2 %reduce.9 = bf16[1260,1024]{1,0:T(8,128)(2,1)} reduce(bf16[1260,1,1024]{2,1,0:T(2,128)(2,1)} %reshape.402, bf16[]{:T(256)} %constant.196), dimensions={1}, to_apply=%all_to_all.53.reduce_sub_computation | reduce | bytes 5160962 | tf_op jit(solution)/shard_map/all_to_all | solution.py:217
  582.9 24.6 %all-to-all-done.1 = bf16[4,2,161280]{2,1,0:T(2,128)(2,1)} async-done(((bf16[4,2,161280]{2,1,0:T(2,128)(2,1)}), bf16[4,2,161280]{2,1,0:T(2,128)(2,1)}, u32[]{:S(2)}, u32[]{:S(2)}) %all-to-all-start.1) | async-done | bytes 2580512 | tf_op jit(solution)/shard_map/all_to_all | solution.py:173
  612.7 16.2 %reduce.8 = bf16[1260,1024]{1,0:T(8,128)(2,1)} reduce(bf16[1260,1,1024]{2,1,0:T(2,128)(2,1)} %reshape.400, bf16[]{:T(256)} %constant.196), dimensions={1}, to_apply=%all_to_all.47.reduce_sub_computation | reduce | bytes 5160962 | tf_op jit(solution)/shard_map/all_to_all | solution.py:173
  643.5 17.3 %gather_fusion.2 = bf16[3152,1024]{1,0:T(8,128)(2,1)} fusion(bf16[1260,1024]{1,0:T(8,128)(2,1)} %reshape.296, s32[4096]{0:T(1024)S(1)} %pad_clamp_fusion), kind=kCustom, calls=%fused_computation.clone | custom fusion | bytes 12923200 | tf_op jit(solution)/shard_map/jit(_take)/gather | solution.py:176
  660.7 10.9 gather_fusion.3
  671.7 12.7 select_convert_fusion
  684.4 15.5 %reshape.304 = f32[1576,2,1024]{2,1,0:T(2,128)} reshape(f32[3152,1024]{1,0:T(8,128)} %get-tuple-element.141) | data formatting | bytes 25821184 | tf_op jit(solution)/shard_map/convert_element_type | solution.py:222
  699.9 20.9 %multiply_reduce_fusion.1 = f32[1576,1024]{1,0:T(8,128)} fusion(f32[1576,2,1024]{2,1,0:T(2,128)} %reshape.304, f32[1576,2]{1,0:T(8,128)S(1)} %copy.179), kind=kLoop, calls=%fused_computation.30 | loop fusion | flops 4841472 | bytes 19378496 | tf_op jit(solution)/shard_map/reduce_sum | solution.py:224
  722.7 29.5 %mul.365 = f32[1576,2,1024]{2,1,0:T(2,128)} broadcast(bf16[1576,1024]{1,0:T(8,128)(2,1)S(1)} %copy-done.4), dimensions={0,2} | broadcast | bytes 16138240 | tf_op jit(solution)/shard_map/mul | solution.py:189
  752.1 16.1 %mul.366 = f32[3152,1024]{1,0:T(8,128)} reshape(f32[1576,2,1024]{2,1,0:T(2,128)} %mul.365) | data formatting | bytes 25821184 | tf_op jit(solution)/shard_map/mul | solution.py:189
  782.9 16.0 %psum.94 = f32[1576,2]{0,1:T(2,128)S(1)} all-reduce(f32[1576,2]{0,1:T(2,128)S(1)} %broadcast_select_fusion.1), channel_id=1, replica_groups=mesh['dp'=4,'mp'=4,'grid'=2] {'mp'}, use_global_device_ids=true, to_apply=%region_23.25 | all-reduce | flops 3152 | bytes 25216 | tf_op jit(solution)/shard_map/psum | solution.py:225
  799.6 61.1 %all-reduce.16.cloned.1.call-done = f32[1576,1024]{1,0:T(8,128)} async-done(((f32[1576,1024]{1,0:T(8,128)}), f32[1576,1024]{1,0:T(8,128)}) %all-reduce.16.cloned.1.call-update) | async-done | bytes 6455312 | tf_op jit(solution)/shard_map/psum | solution.py:225
  942.0 16.3 %reshape.303 = f32[1576,2,1024]{2,1,0:T(2,128)} reshape(f32[3152,1024]{1,0:T(8,128)} %get-tuple-element.142) | data formatting | bytes 25821184 | tf_op jit(solution)/shard_map/convert_element_type | solution.py:178
  958.3 23.0 %multiply_reduce_fusion.2 = bf16[1576,1024]{1,0:T(8,128)(2,1)} fusion(f32[1576,2,1024]{2,1,0:T(2,128)} %reshape.303, f32[1576,2]{1,0:T(8,128)S(1)} %copy-done.20, f32[1576,2]{1,0:T(8,128)} %copy.166), kind=kLoop, calls=%fused_computation.31 | loop fusion | flops 8069120 | bytes 16163456 | tf_op jit(solution)/shard_map/reduce_sum | solution.py:182
  987.2 22.4 %convert_bitcast_fusion = bf16[1,4096,1024]{2,1,0:T(8,128)(2,1)} fusion(bf16[1260,1024]{1,0:T(8,128)(2,1)S(1)} %copy-done.31, f32[1260,4096]{1,0:T(8,128)} %fusion.25, f32[4096]{0:T(1024)S(1)} %bitcast.262), kind=kOutput, calls=%fused_computation.48 | convolution fusion | flops 10625449984 | bytes 31629312 | tf_op jit(solution)/shard_map/rxf,rxd->xfd/dot_general | solution.py:211
  1011.3 17.7 %convert_bitcast_fusion.1 = bf16[1,1024,4096]{2,1,0:T(8,128)(2,1)} fusion(bf16[1260,1024]{1,0:T(8,128)(2,1)S(1)} %copy-done.29, bf16[1260,1,4096]{2,0,1:T(8,128)(2,1)} %get-tuple-element.159), kind=kOutput, calls=%fused_computation.49 | convolution fusion | flops 10573840384 | bytes 21291008 | tf_op jit(solution)/shard_map/rxd,rxf->xdf/dot_general | solution.py:212
  1033.8 93.5 %all-reduce.18.cloned.1.call-done = (bf16[1576,1024]{1,0:T(8,128)(2,1)}, bf16[1576,1024]{1,0:T(8,128)(2,1)}) async-done(((bf16[1576,1024]{1,0:T(8,128)(2,1)}, bf16[1576,1024]{1,0:T(8,128)(2,1)}), (bf16[1576,1024]{1,0:T(8,128)(2,1)}, bf16[1576,1024]{1,0:T(8,128)(2,1)})) %all-reduce.18.cloned.1.call-update) | async-done | bytes 6455312 | tf_op jit(solution)/shard_map/psum | solution.py:183
  1148.9 33.5 %all-reduce.20.cloned.1.call-done = (bf16[512,3,256]{2,0,1:T(8,128)(2,1)}, bf16[256,512]{1,0:T(8,128)(2,1)}) async-done(((bf16[512,3,256]{2,0,1:T(8,128)(2,1)}, bf16[256,512]{1,0:T(8,128)(2,1)}), (bf16[512,3,256]{2,0,1:T(8,128)(2,1)}, bf16[256,512]{1,0:T(8,128)(2,1)})) %all-reduce.20.cloned.1.call-update) | async-done | bytes 1048592 | tf_op jit(solution)/shard_map/psum | solution.py:325
  1186.6 14.9 %reduce-scatter.26.cloned.1.call-done = bf16[1,4096,512]{2,1,0:T(8,128)(2,1)} async-done(((bf16[1,4096,1024]{2,1,0:T(8,128)(2,1)}), bf16[1,4096,512]{2,1,0:T(8,128)(2,1)}) %reduce-scatter.26.cloned.1.call-update) | async-done | bytes 4194320 | tf_op jit(solution)/shard_map/reduce_scatter | solution.py:304
  1208.2 14.1 %reduce-scatter.24.cloned.1.call-done = bf16[1,512,4096]{2,1,0:T(8,128)(2,1)} async-done(((bf16[1,1024,4096]{2,1,0:T(8,128)(2,1)}), bf16[1,512,4096]{2,1,0:T(8,128)(2,1)}) %reduce-scatter.24.cloned.1.call-update) | async-done | bytes 4194320 | tf_op jit(solution)/shard_map/reduce_scatter | solution.py:301
  1255.8 11.2 reduce-scatter.22.cloned.1.call-done
  1267.0 20.1 %all-reduce.6 = (bf16[1,256]{1,0:T(2,128)(2,1)S(1)}, bf16[512]{0:T(512)(128)(2,1)S(1)}, bf16[2,512]{1,0:T(2,128)(2,1)S(1)}, bf16[2,512]{1,0:T(2,128)(2,1)S(1)}, ...) all-reduce(bf16[1,256]{1,0:T(2,128)(2,1)S(1)} %constant_dynamic-sli, ...), channel_id=1, replica_groups=mesh['dp'=4,'mp'=4,'grid'=2] {'dp'}, use_global_device_ids=true, to_apply=%region_37.39 | all-reduce | flops 19200 | bytes 76800 | tf_op jit(solution)/shard_map/psum | solution.py:326
  (407 shorter events, 404.9 us)
Async XLA Ops:
  7.2 14.9 %all-gather.7.cloned.1.call-start = ((), (), s32[]{:S(2)}) async-start(), calls=%async_computation.13 | async-start | bytes 2359296 | tf_op jit(solution)/shard_map/all_gather | solution.py:70
  7.9 194.4 %all-reduce.14.cloned.1.call-start = ((), (), s32[]{:S(2)}) async-start(), calls=%async_computation.14 | async-start | bytes 12910592 | tf_op jit(solution)/shard_map/psum | solution.py:127
  18.3 189.6 %copy-start.65 = (f32[1,1024]{1,0:T(1,128)}, f32[1,1024]{1,0:T(1,128)S(1)}, u32[]{:S(2)}) copy-start(f32[1,1024]{1,0:T(1,128)S(1)} %get-tuple-element.143) | copy-start | bytes 12292
  58.5 349.1 %all-gather.9.cloned.1.call-start = ((), (), s32[]{:S(2)}) async-start(), calls=%async_computation.15 | async-start | bytes 12582912 | tf_op jit(solution)/shard_map/all_gather | solution.py:78
  85.2 124.5 %copy-start.40 = (bf16[1024,16]{0,1:T(8,128)(2,1)}, bf16[1024,16]{0,1:T(8,128)(2,1)S(1)}, u32[]{:S(2)}) copy-start(bf16[1024,16]{0,1:T(8,128)(2,1)S(1)} %all_gather.44) | copy-start | bytes 98308
  93.4 120.1 %copy-start.51 = (f32[3152]{0:T(1024)}, f32[3152]{0:T(1024)S(1)}, u32[]{:S(2)}) copy-start(f32[3152]{0:T(1024)S(1)} %fusion.78) | copy-start | bytes 37828
  211.5 51.2 %copy-start.47 = (f32[1576]{0:T(1024)}, f32[1576]{0:T(1024)S(1)}, u32[]{:S(2)}) copy-start(f32[1576]{0:T(1024)S(1)} %get-tuple-element.153) | copy-start | bytes 18916
  278.4 64.3 %all-to-all-start.2 = ((bf16[315,4,1024]{2,0,1:T(8,128)(2,1)}), bf16[315,4,1024]{2,0,1:T(8,128)(2,1)}, u32[]{:S(2)}, u32[]{:S(2)}) async-start(bf16[315,4,1024]{2,0,1:T(8,128)(2,1)} %fusion.48), calls=%async_computation.2 | async-start | bytes 5242880 | tf_op jit(solution)/shard_map/all_to_all | solution.py:205
  283.0 143.0 %all-gather.11.cloned.1.call-start = ((), (), s32[]{:S(2)}) async-start(), calls=%async_computation.16 | async-start | bytes 12582912 | tf_op jit(solution)/shard_map/all_gather | solution.py:79
  295.4 51.0 %copy-start.79 = (bf16[1,2048]{1,0:T(2,128)(2,1)S(1)}, bf16[1,2048]{1,0:T(2,128)(2,1)}, u32[]{:S(2)}) copy-start(bf16[1,2048]{1,0:T(2,128)(2,1)} %param.31) | copy-start | bytes 12292
  342.8 62.6 %all-to-all-start = ((bf16[315,4,1024]{2,0,1:T(8,128)(2,1)}), bf16[315,4,1024]{2,0,1:T(8,128)(2,1)S(1)}, u32[]{:S(2)}, u32[]{:S(2)}) async-start(bf16[315,4,1024]{2,0,1:T(8,128)(2,1)} %copy_select_fusion.1), calls=%async_computation | async-start | bytes 5242880 | tf_op jit(solution)/shard_map/all_to_all | solution.py:164
  348.3 138.4 %copy-start.74 = (f32[1,4096]{1,0:T(1,128)}, f32[1,4096]{1,0:T(1,128)S(1)}, u32[]{:S(2)}) copy-start(f32[1,4096]{1,0:T(1,128)S(1)} %add.285) | copy-start | bytes 49156
  481.9 62.8 %all-to-all-start.3 = ((bf16[4,2,161280]{2,1,0:T(2,128)(2,1)}), bf16[4,2,161280]{2,1,0:T(2,128)(2,1)}, u32[]{:S(2)}, u32[]{:S(2)}) async-start(bf16[4,2,161280]{2,1,0:T(2,128)(2,1)} %reshape.401), calls=%async_computation.3 | async-start | bytes 5160960 | tf_op jit(solution)/shard_map/all_to_all | solution.py:217
  544.8 62.7 %all-to-all-start.1 = ((bf16[4,2,161280]{2,1,0:T(2,128)(2,1)}), bf16[4,2,161280]{2,1,0:T(2,128)(2,1)}, u32[]{:S(2)}, u32[]{:S(2)}) async-start(bf16[4,2,161280]{2,1,0:T(2,128)(2,1)} %reshape.399), calls=%async_computation.1 | async-start | bytes 5160960 | tf_op jit(solution)/shard_map/all_to_all | solution.py:173
  549.3 311.4 %all-reduce.16.cloned.1.call-start = ((), (), s32[]{:S(2)}) async-start(), calls=%async_computation.17 | async-start | bytes 12910592 | tf_op jit(solution)/shard_map/psum | solution.py:225
  720.8 264.8 %reduce-scatter.18.cloned.1.call-start = ((), (), s32[]{:S(2)}) async-start(), calls=%async_computation.19 | async-start | bytes 786432 | tf_op jit(solution)/shard_map/reduce_scatter | solution.py:283
  771.1 89.6 %copy-start.41 = (bf16[1024,16]{0,1:T(8,128)(2,1)S(1)}, bf16[1024,16]{0,1:T(8,128)(2,1)}, u32[]{:S(2)}) copy-start(bf16[1024,16]{0,1:T(8,128)(2,1)} %copy-done.40) | copy-start | bytes 98308
  771.1 89.6 %copy-start.50 = (f32[1576]{0:T(1024)S(1)}, f32[1576]{0:T(1024)}, u32[]{:S(2)}) copy-start(f32[1576]{0:T(1024)} %copy-done.49) | copy-start | bytes 18916
  799.6 68.5 %copy-start.36 = (bf16[1576,16]{0,1:T(8,128)(2,1)}, bf16[1576,16]{0,1:T(8,128)(2,1)S(1)}, u32[]{:S(2)}) copy-start(bf16[1576,16]{0,1:T(8,128)(2,1)S(1)} %multiply_convert_fusion.6) | copy-start | bytes 151300
  799.6 68.5 %copy-start.58 = (f32[1576]{0:T(1024)S(1)}, f32[1576]{0:T(1024)}, u32[]{:S(2)}) copy-start(f32[1576]{0:T(1024)} %copy-done.57) | copy-start | bytes 18916
  799.6 68.5 %copy-start.66 = (f32[1,1024]{1,0:T(1,128)S(1)}, f32[1,1024]{1,0:T(1,128)}, u32[]{:S(2)}) copy-start(f32[1,1024]{1,0:T(1,128)} %copy-done.65) | copy-start | bytes 12292
  909.9 75.7 %reduce-scatter.16.cloned.1.call-start = ((), (), s32[]{:S(2)}) async-start(), calls=%async_computation.18 | async-start | bytes 2359296 | tf_op jit(solution)/shard_map/reduce_scatter | solution.py:277
  939.0 92.9 %reduce-scatter.32.cloned.1.call-start = ((), (), s32[]{:S(2)}) async-start(), calls=%async_computation.26 | async-start | bytes 1572864
  940.8 186.6 %all-reduce.18.cloned.1.call-start = ((), (), s32[]{:S(2)}) async-start(), calls=%async_computation.27 | async-start | bytes 12910592 | tf_op jit(solution)/shard_map/psum | solution.py:183
  985.5 196.8 %all-reduce.20.cloned.1.call-start = ((), (), s32[]{:S(2)}) async-start(), calls=%async_computation.28 | async-start | bytes 2097152 | tf_op jit(solution)/shard_map/psum | solution.py:325
  986.1 215.3 %reduce-scatter.26.cloned.1.call-start = ((), (), s32[]{:S(2)}) async-start(), calls=%async_computation.23 | async-start | bytes 12582912 | tf_op jit(solution)/shard_map/reduce_scatter | solution.py:304
  1009.6 212.7 %reduce-scatter.24.cloned.1.call-start = ((), (), s32[]{:S(2)}) async-start(), calls=%async_computation.22 | async-start | bytes 12582912 | tf_op jit(solution)/shard_map/reduce_scatter | solution.py:301
  1029.1 211.5 %reduce-scatter.28.cloned.1.call-start = ((), (), s32[]{:S(2)}) async-start(), calls=%async_computation.24 | async-start | bytes 393216
  1031.0 107.3 %copy-start.37 = (bf16[1576,16]{0,1:T(8,128)(2,1)S(1)}, bf16[1576,16]{0,1:T(8,128)(2,1)}, u32[]{:S(2)}) copy-start(bf16[1576,16]{0,1:T(8,128)(2,1)} %copy-done.36) | copy-start | bytes 151300
  1137.2 107.4 %reduce-scatter.30.cloned.1.call-start = ((), (), s32[]{:S(2)}) async-start(), calls=%async_computation.25 | async-start | bytes 393216
  1138.2 117.6 %reduce-scatter.20.cloned.1.call-start = ((), (), s32[]{:S(2)}) async-start(), calls=%async_computation.20 | async-start | bytes 49152 | tf_op jit(solution)/shard_map/reduce_scatter | solution.py:295
  1141.4 125.7 %reduce-scatter.22.cloned.1.call-start = ((), (), s32[]{:S(2)}) async-start(), calls=%async_computation.21 | async-start | bytes 49152 | tf_op jit(solution)/shard_map/reduce_scatter | solution.py:298
  (79 other events, 1079.3 us)
Sparse Core Ops, SparseCore 0:
  9.6 12.5 all-gather.6
  58.6 143.6 all-reduce.13
  203.9 20.1 all-gather.8
  285.1 20.6 all-gather.10
  720.9 139.7 all-reduce.15
  910.0 8.2 reduce-scatter.17
  939.2 9.3 reduce-scatter.15
  950.8 9.7 reduce-scatter.31
  985.7 141.6 all-reduce.17
  1129.8 52.5 all-reduce.19
  1185.2 16.1 reduce-scatter.25
  1204.2 18.0 reduce-scatter.23
  1224.6 8.9 reduce-scatter.27
  1235.7 8.8 reduce-scatter.29
  1247.2 8.5 reduce-scatter.19
  1258.5 8.5 reduce-scatter.21
where the time goes:
time: 1310 us; the launch traced here: 1300 us
  waiting for transfers between devices  503 us (38%)
  local copies, waits for them, and re-layouts  312 us (24%)
  matrix products  194 us (15%)
  other arithmetic  188 us (14%)
  blocking collectives  65.6 us (5%)
  starting transfers between devices  18.2 us (1%)
  between operations  17.1 us (1%)
    psum x1, waiting for transfers between devices, local(): lax.psum(jnp.dot(head_mix, proj_full, preferred_element_type=jnp.float32)...  108 us
    psum x1, waiting for transfers between devices, local(): lax.psum(expert_part.astype(jnp.bfloat16), 'mp').astype(jnp.float32)  93.5 us
    psum x1, waiting for transfers between devices, local(): grad_two, gate_part = lax.psum((grad_disp, grad_pair), 'mp')  61.1 us
    all_to_all x1, waiting for transfers between devices, local(): lax.all_to_all(outgoing, 'dp', split_axis=1, concat_axis=0, tiled=True)  53.2 us
    unnamed x206, local copies, waits for them, and re-layouts  52.1 us
    mul x2, local copies, waits for them, and re-layouts, local(): grad_pair = jnp.sum(grad_out[:, None, :] * pair_out, axis=-1) * keep_float  45.6 us
    all_to_all x1, waiting for transfers between devices, local(): lax.all_to_all(grad_slots, 'dp', split_axis=1, concat_axis=0, tiled=True)  44.2 us
    psum x1, waiting for transfers between devices, local(): lax.psum(part_qkv.astype(jnp.bfloat16), 'dp').astype(jnp.float32)  33.5 us
  transfers between devices with their start and end apart: 20, of which 14 were waited for; matrix products, arithmetic and copies ran while one was open for 33% of the time, Pallas kernels for 0%

commit v1 on v0

v1 whole, which is shorter than its diff:
```python
import functools
from typing import NamedTuple

import jax
import jax.numpy as jnp
from jax import lax
from jax.experimental import pallas as pl
from jax.experimental.pallas import tpu as pltpu
from jax.sharding import PartitionSpec as P

HEAD = 64
IMG_LEN = 197
EXP_DEV = 4
BF = jnp.bfloat16
F32 = jnp.float32
I32 = jnp.int32
VMEM_BYTES = 56 * 1024 * 1024
LOW = -1e30


class Sizes(NamedTuple):
    T: int
    D: int
    half: int
    n: int
    X: int
    E: int
    S: int
    SP: int
    CR: int
    R: int
    TP: int
    W: int
    images: int
    quarters: int
    F: int
    cap: int
    win: int
    fblk: int
    key: int


class Order:
    def __init__(self):
        self.last = None


def up(value, step):
    return -(-value // step) * step


def dot_nn(a, b):
    return jnp.dot(a, b, preferred_element_type=F32)


def dot_nt(a, b):
    return lax.dot_general(a, b, (((1,), (1,)), ((), ())), preferred_element_type=F32)


def dot_tn(a, b):
    return lax.dot_general(a, b, (((0,), (0,)), ((), ())), preferred_element_type=F32)


def split_low(values):
    high = values.astype(BF)
    return high, (values - high.astype(F32)).astype(BF)


def shape_of(dims, dtype):
    return jax.ShapeDtypeStruct(dims, dtype)


def whole(array, buffers=None):
    dims = tuple(array.shape)
    extra = {} if buffers is None else {"pipeline_mode": pl.Buffered(buffers)}
    return pl.BlockSpec(dims, lambda i, s: (0,) * len(dims), **extra)


def rows_of(dims):
    return pl.BlockSpec(dims, lambda i, s: (i,) + (0,) * (len(dims) - 1))


def cols_of(dims):
    return pl.BlockSpec(dims, lambda i, s: (0,) * (len(dims) - 1) + (i,))


def call(order, body, place, args, specs, outs, out_specs, grid, scratch=(), name=None):
    extra = [] if order.last is None else [order.last]
    count = len(args)

    def wrapped(place, *refs):
        body(place, *refs[:count], *refs[count + len(extra) :])

    result = pl.pallas_call(
        wrapped,
        grid_spec=pltpu.PrefetchScalarGridSpec(
            num_scalar_prefetch=1,
            grid=grid,
            in_specs=list(specs) + [pl.BlockSpec(memory_space=pl.ANY)] * len(extra),
            out_specs=list(out_specs),
            scratch_shapes=list(scratch),
        ),
        out_shape=list(outs),
        compiler_params=pltpu.CompilerParams(
            dimension_semantics=("arbitrary",) * len(grid), vmem_limit_bytes=VMEM_BYTES
        ),
        cost_estimate=pl.CostEstimate(flops=1000, bytes_accessed=1000, transcendentals=0),
        name=name,
    )(place, *args, *extra)
    order.last = min(result, key=lambda o: o.size)
    return result


def swap_mp(c, value, mask):
    return lax.ppermute(value, "mp", [(i, i ^ mask) for i in range(c.n)])


def swap_grid(value):
    return lax.ppermute(value, "grid", [(0, 1), (1, 0)])


def trade(value, axis):
    return lax.all_to_all(value, axis, split_axis=0, concat_axis=0, tiled=True)


def groups_a(c):
    return [[0, 2], [1, 3]] if c.n == 4 else [[k] for k in range(c.n)]


def groups_b(c):
    return [[0, 1], [2, 3]] if c.n == 4 else [[k] for k in range(c.n)]


def reduce_mp(c, arrays):
    a, b = arrays[: len(arrays) // 2], arrays[len(arrays) // 2 :]
    if c.n != 4:
        return [[x[0]] + [swap_mp(c, x[k], k) for k in range(1, c.n)] for x in (a, b)]
    ra = swap_mp(c, a[1], 1)
    rb = swap_mp(c, b[1], 2)
    ta = (a[0][1:].astype(F32) + ra[1:].astype(F32)).astype(BF)
    tb = (b[0][1:].astype(F32) + rb[1:].astype(F32)).astype(BF)
    return [[a[0], ra, swap_mp(c, ta, 2)], [b[0], rb, swap_mp(c, tb, 1)]]


def piece_outs(c, more_a=0, more_b=0):
    outs = [shape_of((len(g), c.R + more_a, c.half), BF) for g in groups_a(c)]
    return outs + [shape_of((len(g), c.R + more_b, c.half), BF) for g in groups_b(c)]


def first_block(array):
    dims = tuple(array.shape)
    return pl.BlockSpec((None,) + dims[1:], lambda i, s: (0, 0, 0))


def add_up(refs):
    total = refs[0][...].astype(F32)
    for ref in refs[1:]:
        total = total + ref[...].astype(F32)
    return total


def gather_mp(c, value):
    if c.n != 4 or value.shape[0] != 2:
        parts = [value] + [swap_mp(c, value, k) for k in range(1, c.n)]
        return [[(p, h) for h in range(value.shape[0])] for p in parts]
    one = swap_mp(c, value, 1)
    two = swap_mp(c, value, 2)
    far_a = swap_mp(c, one[0:1], 2)
    far_b = swap_mp(c, two[1:2], 1)
    near = [[(p, 0), (p, 1)] for p in (value, one, two)]
    return near + [[(far_a, 0), (far_b, 0)]]


def flat(pieces):
    return [pair for piece in pieces for pair in piece]


def fold(c, value, axes):
    for axis, size in axes:
        mask = 1
        while mask < size:
            value = value + lax.ppermute(value, axis, [(i, i ^ mask) for i in range(size)])
            mask *= 2
    return value


def finish_sums(c, one, parts, grid):
    def half_of(side):
        cols = lax.dynamic_slice_in_dim(one, side * c.half, c.half, 1)
        row = lax.dynamic_index_in_dim(parts, side, 0, True)
        return jnp.concatenate([cols, jnp.pad(row, ((0, 0), (0, c.half - c.W)))], axis=0)

    return fold(c, half_of(grid) + swap_grid(half_of(1 - grid)), (("dp", c.X),))


def sum_proj(c, value):
    if c.n != 4:
        return jnp.sum(trade(value, "mp").astype(F32), axis=0).astype(BF)
    pair = (value[:2].astype(F32) + swap_mp(c, value[2:], 1).astype(F32)).astype(BF)
    return (pair[0].astype(F32) + swap_mp(c, pair[1], 2).astype(F32)).astype(BF)


def sum_dp(c, value):
    parts = trade(value.reshape((c.X, value.shape[0] // c.X) + value.shape[1:]), "dp")
    total = jnp.sum(parts.astype(F32), axis=0).astype(BF)
    spread = jnp.broadcast_to(total[None], (c.X,) + total.shape)
    return trade(spread, "dp").reshape(value.shape).astype(F32)


def expert_of(c, place, j):
    return j * EXP_DEV + place[3]


def offset_at(place, j):
    return place[4 + j]


def window_out(c, place, j):
    return place[4 + c.X + j]


def window_in(c, place, j):
    return pl.multiple_of(place[4 + 2 * c.X + j], 16)


def windows_body(c, place, counts, out_ref, off_ref):
    def window(offset):
        return jnp.minimum((offset >> 4) << 4, c.CR - c.SP)

    def before(e, source):
        total = jnp.int32(0)
        for b in range(c.X):
            total = total + jnp.where(b < source, counts[b, e], 0)
        return total

    for i in range(4):
        out_ref[i] = place[i]
    for i in range(4 + 3 * c.X, 32):
        out_ref[i] = jnp.int32(0)
    here = place[0] * EXP_DEV + place[3]
    for j in range(c.X):
        offset = before(expert_of(c, place, j), place[0])
        out_ref[4 + j] = offset
        out_ref[4 + c.X + j] = window(offset)
        out_ref[4 + 2 * c.X + j] = window(before(here, j))
    for e in range(c.E):
        off_ref[e : e + 1, :] = jnp.full((1, 128), before(e, place[0]), I32)


def windows(c, order, place, counts):
    return call(
        order,
        functools.partial(windows_body, c),
        place,
        [counts],
        [pl.BlockSpec(memory_space=pltpu.SMEM)],
        [shape_of((32,), I32), shape_of((c.E, 128), I32)],
        [pl.BlockSpec(memory_space=pltpu.SMEM), whole(shape_of((c.E, 128), I32))],
        (1,),
        name="windows",
    )


def route_body(c, place, row_ref, col_ref, rt_ref, slot_ref, rtb_ref, all_ref):
    first = jnp.broadcast_to(row_ref[0:1, :], (8, c.TP))
    second = jnp.broadcast_to(row_ref[1:2, :], (8, c.TP))

    def one(i, state):
        a, b = state
        for q in range(8):
            keys = col_ref[pl.ds(pl.multiple_of(i * 64 + q * 8, 8), 8), :]
            for k in range(2):
                key = keys[:, k : k + 1]
                a = a + (key < first).astype(I32)
                b = b + (key < second).astype(I32)
        return a, b

    zero = jnp.zeros((8, c.TP), I32)
    a, b = lax.fori_loop(0, c.TP // 64, one, (zero, zero))
    a = jnp.sum(a, axis=0, keepdims=True)
    b = jnp.sum(b, axis=0, keepdims=True)
    rt = rt_ref[...]
    start = jnp.zeros((1, 1), I32)
    for e in range(c.E):
        in_first = rt[0:1, :] == e
        in_second = rt[1:2, :] == e
        number = jnp.sum(in_first.astype(I32) + in_second.astype(I32), axis=1, keepdims=True)
        all_ref[e : e + 1, :] = jnp.where(in_first, a - start, jnp.where(in_second, b - start, -1))
        start = start + number
    for r in range(c.n):
        slot_ref[r] = all_ref[:, r * c.R : (r + 1) * c.R]
        rtb_ref[r] = jnp.concatenate([rt[:, r * c.R : (r + 1) * c.R]] * 4, axis=0)


def route(c, order, place, routes, priority):
    key = routes * c.key + priority
    big = 1 << 30
    pad = c.TP - c.T
    row = jnp.pad(key.T, ((0, 0), (0, pad)), constant_values=big)
    col = jnp.pad(key, ((0, pad), (0, 0)), constant_values=big)
    rt = jnp.pad(routes.T, ((0, 0), (0, pad)), constant_values=-1)
    outs = [shape_of((c.n, c.E, c.R), I32), shape_of((c.n, 8, c.R), I32)]
    return call(
        order,
        functools.partial(route_body, c),
        place,
        [row, col, rt],
        [whole(row), whole(col), whole(rt)],
        outs,
        [whole(o) for o in outs],
        (1,),
        [pltpu.VMEM((c.E, c.TP), I32)],
        name="route",
    )


def last_rows(c, tile, high, low):
    row = lax.broadcasted_iota(I32, (16, 1), 0)
    return jnp.where(row == 14, high, jnp.where(row == 15, low, tile))


def dispatch_body(c, rows_all, weighted, place, *refs):
    refs = list(refs)
    slot_ref, src_ref = refs[:2]
    refs = refs[2:]
    if weighted:
        weight_ref = refs.pop(0)
    out_ref, hot_ref, *refs = refs

    @pl.when(pl.program_id(0) == 0)
    def _():
        for j in range(c.X):
            e = expert_of(c, place, j)
            offset = offset_at(place, j)
            total = jnp.zeros((8, c.half), F32)
            for r in range(c.n):
                slot = slot_ref[r, pl.ds(e, 1), :]
                kept = (slot >= 0) & (slot + offset < c.cap)
                row = jnp.where(kept, slot + (offset - window_out(c, place, j)), -1)
                hot = (lax.broadcasted_iota(I32, (c.half, c.R), 0) == row).astype(BF)
                hot_ref[j, r] = hot[: c.SP]
                if weighted:
                    high, low = split_low(weight_ref[r, pl.ds(e, 1), :])
                    both = jnp.concatenate(
                        [jnp.broadcast_to(high, (8, c.R)), jnp.broadcast_to(low, (8, c.R))], axis=0
                    )
                    got = dot_nt(both, hot)
                    total = total + jnp.where(
                        lax.broadcasted_iota(I32, (8, 1), 0) == 0, got[0:8], got[8:16]
                    )
            if weighted:
                refs[0][j] = total

    for j in range(c.X):
        acc = None
        for r in range(c.n):
            length = min(c.R, rows_all - r * c.R)
            if length <= 0:
                continue
            part = dot_nn(hot_ref[j, r, :, :length], src_ref[r * c.R : r * c.R + length, :])
            acc = part if acc is None else acc + part
        out_ref[j] = acc.astype(BF)
        if weighted:

            @pl.when(pl.program_id(0) == 0)
            def _():
                tile = last_rows(c, acc[c.SP - 16 :], refs[0][j, 0:1, :], refs[0][j, 1:2, :])
                out_ref[j, c.SP - 16 :, :] = tile.astype(BF)


def dispatch(c, order, place, slot, source, weight=None):
    rows_all = source.shape[0]
    args = [slot, source]
    specs = [whole(slot), pl.BlockSpec((rows_all, c.half), lambda i, s: (0, i ^ s[2]))]
    scratch = [pltpu.VMEM((c.X, c.n, c.SP, c.R), BF)]
    if weight is not None:
        args.append(weight)
        specs.append(whole(weight))
        scratch.append(pltpu.VMEM((c.X, 8, c.half), F32))
    return call(
        order,
        functools.partial(dispatch_body, c, rows_all, weight is not None),
        place,
        args,
        specs,
        [shape_of((c.X, c.SP, c.D), BF)],
        [cols_of((c.X, c.SP, c.half))],
        (2,),
        scratch,
        name="dispatch",
    )[0]


def norm_rows(values):
    centred = values - jnp.mean(values, axis=-1, keepdims=True)
    inv_std = lax.rsqrt(jnp.mean(centred * centred, axis=-1, keepdims=True) + 1e-06)
    return centred * inv_std, inv_std


def norm_back(grad_norm, gain, normed, inv_std):
    scaled = grad_norm * gain
    return inv_std * (
        scaled
        - jnp.mean(scaled, axis=-1, keepdims=True)
        - normed * jnp.mean(scaled * normed, axis=-1, keepdims=True)
    )


def small_row(c, small_ref, index, count=1):
    return small_ref[index : index + count, :].astype(F32)


def own_cols(c, place):
    return pl.ds(pl.multiple_of(place[2] * c.half, c.half), c.half)


def other_cols(c, place):
    return pl.ds(pl.multiple_of((1 - place[2]) * c.half, c.half), c.half)


def live_rows(c, first, count):
    return (first + lax.broadcasted_iota(I32, (count, 1), 0)) < c.T


def qkv_body(c, place, tok_ref, small_ref, own_ref, oth_ref, hid_ref, qkv_ref, normed_ref):
    live = live_rows(c, pl.program_id(0) * c.R, c.R)
    values = jnp.where(live, tok_ref[...].astype(F32), 0.0)
    normed, _ = norm_rows(values)
    hidden = normed * small_row(c, small_ref, 0) + small_row(c, small_ref, 2)
    normed_ref[...] = normed.astype(BF)
    hid_ref[...] = jnp.where(live, hidden, 0.0).astype(BF)
    own = hid_ref[:, own_cols(c, place)]
    oth = hid_ref[:, other_cols(c, place)]
    for part in range(3):
        acc = dot_nn(own, own_ref[part]) + dot_nn(oth, oth_ref[part])
        if part != 1:
            bias = small_row(c, small_ref, 5)
            at = 0 if part == 0 else c.half
            acc = acc + bias[:, at : at + c.W]
        qkv_ref[:, part * c.W : (part + 1) * c.W] = acc.astype(BF)


def image_window(c):
    start = pl.program_id(0) * IMG_LEN
    low = pl.multiple_of(start // 16 * 16, 16)
    return low, start - low


def groups_of(c):
    lanes = min(128, c.W)
    return [(at, lanes) for at in range(0, c.W, lanes)]


def head_mask(lanes, head):
    lane = lax.broadcasted_iota(I32, (1, lanes), 1)
    return (lane >= head * HEAD) & (lane < (head + 1) * HEAD)


def attend_body(c, place, qkv_ref, mix_ref):
    @pl.when(pl.program_id(0) == 0)
    def _():
        mix_ref[...] = jnp.zeros_like(mix_ref)

    low, off = image_window(c)
    row = lax.broadcasted_iota(I32, (c.win, 1), 0)
    col = lax.broadcasted_iota(I32, (1, c.win), 1)
    in_row = (row >= off) & (row < off + IMG_LEN)
    in_col = (col >= off) & (col < off + IMG_LEN)
    for group, (at, lanes) in enumerate(groups_of(c)):
        q = qkv_ref[pl.ds(low, c.win), at : at + lanes] * BF(HEAD**-0.5)
        k = qkv_ref[pl.ds(low, c.win), c.W + at : c.W + at + lanes]
        v = qkv_ref[pl.ds(low, c.win), 2 * c.W + at : 2 * c.W + at + lanes]
        total = jnp.zeros((c.win, lanes), F32)
        for head in range(lanes // HEAD):
            mask = head_mask(lanes, head)
            scores = dot_nt(jnp.where(mask, q, BF(0)), k)
            scores = jnp.where(in_col, scores, LOW)
            top = jnp.max(scores, axis=-1, keepdims=True)
            exps = jnp.exp(scores - top)
            probs = exps / jnp.sum(exps, axis=-1, keepdims=True)
            total = total + dot_nn(probs.astype(BF), jnp.where(mask, v, BF(0)))
        old = mix_ref[group, pl.ds(low, c.win), :]
        mix_ref[group, pl.ds(low, c.win), :] = jnp.where(in_row, total.astype(BF), old)


def attend_back_body(c, place, qkv_ref, *refs):
    pieces, (out_ref, sums_ref, grad_ref) = refs[: c.n], refs[c.n :]
    @pl.when(pl.program_id(0) == 0)
    def _():
        out_ref[...] = jnp.zeros_like(out_ref)
        sums_ref[...] = jnp.zeros_like(sums_ref)
        for k in range(c.n):
            at = pl.multiple_of((place[1] ^ k) * c.R, 16)
            grad_ref[pl.ds(at, c.R), :] = pieces[k][...]

    low, off = image_window(c)
    row = lax.broadcasted_iota(I32, (c.win, 1), 0)
    in_row = (row >= off) & (row < off + IMG_LEN)
    scale = HEAD**-0.5
    for at, lanes in groups_of(c):
        q = qkv_ref[pl.ds(low, c.win), at : at + lanes] * BF(scale)
        k = qkv_ref[pl.ds(low, c.win), c.W + at : c.W + at + lanes]
        v = qkv_ref[pl.ds(low, c.win), 2 * c.W + at : 2 * c.W + at + lanes]
        do = jnp.where(in_row, grad_ref[pl.ds(low, c.win), at : at + lanes], BF(0))
        dq = jnp.zeros((c.win, lanes), F32)
        dk = jnp.zeros((c.win, lanes), F32)
        dv = jnp.zeros((c.win, lanes), F32)
        for head in range(lanes // HEAD):
            mask = head_mask(lanes, head)
            qh = jnp.where(mask, q, BF(0))
            doh = jnp.where(mask, do, BF(0))
            kh = jnp.where(mask, k, BF(0))
            scores = jnp.where(in_row, dot_nt(k, qh), LOW)
            top = jnp.max(scores, axis=0, keepdims=True)
            exps = jnp.exp(scores - top)
            soft = exps / jnp.sum(exps, axis=0, keepdims=True)
            dp = dot_nt(v, doh)
            delta = jnp.sum(soft * dp, axis=0, keepdims=True)
            ds = (soft * (dp - delta)).astype(BF)
            dq = dq + dot_tn(ds, kh)
            dk = dk + dot_nn(ds, qh)
            dv = dv + dot_nn(soft.astype(BF), doh)
        for part, grad in enumerate((dq * scale, dk, dv)):
            lane = part * c.W + at
            low_grad = jnp.where(in_row, grad, 0.0).astype(BF)
            old = out_ref[pl.ds(low, c.win), lane : lane + lanes]
            out_ref[pl.ds(low, c.win), lane : lane + lanes] = jnp.where(in_row, low_grad, old)
            summed = jnp.sum(low_grad.astype(F32), axis=0, keepdims=True)
            sums_ref[0:1, lane : lane + lanes] += summed


def middle_body(c, place, *refs):
    refs = list(refs)
    groups = groups_of(c)
    count = c.n * len(groups)
    mixes, refs = refs[:count], refs[count:]
    w_ref, tok_ref, small_ref, off_ref, slot_ref, rt_ref = refs[:6]
    hid_ref, weight_ref, mine_ref, keep_ref = refs[6:10]
    after_ref, probs_ref, keep_lane_ref, weight_lane_ref, acc_ref = refs[10:]
    step = pl.program_id(0)
    for h in range(2):
        acc = None
        for k in range(c.n):
            for group, (at, lanes) in enumerate(groups):
                weights = w_ref[(place[1] ^ k) * 2 + h, at : at + lanes, :]
                part = dot_nn(mixes[k * len(groups) + group][...], weights)
                acc = part if acc is None else acc + part
        acc_ref[:, h * c.half : (h + 1) * c.half] = acc
    live = live_rows(c, step * c.R, c.R)
    tok = jnp.where(live, tok_ref[...].astype(F32), 0.0)
    after = tok + acc_ref[...] + small_row(c, small_ref, 4)
    normed, _ = norm_rows(after)
    hidden = (normed * small_row(c, small_ref, 1) + small_row(c, small_ref, 3)).astype(BF)
    hid_ref[...] = hidden
    router = small_ref[6 + c.E : 6 + 2 * c.E, :]
    logits = dot_nt(router, hidden)
    exps = jnp.exp(logits - jnp.max(logits, axis=0, keepdims=True))
    probs = exps / jnp.sum(exps, axis=0, keepdims=True)
    slot = slot_ref[0]
    kept = (slot >= 0) & (slot + off_ref[:, 0:1] < c.cap)
    weight = jnp.where(kept, probs, 0.0)
    weight_ref[0] = weight
    for j in range(c.X):
        e = expert_of(c, place, j)
        offset = offset_at(place, j)
        slot_j = slot_ref[0, pl.ds(e, 1), :]
        kept_j = (slot_j >= 0) & (slot_j + offset < c.cap)
        row = jnp.where(kept_j, slot_j + (offset - window_out(c, place, j)), -1)
        mine_ref[0, j : j + 1, :] = row
    for j in range(c.X, 8):
        mine_ref[0, j : j + 1, :] = jnp.full((1, c.R), -1, I32)
    expert = lax.broadcasted_iota(I32, (c.E, c.R), 0)
    rows = []
    for k in range(2):
        picked = jnp.where((rt_ref[0, k : k + 1, :] == expert) & kept, 1.0, 0.0)
        rows.append(jnp.sum(picked, axis=0, keepdims=True))
    keep_ref[0] = jnp.concatenate(rows * 4, axis=0)

    @pl.when(step == place[1])
    def _():
        after_ref[...] = after
        probs_ref[...] = probs
        keep_lane_ref[...] = jnp.where(kept, 1.0, 0.0)
        weight_lane_ref[...] = weight


def middle(c, order, place, mixes, proj, tokens, small, offsets, slot, rt):
    args = [pair[0] for pair in flat(mixes)] + [proj, tokens, small, offsets, slot, rt]
    specs = [
        pl.BlockSpec((None, c.R, a.shape[2]), lambda i, s, at=at: (at, i, 0))
        for a, at in flat(mixes)
    ]
    specs += [whole(proj), rows_of((c.R, c.D)), whole(small), whole(offsets)]
    specs += [rows_of((1, c.E, c.R)), rows_of((1, 8, c.R))]
    outs = [
        shape_of((c.TP, c.D), BF),
        shape_of((c.n, c.E, c.R), F32),
        shape_of((c.n, 8, c.R), I32),
        shape_of((c.n, 8, c.R), F32),
        shape_of((c.R, c.D), F32),
        shape_of((c.E, c.R), F32),
        shape_of((c.E, c.R), F32),
        shape_of((c.E, c.R), F32),
    ]
    out_specs = [
        rows_of((c.R, c.D)),
        rows_of((1, c.E, c.R)),
        rows_of((1, 8, c.R)),
        rows_of((1, 8, c.R)),
    ] + [whole(o) for o in outs[4:]]
    return call(
        order,
        functools.partial(middle_body, c),
        place,
        args,
        specs,
        outs,
        out_specs,
        (c.n,),
        [pltpu.VMEM((c.R, c.D), F32)],
        name="middle",
    )


def pack_rows(c, place, rows, out_ref):
    main = c.SP - 16
    used = lax.broadcasted_iota(I32, (16, 1), 0) < c.S + 15 - main
    out_ref[...] = jnp.zeros_like(out_ref)
    for j in range(c.X):
        at = window_in(c, place, j)
        out_ref[pl.ds(at, main), :] += rows[j, :main, :]
        tail = jnp.where(used, rows[j, main:, :], BF(0))
        out_ref[pl.ds(pl.multiple_of(at + main, 16), 16), :] += tail


def last_pair(c, tile, lanes):
    tile = tile[:, :lanes].astype(F32)
    return tile[14:15, :], tile[15:16, :]


def row_chunks(c, size):
    return [(at, min(size, c.CR - at)) for at in range(0, c.CR, size)]


def grad_active_body(c, place, *refs):
    rows, own_ref, oth_ref, out_ref, all_ref = refs

    @pl.when(pl.program_id(0) == 0)
    def _():
        pack_rows(c, place, rows, all_ref)

    weights = jnp.concatenate([own_ref[...], oth_ref[...]], axis=1)
    for at, size in row_chunks(c, 448):
        out_ref[at : at + size, :] = dot_nt(all_ref[at : at + size, :], weights).astype(BF)


def grad_active(c, order, place, rows, own_w, oth_w):
    outs = [shape_of((c.CR, c.F), BF), shape_of((c.CR, c.D), BF)]
    return call(
        order,
        functools.partial(grad_active_body, c),
        place,
        [rows, own_w, oth_w],
        [whole(rows, 1)] + [rows_of((c.fblk, c.half))] * 2,
        outs,
        [cols_of((c.CR, c.fblk)), whole(outs[1])],
        (c.F // c.fblk,),
        name="grad_active",
    )


def expert_body(c, place, *refs):
    rows, own_ref, oth_ref, bias_ref, ga_ref = refs[:5]
    act_ref, gp_ref, gb_ref, all_ref, col_ref, back_ref = refs[5:11]
    acc_ref, dot_ref, row_ref = refs[11:]
    step = pl.program_id(0)

    @pl.when(step == 0)
    def _():
        acc_ref[...] = jnp.zeros_like(acc_ref)
        dot_ref[...] = jnp.zeros_like(dot_ref)
        pack_rows(c, place, rows, all_ref)
        col_ref[...] = jnp.zeros_like(col_ref)
        eye = lax.broadcasted_iota(I32, (c.SP, c.SP), 0) == lax.broadcasted_iota(I32, (c.SP, c.SP), 1)
        for j in range(c.X):
            high, low = last_pair(c, rows[j, c.SP - 16 :, :], c.SP)
            col = jnp.sum(jnp.where(eye, high + low, 0.0), axis=1, keepdims=True)
            col_ref[pl.ds(window_in(c, place, j), c.SP), :] += jnp.broadcast_to(col, (c.SP, 128))

    bias = bias_ref[...]
    weights = jnp.concatenate([own_ref[...], oth_ref[...]], axis=0)
    summed = jnp.zeros((1, c.fblk), F32)
    lead = 0.7978845608028654
    cube = lead * 0.044715
    for at, size in row_chunks(c, 224):
        rows_at = slice(at, at + size)
        pre = dot_nn(all_ref[rows_at, :], weights) + bias
        square = pre * pre
        turn = jnp.tanh(pre * (cube * square + lead))
        above = 1.0 + turn
        active = (0.5 * pre) * above
        slope = above * (1.0 + (1.0 - turn) * (pre * (3 * cube * square + lead)))
        ga = ga_ref[rows_at, :].astype(F32)
        product = active * ga
        part = product[:, 0:128]
        for lane in range(128, c.fblk, 128):
            part = part + product[:, lane : lane + 128]
        dot_ref[rows_at, :] += part
        grad = ga * slope * (0.5 * col_ref[rows_at, 0:1])
        act_ref[rows_at, :] = active.astype(BF)
        grad_low = grad.astype(BF)
        gp_ref[rows_at, :] = grad_low
        summed = summed + jnp.sum(grad, axis=0, keepdims=True)
        acc_ref[rows_at, :] += dot_nt(grad_low, weights)
    gb_ref[...] = jnp.broadcast_to(summed, (8, c.fblk))

    @pl.when(step == pl.num_programs(0) - 1)
    def _():
        ones = jnp.ones((8, 128), BF)
        row_ref[...] = jnp.zeros_like(row_ref)
        for j in range(c.X):
            at = window_in(c, place, j)
            back_ref[j] = acc_ref[pl.ds(at, c.SP), :].astype(BF)
            a, rest = split_low(dot_ref[pl.ds(at, c.SP), :])
            total = dot_nt(ones, a) + dot_nt(ones, rest)
            high = total.astype(BF).astype(F32)
            row_ref[0:8, : c.SP] = high
            row_ref[8:16, : c.SP] = total - high
            tile = back_ref[j, c.SP - 16 :, : c.half].astype(F32)
            tile = last_rows(c, tile, row_ref[0:1, :], row_ref[8:9, :])
            back_ref[j, c.SP - 16 :, : c.half] = tile.astype(BF)


def expert(c, order, place, rows, own_w, oth_w, bias, ga):
    args = [rows, own_w, oth_w, bias, ga]
    specs = [whole(rows, 1)]
    specs += [cols_of((c.half, c.fblk))] * 2
    specs += [cols_of((1, c.fblk)), cols_of((c.CR, c.fblk))]
    outs = [
        shape_of((c.CR, c.F), BF),
        shape_of((c.CR, c.F), BF),
        shape_of((8, c.F), F32),
    ]
    out_specs = [cols_of((c.CR, c.fblk))] * 2 + [cols_of((8, c.fblk))]
    late = [shape_of((c.CR, c.D), BF), shape_of((c.CR, 128), F32)]
    late.append(shape_of((c.X, c.SP, c.D), BF))
    return call(
        order,
        functools.partial(expert_body, c),
        place,
        args,
        specs,
        outs + late,
        out_specs + [whole(o, 1) for o in late],
        (c.F // c.fblk,),
        [
            pltpu.VMEM((c.CR, c.D), F32),
            pltpu.VMEM((c.CR, 128), F32),
            pltpu.VMEM((16, c.half), F32),
        ],
        name="expert",
    )


def produce_body(c, place, *refs):
    col_ref, act_ref, own_ref, oth_ref, out_ref, acc_ref = refs
    step = pl.program_id(0)

    @pl.when(step == 0)
    def _():
        acc_ref[...] = jnp.zeros_like(acc_ref)

    weights = jnp.concatenate([own_ref[...], oth_ref[...]], axis=1)
    for at, size in row_chunks(c, 448):
        acc_ref[at : at + size, :] += dot_nn(act_ref[at : at + size, :], weights)

    @pl.when(step == pl.num_programs(0) - 1)
    def _():
        for j in range(c.X):
            rows_at = pl.ds(window_in(c, place, j), c.SP)
            col = col_ref[rows_at, 0:1]
            out_ref[j] = (acc_ref[rows_at, :] * col).astype(BF)


def produce(c, order, place, col, act, own_w, oth_w):
    out = shape_of((c.X, c.SP, c.D), BF)
    return call(
        order,
        functools.partial(produce_body, c),
        place,
        [col, act, own_w, oth_w],
        [
            whole(col),
            cols_of((c.CR, c.fblk)),
            rows_of((c.fblk, c.half)),
            rows_of((c.fblk, c.half)),
        ],
        [out],
        [whole(out, 1)],
        (c.F // c.fblk,),
        [pltpu.VMEM((c.CR, c.D), F32)],
        name="produce",
    )[0]


def grad_second_body(c, own, place, *refs):
    refs = list(refs)
    all_ref, col_ref, act_ref = refs[:3]
    out_ref, row_ref = refs[-2:]

    @pl.when(pl.program_id(0) == 0)
    def _():
        row_ref[...] = (all_ref[...].astype(F32) * col_ref[:, 0:1]).astype(BF)

    acc = dot_tn(act_ref[...], row_ref[...])
    if own:
        acc = acc + refs[3][...].astype(F32)
    out_ref[...] = acc.astype(out_ref.dtype)


def grad_second(c, order, place, rows, col, act, add=None):
    own = add is not None
    args = [rows, col, act]
    specs = [
        pl.BlockSpec((c.CR, c.half), lambda i, s: (0, 0 if own else 1)),
        whole(col),
        cols_of((c.CR, c.fblk)),
    ]
    if own:
        args.append(add)
        specs.append(rows_of((c.fblk, c.half)))
    out = shape_of((c.F, c.half), F32 if own else BF)
    return call(
        order,
        functools.partial(grad_second_body, c, own),
        place,
        args,
        specs,
        [out],
        [rows_of((c.fblk, c.half))],
        (c.F // c.fblk,),
        [pltpu.VMEM((c.CR, c.half), BF)],
        name="grad_second",
    )[0]


def grad_first_body(c, own, place, *refs):
    acc = dot_tn(refs[0][...], refs[1][...])
    if own:
        acc = acc + refs[2][...].astype(F32)
    refs[-1][...] = acc.astype(refs[-1].dtype)


def grad_first(c, order, place, rows, gp, add=None):
    own = add is not None
    args = [rows, gp]
    specs = [
        pl.BlockSpec((c.CR, c.half), lambda i, s: (0, 0 if own else 1)),
        cols_of((c.CR, c.fblk)),
    ]
    if own:
        args.append(add)
        specs.append(cols_of((c.half, c.fblk)))
    out = shape_of((c.half, c.F), F32 if own else BF)
    return call(
        order,
        functools.partial(grad_first_body, c, own),
        place,
        args,
        specs,
        [out],
        [cols_of((c.half, c.fblk))],
        (c.F // c.fblk,),
        name="grad_first",
    )[0]


def combine_body(c, with_dots, place, *refs):
    refs = list(refs)
    rows_ref = refs.pop(0)
    tail_ref = refs.pop(0) if with_dots else None
    mine_ref = refs.pop(0)
    groups = [(0, g) for g in groups_a(c)] + [(1, g) for g in groups_b(c)]
    outs, (hot_ref, row_ref) = refs[: len(groups)], refs[len(groups) :]
    pad = hot_ref.shape[2] // c.X

    @pl.when(pl.program_id(0) == 0)
    def _():
        row_ref[...] = jnp.zeros_like(row_ref)
        slots = lax.broadcasted_iota(I32, (c.R, pad), 1)
        expert = lax.broadcasted_iota(I32, (c.E, 1), 0)
        for k in range(c.n):
            at = pl.multiple_of((place[1] ^ k) * c.R, 16)
            pulls = jnp.zeros((c.E, c.R), F32)
            for j in range(c.X):
                hot = (mine_ref[pl.ds(at, c.R), j : j + 1] == slots).astype(BF)
                hot_ref[k, :, j * pad : (j + 1) * pad] = hot
                if with_dots:
                    high, low = last_pair(c, tail_ref[j], pad)
                    both = jnp.concatenate(
                        [jnp.broadcast_to(high, (8, pad)), jnp.broadcast_to(low, (8, pad))], axis=0
                    )
                    got = dot_nt(both.astype(BF), hot)
                    got = got[0:1, :] + got[8:9, :]
                    pulls = jnp.where(expert == expert_of(c, place, j), got, pulls)
            if with_dots:
                for (side, group), out_ref in zip(groups, outs):
                    if side == 0 and k in group:
                        at = group.index(k)
                        out_ref[at, c.R :, :] = jnp.zeros((c.E, c.half), BF)
                        out_ref[at, c.R :, : c.R] = pulls.astype(BF)

    for j in range(c.X):
        row_ref[j * pad : j * pad + c.SP, :] = rows_ref[j]
    for half in range(2):

        @pl.when(pl.program_id(0) == half)
        def _():
            for (side, group), out_ref in zip(groups, outs):
                if side == half:
                    for at, k in enumerate(group):
                        out_ref[at, : c.R, :] = dot_nn(hot_ref[k], row_ref[...]).astype(BF)


def combine(c, order, place, rows, mine, with_dots=False):
    pad = up(c.SP, 128)
    args = [rows]
    specs = [pl.BlockSpec((c.X, c.SP, c.half), lambda i, s: (0, 0, i ^ s[2]))]
    if with_dots:
        args.append(rows)
        specs.append(pl.BlockSpec((c.X, 16, c.half), lambda i, s: (0, c.SP // 16 - 1, 0)))
    args.append(mine)
    specs.append(whole(mine))
    outs = piece_outs(c, c.E if with_dots else 0)
    result = call(
        order,
        functools.partial(combine_body, c, with_dots),
        place,
        args,
        specs,
        outs,
        [whole(o, 1) for o in outs],
        (2,),
        [pltpu.VMEM((c.n, c.R, c.X * pad), BF), pltpu.VMEM((c.X * pad, c.half), BF)],
        name="combine",
    )
    return list(result)


def back_two_body(c, place, *refs):
    refs = list(refs)
    count = (len(refs) - 11 - c.n) // 2
    a, b, refs = refs[:count], refs[count : 2 * count], refs[2 * count :]
    w_ref, after_ref, probs_ref, keep_ref, weight_ref, cot_ref, hid_ref, small_ref = refs[:8]
    ga_ref, gb_ref, sums_ref = refs[8:11]
    mixes = refs[11:]
    sum_a = add_up(a)
    live = live_rows(c, place[1] * c.R, c.R)
    cot = jnp.where(live, cot_ref[...], BF(0))
    eshift = small_ref[6 : 6 + c.E, :]
    router = small_ref[6 + c.E : 6 + 2 * c.E, :]
    kept = keep_ref[...] > 0
    pulls = jnp.where(kept, sum_a[c.R :, : c.R] + dot_nt(eshift, cot), 0.0)
    probs = probs_ref[...]
    glog = (probs * (pulls - jnp.sum(probs * pulls, axis=0, keepdims=True))).astype(BF)
    two = jnp.concatenate([sum_a[: c.R], add_up(b)], axis=1) + dot_tn(glog, router)
    normed, inv_std = norm_rows(after_ref[...])
    grad_after = cot.astype(F32) + norm_back(two, small_row(c, small_ref, 1), normed, inv_std)
    ga_ref[...] = grad_after
    low = grad_after.astype(BF)
    gb_ref[...] = low
    high, rest = split_low(weight_ref[...])
    hid = jnp.where(live, hid_ref[...], BF(0))
    sums_ref[0:1, :] = jnp.sum(two * normed, axis=0, keepdims=True)
    sums_ref[1:2, :] = jnp.sum(two, axis=0, keepdims=True)
    sums_ref[2:3, :] = jnp.sum(low.astype(F32), axis=0, keepdims=True)
    sums_ref[3:8, :] = jnp.zeros((5, c.D), F32)
    sums_ref[8 : 8 + c.E, :] = dot_nn(high, cot) + dot_nn(rest, cot)
    sums_ref[8 + c.E : 8 + 2 * c.E, :] = dot_nn(glog, hid)
    for k in range(c.n):
        lane = place[1] ^ k
        mix = dot_nt(gb_ref[:, : c.half], w_ref[2 * lane])
        mix = mix + dot_nt(gb_ref[:, c.half :], w_ref[2 * lane + 1])
        mixes[k][...] = mix.astype(BF)


def back_two(c, order, place, sums, proj, lanes, cotangent, hidden, small):
    args = [*sums[0], *sums[1], proj, *lanes, cotangent, hidden, small]
    lane_rows = pl.BlockSpec((c.R, c.D), lambda i, s: (s[1], 0))
    specs = [first_block(a) for a in [*sums[0], *sums[1]]]
    specs += [whole(a) for a in [proj, *lanes]] + [lane_rows, lane_rows, whole(small)]
    outs = [
        shape_of((c.R, c.D), F32),
        shape_of((c.R, c.D), BF),
        shape_of((8 + 2 * c.E, c.D), F32),
    ] + [shape_of((c.R, c.W), BF) for _ in range(c.n)]
    result = call(
        order,
        functools.partial(back_two_body, c),
        place,
        args,
        specs,
        outs,
        [whole(o) for o in outs],
        (1,),
        name="back_two",
    )
    return (*result[:3], list(result[3:]))


def block_out_body(c, place, *refs):
    refs = list(refs)
    count = (len(refs) - 4) // 2
    a, b, refs = refs[:count], refs[count : 2 * count], refs[2 * count :]
    after_ref, weight_ref, small_ref, out_ref = refs
    high, low = split_low(weight_ref[...])
    eshift = small_ref[6 : 6 + c.E, :]
    shift = dot_tn(high, eshift) + dot_tn(low, eshift)
    for h, pieces in enumerate((a, b)):
        cols = slice(h * c.half, (h + 1) * c.half)
        out_ref[h] = (after_ref[:, cols] + add_up(pieces) + shift[:, cols]).astype(BF)


def block_out(c, order, place, sums, after, weight, small):
    args = [*sums[0], *sums[1], after, weight, small]
    out = shape_of((2, c.R, c.half), BF)
    return call(
        order,
        functools.partial(block_out_body, c),
        place,
        args,
        [first_block(a) for a in args[:-3]] + [whole(a) for a in args[-3:]],
        [out],
        [whole(out)],
        (1,),
        name="block_out",
    )[0]


def grad_proj_body(c, place, *refs):
    groups = groups_of(c)
    count = c.n * len(groups)
    mixes, (gb_ref, sums_ref, own_ref, oth_ref) = refs[:count], refs[count:]
    height = sums_ref.shape[0]
    slot = [0, 2, 1, 3] if c.n == 4 else [place[1] ^ k for k in range(c.n)]
    for cols, out_ref in ((own_cols(c, place), own_ref), (other_cols(c, place), oth_ref)):
        out_ref[...] = jnp.zeros_like(out_ref)
        sums = sums_ref[:, cols].astype(BF)
        for k in range(c.n):
            for group, (at, lanes) in enumerate(groups):
                part = dot_tn(mixes[k * len(groups) + group][...], gb_ref[:, cols])
                out_ref[slot[k], at : at + lanes, :] = part.astype(BF)
            out_ref[slot[k], c.W : c.W + height, :] = sums


def grad_proj(c, order, place, mixes, grad_branch, sums):
    rows = up(c.W + sums.shape[0], 16 * c.X)
    specs = [
        pl.BlockSpec((None, c.R, a.shape[2]), lambda i, s, at=at: (at, s[1], 0))
        for a, at in flat(mixes)
    ]
    outs = [shape_of((c.n, rows, c.half), BF)] * 2
    return call(
        order,
        functools.partial(grad_proj_body, c),
        place,
        [pair[0] for pair in flat(mixes)] + [grad_branch, sums],
        specs + [whole(grad_branch), whole(sums)],
        outs,
        [whole(o) for o in outs],
        (1,),
        name="grad_proj",
    )


def grad_one_body(c, place, dqkv_ref, normed_ref, own_ref, oth_ref, *outs):
    sums_ref = outs[-1]
    groups = [(0, g) for g in groups_a(c)] + [(1, g) for g in groups_b(c)]
    for side in range(2):
        cols = slice(side * c.half, (side + 1) * c.half)
        weights = [jnp.where(place[2] == side, own_ref[p], oth_ref[p]) for p in range(3)]
        gain = jnp.zeros((1, c.half), F32)
        shift = jnp.zeros((1, c.half), F32)
        for (where, group), out_ref in zip(groups, outs):
            if where != side:
                continue
            for row, k in enumerate(group):
                rows_at = pl.ds(pl.multiple_of((place[1] ^ k) * c.R, 16), c.R)
                acc = None
                for part in range(3):
                    rows = dqkv_ref[rows_at, part * c.W : (part + 1) * c.W]
                    term = dot_nt(rows, weights[part])
                    acc = term if acc is None else acc + term
                out_ref[row, : c.R, :] = acc.astype(BF)
                normed = normed_ref[rows_at, cols].astype(F32)
                gain = gain + jnp.sum(acc * normed, axis=0, keepdims=True)
                shift = shift + jnp.sum(acc, axis=0, keepdims=True)
        sums_ref[0:1, cols] = gain
        sums_ref[1:2, cols] = shift
        row = lax.broadcasted_iota(I32, (16, 1), 0)
        tile = jnp.where(row == 0, gain, jnp.where(row == 1, shift, 0.0)).astype(BF)
        for (where, group), out_ref in zip(groups, outs):
            if where == side:
                for at in range(len(group)):
                    out_ref[at, c.R :, :] = tile


def grad_one(c, order, place, dqkv, normed, own_w, oth_w):
    outs = piece_outs(c, 16, 16) + [shape_of((2, c.D), F32)]
    result = call(
        order,
        functools.partial(grad_one_body, c),
        place,
        [dqkv, normed, own_w, oth_w],
        [whole(dqkv), whole(normed), whole(own_w), whole(oth_w)],
        outs,
        [whole(o) for o in outs],
        (1,),
        name="grad_one",
    )
    return list(result[:-1]), result[-1]


def grad_qkv_body(c, own, place, *refs):
    hid_ref, dqkv_ref = refs[:2]
    add_ref = refs[2] if own else None
    out_ref = refs[-1]
    acc = dot_tn(hid_ref[...], dqkv_ref[...])
    if own:
        acc = acc + add_ref[0].astype(F32)
    out_ref[0] = acc.astype(BF)


def grad_qkv(c, order, place, hidden, dqkv, add=None):
    own = add is not None
    args = [hidden, dqkv]
    specs = [
        pl.BlockSpec((c.TP, c.half), lambda i, s: (0, s[2] if own else 1 - s[2])),
        cols_of((c.TP, c.W)),
    ]
    if c.W % 128:
        dqkv = dqkv.reshape(c.TP, 3, c.W).transpose(1, 0, 2)
        args[1] = dqkv
        specs[1] = pl.BlockSpec((None, c.TP, c.W), lambda i, s: (i, 0, 0))
    if own:
        args.append(add)
        specs.append(rows_of((1, c.half, c.W)))
    out = shape_of((3, c.half, c.W), BF)
    return call(
        order,
        functools.partial(grad_qkv_body, c, own),
        place,
        args,
        specs,
        [out],
        [rows_of((1, c.half, c.W))],
        (3,),
        name="grad_qkv",
    )[0]


def back_one_body(c, place, *refs):
    refs = list(refs)
    count = (len(refs) - 5) // 2
    a, b, refs = refs[:count], refs[count : 2 * count], refs[2 * count :]
    tok_ref, after_ref, small_ref, out_ref, sums_ref = refs
    live = live_rows(c, place[1] * c.R, c.R)
    normed, inv_std = norm_rows(jnp.where(live, tok_ref[...].astype(F32), 0.0))
    one = jnp.concatenate([add_up(a)[: c.R], add_up(b)[: c.R]], axis=1)
    grad = after_ref[...] + norm_back(one, small_row(c, small_ref, 0), normed, inv_std)
    for h in range(2):
        out_ref[h] = grad[:, h * c.half : (h + 1) * c.half].astype(BF)
    for h, refs in enumerate((a, b)):
        tiles = [ref[c.R :, :].astype(F32) for ref in refs]
        pair = (tiles[0] + tiles[1]).astype(BF).astype(F32)
        for tile in tiles[2:]:
            pair = pair + tile
        sums_ref[:, h * c.half : (h + 1) * c.half] = pair[0:2]


def back_one(c, order, place, sums, tokens, after, small):
    args = [*sums[0], *sums[1], tokens, after, small]
    lane_rows = pl.BlockSpec((c.R, c.D), lambda i, s: (s[1], 0))
    specs = [first_block(a) for a in args[:-3]] + [lane_rows, whole(after), whole(small)]
    outs = [shape_of((2, c.R, c.half), BF), shape_of((2, c.D), F32)]
    return call(
        order,
        functools.partial(back_one_body, c),
        place,
        args,
        specs,
        outs,
        [whole(o) for o in outs],
        (1,),
        name="back_one",
    )


def assemble_body(c, place, *refs):
    pieces, out_ref = refs[:-1], refs[-1]
    for k in range(c.n):

        @pl.when((place[1] ^ k) == pl.program_id(0))
        def _():
            for h in range(2):
                values = pieces[2 * k + h][...].astype(out_ref.dtype)
                out_ref[:, h * c.half : (h + 1) * c.half] = values


def assemble(c, order, place, pieces, dtype):
    out = shape_of((c.T, c.D), dtype)
    return call(
        order,
        functools.partial(assemble_body, c),
        place,
        [pair[0] for pair in flat(pieces)],
        [
            pl.BlockSpec((None, c.R, c.half), lambda i, s, at=at: (at, 0, 0))
            for _, at in flat(pieces)
        ],
        [out],
        [rows_of((c.R, c.D))],
        (-(-c.T // c.R),),
        name="assemble",
    )[0]


def local(
    tokens,
    cotangent,
    w_qkv,
    qv_bias,
    w_proj,
    proj_bias,
    norm_gains,
    norm_shifts,
    w_router,
    expert_shift,
    w_first,
    w_second,
    first_bias,
    routes,
    priority,
):
    T, D = tokens.shape
    n = lax.axis_size("mp")
    E = w_router.shape[1]
    S = 16 * T // (5 * E)
    R = up(-(-T // n), 16)
    F = w_first.shape[2]
    W = w_proj.shape[0]
    win = up(IMG_LEN + 15, 16)
    SP = up(S + 17, 16)
    cap = (9 * T + 4 * EXP_DEV - 1) // (4 * EXP_DEV)
    c = Sizes(
        T=T,
        D=D,
        half=D // 2,
        n=n,
        X=E // EXP_DEV,
        E=E,
        S=S,
        SP=SP,
        CR=up(cap, 128),
        R=R,
        TP=n * R,
        W=W,
        images=T // IMG_LEN,
        quarters=n // EXP_DEV,
        F=F,
        cap=cap,
        win=win,
        fblk=min(1024, F),
        key=4 * T,
    )
    order = Order()
    dp, mp, grid = lax.axis_index("dp"), lax.axis_index("mp"), lax.axis_index("grid")
    here = jnp.stack([dp, mp, grid, mp // c.quarters]).astype(I32)

    experts = jnp.arange(E, dtype=I32)[:, None, None]
    count = jnp.sum((routes.T[None] == experts).astype(I32), axis=(1, 2))[None]
    counts = trade(jnp.broadcast_to(count, (c.X, E)), "dp")
    slot, rt = route(c, order, here, routes, priority)
    place, offsets = windows(c, order, here, counts)
    grad_out = dispatch(c, order, place, slot, cotangent)
    grad_in = trade(grad_out, "dp")

    bias_rows = F // 2 // c.half
    packed = jnp.concatenate(
        [
            norm_gains,
            norm_shifts,
            proj_bias[None],
            jnp.pad(qv_bias, ((0, 0), (0, c.half - W))),
            expert_shift,
            w_router.T,
            first_bias.reshape(bias_rows, c.half),
        ],
        axis=0,
    )
    packed = jnp.pad(packed, ((0, up(packed.shape[0], 16) - packed.shape[0]), (0, 0)))
    packed_oth = swap_grid(packed)
    small = jnp.where(
        grid == 0,
        jnp.concatenate([packed, packed_oth], axis=1),
        jnp.concatenate([packed_oth, packed], axis=1),
    )
    bias = small[6 + 2 * E : 6 + 2 * E + bias_rows].reshape(bias_rows, 2, c.half)
    bias = bias.transpose(1, 0, 2).reshape(1, F).astype(F32)
    qkv_own = w_qkv.transpose(1, 0, 2)
    qkv_oth = swap_grid(qkv_own)
    first_own = w_first[0]
    second_own = w_second[0]
    proj_tied, second_tied, first_tied, _ = lax.optimization_barrier(
        (w_proj, second_own, first_own, grad_out)
    )
    proj = lax.all_gather(proj_tied, ("mp", "grid"))
    second_oth = swap_grid(second_tied)
    first_oth = swap_grid(first_tied)

    outs = [shape_of((c.TP, D), BF), shape_of((c.TP, 3 * W), BF), shape_of((c.TP, D), BF)]
    hidden_one, qkv, normed_one = call(
        order,
        functools.partial(qkv_body, c),
        place,
        [tokens, small, qkv_own, qkv_oth],
        [rows_of((c.R, D)), whole(small), whole(qkv_own), whole(qkv_oth)],
        outs,
        [rows_of((c.R, D)), rows_of((c.R, 3 * W)), rows_of((c.R, D))],
        (n,),
        name="qkv",
    )
    groups = groups_of(c)
    out = shape_of((len(groups), c.TP, groups[0][1]), BF)
    mix = call(
        order,
        functools.partial(attend_body, c),
        place,
        [qkv],
        [whole(qkv)],
        [out],
        [whole(out)],
        (c.images,),
        name="attend",
    )[0]
    mixes = gather_mp(c, mix)
    hidden_two, weight, mine, keep, after, probs, keep_lane, weight_lane = middle(
        c, order, place, mixes, proj, tokens, small, offsets, slot, rt
    )
    keep_mask = keep[:, :2, :].transpose(0, 2, 1).reshape(c.TP, 2)[:T].astype(I32)
    mine = mine.transpose(0, 2, 1).reshape(c.TP, 8)

    rows_in = trade(dispatch(c, order, place, slot, hidden_two, weight), "dp")
    ga, grad_all = grad_active(c, order, place, grad_in, second_own, second_oth)
    act, gp, gb, row_all, col, back = expert(
        c, order, place, rows_in, first_own, first_oth, bias, ga
    )
    back = trade(back, "dp")
    second_part = swap_grid(grad_second(c, order, place, grad_all, col, act))
    first_part = swap_grid(grad_first(c, order, place, row_all, gp))
    gb = gb[0:1].reshape(2, F // 2)
    gb_own = lax.dynamic_index_in_dim(gb, grid, 0, True)
    gb_oth = lax.dynamic_index_in_dim(gb, 1 - grid, 0, True)
    grad_fbias = gb_own + swap_grid(gb_oth)
    prod = produce(c, order, place, col, act, second_own, second_oth)

    two_sums = reduce_mp(c, combine(c, order, place, back, mine, True))
    prod = trade(prod, "dp")
    grad_second_out = grad_second(c, order, place, grad_all, col, act, second_part)
    grad_first_out = grad_first(c, order, place, row_all, gp, first_part)
    grad_after, grad_branch, sums_two, grad_mix = back_two(
        c,
        order,
        place,
        two_sums,
        proj,
        [after, probs, keep_lane, weight_lane],
        cotangent,
        hidden_two,
        small,
    )
    grad_mix = [grad_mix[0]] + [swap_mp(c, grad_mix[k], k) for k in range(1, n)]
    proj_a, proj_b = grad_proj(c, order, place, mixes, grad_branch, sums_two)

    outs = [shape_of((c.TP, 3 * W), BF), shape_of((8, 3 * W), F32)]
    dqkv, dqkv_sums = call(
        order,
        functools.partial(attend_back_body, c),
        place,
        [qkv, *grad_mix],
        [whole(qkv)] + [whole(p) for p in grad_mix],
        outs,
        [whole(o) for o in outs],
        (c.images,),
        [pltpu.VMEM((c.TP, W), BF)],
        name="attend_back",
    )
    one_pieces, one_parts = grad_one(c, order, place, dqkv, normed_one, qkv_own, qkv_oth)
    one_sums = reduce_mp(c, one_pieces)
    qkv_part = swap_grid(grad_qkv(c, order, place, hidden_one, dqkv))
    grad_w_qkv = grad_qkv(c, order, place, hidden_one, dqkv, qkv_part)
    grad_w_qkv = sum_dp(c, grad_w_qkv.reshape(3 * c.half, W)).reshape(3, c.half, W)
    prod_pieces = combine(c, order, place, prod, mine)
    grad_low, sums_one = back_one(c, order, place, one_sums, tokens, grad_after, small)
    grad_low = gather_mp(c, grad_low)
    out_sums = reduce_mp(c, prod_pieces)
    out_lane = block_out(c, order, place, out_sums, after, weight_lane, small)
    out_lane = gather_mp(c, out_lane)

    proj_low = (proj_a.astype(F32) + swap_grid(proj_b).astype(F32)).astype(BF)
    proj_sum = sum_dp(c, sum_proj(c, proj_low))
    rest = proj_sum[W : W + 8 + 2 * E]
    qv_rows = jnp.concatenate([dqkv_sums[0:1, :W], dqkv_sums[0:1, 2 * W :]], axis=0)
    if n != 4:
        sums_one = fold(c, one_parts, (("mp", n),))
    sums_one = finish_sums(c, sums_one, qv_rows, grid)
    grad_tokens = assemble(c, order, place, grad_low, F32)
    block = assemble(c, order, place, out_lane, BF)
    return (
        block,
        grad_tokens,
        grad_w_qkv.transpose(1, 0, 2),
        sums_one[2:3, :W],
        proj_sum[:W],
        rest[2],
        jnp.stack([sums_one[0], rest[0]]),
        jnp.stack([sums_one[1], rest[1]]),
        rest[8 + E : 8 + 2 * E].T,
        rest[8 : 8 + E],
        grad_first_out[None],
        grad_second_out[None],
        grad_fbias,
        keep_mask,
    )


def solution(mesh):
    return jax.shard_map(
        local,
        mesh=mesh,
        in_specs=(
            P(("dp", "grid"), None),
            P(("dp", "grid"), None),
            P("grid", None, "mp"),
            P("grid", "mp"),
            P("mp", "grid"),
            P("grid"),
            P(None, "grid"),
            P(None, "grid"),
            P("grid", None),
            P(None, "grid"),
            P(("dp", "mp"), "grid", None),
            P(("dp", "mp"), None, "grid"),
            P(("dp", "mp"), "grid"),
            P(("dp", "grid"), None),
            P(("dp", "grid"), None),
        ),
        out_specs=(
            P(("dp", "grid"), None),
            P(("dp", "grid"), None),
            P("grid", None, "mp"),
            P("grid", "mp"),
            P("mp", "grid"),
            P("grid"),
            P(None, "grid"),
            P(None, "grid"),
            P("grid", None),
            P(None, "grid"),
            P(("dp", "mp"), "grid", None),
            P(("dp", "mp"), None, "grid"),
            P(("dp", "mp"), "grid"),
            P(("dp", "grid"), None),
        ),
        check_vma=False,
    )
```

time: 1310 us -> 599 us (0.46)
  waiting for transfers between devices: 503 us -> 189 us
  local copies, waits for them, and re-layouts: 312 us -> 28 us
  Pallas kernels: 0 us -> 264 us
  matrix products: 194 us -> 0 us
  other arithmetic: 188 us -> 23.5 us
  blocking collectives: 65.6 us -> 0 us
  starting transfers between devices: 18.2 us -> 73.2 us
    psum x4 -> x0, waiting for transfers between devices: 296 us -> none  [the longest x1 108 us: local(): lax.psum(jnp.dot(head_mix, proj_full, preferred_element_type=jnp.float32)...]
    pallas_call x0 -> x26, Pallas kernels: none -> 264 us  [call(): pl.pallas_call(wrapped, grid_spec=pltpu.PrefetchScalarGridSpec(num_scalar...]
    dot_general x25 -> x0, matrix products: 194 us -> none  [the longest x1 32.5 us: local(): jnp.einsum('rxd,xfd->rxf', grad_in, second_full, preferred_element_type=j...]
    ppermute x0 -> x41, waiting for transfers between devices: none -> 111 us  [the longest x29 107 us: swap_mp(): return lax.ppermute(value, 'mp', [(i, i ^ mask) for i in range(c.n)])]
    reduce_sum x18 -> x3, other arithmetic: 80.8 us -> 3.16 us  [the longest x2 2.31 us: sum_dp(): total = jnp.sum(parts.astype(F32), axis=0).astype(BF)]
    all_to_all x4 -> x9, waiting for transfers between devices: 151 us -> 77.4 us  [trade(): return lax.all_to_all(value, axis, split_axis=0, concat_axis=0, tiled=True)]
    gather x6 -> x0, local copies, waits for them, and re-layouts: 54.7 us -> none  [the longest x1 17.3 us: local(): jnp.take(returned_flat, return_index, axis=0)]
    reduce_scatter x6 -> x0, waiting for transfers between devices: 50.5 us -> none  [the longest x1 14.9 us: local(): lax.psum_scatter(grad_second.astype(jnp.bfloat16), 'grid', scatter_dimens...]
  transfers between devices with their start and end apart: 20 -> 51, of which waited for: 14 -> 16; matrix products, arithmetic and copies ran while one was open for 33% -> 6% of each run, Pallas kernels for 0% -> 36%
where the time goes in v1:
time: 599 us; the launch traced here: 593 us
  Pallas kernels  264 us (44%)
  waiting for transfers between devices  189 us (32%)
  starting transfers between devices  73.2 us (12%)
  local copies, waits for them, and re-layouts  28 us (5%)
  other arithmetic  23.5 us (4%)
  between operations  14.9 us (2%)
    pallas_call x26, Pallas kernels, call(): pl.pallas_call(wrapped, grid_spec=pltpu.PrefetchScalarGridSpec(num_scalar...  264 us
    ppermute x29, waiting for transfers between devices, swap_mp(): return lax.ppermute(value, 'mp', [(i, i ^ mask) for i in range(c.n)])  107 us
    all_to_all x9, waiting for transfers between devices, trade(): return lax.all_to_all(value, axis, split_axis=0, concat_axis=0, tiled=True)  77.4 us
    all_to_all x9, starting transfers between devices, trade(): return lax.all_to_all(value, axis, split_axis=0, concat_axis=0, tiled=True)  39.6 us
    ppermute x29, starting transfers between devices, swap_mp(): return lax.ppermute(value, 'mp', [(i, i ^ mask) for i in range(c.n)])  31.5 us
  transfers between devices with their start and end apart: 51, of which 16 were waited for; matrix products, arithmetic and copies ran while one was open for 6% of the time, Pallas kernels for 36%

profile of v1, /device:TPU:0, one launch (start us, length us, event | category | flops | bytes accessed | tf_op | source)
XLA Modules:
  0.0 593.0 jit_solution(5109141304043374250)
XLA Ops:
  8.6 6.3 %all-to-all-start = ((s32[4,1,16]{2,1,0:T(1,128)}), s32[4,1,16]{2,1,0:T(1,128)S(1)}, u32[]{:S(2)}, u32[]{:S(2)}) async-start(s32[4,1,16]{2,1,0:T(1,128)} %broadcast_in_dim.12), calls=%async_computation | async-start | bytes 4096 | tf_op jit(solution)/shard_map/all_to_all | solution.py:123
  19.4 8.9 %route.1 = (s32[4,16,400]{2,1,0:T(8,128)}, s32[4,8,400]{2,1,0:T(8,128)}) custom-call(s32[4]{0:T(128)} %pad_add_fusion.place, s32[2,1600]{1,0:T(2,128)} %pad.26.refs_0_, s32[1600,2]{1,0:T(8,128)} %pad.27.refs_1_, s32[2,1600]{1,0:T(2,128)} %pad.28.refs_2_), custom_call_target="tpu_custom_call" | custom-call | flops 1000 | bytes 1000 | tf_op jit(solution)/shard_map/route/pallas_call | solution.py:94
  31.0 10.1 %dispatch.2.refs_4_ = bf16[4,336,1024]{2,1,0:T(8,128)(2,1)} custom-call(s32[32]{0:T(128)} %get-tuple-element.67.place.refs_2_, s32[4,16,400]{2,1,0:T(8,128)} %get-tuple-element.68.refs_0_.refs_12_, bf16[1576,1024]{1,0:T(8,128)(2,1)} %refs_11_.1, s32[32]{0:T(128)} %get-tuple-element.67.place.refs_2_), custom_call_target="tpu_custom_call" | custom-call | flops 1000 | bytes 1000 | tf_op jit(solution)/shard_map/dispatch/pallas_call | solution.py:94
  51.1 10.8 %qkv.1 = (bf16[1600,1024]{1,0:T(8,128)(2,1)}, bf16[1600,768]{1,0:T(8,128)(2,1)}, bf16[1600,1024]{1,0:T(8,128)(2,1)}) custom-call(s32[32]{0:T(128)} %get-tuple-element.67.place.refs_2_, bf16[1576,1024]{1,0:T(8,128)(2,1)} %refs_6_.1, bf16[48,1024]{1,0:T(8,128)(2,1)} %maximum_select_fusion.refs_1_.refs_10_.refs_13_.refs_8_, bf16[3,512,256]{2,1,0:T(8,128)(2,1)} %bitcast.45, ...), custom_call_target="tpu_custom_call" | custom-call | flops 1000 | bytes 1000 | tf_op jit(solution)/shard_map/qkv/pallas_call | solution.py:94
  61.9 10.8 %attend.1.refs_0_.refs_1_.refs_14_ = bf16[2,1600,128]{2,1,0:T(8,128)(2,1)} custom-call(s32[32]{0:T(128)} %get-tuple-element.67.place.refs_2_, bf16[1600,768]{1,0:T(8,128)(2,1)} %get-tuple-element.69.refs_0_.refs_1_, bf16[1600,768]{1,0:T(8,128)(2,1)} %get-tuple-element.69.refs_0_.refs_1_), custom_call_target="tpu_custom_call" | custom-call | flops 1000 | bytes 1000 | tf_op jit(solution)/shard_map/attend/pallas_call | solution.py:94
  75.8 18.7 %collective-permute-done.2.refs_2_.refs_3_ = bf16[2,1600,128]{2,1,0:T(8,128)(2,1)S(1)} collective-permute-done((bf16[2,1600,128]{2,1,0:T(8,128)(2,1)}, bf16[2,1600,128]{2,1,0:T(8,128)(2,1)S(1)}, u32[]{:S(2)}, u32[]{:S(2)}) %collective-permute-start.2) | collective-permute-done | bytes 819232 | tf_op jit(solution)/shard_map/ppermute | solution.py:115
  97.2 8.6 %collective-permute-done.4.refs_6_ = bf16[1,1600,128]{2,1,0:T(8,128)(2,1)S(1)} collective-permute-done((bf16[1,1600,128]{2,1,0:T(8,128)(2,1)S(1)}, bf16[1,1600,128]{2,1,0:T(8,128)(2,1)S(1)}, u32[]{:S(2)}, u32[]{:S(2)}) %collective-permute-start.4) | collective-permute-done | bytes 409632 | tf_op jit(solution)/shard_map/ppermute | solution.py:115
  107.8 14.8 %middle.1 = (bf16[1600,1024]{1,0:T(8,128)(2,1)}, f32[4,16,400]{2,1,0:T(8,128)}, s32[4,8,400]{2,1,0:T(8,128)}, f32[4,8,400]{2,1,0:T(8,128)}, f32[400,1024]{1,0:T(...) custom-call(s32[32]{0:T(128)} %get-tuple-element.67.place.refs_2_, ...), custom_call_target="tpu_custom_call" | custom-call | flops 1000 | bytes 1000 | tf_op jit(solution)/shard_map/middle/pallas_call | solution.py:94
  122.6 13.0 %dispatch.3.refs_3_ = bf16[4,336,1024]{2,1,0:T(8,128)(2,1)} custom-call(s32[32]{0:T(128)} %get-tuple-element.67.place.refs_2_, s32[4,16,400]{2,1,0:T(8,128)} %get-tuple-element.68.refs_0_.refs_12_, bf16[1600,1024]{1,0:T(8,128)(2,1)} %get-tuple-element.72.refs_1_.refs_12_, f32[4,16,400]{2,1,0:T(8,128)} %get-tuple-element.73.refs_2_, ...), custom_call_target="tpu_custom_call" | custom-call | flops 1000 | bytes 1000 | tf_op jit(solution)/shard_map/dispatch/pallas_call | solution.py:94
  142.0 13.6 %grad_active.1 = (bf16[896,4096]{1,0:T(8,128)(2,1)}, bf16[896,1024]{1,0:T(8,128)(2,1)}) custom-call(s32[32]{0:T(128)} %get-tuple-element.67.place.refs_2_, bf16[4,336,1024]{2,1,0:T(8,128)(2,1)} %all-to-all-done.2.refs_0_, bf16[4096,512]{1,0:T(8,128)(2,1)} %bitcast.8.refs_1_.refs_2_, bf16[4096,512]{1,0:T(8,128)(2,1)} %collective-permute-done.7.refs_2_.refs_3_, ...), custom_call_target="tpu_custom_call" | custom-call | flops 1000 | bytes 1000 | tf_op jit(solution)/shard_map/grad_active/pallas_call | solution.py:94
  155.5 46.2 %all-to-all-done.1.refs_0_ = bf16[4,336,1024]{2,1,0:T(8,128)(2,1)S(1)} async-done(((bf16[4,336,1024]{2,1,0:T(8,128)(2,1)}), bf16[4,336,1024]{2,1,0:T(8,128)(2,1)S(1)}, u32[]{:S(2)}, u32[]{:S(2)}) %all-to-all-start.1) | async-done | bytes 2752544 | tf_op jit(solution)/shard_map/all_to_all | solution.py:123
  203.3 32.7 %expert.1 = (bf16[896,4096]{1,0:T(8,128)(2,1)}, bf16[896,4096]{1,0:T(8,128)(2,1)}, f32[8,4096]{1,0:T(8,128)}, bf16[896,1024]{1,0:T(8,128)(2,1)}, f32[896,128]{1,0:T(8,128)}, /*index=5*/bf16[4,336,1024]{2,1,0:T(8,128)(2,1)}) custom-call(s32[32]{0:T(128)} %get-tuple-element.67.place.refs_2_, bf16[4,336,1024]{2,1,0:T(8,128)(2,1)} %copy-done.3, ...), custom_call_target="tpu_custom_call" | custom-call | flops 1000 | bytes 1000 | tf_op jit(solution)/shard_map/expert/pallas_call | solution.py:94
  240.1 9.6 %grad_second.2.refs_2_ = bf16[4096,512]{1,0:T(8,128)(2,1)} custom-call(s32[32]{0:T(128)} %get-tuple-element.67.place.refs_2_, bf16[896,1024]{1,0:T(8,128)(2,1)} %get-tuple-element.78.refs_5_.refs_0_, f32[896,128]{1,0:T(8,128)} %get-tuple-element.79.refs_1_.refs_0_, bf16[896,4096]{1,0:T(8,128)(2,1)} %get-tuple-element.80.refs_2_.refs_1_, ...), custom_call_target="tpu_custom_call" | custom-call | flops 1000 | bytes 1000 | tf_op jit(solution)/shard_map/grad_second/pallas_call | solution.py:94
  249.8 9.4 %grad_first.2.refs_4_ = bf16[512,4096]{1,0:T(8,128)(2,1)} custom-call(s32[32]{0:T(128)} %get-tuple-element.67.place.refs_2_, bf16[896,1024]{1,0:T(8,128)(2,1)} %get-tuple-element.81.refs_0_, bf16[896,4096]{1,0:T(8,128)(2,1)} %get-tuple-element.82.refs_1_, bf16[4096,512]{1,0:T(8,128)(2,1)} %grad_second.2.refs_2_), custom_call_target="tpu_custom_call" | custom-call | flops 1000 | bytes 1000 | tf_op jit(solution)/shard_map/grad_first/pallas_call | solution.py:94
  260.8 13.7 %produce.1.refs_3_ = bf16[4,336,1024]{2,1,0:T(8,128)(2,1)} custom-call(s32[32]{0:T(128)} %get-tuple-element.67.place.refs_2_, f32[896,128]{1,0:T(8,128)} %get-tuple-element.79.refs_1_.refs_0_, bf16[896,4096]{1,0:T(8,128)(2,1)} %get-tuple-element.80.refs_2_.refs_1_, bf16[4096,512]{1,0:T(8,128)(2,1)} %bitcast.8.refs_1_.refs_2_, ...), custom_call_target="tpu_custom_call" | custom-call | flops 1000 | bytes 1000 | tf_op jit(solution)/shard_map/produce/pallas_call | solution.py:94
  274.5 27.3 %all-to-all-done.4.refs_0_.refs_1_ = bf16[4,336,1024]{2,1,0:T(8,128)(2,1)S(1)} async-done(((bf16[4,336,1024]{2,1,0:T(8,128)(2,1)}), bf16[4,336,1024]{2,1,0:T(8,128)(2,1)S(1)}, u32[]{:S(2)}, u32[]{:S(2)}) %all-to-all-start.4) | async-done | bytes 2752544 | tf_op jit(solution)/shard_map/all_to_all | solution.py:123
  303.3 12.0 %combine.2 = (bf16[2,416,512]{2,1,0:T(8,128)(2,1)}, bf16[2,416,512]{2,1,0:T(8,128)(2,1)}, bf16[2,400,512]{2,1,0:T(8,128)(2,1)}, bf16[2,400,512]{2,1,0:T(8,128)(2,1)}) custom-call(s32[32]{0:T(128)} %get-tuple-element.67.place.refs_2_, bf16[4,336,1024]{2,1,0:T(8,128)(2,1)} %copy-done, bf16[4,336,1024]{2,1,0:T(8,128)(2,1)} %copy-done, s32[1600,8]{1,0:T(8,128)} %bitcast.43, ...), custom_call_target="tpu_custom_call" | custom-call | flops 1000 | bytes 1000 | tf_op jit(solution)/shard_map/combine/pallas_call | solution.py:94
  319.8 15.7 %collective-permute-done.8.refs_1_ = bf16[2,416,512]{2,1,0:T(8,128)(2,1)} collective-permute-done((bf16[2,416,512]{2,1,0:T(8,128)(2,1)}, bf16[2,416,512]{2,1,0:T(8,128)(2,1)}, u32[]{:S(2)}, u32[]{:S(2)}) %collective-permute-start.8) | collective-permute-done | bytes 852000 | tf_op jit(solution)/shard_map/ppermute | solution.py:115
  339.1 11.6 %grad_second.3.refs_3_ = f32[4096,512]{1,0:T(8,128)} custom-call(s32[32]{0:T(128)} %get-tuple-element.67.place.refs_2_, bf16[896,1024]{1,0:T(8,128)(2,1)} %get-tuple-element.78.refs_5_.refs_0_, f32[896,128]{1,0:T(8,128)} %get-tuple-element.79.refs_1_.refs_0_, bf16[896,4096]{1,0:T(8,128)(2,1)} %get-tuple-element.80.refs_2_.refs_1_, ...), custom_call_target="tpu_custom_call" | custom-call | flops 1000 | bytes 1000 | tf_op jit(solution)/shard_map/grad_second/pallas_call | solution.py:94
  350.8 11.3 %grad_first.3.refs_14_ = f32[512,4096]{1,0:T(8,128)} custom-call(s32[32]{0:T(128)} %get-tuple-element.67.place.refs_2_, bf16[896,1024]{1,0:T(8,128)(2,1)} %get-tuple-element.81.refs_0_, bf16[896,4096]{1,0:T(8,128)(2,1)} %get-tuple-element.82.refs_1_, bf16[512,4096]{1,0:T(8,128)(2,1)} %collective-permute-done.12.refs_2_, f32[4096,512]{1,0:T(8,128)} %grad_second.3.refs_3_), custom_call_target="tpu_custom_call" | custom-call | flops 1000 | bytes 1000 | tf_op jit(solution)/shard_map/grad_first/pallas_call | solution.py:94
  362.9 8.0 %back_two.1 = (f32[400,1024]{1,0:T(8,128)}, bf16[400,1024]{1,0:T(8,128)(2,1)}, f32[40,1024]{1,0:T(8,128)}, bf16[400,256]{1,0:T(8,128)(2,1)}, bf16[400,256]{1,0:T...) custom-call(s32[32]{0:T(128)} %get-tuple-element.67.place.refs_2_, ...), custom_call_target="tpu_custom_call" | custom-call | flops 1000 | bytes 1000 | tf_op jit(solution)/shard_map/back_two/pallas_call | solution.py:94
  386.2 16.7 %collective-permute-done.14.refs_2_ = bf16[400,256]{1,0:T(8,128)(2,1)S(1)} collective-permute-done((bf16[400,256]{1,0:T(8,128)(2,1)S(1)}, bf16[400,256]{1,0:T(8,128)(2,1)S(1)}, u32[]{:S(2)}, u32[]{:S(2)}) %collective-permute-start.14) | collective-permute-done | bytes 204832 | tf_op jit(solution)/shard_map/ppermute | solution.py:115
  408.0 16.0 %attend_back.1 = (bf16[1600,768]{1,0:T(8,128)(2,1)}, f32[8,768]{1,0:T(8,128)}) custom-call(s32[32]{0:T(128)} %get-tuple-element.67.place.refs_2_, bf16[1600,768]{1,0:T(8,128)(2,1)} %get-tuple-element.69.refs_0_.refs_1_, bf16[400,256]{1,0:T(8,128)(2,1)} %get-tuple-element.94.refs_1_, bf16[400,256]{1,0:T(8,128)(2,1)} %copy-done.26, ...), custom_call_target="tpu_custom_call" | custom-call | flops 1000 | bytes 1000 | tf_op jit(solution)/shard_map/attend_back/pallas_call | solution.py:94
  424.0 8.3 %grad_one.1 = (bf16[2,416,512]{2,1,0:T(8,128)(2,1)}, bf16[2,416,512]{2,1,0:T(8,128)(2,1)}, bf16[2,416,512]{2,1,0:T(8,128)(2,1)}, bf16[2,416,512]{2,1,0:T(8,128)(2,1)}, f32[2,1024]{1,0:T(2,128)}) custom-call(s32[32]{0:T(128)} %get-tuple-element.67.place.refs_2_, bf16[1600,768]{1,0:T(8,128)(2,1)} %get-tuple-element.101.refs_0_.refs_1_, ...), custom_call_target="tpu_custom_call" | custom-call | flops 1000 | bytes 1000 | tf_op jit(solution)/shard_map/grad_one/pallas_call | solution.py:94
  434.7 5.9 %grad_qkv.2.refs_3_ = bf16[3,512,256]{2,1,0:T(8,128)(2,1)} custom-call(s32[32]{0:T(128)} %get-tuple-element.67.place.refs_2_, bf16[1600,1024]{1,0:T(8,128)(2,1)} %get-tuple-element.85.refs_0_, bf16[1600,768]{1,0:T(8,128)(2,1)} %get-tuple-element.101.refs_0_.refs_1_, f32[2,1024]{1,0:T(2,128)} %get-tuple-element.104.refs_2_), custom_call_target="tpu_custom_call" | custom-call | flops 1000 | bytes 1000 | tf_op jit(solution)/shard_map/grad_qkv/pallas_call | solution.py:94
  443.9 5.9 grad_qkv.3.refs_2_
  451.3 10.5 %combine.3 = (bf16[2,400,512]{2,1,0:T(8,128)(2,1)}, bf16[2,400,512]{2,1,0:T(8,128)(2,1)}, bf16[2,400,512]{2,1,0:T(8,128)(2,1)}, bf16[2,400,512]{2,1,0:T(8,128)(2,1)}) custom-call(s32[32]{0:T(128)} %get-tuple-element.67.place.refs_2_, bf16[4,336,1024]{2,1,0:T(8,128)(2,1)} %copy-done.4, s32[1600,8]{1,0:T(8,128)} %bitcast.44, bf16[3,512,256]{2,1,0:T(8,128)(2,1)} %grad_qkv.3.refs_2_), custom_call_target="tpu_custom_call" | custom-call | flops 1000 | bytes 1000 | tf_op jit(solution)/shard_map/combine/pallas_call | solution.py:94
  482.6 9.2 %collective-permute-done.25.refs_5_ = bf16[1,416,512]{2,1,0:T(8,128)(2,1)S(1)} collective-permute-done((bf16[1,416,512]{2,1,0:T(8,128)(2,1)S(1)}, bf16[1,416,512]{2,1,0:T(8,128)(2,1)S(1)}, u32[]{:S(2)}, u32[]{:S(2)}) %collective-permute-start.25) | collective-permute-done | bytes 426016 | tf_op jit(solution)/shard_map/ppermute | solution.py:115
  492.8 5.4 back_one.1
  512.9 13.5 %collective-permute-done.21.refs_5_ = bf16[1,400,512]{2,1,0:T(8,128)(2,1)} collective-permute-done((bf16[1,400,512]{2,1,0:T(8,128)(2,1)}, bf16[1,400,512]{2,1,0:T(8,128)(2,1)}, u32[]{:S(2)}, u32[]{:S(2)}) %collective-permute-start.21) | collective-permute-done | bytes 409632 | tf_op jit(solution)/shard_map/ppermute | solution.py:115
  545.9 15.6 %collective-permute-done.32.refs_6_ = bf16[1,400,512]{2,1,0:T(8,128)(2,1)} collective-permute-done((bf16[1,400,512]{2,1,0:T(8,128)(2,1)}, bf16[1,400,512]{2,1,0:T(8,128)(2,1)}, u32[]{:S(2)}, u32[]{:S(2)}) %collective-permute-start.32) | collective-permute-done | bytes 409632 | tf_op jit(solution)/shard_map/ppermute | solution.py:115
  562.3 5.6 assemble.2.refs_8_
  (243 shorter events, 152.1 us)
Async XLA Ops:
  41.2 94.5 %all-to-all-start.2 = ((bf16[4,336,1024]{2,1,0:T(8,128)(2,1)}), bf16[4,336,1024]{2,1,0:T(8,128)(2,1)}, u32[]{:S(2)}, u32[]{:S(2)}) async-start(bf16[4,336,1024]{2,1,0:T(8,128)(2,1)} %dispatch.2.refs_4_), calls=%async_computation.2 | async-start | bytes 5505024 | tf_op jit(solution)/shard_map/all_to_all | solution.py:123
  46.4 60.7 %all-gather.3.cloned.1.call-start = ((), (), s32[]{:S(2)}) async-start(), calls=%async_computation.9 | async-start | bytes 2359296 | tf_op jit(solution)/shard_map/all_gather | solution.py:1317
  72.8 21.7 %collective-permute-start.2 = (bf16[2,1600,128]{2,1,0:T(8,128)(2,1)}, bf16[2,1600,128]{2,1,0:T(8,128)(2,1)S(1)}, u32[]{:S(2)}, u32[]{:S(2)}) collective-permute-start(bf16[2,1600,128]{2,1,0:T(8,128)(2,1)} %attend.1.refs_0_.refs_1_.refs_14_), channel_id=1, source_target_pairs={{0,2},{2,0},{4,6},{6,4},{1,3},{3,1},{5,7},{7,5},{8,10},{10,8},{12,... | collective-permute-start | bytes 2457608 | tf_op jit(solution)/shard_map/ppermute | solution.py:115
  74.3 21.8 %collective-permute-start.3 = (bf16[2,1600,128]{2,1,0:T(8,128)(2,1)}, bf16[2,1600,128]{2,1,0:T(8,128)(2,1)S(1)}, u32[]{:S(2)}, u32[]{:S(2)}) collective-permute-start(bf16[2,1600,128]{2,1,0:T(8,128)(2,1)} %attend.1.refs_0_.refs_1_.refs_14_), channel_id=1, source_target_pairs={{0,4},{2,6},{4,0},{6,2},{1,5},{3,7},{5,1},{7,3},{8,12},{10,14},{12... | collective-permute-start | bytes 2457608 | tf_op jit(solution)/shard_map/ppermute | solution.py:115
  96.7 45.3 %collective-permute-start.7 = (bf16[4096,512]{1,0:T(8,128)(2,1)}, bf16[4096,512]{1,0:T(8,128)(2,1)}, u32[]{:S(2)}, u32[]{:S(2)}) collective-permute-start(bf16[4096,512]{1,0:T(8,128)(2,1)} %bitcast.8.refs_1_.refs_2_), channel_id=1, source_target_pairs={{0,1},{1,0},{2,3},{3,2},{4,5},{5,4},{6,7},{7,6},{8,9},{9,8},{10,11... | collective-permute-start | bytes 12582920 | tf_op jit(solution)/shard_map/ppermute | solution.py:119
  96.7 58.8 %collective-permute-start.6 = (bf16[512,4096]{1,0:T(8,128)(2,1)}, bf16[512,4096]{1,0:T(8,128)(2,1)}, u32[]{:S(2)}, u32[]{:S(2)}) collective-permute-start(bf16[512,4096]{1,0:T(8,128)(2,1)} %bitcast.9.refs_1_), channel_id=1, source_target_pairs={{0,1},{1,0},{2,3},{3,2},{4,5},{5,4},{6,7},{7,6},{8,9},{9,8},{10,11... | collective-permute-start | bytes 12582920 | tf_op jit(solution)/shard_map/ppermute | solution.py:119
  135.6 66.1 %all-to-all-start.1 = ((bf16[4,336,1024]{2,1,0:T(8,128)(2,1)}), bf16[4,336,1024]{2,1,0:T(8,128)(2,1)S(1)}, u32[]{:S(2)}, u32[]{:S(2)}) async-start(bf16[4,336,1024]{2,1,0:T(8,128)(2,1)} %dispatch.3.refs_3_), calls=%async_computation.1 | async-start | bytes 5505024 | tf_op jit(solution)/shard_map/all_to_all | solution.py:123
  236.0 65.8 %all-to-all-start.4 = ((bf16[4,336,1024]{2,1,0:T(8,128)(2,1)}), bf16[4,336,1024]{2,1,0:T(8,128)(2,1)S(1)}, u32[]{:S(2)}, u32[]{:S(2)}) async-start(bf16[4,336,1024]{2,1,0:T(8,128)(2,1)} %get-tuple-element.86), calls=%async_computation.4 | async-start | bytes 5505024 | tf_op jit(solution)/shard_map/all_to_all | solution.py:123
  249.7 89.4 %collective-permute-start.13 = (bf16[4096,512]{1,0:T(8,128)(2,1)}, bf16[4096,512]{1,0:T(8,128)(2,1)}, u32[]{:S(2)}, u32[]{:S(2)}) collective-permute-start(bf16[4096,512]{1,0:T(8,128)(2,1)} %grad_second.2.refs_2_), channel_id=1, source_target_pairs={{0,1},{1,0},{2,3},{3,2},{4,5},{5,4},{6,7},{7,6},{8,9},{9,8},{10,11... | collective-permute-start | bytes 12582920 | tf_op jit(solution)/shard_map/ppermute | solution.py:119
  259.1 91.6 %collective-permute-start.12 = (bf16[512,4096]{1,0:T(8,128)(2,1)}, bf16[512,4096]{1,0:T(8,128)(2,1)}, u32[]{:S(2)}, u32[]{:S(2)}) collective-permute-start(bf16[512,4096]{1,0:T(8,128)(2,1)} %grad_first.2.refs_4_), channel_id=1, source_target_pairs={{0,1},{1,0},{2,3},{3,2},{4,5},{5,4},{6,7},{7,6},{8,9},{9,8},{10,11... | collective-permute-start | bytes 12582920 | tf_op jit(solution)/shard_map/ppermute | solution.py:119
  315.3 22.2 %collective-permute-start.10 = (bf16[2,400,512]{2,1,0:T(8,128)(2,1)}, bf16[2,400,512]{2,1,0:T(8,128)(2,1)}, u32[]{:S(2)}, u32[]{:S(2)}) collective-permute-start(bf16[2,400,512]{2,1,0:T(8,128)(2,1)} %get-tuple-element.90), channel_id=1, source_target_pairs={{0,4},{2,6},{4,0},{6,2},{1,5},{3,7},{5,1},{7,3},{8,12},{10,14},{12... | collective-permute-start | bytes 2457608 | tf_op jit(solution)/shard_map/ppermute | solution.py:115
  316.0 133.7 %all-to-all-start.3 = ((bf16[4,336,1024]{2,1,0:T(8,128)(2,1)}), bf16[4,336,1024]{2,1,0:T(8,128)(2,1)S(1)}, u32[]{:S(2)}, u32[]{:S(2)}) async-start(bf16[4,336,1024]{2,1,0:T(8,128)(2,1)} %produce.1.refs_3_), calls=%async_computation.3 | async-start | bytes 5505024 | tf_op jit(solution)/shard_map/all_to_all | solution.py:123
  336.8 25.2 %collective-permute-start.9 = (bf16[1,416,512]{2,1,0:T(8,128)(2,1)S(1)}, bf16[1,416,512]{2,1,0:T(8,128)(2,1)S(1)}, u32[]{:S(2)}, u32[]{:S(2)}) collective-permute-start(bf16[1,416,512]{2,1,0:T(8,128)(2,1)S(1)} %add_convert_fusion.4), channel_id=1, source_target_pairs={{0,4},{2,6},{4,0},{6,2},{1,5},{3,7},{5,1},{7,3},{8,12},{10,14},{12... | collective-permute-start | bytes 1277960 | tf_op jit(solution)/shard_map/ppermute | solution.py:115
  338.8 23.3 %collective-permute-start.11 = (bf16[1,400,512]{2,1,0:T(8,128)(2,1)S(1)}, bf16[1,400,512]{2,1,0:T(8,128)(2,1)S(1)}, u32[]{:S(2)}, u32[]{:S(2)}) collective-permute-start(bf16[1,400,512]{2,1,0:T(8,128)(2,1)S(1)} %add_convert_fusion.7), channel_id=1, source_target_pairs={{0,2},{2,0},{4,6},{6,4},{1,3},{3,1},{5,7},{7,5},{8,10},{10,8},{12,... | collective-permute-start | bytes 1228808 | tf_op jit(solution)/shard_map/ppermute | solution.py:115
  380.9 59.7 %collective-permute-start.38 = (bf16[2,320,512]{2,1,0:T(8,128)(2,1)S(1)}, bf16[2,320,512]{2,1,0:T(8,128)(2,1)S(1)}, u32[]{:S(2)}, u32[]{:S(2)}) collective-permute-start(bf16[2,320,512]{2,1,0:T(8,128)(2,1)S(1)} %slice.169), channel_id=1, source_target_pairs={{0,2},{2,0},{4,6},{6,4},{1,3},{3,1},{5,7},{7,5},{8,10},{10,8},{12,... | collective-permute-start | bytes 1966088 | tf_op jit(solution)/shard_map/ppermute | solution.py:115
  384.3 23.0 %collective-permute-start.16 = (bf16[400,256]{1,0:T(8,128)(2,1)S(1)}, bf16[400,256]{1,0:T(8,128)(2,1)S(1)}, u32[]{:S(2)}, u32[]{:S(2)}) collective-permute-start(bf16[400,256]{1,0:T(8,128)(2,1)S(1)} %copy-done.38), channel_id=1, source_target_pairs={{0,6},{2,4},{4,2},{6,0},{1,7},{3,5},{5,3},{7,1},{8,14},{10,12},{12... | collective-permute-start | bytes 614408 | tf_op jit(solution)/shard_map/ppermute | solution.py:115
  432.3 35.8 %collective-permute-start.24 = (bf16[2,416,512]{2,1,0:T(8,128)(2,1)}, bf16[2,416,512]{2,1,0:T(8,128)(2,1)}, u32[]{:S(2)}, u32[]{:S(2)}) collective-permute-start(bf16[2,416,512]{2,1,0:T(8,128)(2,1)} %get-tuple-element.112), channel_id=1, source_target_pairs={{0,4},{2,6},{4,0},{6,2},{1,5},{3,7},{5,1},{7,3},{8,12},{10,14},{12... | collective-permute-start | bytes 2555912 | tf_op jit(solution)/shard_map/ppermute | solution.py:115
  433.0 38.1 %collective-permute-start.22 = (bf16[2,416,512]{2,1,0:T(8,128)(2,1)}, bf16[2,416,512]{2,1,0:T(8,128)(2,1)}, u32[]{:S(2)}, u32[]{:S(2)}) collective-permute-start(bf16[2,416,512]{2,1,0:T(8,128)(2,1)} %get-tuple-element.110), channel_id=1, source_target_pairs={{0,2},{2,0},{4,6},{6,4},{1,3},{3,1},{5,7},{7,5},{8,10},{10,8},{12,... | collective-permute-start | bytes 2555912 | tf_op jit(solution)/shard_map/ppermute | solution.py:115
  441.5 21.3 %collective-permute-start.39 = (bf16[320,512]{1,0:T(8,128)(2,1)}, bf16[320,512]{1,0:T(8,128)(2,1)}, u32[]{:S(2)}, u32[]{:S(2)}) collective-permute-start(bf16[320,512]{1,0:T(8,128)(2,1)} %slice_bitcast_fusion), channel_id=1, source_target_pairs={{0,4},{2,6},{4,0},{6,2},{1,5},{3,7},{5,1},{7,3},{8,12},{10,14},{12... | collective-permute-start | bytes 983048 | tf_op jit(solution)/shard_map/ppermute | solution.py:115
  461.8 38.9 %collective-permute-start.20 = (bf16[2,400,512]{2,1,0:T(8,128)(2,1)}, bf16[2,400,512]{2,1,0:T(8,128)(2,1)}, u32[]{:S(2)}, u32[]{:S(2)}) collective-permute-start(bf16[2,400,512]{2,1,0:T(8,128)(2,1)} %get-tuple-element.108), channel_id=1, source_target_pairs={{0,4},{2,6},{4,0},{6,2},{1,5},{3,7},{5,1},{7,3},{8,12},{10,14},{12... | collective-permute-start | bytes 2457608 | tf_op jit(solution)/shard_map/ppermute | solution.py:115
  462.5 41.8 %collective-permute-start.18 = (bf16[2,400,512]{2,1,0:T(8,128)(2,1)}, bf16[2,400,512]{2,1,0:T(8,128)(2,1)}, u32[]{:S(2)}, u32[]{:S(2)}) collective-permute-start(bf16[2,400,512]{2,1,0:T(8,128)(2,1)} %get-tuple-element.106), channel_id=1, source_target_pairs={{0,2},{2,0},{4,6},{6,4},{1,3},{3,1},{5,7},{7,5},{8,10},{10,8},{12,... | collective-permute-start | bytes 2457608 | tf_op jit(solution)/shard_map/ppermute | solution.py:115
  469.3 22.5 %collective-permute-start.25 = (bf16[1,416,512]{2,1,0:T(8,128)(2,1)S(1)}, bf16[1,416,512]{2,1,0:T(8,128)(2,1)S(1)}, u32[]{:S(2)}, u32[]{:S(2)}) collective-permute-start(bf16[1,416,512]{2,1,0:T(8,128)(2,1)S(1)} %add_convert_fusion.2), channel_id=1, source_target_pairs={{0,2},{2,0},{4,6},{6,4},{1,3},{3,1},{5,7},{7,5},{8,10},{10,8},{12,... | collective-permute-start | bytes 1277960 | tf_op jit(solution)/shard_map/ppermute | solution.py:115
  478.4 29.6 %all-to-all-start.5 = ((bf16[4,384,256]{2,1,0:T(8,128)(2,1)}), bf16[4,384,256]{2,1,0:T(8,128)(2,1)S(1)}, u32[]{:S(2)}, u32[]{:S(2)}) async-start(bf16[4,384,256]{2,1,0:T(8,128)(2,1)} %bitcast.14), calls=%async_computation.5 | async-start | bytes 1572864 | tf_op jit(solution)/shard_map/all_to_all | solution.py:123
  498.2 38.5 %collective-permute-start.30 = (bf16[2,400,512]{2,1,0:T(8,128)(2,1)}, bf16[2,400,512]{2,1,0:T(8,128)(2,1)S(1)}, u32[]{:S(2)}, u32[]{:S(2)}) collective-permute-start(bf16[2,400,512]{2,1,0:T(8,128)(2,1)} %get-tuple-element.115.refs_0_.refs_1_), channel_id=1, source_target_pairs={{0,2},{2,0},{4,6},{6,4},{1,3},{3,1},{5,7},{7,5},{8,10},{10,8},{12,... | collective-permute-start | bytes 2457608 | tf_op jit(solution)/shard_map/ppermute | solution.py:115
  498.5 39.2 %collective-permute-start.31 = (bf16[2,400,512]{2,1,0:T(8,128)(2,1)}, bf16[2,400,512]{2,1,0:T(8,128)(2,1)S(1)}, u32[]{:S(2)}, u32[]{:S(2)}) collective-permute-start(bf16[2,400,512]{2,1,0:T(8,128)(2,1)} %get-tuple-element.115.refs_0_.refs_1_), channel_id=1, source_target_pairs={{0,4},{2,6},{4,0},{6,2},{1,5},{3,7},{5,1},{7,3},{8,12},{10,14},{12... | collective-permute-start | bytes 2457608 | tf_op jit(solution)/shard_map/ppermute | solution.py:115
  502.6 23.9 %collective-permute-start.21 = (bf16[1,400,512]{2,1,0:T(8,128)(2,1)}, bf16[1,400,512]{2,1,0:T(8,128)(2,1)}, u32[]{:S(2)}, u32[]{:S(2)}) collective-permute-start(bf16[1,400,512]{2,1,0:T(8,128)(2,1)} %add_convert_fusion.5), channel_id=1, source_target_pairs={{0,2},{2,0},{4,6},{6,4},{1,3},{3,1},{5,7},{7,5},{8,10},{10,8},{12,... | collective-permute-start | bytes 1228808 | tf_op jit(solution)/shard_map/ppermute | solution.py:115
  506.8 26.6 %collective-permute-start.35 = (f32[3,512]{1,0:T(4,128)S(1)}, f32[3,512]{1,0:T(4,128)S(1)}, u32[]{:S(2)}, u32[]{:S(2)}) collective-permute-start(f32[3,512]{1,0:T(4,128)S(1)} %fusion.1), channel_id=1, source_target_pairs={{0,8},{8,0},{16,24},{24,16},{1,9},{9,1},{17,25},{25,17},{2,10},{10... | collective-permute-start | bytes 18440 | tf_op jit(solution)/shard_map/ppermute | solution.py:182
  508.8 30.3 %all-to-all-start.8 = ((bf16[4,80,512]{2,1,0:T(8,128)(2,1)}), bf16[4,80,512]{2,1,0:T(8,128)(2,1)}, u32[]{:S(2)}, u32[]{:S(2)}) async-start(bf16[4,80,512]{2,1,0:T(8,128)(2,1)} %broadcast_in_dim.15), calls=%async_computation.8 | async-start | bytes 655360 | tf_op jit(solution)/shard_map/all_to_all | solution.py:123
  531.7 36.2 %collective-permute-start.26 = (bf16[2,400,512]{2,1,0:T(8,128)(2,1)}, bf16[2,400,512]{2,1,0:T(8,128)(2,1)S(1)}, u32[]{:S(2)}, u32[]{:S(2)}) collective-permute-start(bf16[2,400,512]{2,1,0:T(8,128)(2,1)} %block_out.1.refs_8_.refs_0_.refs_1_), channel_id=1, source_target_pairs={{0,2},{2,0},{4,6},{6,4},{1,3},{3,1},{5,7},{7,5},{8,10},{10,8},{12,... | collective-permute-start | bytes 2457608 | tf_op jit(solution)/shard_map/ppermute | solution.py:115
  533.4 36.1 %collective-permute-start.27 = (bf16[2,400,512]{2,1,0:T(8,128)(2,1)}, bf16[2,400,512]{2,1,0:T(8,128)(2,1)S(1)}, u32[]{:S(2)}, u32[]{:S(2)}) collective-permute-start(bf16[2,400,512]{2,1,0:T(8,128)(2,1)} %block_out.1.refs_8_.refs_0_.refs_1_), channel_id=1, source_target_pairs={{0,4},{2,6},{4,0},{6,2},{1,5},{3,7},{5,1},{7,3},{8,12},{10,14},{12... | collective-permute-start | bytes 2457608 | tf_op jit(solution)/shard_map/ppermute | solution.py:115
  537.7 23.8 %collective-permute-start.32 = (bf16[1,400,512]{2,1,0:T(8,128)(2,1)}, bf16[1,400,512]{2,1,0:T(8,128)(2,1)}, u32[]{:S(2)}, u32[]{:S(2)}) collective-permute-start(bf16[1,400,512]{2,1,0:T(8,128)(2,1)} %slice.165), channel_id=1, source_target_pairs={{0,4},{2,6},{4,0},{6,2},{1,5},{3,7},{5,1},{7,3},{8,12},{10,14},{12... | collective-permute-start | bytes 1228808 | tf_op jit(solution)/shard_map/ppermute | solution.py:115
  540.1 34.9 %all-to-all-start.6 = ((bf16[4,384,256]{2,1,0:T(8,128)(2,1)}), bf16[4,384,256]{2,1,0:T(8,128)(2,1)}, u32[]{:S(2)}, u32[]{:S(2)}) async-start(bf16[4,384,256]{2,1,0:T(8,128)(2,1)} %broadcast_in_dim.14), calls=%async_computation.6 | async-start | bytes 1572864 | tf_op jit(solution)/shard_map/all_to_all | solution.py:123
  (60 other events, 510.5 us)
Sparse Core Ops, SparseCore 0:
  49.1 30.4 all-gather.2

commit v2 on v1

--- a/solution.py
+++ b/solution.py
@@ -26,8 +26,9 @@
     X: int
     E: int
     S: int
+    Q: int
     SP: int
-    CR: int
+    CR: tuple
     R: int
     TP: int
     W: int
@@ -42,7 +43,13 @@
 
 class Order:
     def __init__(self):
-        self.last = None
+        self.after = []
+
+    def tie(self, value):
+        self.after.append(value)
+
+    def hold(self, *values):
+        return lax.optimization_barrier((*values, *self.after))[: len(values)]
 
 
 def up(value, step):
@@ -84,8 +91,8 @@
     return pl.BlockSpec(dims, lambda i, s: (0,) * (len(dims) - 1) + (i,))
 
 
-def call(order, body, place, args, specs, outs, out_specs, grid, scratch=(), name=None):
-    extra = [] if order.last is None else [order.last]
+def call(order, body, place, args, specs, outs, out_specs, grid, scratch=(), name=None, cost=0):
+    extra = order.after
     count = len(args)
 
     def wrapped(place, *refs):
@@ -104,10 +111,12 @@
         compiler_params=pltpu.CompilerParams(
             dimension_semantics=("arbitrary",) * len(grid), vmem_limit_bytes=VMEM_BYTES
         ),
-        cost_estimate=pl.CostEstimate(flops=1000, bytes_accessed=1000, transcendentals=0),
+        cost_estimate=pl.CostEstimate(
+            flops=1000 + int(1.1e9 * cost), bytes_accessed=1000, transcendentals=0
+        ),
         name=name,
     )(place, *args, *extra)
-    order.last = min(result, key=lambda o: o.size)
+    order.after = [min(result, key=lambda o: o.size)]
     return result
 
 
@@ -119,6 +128,10 @@
     return lax.ppermute(value, "grid", [(0, 1), (1, 0)])
 
 
+def held(value, *others):
+    return lax.optimization_barrier((value, *others))[0]
+
+
 def trade(value, axis):
     return lax.all_to_all(value, axis, split_axis=0, concat_axis=0, tiled=True)
 
@@ -131,15 +144,23 @@
     return [[0, 1], [2, 3]] if c.n == 4 else [[k] for k in range(c.n)]
 
 
-def reduce_mp(c, arrays):
+def reduce_start(c, arrays):
     a, b = arrays[: len(arrays) // 2], arrays[len(arrays) // 2 :]
     if c.n != 4:
         return [[x[0]] + [swap_mp(c, x[k], k) for k in range(1, c.n)] for x in (a, b)]
-    ra = swap_mp(c, a[1], 1)
-    rb = swap_mp(c, b[1], 2)
-    ta = (a[0][1:].astype(F32) + ra[1:].astype(F32)).astype(BF)
-    tb = (b[0][1:].astype(F32) + rb[1:].astype(F32)).astype(BF)
-    return [[a[0], ra, swap_mp(c, ta, 2)], [b[0], rb, swap_mp(c, tb, 1)]]
+    return [[a[0], swap_mp(c, a[1], 1)], [b[0], swap_mp(c, b[1], 2)]]
+
+
+def reduce_end(c, order, state):
+    if c.n != 4:
+        return state
+    (a, ra), (b, rb) = state
+    ra, rb = order.hold(ra, rb)
+    ta = (a[1:].astype(F32) + ra[1:].astype(F32)).astype(BF)
+    tb = (b[1:].astype(F32) + rb[1:].astype(F32)).astype(BF)
+    order.tie(ta)
+    order.tie(tb)
+    return [[a, ra, swap_mp(c, ta, 2)], [b, rb, swap_mp(c, tb, 1)]]
 
 
 def piece_outs(c, more_a=0, more_b=0):
@@ -200,13 +221,6 @@
     return (pair[0].astype(F32) + swap_mp(c, pair[1], 2).astype(F32)).astype(BF)
 
 
-def sum_dp(c, value):
-    parts = trade(value.reshape((c.X, value.shape[0] // c.X) + value.shape[1:]), "dp")
-    total = jnp.sum(parts.astype(F32), axis=0).astype(BF)
-    spread = jnp.broadcast_to(total[None], (c.X,) + total.shape)
-    return trade(spread, "dp").reshape(value.shape).astype(F32)
-
-
 def expert_of(c, place, j):
     return j * EXP_DEV + place[3]
 
@@ -215,36 +229,44 @@
     return place[4 + j]
 
 
-def window_out(c, place, j):
-    return place[4 + c.X + j]
-
-
-def window_in(c, place, j):
-    return pl.multiple_of(place[4 + 2 * c.X + j], 16)
+def window_slot(c, place, j, slot):
+    return slot + jnp.where(slot < c.Q, place[4 + c.X + j], place[4 + 2 * c.X + j])
+
+
+def window_in(c, place, half, j):
+    return pl.multiple_of(place[4 + (3 + half) * c.X + j], 16)
 
 
 def windows_body(c, place, counts, out_ref, off_ref):
-    def window(offset):
-        return jnp.minimum((offset >> 4) << 4, c.CR - c.SP)
+    def window(offset, half):
+        return jnp.minimum((offset >> 4) << 4, c.CR[half] - c.SP)
 
     def before(e, source):
-        total = jnp.int32(0)
+        state = (jnp.int32(0),) * 3
+        result = state
         for b in range(c.X):
-            total = total + jnp.where(b < source, counts[b, e], 0)
-        return total
+            result = [jnp.where(source == b, new, old) for new, old in zip(state, result)]
+            number = counts[b, e]
+            kept = jnp.clip(c.cap - state[0], 0, number)
+            first = jnp.minimum(kept, c.Q)
+            state = (state[0] + number, state[1] + first, state[2] + kept - first)
+        return result
 
     for i in range(4):
         out_ref[i] = place[i]
-    for i in range(4 + 3 * c.X, 32):
+    for i in range(4 + 5 * c.X, 64):
         out_ref[i] = jnp.int32(0)
     here = place[0] * EXP_DEV + place[3]
     for j in range(c.X):
-        offset = before(expert_of(c, place, j), place[0])
+        offset, first, second = before(expert_of(c, place, j), place[0])
         out_ref[4 + j] = offset
-        out_ref[4 + c.X + j] = window(offset)
-        out_ref[4 + 2 * c.X + j] = window(before(here, j))
+        out_ref[4 + c.X + j] = first - window(first, 0)
+        out_ref[4 + 2 * c.X + j] = c.SP + second - c.Q - window(second, 1)
+        _, first, second = before(here, j)
+        out_ref[4 + 3 * c.X + j] = window(first, 0)
+        out_ref[4 + 4 * c.X + j] = window(second, 1)
     for e in range(c.E):
-        off_ref[e : e + 1, :] = jnp.full((1, 128), before(e, place[0]), I32)
+        off_ref[e : e + 1, :] = jnp.full((1, 128), before(e, place[0])[0], I32)
 
 
 def windows(c, order, place, counts):
@@ -254,62 +276,70 @@
         place,
         [counts],
         [pl.BlockSpec(memory_space=pltpu.SMEM)],
-        [shape_of((32,), I32), shape_of((c.E, 128), I32)],
+        [shape_of((64,), I32), shape_of((c.E, 128), I32)],
         [pl.BlockSpec(memory_space=pltpu.SMEM), whole(shape_of((c.E, 128), I32))],
         (1,),
         name="windows",
     )
 
 
-def route_body(c, place, row_ref, col_ref, rt_ref, slot_ref, rtb_ref, all_ref):
-    first = jnp.broadcast_to(row_ref[0:1, :], (8, c.TP))
-    second = jnp.broadcast_to(row_ref[1:2, :], (8, c.TP))
+def route_body(c, place, row_ref, col_ref, rt_ref, slot_ref, blocks_ref, rtb_ref):
+    pad = jnp.full((1, c.TP - c.T), 1 << 30, I32)
+    first = jnp.broadcast_to(jnp.concatenate([row_ref[0:1, :], pad], axis=1), (8, c.TP))
+    second = jnp.broadcast_to(jnp.concatenate([row_ref[1:2, :], pad], axis=1), (8, c.TP))
+
+    def count(at, state):
+        a, b = state
+        keys = col_ref[pl.ds(at, 8), :]
+        for k in range(2):
+            key = keys[:, k : k + 1]
+            a = a + (key < first).astype(I32)
+            b = b + (key < second).astype(I32)
+        return a, b
 
     def one(i, state):
-        a, b = state
         for q in range(8):
-            keys = col_ref[pl.ds(pl.multiple_of(i * 64 + q * 8, 8), 8), :]
-            for k in range(2):
-                key = keys[:, k : k + 1]
-                a = a + (key < first).astype(I32)
-                b = b + (key < second).astype(I32)
-        return a, b
+            state = count(pl.multiple_of(i * 64 + q * 8, 8), state)
+        return state
 
     zero = jnp.zeros((8, c.TP), I32)
-    a, b = lax.fori_loop(0, c.TP // 64, one, (zero, zero))
-    a = jnp.sum(a, axis=0, keepdims=True)
-    b = jnp.sum(b, axis=0, keepdims=True)
-    rt = rt_ref[...]
+    state = lax.fori_loop(0, c.T // 64, one, (zero, zero))
+    for at in range(c.T // 64 * 64, c.T, 8):
+        state = count(at, state)
+    a = jnp.sum(state[0], axis=0, keepdims=True)
+    b = jnp.sum(state[1], axis=0, keepdims=True)
+    pad = jnp.full((2, c.TP - c.T), -1, I32)
+    rt = jnp.concatenate([rt_ref[...], pad], axis=1)
     start = jnp.zeros((1, 1), I32)
     for e in range(c.E):
         in_first = rt[0:1, :] == e
         in_second = rt[1:2, :] == e
         number = jnp.sum(in_first.astype(I32) + in_second.astype(I32), axis=1, keepdims=True)
-        all_ref[e : e + 1, :] = jnp.where(in_first, a - start, jnp.where(in_second, b - start, -1))
+        slot_ref[e : e + 1, :] = jnp.where(in_first, a - start, jnp.where(in_second, b - start, -1))
         start = start + number
     for r in range(c.n):
-        slot_ref[r] = all_ref[:, r * c.R : (r + 1) * c.R]
+        blocks_ref[r] = slot_ref[:, r * c.R : (r + 1) * c.R]
         rtb_ref[r] = jnp.concatenate([rt[:, r * c.R : (r + 1) * c.R]] * 4, axis=0)
 
 
 def route(c, order, place, routes, priority):
     key = routes * c.key + priority
-    big = 1 << 30
-    pad = c.TP - c.T
-    row = jnp.pad(key.T, ((0, 0), (0, pad)), constant_values=big)
-    col = jnp.pad(key, ((0, pad), (0, 0)), constant_values=big)
-    rt = jnp.pad(routes.T, ((0, 0), (0, pad)), constant_values=-1)
-    outs = [shape_of((c.n, c.E, c.R), I32), shape_of((c.n, 8, c.R), I32)]
+    row = routes.T * c.key + priority.T
+    rt = routes.T
+    outs = [
+        shape_of((c.E, c.TP), I32),
+        shape_of((c.n, c.E, c.R), I32),
+        shape_of((c.n, 8, c.R), I32),
+    ]
     return call(
         order,
         functools.partial(route_body, c),
         place,
-        [row, col, rt],
-        [whole(row), whole(col), whole(rt)],
+        [row, key, rt],
+        [whole(row), whole(key), whole(rt)],
         outs,
         [whole(o) for o in outs],
         (1,),
-        [pltpu.VMEM((c.E, c.TP), I32)],
         name="route",
     )
 
@@ -319,76 +349,69 @@
     return jnp.where(row == 14, high, jnp.where(row == 15, low, tile))
 
 
-def dispatch_body(c, rows_all, weighted, place, *refs):
+def dispatch_body(c, rows_all, halves, weighted, place, *refs):
     refs = list(refs)
     slot_ref, src_ref = refs[:2]
     refs = refs[2:]
     if weighted:
         weight_ref = refs.pop(0)
-    out_ref, hot_ref, *refs = refs
+    out_ref, hot_ref = refs
 
     @pl.when(pl.program_id(0) == 0)
     def _():
         for j in range(c.X):
-            e = expert_of(c, place, j)
-            offset = offset_at(place, j)
-            total = jnp.zeros((8, c.half), F32)
-            for r in range(c.n):
-                slot = slot_ref[r, pl.ds(e, 1), :]
-                kept = (slot >= 0) & (slot + offset < c.cap)
-                row = jnp.where(kept, slot + (offset - window_out(c, place, j)), -1)
-                hot = (lax.broadcasted_iota(I32, (c.half, c.R), 0) == row).astype(BF)
-                hot_ref[j, r] = hot[: c.SP]
-                if weighted:
-                    high, low = split_low(weight_ref[r, pl.ds(e, 1), :])
-                    both = jnp.concatenate(
-                        [jnp.broadcast_to(high, (8, c.R)), jnp.broadcast_to(low, (8, c.R))], axis=0
-                    )
-                    got = dot_nt(both, hot)
-                    total = total + jnp.where(
-                        lax.broadcasted_iota(I32, (8, 1), 0) == 0, got[0:8], got[8:16]
-                    )
-            if weighted:
-                refs[0][j] = total
-
-    for j in range(c.X):
-        acc = None
-        for r in range(c.n):
-            length = min(c.R, rows_all - r * c.R)
-            if length <= 0:
-                continue
-            part = dot_nn(hot_ref[j, r, :, :length], src_ref[r * c.R : r * c.R + length, :])
-            acc = part if acc is None else acc + part
-        out_ref[j] = acc.astype(BF)
+            slot = slot_ref[pl.ds(expert_of(c, place, j), 1), :]
+            kept = (slot >= 0) & (slot + offset_at(place, j) < c.cap)
+            row = jnp.where(kept, window_slot(c, place, j, slot), -1)
+            for index, half in enumerate(halves):
+                slots = lax.broadcasted_iota(I32, (c.SP, c.TP), 0) + half * c.SP
+                hot_ref[index, j * c.SP : (j + 1) * c.SP, :] = (slots == row).astype(BF)
+
+    for index in range(len(halves)):
+        acc = dot_nn(hot_ref[index, :, :rows_all], src_ref[...])
+        for j in range(c.X):
+            at = (len(halves) * j + index) * c.SP
+            out_ref[at : at + c.SP, :] = acc[j * c.SP : (j + 1) * c.SP].astype(BF)
         if weighted:
 
             @pl.when(pl.program_id(0) == 0)
             def _():
-                tile = last_rows(c, acc[c.SP - 16 :], refs[0][j, 0:1, :], refs[0][j, 1:2, :])
-                out_ref[j, c.SP - 16 :, :] = tile.astype(BF)
-
-
-def dispatch(c, order, place, slot, source, weight=None):
+                gates = dot_nn(hot_ref[index], weight_ref[...])
+                lane = lax.broadcasted_iota(I32, (1, 128), 1)
+                wide = (c.SP, c.half)
+                eye = lax.broadcasted_iota(I32, wide, 0) == lax.broadcasted_iota(I32, wide, 1)
+                for j in range(c.X):
+                    e = expert_of(c, place, j)
+                    mine = gates[j * c.SP : (j + 1) * c.SP]
+                    rows = []
+                    for at in (e, e + 64):
+                        col = jnp.sum(jnp.where(lane == at, mine, 0.0), axis=1, keepdims=True)
+                        rows.append(jnp.sum(jnp.where(eye, col, 0.0), axis=0, keepdims=True))
+                    end = (j + 1) * c.SP
+                    tile = last_rows(c, acc[end - 16 : end], rows[0], rows[1])
+                    out_ref[end - 16 : end, :] = tile.astype(BF)
+
+
+def dispatch(c, order, place, slot, source, halves, weight=None):
     rows_all = source.shape[0]
     args = [slot, source]
     specs = [whole(slot), pl.BlockSpec((rows_all, c.half), lambda i, s: (0, i ^ s[2]))]
-    scratch = [pltpu.VMEM((c.X, c.n, c.SP, c.R), BF)]
     if weight is not None:
         args.append(weight)
         specs.append(whole(weight))
-        scratch.append(pltpu.VMEM((c.X, 8, c.half), F32))
+    size = len(halves) * c.SP
     return call(
         order,
-        functools.partial(dispatch_body, c, rows_all, weight is not None),
+        functools.partial(dispatch_body, c, rows_all, halves, weight is not None),
         place,
         args,
         specs,
-        [shape_of((c.X, c.SP, c.D), BF)],
-        [cols_of((c.X, c.SP, c.half))],
+        [shape_of((c.X * size, c.D), BF)],
+        [cols_of((c.X * size, c.half))],
         (2,),
-        scratch,
+        [pltpu.VMEM((len(halves), c.X * c.SP, c.TP), BF)],
         name="dispatch",
-    )[0]
+    )[0].reshape(c.X, size, c.D)
 
 
 def norm_rows(values):
@@ -422,22 +445,26 @@
     return (first + lax.broadcasted_iota(I32, (count, 1), 0)) < c.T
 
 
-def qkv_body(c, place, tok_ref, small_ref, own_ref, oth_ref, hid_ref, qkv_ref, normed_ref):
+def qkv_body(c, place, tok_ref, small_ref, own_ref, oth_ref, hid_ref, qkv_ref, normed_ref, w_ref):
+    @pl.when(pl.program_id(0) == 0)
+    def _():
+        for part in range(3):
+            lanes = slice(part * c.W, (part + 1) * c.W)
+            w_ref[own_cols(c, place), lanes] = own_ref[part]
+            w_ref[other_cols(c, place), lanes] = oth_ref[part]
+
     live = live_rows(c, pl.program_id(0) * c.R, c.R)
     values = jnp.where(live, tok_ref[...].astype(F32), 0.0)
     normed, _ = norm_rows(values)
     hidden = normed * small_row(c, small_ref, 0) + small_row(c, small_ref, 2)
     normed_ref[...] = normed.astype(BF)
-    hid_ref[...] = jnp.where(live, hidden, 0.0).astype(BF)
-    own = hid_ref[:, own_cols(c, place)]
-    oth = hid_ref[:, other_cols(c, place)]
-    for part in range(3):
-        acc = dot_nn(own, own_ref[part]) + dot_nn(oth, oth_ref[part])
-        if part != 1:
-            bias = small_row(c, small_ref, 5)
-            at = 0 if part == 0 else c.half
-            acc = acc + bias[:, at : at + c.W]
-        qkv_ref[:, part * c.W : (part + 1) * c.W] = acc.astype(BF)
+    hidden = jnp.where(live, hidden, 0.0).astype(BF)
+    hid_ref[...] = hidden
+    acc = dot_nn(hidden, w_ref[...])
+    bias = small_row(c, small_ref, 5)
+    zero = jnp.zeros((1, c.W), F32)
+    shift = jnp.concatenate([bias[:, : c.W], zero, bias[:, c.half : c.half + c.W]], axis=1)
+    qkv_ref[...] = (acc + shift).astype(BF)
 
 
 def image_window(c):
@@ -454,6 +481,19 @@
 def head_mask(lanes, head):
     lane = lax.broadcasted_iota(I32, (1, lanes), 1)
     return (lane >= head * HEAD) & (lane < (head + 1) * HEAD)
+
+
+def stack_heads(c, values):
+    heads = range(c.W // HEAD)
+    return jnp.concatenate([jnp.where(head_mask(c.W, h), values, BF(0)) for h in heads], axis=0)
+
+
+def pick_heads(c, values):
+    total = None
+    for h in range(c.W // HEAD):
+        part = jnp.where(head_mask(c.W, h), values[h * c.win : (h + 1) * c.win], 0.0)
+        total = part if total is None else total + part
+    return total
 
 
 def attend_body(c, place, qkv_ref, mix_ref):
@@ -466,25 +506,21 @@
     col = lax.broadcasted_iota(I32, (1, c.win), 1)
     in_row = (row >= off) & (row < off + IMG_LEN)
     in_col = (col >= off) & (col < off + IMG_LEN)
+    q = stack_heads(c, qkv_ref[pl.ds(low, c.win), : c.W] * BF(HEAD**-0.5))
+    k = qkv_ref[pl.ds(low, c.win), c.W : 2 * c.W]
+    v = qkv_ref[pl.ds(low, c.win), 2 * c.W :]
+    scores = jnp.where(in_col, dot_nt(q, k), LOW)
+    exps = jnp.exp(scores - jnp.max(scores, axis=-1, keepdims=True))
+    probs = exps * (1.0 / jnp.sum(exps, axis=-1, keepdims=True))
+    total = pick_heads(c, dot_nn(probs.astype(BF), v)).astype(BF)
     for group, (at, lanes) in enumerate(groups_of(c)):
-        q = qkv_ref[pl.ds(low, c.win), at : at + lanes] * BF(HEAD**-0.5)
-        k = qkv_ref[pl.ds(low, c.win), c.W + at : c.W + at + lanes]
-        v = qkv_ref[pl.ds(low, c.win), 2 * c.W + at : 2 * c.W + at + lanes]
-        total = jnp.zeros((c.win, lanes), F32)
-        for head in range(lanes // HEAD):
-            mask = head_mask(lanes, head)
-            scores = dot_nt(jnp.where(mask, q, BF(0)), k)
-            scores = jnp.where(in_col, scores, LOW)
-            top = jnp.max(scores, axis=-1, keepdims=True)
-            exps = jnp.exp(scores - top)
-            probs = exps / jnp.sum(exps, axis=-1, keepdims=True)
-            total = total + dot_nn(probs.astype(BF), jnp.where(mask, v, BF(0)))
         old = mix_ref[group, pl.ds(low, c.win), :]
-        mix_ref[group, pl.ds(low, c.win), :] = jnp.where(in_row, total.astype(BF), old)
+        mix_ref[group, pl.ds(low, c.win), :] = jnp.where(in_row, total[:, at : at + lanes], old)
 
 
 def attend_back_body(c, place, qkv_ref, *refs):
     pieces, (out_ref, sums_ref, grad_ref) = refs[: c.n], refs[c.n :]
+
     @pl.when(pl.program_id(0) == 0)
     def _():
         out_ref[...] = jnp.zeros_like(out_ref)
@@ -497,36 +533,25 @@
     row = lax.broadcasted_iota(I32, (c.win, 1), 0)
     in_row = (row >= off) & (row < off + IMG_LEN)
     scale = HEAD**-0.5
-    for at, lanes in groups_of(c):
-        q = qkv_ref[pl.ds(low, c.win), at : at + lanes] * BF(scale)
-        k = qkv_ref[pl.ds(low, c.win), c.W + at : c.W + at + lanes]
-        v = qkv_ref[pl.ds(low, c.win), 2 * c.W + at : 2 * c.W + at + lanes]
-        do = jnp.where(in_row, grad_ref[pl.ds(low, c.win), at : at + lanes], BF(0))
-        dq = jnp.zeros((c.win, lanes), F32)
-        dk = jnp.zeros((c.win, lanes), F32)
-        dv = jnp.zeros((c.win, lanes), F32)
-        for head in range(lanes // HEAD):
-            mask = head_mask(lanes, head)
-            qh = jnp.where(mask, q, BF(0))
-            doh = jnp.where(mask, do, BF(0))
-            kh = jnp.where(mask, k, BF(0))
-            scores = jnp.where(in_row, dot_nt(k, qh), LOW)
-            top = jnp.max(scores, axis=0, keepdims=True)
-            exps = jnp.exp(scores - top)
-            soft = exps / jnp.sum(exps, axis=0, keepdims=True)
-            dp = dot_nt(v, doh)
-            delta = jnp.sum(soft * dp, axis=0, keepdims=True)
-            ds = (soft * (dp - delta)).astype(BF)
-            dq = dq + dot_tn(ds, kh)
-            dk = dk + dot_nn(ds, qh)
-            dv = dv + dot_nn(soft.astype(BF), doh)
-        for part, grad in enumerate((dq * scale, dk, dv)):
-            lane = part * c.W + at
-            low_grad = jnp.where(in_row, grad, 0.0).astype(BF)
-            old = out_ref[pl.ds(low, c.win), lane : lane + lanes]
-            out_ref[pl.ds(low, c.win), lane : lane + lanes] = jnp.where(in_row, low_grad, old)
-            summed = jnp.sum(low_grad.astype(F32), axis=0, keepdims=True)
-            sums_ref[0:1, lane : lane + lanes] += summed
+    q = stack_heads(c, qkv_ref[pl.ds(low, c.win), : c.W] * BF(scale))
+    k = qkv_ref[pl.ds(low, c.win), c.W : 2 * c.W]
+    v = qkv_ref[pl.ds(low, c.win), 2 * c.W :]
+    do = stack_heads(c, jnp.where(in_row, grad_ref[pl.ds(low, c.win), :], BF(0)))
+    scores = jnp.where(in_row, dot_nt(k, q), LOW)
+    exps = jnp.exp(scores - jnp.max(scores, axis=0, keepdims=True))
+    soft = exps * (1.0 / jnp.sum(exps, axis=0, keepdims=True))
+    dp = dot_nt(v, do)
+    delta = jnp.sum(soft * dp, axis=0, keepdims=True)
+    ds = (soft * (dp - delta)).astype(BF)
+    dq = pick_heads(c, dot_tn(ds, k)) * scale
+    dk = dot_nn(ds, q)
+    dv = dot_nn(soft.astype(BF), do)
+    for part, grad in enumerate((dq, dk, dv)):
+        lanes = slice(part * c.W, (part + 1) * c.W)
+        low_grad = jnp.where(in_row, grad, 0.0).astype(BF)
+        old = out_ref[pl.ds(low, c.win), lanes]
+        out_ref[pl.ds(low, c.win), lanes] = jnp.where(in_row, low_grad, old)
+        sums_ref[0:1, lanes] += jnp.sum(low_grad.astype(F32), axis=0, keepdims=True)
 
 
 def middle_body(c, place, *refs):
@@ -536,19 +561,20 @@
     mixes, refs = refs[:count], refs[count:]
     w_ref, tok_ref, small_ref, off_ref, slot_ref, rt_ref = refs[:6]
     hid_ref, weight_ref, mine_ref, keep_ref = refs[6:10]
-    after_ref, probs_ref, keep_lane_ref, weight_lane_ref, acc_ref = refs[10:]
+    after_ref, probs_ref, keep_lane_ref, weight_lane_ref, proj_ref = refs[10:]
     step = pl.program_id(0)
-    for h in range(2):
-        acc = None
+
+    @pl.when(step == 0)
+    def _():
         for k in range(c.n):
-            for group, (at, lanes) in enumerate(groups):
-                weights = w_ref[(place[1] ^ k) * 2 + h, at : at + lanes, :]
-                part = dot_nn(mixes[k * len(groups) + group][...], weights)
-                acc = part if acc is None else acc + part
-        acc_ref[:, h * c.half : (h + 1) * c.half] = acc
+            for h in range(2):
+                cols = slice(h * c.half, (h + 1) * c.half)
+                proj_ref[k * c.W : (k + 1) * c.W, cols] = w_ref[(place[1] ^ k) * 2 + h]
+
+    branch = dot_nn(jnp.concatenate([mix[...] for mix in mixes], axis=1), proj_ref[...])
     live = live_rows(c, step * c.R, c.R)
     tok = jnp.where(live, tok_ref[...].astype(F32), 0.0)
-    after = tok + acc_ref[...] + small_row(c, small_ref, 4)
+    after = tok + branch + small_row(c, small_ref, 4)
     normed, _ = norm_rows(after)
     hidden = (normed * small_row(c, small_ref, 1) + small_row(c, small_ref, 3)).astype(BF)
     hid_ref[...] = hidden
@@ -559,13 +585,16 @@
     slot = slot_ref[0]
     kept = (slot >= 0) & (slot + off_ref[:, 0:1] < c.cap)
     weight = jnp.where(kept, probs, 0.0)
-    weight_ref[0] = weight
+    high, rest = split_low(weight)
+    lane = lax.broadcasted_iota(I32, (c.E, 128), 1)
+    index = lax.broadcasted_iota(I32, (c.E, 128), 0)
+    both = dot_tn(high, (lane == index).astype(BF)) + dot_tn(rest, (lane == index + 64).astype(BF))
+    weight_ref[...] = both.astype(BF)
     for j in range(c.X):
         e = expert_of(c, place, j)
-        offset = offset_at(place, j)
         slot_j = slot_ref[0, pl.ds(e, 1), :]
-        kept_j = (slot_j >= 0) & (slot_j + offset < c.cap)
-        row = jnp.where(kept_j, slot_j + (offset - window_out(c, place, j)), -1)
+        kept_j = (slot_j >= 0) & (slot_j + offset_at(place, j) < c.cap)
+        row = jnp.where(kept_j, window_slot(c, place, j, slot_j), -1)
         mine_ref[0, j : j + 1, :] = row
     for j in range(c.X, 8):
         mine_ref[0, j : j + 1, :] = jnp.full((1, c.R), -1, I32)
@@ -594,7 +623,7 @@
     specs += [rows_of((1, c.E, c.R)), rows_of((1, 8, c.R))]
     outs = [
         shape_of((c.TP, c.D), BF),
-        shape_of((c.n, c.E, c.R), F32),
+        shape_of((c.TP, 128), BF),
         shape_of((c.n, 8, c.R), I32),
         shape_of((c.n, 8, c.R), F32),
         shape_of((c.R, c.D), F32),
@@ -604,7 +633,7 @@
     ]
     out_specs = [
         rows_of((c.R, c.D)),
-        rows_of((1, c.E, c.R)),
+        rows_of((c.R, 128)),
         rows_of((1, 8, c.R)),
         rows_of((1, 8, c.R)),
     ] + [whole(o) for o in outs[4:]]
@@ -617,19 +646,19 @@
         outs,
         out_specs,
         (c.n,),
-        [pltpu.VMEM((c.R, c.D), F32)],
+        [pltpu.VMEM((c.D, c.D), BF)],
         name="middle",
     )
 
 
-def pack_rows(c, place, rows, out_ref):
+def pack_rows(c, place, half, rows, out_ref, base=0, start=0):
     main = c.SP - 16
-    used = lax.broadcasted_iota(I32, (16, 1), 0) < c.S + 15 - main
-    out_ref[...] = jnp.zeros_like(out_ref)
+    used = lax.broadcasted_iota(I32, (16, 1), 0) < 14
+    out_ref[base : base + c.CR[half], :] = jnp.zeros((c.CR[half], c.D), BF)
     for j in range(c.X):
-        at = window_in(c, place, j)
-        out_ref[pl.ds(at, main), :] += rows[j, :main, :]
-        tail = jnp.where(used, rows[j, main:, :], BF(0))
+        at = pl.multiple_of(window_in(c, place, half, j) + base, 16)
+        out_ref[pl.ds(at, main), :] += rows[j, start : start + main, :]
+        tail = jnp.where(used, rows[j, start + main : start + c.SP, :], BF(0))
         out_ref[pl.ds(pl.multiple_of(at + main, 16), 16), :] += tail
 
 
@@ -638,24 +667,27 @@
     return tile[14:15, :], tile[15:16, :]
 
 
-def row_chunks(c, size):
-    return [(at, min(size, c.CR - at)) for at in range(0, c.CR, size)]
+def row_chunks(rows, size):
+    return [slice(at, min(at + size, rows)) for at in range(0, rows, size)]
 
 
 def grad_active_body(c, place, *refs):
-    rows, own_ref, oth_ref, out_ref, all_ref = refs
+    rows, own_ref, oth_ref, *outs, all_ref = refs
 
     @pl.when(pl.program_id(0) == 0)
     def _():
-        pack_rows(c, place, rows, all_ref)
+        pack_rows(c, place, 0, rows, all_ref)
+        pack_rows(c, place, 1, rows, all_ref, c.CR[0], c.SP)
 
     weights = jnp.concatenate([own_ref[...], oth_ref[...]], axis=1)
-    for at, size in row_chunks(c, 448):
-        out_ref[at : at + size, :] = dot_nt(all_ref[at : at + size, :], weights).astype(BF)
+    for half, base in enumerate((0, c.CR[0])):
+        for at in row_chunks(c.CR[half], 320):
+            values = all_ref[base + at.start : base + at.stop, :]
+            outs[half][at, :] = dot_nt(values, weights).astype(BF)
 
 
 def grad_active(c, order, place, rows, own_w, oth_w):
-    outs = [shape_of((c.CR, c.F), BF), shape_of((c.CR, c.D), BF)]
+    outs = [shape_of((rows, c.F), BF) for rows in c.CR] + [shape_of((sum(c.CR), c.D), BF)]
     return call(
         order,
         functools.partial(grad_active_body, c),
@@ -663,13 +695,13 @@
         [rows, own_w, oth_w],
         [whole(rows, 1)] + [rows_of((c.fblk, c.half))] * 2,
         outs,
-        [cols_of((c.CR, c.fblk)), whole(outs[1])],
+        [cols_of((rows, c.fblk)) for rows in c.CR] + [whole(outs[2])],
         (c.F // c.fblk,),
         name="grad_active",
     )
 
 
-def expert_body(c, place, *refs):
+def expert_body(c, half, place, *refs):
     rows, own_ref, oth_ref, bias_ref, ga_ref = refs[:5]
     act_ref, gp_ref, gb_ref, all_ref, col_ref, back_ref = refs[5:11]
     acc_ref, dot_ref, row_ref = refs[11:]
@@ -679,22 +711,25 @@
     def _():
         acc_ref[...] = jnp.zeros_like(acc_ref)
         dot_ref[...] = jnp.zeros_like(dot_ref)
-        pack_rows(c, place, rows, all_ref)
+        pack_rows(c, place, half, rows, all_ref)
         col_ref[...] = jnp.zeros_like(col_ref)
         eye = lax.broadcasted_iota(I32, (c.SP, c.SP), 0) == lax.broadcasted_iota(I32, (c.SP, c.SP), 1)
         for j in range(c.X):
             high, low = last_pair(c, rows[j, c.SP - 16 :, :], c.SP)
             col = jnp.sum(jnp.where(eye, high + low, 0.0), axis=1, keepdims=True)
-            col_ref[pl.ds(window_in(c, place, j), c.SP), :] += jnp.broadcast_to(col, (c.SP, 128))
+            col_ref[pl.ds(window_in(c, place, half, j), c.SP), :] += jnp.broadcast_to(col, (c.SP, 128))
 
     bias = bias_ref[...]
     weights = jnp.concatenate([own_ref[...], oth_ref[...]], axis=0)
     summed = jnp.zeros((1, c.fblk), F32)
     lead = 0.7978845608028654
     cube = lead * 0.044715
-    for at, size in row_chunks(c, 224):
-        rows_at = slice(at, at + size)
-        pre = dot_nn(all_ref[rows_at, :], weights) + bias
+    chunks = row_chunks(c.CR[half], 224)
+    ahead = dot_nn(all_ref[chunks[0], :], weights)
+    for i, rows_at in enumerate(chunks):
+        pre = ahead + bias
+        if i + 1 < len(chunks):
+            ahead = dot_nn(all_ref[chunks[i + 1], :], weights)
         square = pre * pre
         turn = jnp.tanh(pre * (cube * square + lead))
         above = 1.0 + turn
@@ -719,7 +754,7 @@
         ones = jnp.ones((8, 128), BF)
         row_ref[...] = jnp.zeros_like(row_ref)
         for j in range(c.X):
-            at = window_in(c, place, j)
+            at = window_in(c, place, half, j)
             back_ref[j] = acc_ref[pl.ds(at, c.SP), :].astype(BF)
             a, rest = split_low(dot_ref[pl.ds(at, c.SP), :])
             total = dot_nt(ones, a) + dot_nt(ones, rest)
@@ -731,22 +766,23 @@
             back_ref[j, c.SP - 16 :, : c.half] = tile.astype(BF)
 
 
-def expert(c, order, place, rows, own_w, oth_w, bias, ga):
+def expert(c, order, place, half, rows, own_w, oth_w, bias, ga):
     args = [rows, own_w, oth_w, bias, ga]
+    count = c.CR[half]
     specs = [whole(rows, 1)]
     specs += [cols_of((c.half, c.fblk))] * 2
-    specs += [cols_of((1, c.fblk)), cols_of((c.CR, c.fblk))]
+    specs += [cols_of((1, c.fblk)), cols_of((count, c.fblk))]
     outs = [
-        shape_of((c.CR, c.F), BF),
-        shape_of((c.CR, c.F), BF),
+        shape_of((count, c.F), BF),
+        shape_of((count, c.F), BF),
         shape_of((8, c.F), F32),
     ]
-    out_specs = [cols_of((c.CR, c.fblk))] * 2 + [cols_of((8, c.fblk))]
-    late = [shape_of((c.CR, c.D), BF), shape_of((c.CR, 128), F32)]
+    out_specs = [cols_of((count, c.fblk))] * 2 + [cols_of((8, c.fblk))]
+    late = [shape_of((count, c.D), BF), shape_of((count, 128), F32)]
     late.append(shape_of((c.X, c.SP, c.D), BF))
     return call(
         order,
-        functools.partial(expert_body, c),
+        functools.partial(expert_body, c, half),
         place,
         args,
         specs,
@@ -754,8 +790,8 @@
         out_specs + [whole(o, 1) for o in late],
         (c.F // c.fblk,),
         [
-            pltpu.VMEM((c.CR, c.D), F32),
-            pltpu.VMEM((c.CR, 128), F32),
+            pltpu.VMEM((count, c.D), F32),
+            pltpu.VMEM((count, 128), F32),
             pltpu.VMEM((16, c.half), F32),
         ],
         name="expert",
@@ -763,69 +799,69 @@
 
 
 def produce_body(c, place, *refs):
-    col_ref, act_ref, own_ref, oth_ref, out_ref, acc_ref = refs
+    cols, acts, own_ref, oth_ref, out_ref, accs = refs[:2], refs[2:4], refs[4], refs[5], refs[6], refs[7:]
     step = pl.program_id(0)
 
     @pl.when(step == 0)
     def _():
-        acc_ref[...] = jnp.zeros_like(acc_ref)
+        for acc_ref in accs:
+            acc_ref[...] = jnp.zeros_like(acc_ref)
 
     weights = jnp.concatenate([own_ref[...], oth_ref[...]], axis=1)
-    for at, size in row_chunks(c, 448):
-        acc_ref[at : at + size, :] += dot_nn(act_ref[at : at + size, :], weights)
+    for half in range(2):
+        for at in row_chunks(c.CR[half], 320):
+            accs[half][at, :] += dot_nn(acts[half][at, :], weights)
 
     @pl.when(step == pl.num_programs(0) - 1)
     def _():
-        for j in range(c.X):
-            rows_at = pl.ds(window_in(c, place, j), c.SP)
-            col = col_ref[rows_at, 0:1]
-            out_ref[j] = (acc_ref[rows_at, :] * col).astype(BF)
-
-
-def produce(c, order, place, col, act, own_w, oth_w):
-    out = shape_of((c.X, c.SP, c.D), BF)
+        for half in range(2):
+            for j in range(c.X):
+                rows_at = pl.ds(window_in(c, place, half, j), c.SP)
+                col = cols[half][rows_at, 0:1]
+                out_ref[j, half * c.SP : (half + 1) * c.SP, :] = (accs[half][rows_at, :] * col).astype(BF)
+
+
+def produce(c, order, place, cols, acts, own_w, oth_w):
+    out = shape_of((c.X, 2 * c.SP, c.D), BF)
     return call(
         order,
         functools.partial(produce_body, c),
         place,
-        [col, act, own_w, oth_w],
-        [
-            whole(col),
-            cols_of((c.CR, c.fblk)),
-            rows_of((c.fblk, c.half)),
-            rows_of((c.fblk, c.half)),
-        ],
+        [*cols, *acts, own_w, oth_w],
+        [whole(col) for col in cols]
+        + [cols_of((rows, c.fblk)) for rows in c.CR]
+        + [rows_of((c.fblk, c.half))] * 2,
         [out],
         [whole(out, 1)],
         (c.F // c.fblk,),
-        [pltpu.VMEM((c.CR, c.D), F32)],
+        [pltpu.VMEM((rows, c.D), F32) for rows in c.CR],
         name="produce",
     )[0]
 
 
 def grad_second_body(c, own, place, *refs):
-    refs = list(refs)
-    all_ref, col_ref, act_ref = refs[:3]
+    all_ref, cols, acts = refs[0], refs[1:3], refs[3:5]
     out_ref, row_ref = refs[-2:]
 
     @pl.when(pl.program_id(0) == 0)
     def _():
-        row_ref[...] = (all_ref[...].astype(F32) * col_ref[:, 0:1]).astype(BF)
-
-    acc = dot_tn(act_ref[...], row_ref[...])
+        for half, base in enumerate((0, c.CR[0])):
+            rows_at = slice(base, base + c.CR[half])
+            row_ref[rows_at, :] = (all_ref[rows_at, :].astype(F32) * cols[half][:, 0:1]).astype(BF)
+
+    acc = dot_tn(acts[0][...], row_ref[: c.CR[0], :])
+    acc = acc + dot_tn(acts[1][...], row_ref[c.CR[0] :, :])
     if own:
-        acc = acc + refs[3][...].astype(F32)
+        acc = acc + refs[5][...].astype(F32)
     out_ref[...] = acc.astype(out_ref.dtype)
 
 
-def grad_second(c, order, place, rows, col, act, add=None):
+def grad_second(c, order, place, rows, cols, acts, add=None):
     own = add is not None
-    args = [rows, col, act]
-    specs = [
-        pl.BlockSpec((c.CR, c.half), lambda i, s: (0, 0 if own else 1)),
-        whole(col),
-        cols_of((c.CR, c.fblk)),
-    ]
+    args = [rows, *cols, *acts]
+    total = sum(c.CR)
+    specs = [pl.BlockSpec((total, c.half), lambda i, s: (0, 0 if own else 1))]
+    specs += [whole(col) for col in cols] + [cols_of((count, c.fblk)) for count in c.CR]
     if own:
         args.append(add)
         specs.append(rows_of((c.fblk, c.half)))
@@ -839,25 +875,23 @@
         [out],
         [rows_of((c.fblk, c.half))],
         (c.F // c.fblk,),
-        [pltpu.VMEM((c.CR, c.half), BF)],
+        [pltpu.VMEM((total, c.half), BF)],
         name="grad_second",
     )[0]
 
 
 def grad_first_body(c, own, place, *refs):
-    acc = dot_tn(refs[0][...], refs[1][...])
+    acc = dot_tn(refs[0][...], refs[2][...]) + dot_tn(refs[1][...], refs[3][...])
     if own:
-        acc = acc + refs[2][...].astype(F32)
+        acc = acc + refs[4][...].astype(F32)
     refs[-1][...] = acc.astype(refs[-1].dtype)
 
 
-def grad_first(c, order, place, rows, gp, add=None):
+def grad_first(c, order, place, rows, gps, add=None):
     own = add is not None
-    args = [rows, gp]
-    specs = [
-        pl.BlockSpec((c.CR, c.half), lambda i, s: (0, 0 if own else 1)),
-        cols_of((c.CR, c.fblk)),
-    ]
+    args = [*rows, *gps]
+    specs = [pl.BlockSpec((count, c.half), lambda i, s: (0, 0 if own else 1)) for count in c.CR]
+    specs += [cols_of((count, c.fblk)) for count in c.CR]
     if own:
         args.append(add)
         specs.append(cols_of((c.half, c.fblk)))
@@ -877,41 +911,55 @@
 
 def combine_body(c, with_dots, place, *refs):
     refs = list(refs)
-    rows_ref = refs.pop(0)
-    tail_ref = refs.pop(0) if with_dots else None
+    halves = 2 if with_dots else 1
+    rows, refs = refs[:halves], refs[halves:]
+    tails = []
+    if with_dots:
+        tails, refs = refs[:2], refs[2:]
     mine_ref = refs.pop(0)
     groups = [(0, g) for g in groups_a(c)] + [(1, g) for g in groups_b(c)]
     outs, (hot_ref, row_ref) = refs[: len(groups)], refs[len(groups) :]
-    pad = hot_ref.shape[2] // c.X
+    pad = hot_ref.shape[1] // c.X
 
     @pl.when(pl.program_id(0) == 0)
     def _():
         row_ref[...] = jnp.zeros_like(row_ref)
         slots = lax.broadcasted_iota(I32, (c.R, pad), 1)
-        expert = lax.broadcasted_iota(I32, (c.E, 1), 0)
         for k in range(c.n):
             at = pl.multiple_of((place[1] ^ k) * c.R, 16)
-            pulls = jnp.zeros((c.E, c.R), F32)
             for j in range(c.X):
                 hot = (mine_ref[pl.ds(at, c.R), j : j + 1] == slots).astype(BF)
-                hot_ref[k, :, j * pad : (j + 1) * pad] = hot
-                if with_dots:
-                    high, low = last_pair(c, tail_ref[j], pad)
-                    both = jnp.concatenate(
-                        [jnp.broadcast_to(high, (8, pad)), jnp.broadcast_to(low, (8, pad))], axis=0
-                    )
-                    got = dot_nt(both.astype(BF), hot)
-                    got = got[0:1, :] + got[8:9, :]
-                    pulls = jnp.where(expert == expert_of(c, place, j), got, pulls)
-            if with_dots:
-                for (side, group), out_ref in zip(groups, outs):
-                    if side == 0 and k in group:
-                        at = group.index(k)
+                hot_ref[k * c.R : (k + 1) * c.R, j * pad : (j + 1) * pad] = hot
+        if with_dots:
+            wide = (c.SP, c.half)
+            eye = lax.broadcasted_iota(I32, wide, 0) == lax.broadcasted_iota(I32, wide, 1)
+            lane = lax.broadcasted_iota(I32, (1, 128), 1)
+            for half in range(2):
+                for j in range(c.X):
+                    high, low = last_pair(c, tails[half][j], c.half)
+                    high = jnp.sum(jnp.where(eye, high, 0.0), axis=1, keepdims=True)
+                    low = jnp.sum(jnp.where(eye, low, 0.0), axis=1, keepdims=True)
+                    e = expert_of(c, place, j)
+                    cols = jnp.where(lane == e, high, jnp.where(lane == e + 64, low, 0.0))
+                    at = j * pad + half * c.SP
+                    row_ref[at : at + c.SP, :128] = cols.astype(BF)
+            pulls = dot_nn(hot_ref[...], row_ref[:, :128]).astype(BF)
+            expert = lax.broadcasted_iota(I32, (c.E, 128), 0)
+            lane = lax.broadcasted_iota(I32, (c.E, 128), 1)
+            pick = ((lane == expert) | (lane == expert + 64)).astype(BF)
+            for (side, group), out_ref in zip(groups, outs):
+                for at, k in enumerate(group):
+                    if side == 0:
+                        got = dot_nt(pick, pulls[k * c.R : (k + 1) * c.R])
                         out_ref[at, c.R :, :] = jnp.zeros((c.E, c.half), BF)
-                        out_ref[at, c.R :, : c.R] = pulls.astype(BF)
-
-    for j in range(c.X):
-        row_ref[j * pad : j * pad + c.SP, :] = rows_ref[j]
+                        out_ref[at, c.R :, : c.R] = got.astype(BF)
+
+    for half, rows_ref in enumerate(rows):
+        size = rows_ref.shape[1]
+        for j in range(c.X):
+            at = j * pad + half * size
+            row_ref[at : at + size, :] = rows_ref[j]
+    result = dot_nn(hot_ref[...], row_ref[...]).astype(BF)
     for half in range(2):
 
         @pl.when(pl.program_id(0) == half)
@@ -919,16 +967,16 @@
             for (side, group), out_ref in zip(groups, outs):
                 if side == half:
                     for at, k in enumerate(group):
-                        out_ref[at, : c.R, :] = dot_nn(hot_ref[k], row_ref[...]).astype(BF)
-
-
-def combine(c, order, place, rows, mine, with_dots=False):
-    pad = up(c.SP, 128)
-    args = [rows]
-    specs = [pl.BlockSpec((c.X, c.SP, c.half), lambda i, s: (0, 0, i ^ s[2]))]
+                        out_ref[at, : c.R, :] = result[k * c.R : (k + 1) * c.R]
+
+
+def combine(c, order, place, rows, mine, with_dots=False, cost=0):
+    pad = up(2 * c.SP, 128)
+    args = list(rows)
+    specs = [pl.BlockSpec((c.X, r.shape[1], c.half), lambda i, s: (0, 0, i ^ s[2])) for r in rows]
     if with_dots:
-        args.append(rows)
-        specs.append(pl.BlockSpec((c.X, 16, c.half), lambda i, s: (0, c.SP // 16 - 1, 0)))
+        args += list(rows)
+        specs += [pl.BlockSpec((c.X, 16, c.half), lambda i, s: (0, c.SP // 16 - 1, 0))] * 2
     args.append(mine)
     specs.append(whole(mine))
     outs = piece_outs(c, c.E if with_dots else 0)
@@ -941,8 +989,9 @@
         outs,
         [whole(o, 1) for o in outs],
         (2,),
-        [pltpu.VMEM((c.n, c.R, c.X * pad), BF), pltpu.VMEM((c.X * pad, c.half), BF)],
+        [pltpu.VMEM((c.n * c.R, c.X * pad), BF), pltpu.VMEM((c.X * pad, c.half), BF)],
         name="combine",
+        cost=cost,
     )
     return list(result)
 
@@ -1121,42 +1170,27 @@
     return list(result[:-1]), result[-1]
 
 
-def grad_qkv_body(c, own, place, *refs):
-    hid_ref, dqkv_ref = refs[:2]
-    add_ref = refs[2] if own else None
-    out_ref = refs[-1]
-    acc = dot_tn(hid_ref[...], dqkv_ref[...])
-    if own:
-        acc = acc + add_ref[0].astype(F32)
-    out_ref[0] = acc.astype(BF)
-
-
-def grad_qkv(c, order, place, hidden, dqkv, add=None):
-    own = add is not None
-    args = [hidden, dqkv]
-    specs = [
-        pl.BlockSpec((c.TP, c.half), lambda i, s: (0, s[2] if own else 1 - s[2])),
-        cols_of((c.TP, c.W)),
-    ]
+def grad_qkv_body(c, place, hid_ref, dqkv_ref, own_ref, oth_ref):
+    own_ref[0] = dot_tn(hid_ref[:, own_cols(c, place)], dqkv_ref[...]).astype(BF)
+    oth_ref[0] = dot_tn(hid_ref[:, other_cols(c, place)], dqkv_ref[...]).astype(BF)
+
+
+def grad_qkv(c, order, place, hidden, dqkv):
+    specs = [whole(hidden, 1), cols_of((c.TP, c.W))]
     if c.W % 128:
         dqkv = dqkv.reshape(c.TP, 3, c.W).transpose(1, 0, 2)
-        args[1] = dqkv
         specs[1] = pl.BlockSpec((None, c.TP, c.W), lambda i, s: (i, 0, 0))
-    if own:
-        args.append(add)
-        specs.append(rows_of((1, c.half, c.W)))
-    out = shape_of((3, c.half, c.W), BF)
     return call(
         order,
-        functools.partial(grad_qkv_body, c, own),
-        place,
-        args,
+        functools.partial(grad_qkv_body, c),
+        place,
+        [hidden, dqkv],
         specs,
-        [out],
-        [rows_of((1, c.half, c.W))],
+        [shape_of((3, c.half, c.W), BF)] * 2,
+        [rows_of((1, c.half, c.W))] * 2,
         (3,),
         name="grad_qkv",
-    )[0]
+    )
 
 
 def back_one_body(c, place, *refs):
@@ -1250,18 +1284,21 @@
     F = w_first.shape[2]
     W = w_proj.shape[0]
     win = up(IMG_LEN + 15, 16)
-    SP = up(S + 17, 16)
+    Q = (S + 1) // 2
     cap = (9 * T + 4 * EXP_DEV - 1) // (4 * EXP_DEV)
+    X = E // EXP_DEV
+    full = min(cap // S, X)
     c = Sizes(
         T=T,
         D=D,
         half=D // 2,
         n=n,
-        X=E // EXP_DEV,
+        X=X,
         E=E,
         S=S,
-        SP=SP,
-        CR=up(cap, 128),
+        Q=Q,
+        SP=up(Q + 17, 16),
+        CR=(up(min(cap, X * Q), 16), up(full * (S - Q) + max(0, cap - full * S - Q), 16)),
         R=R,
         TP=n * R,
         W=W,
@@ -1280,9 +1317,9 @@
     experts = jnp.arange(E, dtype=I32)[:, None, None]
     count = jnp.sum((routes.T[None] == experts).astype(I32), axis=(1, 2))[None]
     counts = trade(jnp.broadcast_to(count, (c.X, E)), "dp")
-    slot, rt = route(c, order, here, routes, priority)
+    slot, blocks, rt = route(c, order, here, routes, priority)
     place, offsets = windows(c, order, here, counts)
-    grad_out = dispatch(c, order, place, slot, cotangent)
+    grad_out = dispatch(c, order, place, slot, cotangent, (0, 1))
     grad_in = trade(grad_out, "dp")
 
     bias_rows = F // 2 // c.half
@@ -1328,6 +1365,7 @@
         outs,
         [rows_of((c.R, D)), rows_of((c.R, 3 * W)), rows_of((c.R, D))],
         (n,),
+        [pltpu.VMEM((D, 3 * W), BF)],
         name="qkv",
     )
     groups = groups_of(c)
@@ -1345,29 +1383,39 @@
     )[0]
     mixes = gather_mp(c, mix)
     hidden_two, weight, mine, keep, after, probs, keep_lane, weight_lane = middle(
-        c, order, place, mixes, proj, tokens, small, offsets, slot, rt
+        c, order, place, mixes, proj, tokens, small, offsets, blocks, rt
     )
     keep_mask = keep[:, :2, :].transpose(0, 2, 1).reshape(c.TP, 2)[:T].astype(I32)
     mine = mine.transpose(0, 2, 1).reshape(c.TP, 8)
 
-    rows_in = trade(dispatch(c, order, place, slot, hidden_two, weight), "dp")
-    ga, grad_all = grad_active(c, order, place, grad_in, second_own, second_oth)
-    act, gp, gb, row_all, col, back = expert(
-        c, order, place, rows_in, first_own, first_oth, bias, ga
-    )
-    back = trade(back, "dp")
-    second_part = swap_grid(grad_second(c, order, place, grad_all, col, act))
-    first_part = swap_grid(grad_first(c, order, place, row_all, gp))
-    gb = gb[0:1].reshape(2, F // 2)
+    rows_a = trade(dispatch(c, order, place, slot, hidden_two, (0,), weight), "dp")
+    rows_b = dispatch(c, order, place, slot, hidden_two, (1,), weight)
+    ga_a, ga_b, grad_all = grad_active(c, order, place, grad_in, second_own, second_oth)
+    rows_b = trade(held(rows_b, rows_a, grad_all), "dp")
+    act_a, gp_a, gb_a, all_a, col_a, back_a = expert(
+        c, order, place, 0, rows_a, first_own, first_oth, bias, ga_a
+    )
+    back_a = trade(held(back_a, rows_b), "dp")
+    act_b, gp_b, gb_b, all_b, col_b, back_b = expert(
+        c, order, place, 1, rows_b, first_own, first_oth, bias, ga_b
+    )
+    back_b = trade(held(back_b, back_a), "dp")
+    order.tie(back_a)
+    cols, acts, gps, alls = [col_a, col_b], [act_a, act_b], [gp_a, gp_b], [all_a, all_b]
+    second_part = swap_grid(grad_second(c, order, place, grad_all, cols, acts))
+    first_part = swap_grid(grad_first(c, order, place, alls, gps))
+    prod = produce(c, order, place, cols, acts, second_own, second_oth)
+    gb = (gb_a + gb_b)[0:1].reshape(2, F // 2)
     gb_own = lax.dynamic_index_in_dim(gb, grid, 0, True)
     gb_oth = lax.dynamic_index_in_dim(gb, 1 - grid, 0, True)
     grad_fbias = gb_own + swap_grid(gb_oth)
-    prod = produce(c, order, place, col, act, second_own, second_oth)
-
-    two_sums = reduce_mp(c, combine(c, order, place, back, mine, True))
-    prod = trade(prod, "dp")
-    grad_second_out = grad_second(c, order, place, grad_all, col, act, second_part)
-    grad_first_out = grad_first(c, order, place, row_all, gp, first_part)
+
+    pieces = combine(c, order, place, [back_a, back_b], mine, True)
+    prod = trade(held(prod, back_b), "dp")
+    two_sums = reduce_start(c, pieces)
+    grad_second_out = grad_second(c, order, place, grad_all, cols, acts, second_part)
+    two_sums = reduce_end(c, order, two_sums)
+    grad_first_out = grad_first(c, order, place, alls, gps, first_part)
     grad_after, grad_branch, sums_two, grad_mix = back_two(
         c,
         order,
@@ -1380,7 +1428,10 @@
         small,
     )
     grad_mix = [grad_mix[0]] + [swap_mp(c, grad_mix[k], k) for k in range(1, n)]
+    pieces = combine(c, order, place, [prod], mine, cost=10)
+    out_sums = reduce_start(c, [held(p, *grad_mix) for p in pieces])
     proj_a, proj_b = grad_proj(c, order, place, mixes, grad_branch, sums_two)
+    proj_b = swap_grid(held(proj_b, *grad_mix))
 
     outs = [shape_of((c.TP, 3 * W), BF), shape_of((8, 3 * W), F32)]
     dqkv, dqkv_sums = call(
@@ -1395,27 +1446,31 @@
         [pltpu.VMEM((c.TP, W), BF)],
         name="attend_back",
     )
+    out_sums = reduce_end(c, order, out_sums)
     one_pieces, one_parts = grad_one(c, order, place, dqkv, normed_one, qkv_own, qkv_oth)
-    one_sums = reduce_mp(c, one_pieces)
-    qkv_part = swap_grid(grad_qkv(c, order, place, hidden_one, dqkv))
-    grad_w_qkv = grad_qkv(c, order, place, hidden_one, dqkv, qkv_part)
-    grad_w_qkv = sum_dp(c, grad_w_qkv.reshape(3 * c.half, W)).reshape(3, c.half, W)
-    prod_pieces = combine(c, order, place, prod, mine)
+    one_sums = reduce_start(c, [held(p, out_sums[0][-1], out_sums[1][-1]) for p in one_pieces])
+    qkv_a, qkv_b = grad_qkv(c, order, place, hidden_one, dqkv)
+    out_lane = block_out(c, order, place, out_sums, after, weight_lane, small)
+    one_sums = reduce_end(c, order, one_sums)
     grad_low, sums_one = back_one(c, order, place, one_sums, tokens, grad_after, small)
+    out_lane = gather_mp(c, held(out_lane, one_sums[0][-1], one_sums[1][-1]))
     grad_low = gather_mp(c, grad_low)
-    out_sums = reduce_mp(c, prod_pieces)
-    out_lane = block_out(c, order, place, out_sums, after, weight_lane, small)
-    out_lane = gather_mp(c, out_lane)
-
-    proj_low = (proj_a.astype(F32) + swap_grid(proj_b).astype(F32)).astype(BF)
-    proj_sum = sum_dp(c, sum_proj(c, proj_low))
+
+    qkv_b = swap_grid(qkv_b)
+    qkv_low = (qkv_a.astype(F32) + qkv_b.astype(F32)).astype(BF)
+    proj_low = (proj_a.astype(F32) + proj_b.astype(F32)).astype(BF)
+    proj_low = sum_proj(c, proj_low)
+    shared = jnp.concatenate([qkv_low.reshape(-1, c.half), proj_low], axis=0)
+    shared = lax.psum(shared, "dp").astype(F32)
+    grad_w_qkv = shared[: 3 * W].reshape(3, c.half, W)
+    proj_sum = shared[3 * W :]
     rest = proj_sum[W : W + 8 + 2 * E]
     qv_rows = jnp.concatenate([dqkv_sums[0:1, :W], dqkv_sums[0:1, 2 * W :]], axis=0)
     if n != 4:
         sums_one = fold(c, one_parts, (("mp", n),))
     sums_one = finish_sums(c, sums_one, qv_rows, grid)
+    block = assemble(c, order, place, out_lane, BF)
     grad_tokens = assemble(c, order, place, grad_low, F32)
-    block = assemble(c, order, place, out_lane, BF)
     return (
         block,
         grad_tokens,

time: 599 us -> 551 us (0.920)
  waiting for transfers between devices: 189 us -> 138 us
  Pallas kernels: 264 us -> 276 us
    all_to_all x9 -> x7, waiting for transfers between devices: 77.4 us -> 34.7 us  [trade(): return lax.all_to_all(value, axis, split_axis=0, concat_axis=0, tiled=True)]
    ppermute x29, waiting for transfers between devices: 107 us -> 83.8 us  [swap_mp(): return lax.ppermute(value, 'mp', [(i, i ^ mask) for i in range(c.n)])]
    pallas_call x26 -> x27, Pallas kernels: 264 us -> 276 us  [call(): pl.pallas_call(wrapped, grid_spec=pltpu.PrefetchScalarGridSpec(num_scalar...]
    psum x0 -> x1, waiting for transfers between devices: none -> 9.69 us  [local(): shared = lax.psum(shared, 'dp').astype(F32)]
    all_to_all x9 -> x7, starting transfers between devices: 39.6 us -> 33 us  [trade(): return lax.all_to_all(value, axis, split_axis=0, concat_axis=0, tiled=True)]
  transfers between devices with their start and end apart: 51 -> 50, of which waited for: 16 -> 18; matrix products, arithmetic and copies ran while one was open for 6% -> 6% of each run, Pallas kernels for 36% -> 48%
where the time goes in v2:
time: 551 us; the launch traced here: 541 us
  Pallas kernels  276 us (50%)
  waiting for transfers between devices  138 us (25%)
  starting transfers between devices  69.6 us (13%)
  local copies, waits for them, and re-layouts  24.2 us (4%)
  other arithmetic  18.1 us (3%)
  between operations  15.2 us (3%)
    pallas_call x27, Pallas kernels, call(): pl.pallas_call(wrapped, grid_spec=pltpu.PrefetchScalarGridSpec(num_scalar...  276 us
    ppermute x29, waiting for transfers between devices, swap_mp(): return lax.ppermute(value, 'mp', [(i, i ^ mask) for i in range(c.n)])  83.8 us
    all_to_all x7, waiting for transfers between devices, trade(): return lax.all_to_all(value, axis, split_axis=0, concat_axis=0, tiled=True)  34.7 us
    all_to_all x7, starting transfers between devices, trade(): return lax.all_to_all(value, axis, split_axis=0, concat_axis=0, tiled=True)  33 us
    ppermute x29, starting transfers between devices, swap_mp(): return lax.ppermute(value, 'mp', [(i, i ^ mask) for i in range(c.n)])  32.5 us
  transfers between devices with their start and end apart: 50, of which 18 were waited for; matrix products, arithmetic and copies ran while one was open for 6% of the time, Pallas kernels for 48%

profile of v2, /device:TPU:0, one launch (start us, length us, event | category | flops | bytes accessed | tf_op | source)
XLA Modules:
  0.0 541.2 jit_solution(5657407725455235045)
XLA Ops:
  18.8 8.9 %route.1 = (s32[16,1600]{1,0:T(8,128)}, s32[4,16,400]{2,1,0:T(8,128)}, s32[4,8,400]{2,1,0:T(8,128)}) custom-call(s32[4]{0:T(128)} %pad_add_fusion.place, s32[2,1576]{1,0:T(2,128)} %bitcast_add_fusion.refs_0_, s32[1576,2]{1,0:T(8,128)} %copy.52.refs_1_, s32[2,1576]{1,0:T(2,128)} %bitcast.55), custom_call_target="tpu_custom_call" | custom-call | flops 1000 | bytes 1000 | tf_op jit(solution)/shard_map/route/pallas_call | solution.py:101
  30.4 9.6 %dispatch.3.refs_4_ = bf16[1408,1024]{1,0:T(8,128)(2,1)} custom-call(s32[64]{0:T(128)} %get-tuple-element.97.place.refs_2_, s32[16,1600]{1,0:T(8,128)} %get-tuple-element.98.refs_0_, bf16[1576,1024]{1,0:T(8,128)(2,1)} %refs_11_.1, s32[64]{0:T(128)} %get-tuple-element.97.place.refs_2_), custom_call_target="tpu_custom_call" | custom-call | flops 1000 | bytes 1000 | tf_op jit(solution)/shard_map/dispatch/pallas_call | solution.py:101
  47.3 6.8 %collective-permute-done = bf16[48,512]{1,0:T(8,128)(2,1)S(1)} collective-permute-done((bf16[48,512]{1,0:T(8,128)(2,1)S(1)}, bf16[48,512]{1,0:T(8,128)(2,1)S(1)}, u32[]{:S(2)}, u32[]{:S(2)}) %collective-permute-start) | collective-permute-done | bytes 49184 | tf_op jit(solution)/shard_map/ppermute | solution.py:128
  55.6 9.3 %qkv.1 = (bf16[1600,1024]{1,0:T(8,128)(2,1)}, bf16[1600,768]{1,0:T(8,128)(2,1)}, bf16[1600,1024]{1,0:T(8,128)(2,1)}) custom-call(s32[64]{0:T(128)} %get-tuple-element.97.place.refs_2_, bf16[1576,1024]{1,0:T(8,128)(2,1)} %refs_6_.1, bf16[48,1024]{1,0:T(8,128)(2,1)} %maximum_select_fusion.refs_1_.refs_10_.refs_13_.refs_8_, bf16[3,512,256]{2,1,0:T(8,128)(2,1)} %bitcast.50, ...), custom_call_target="tpu_custom_call" | custom-call | flops 1000 | bytes 1000 | tf_op jit(solution)/shard_map/qkv/pallas_call | solution.py:101
  65.0 10.5 %attend.1.refs_0_.refs_1_.refs_14_ = bf16[2,1600,128]{2,1,0:T(8,128)(2,1)} custom-call(s32[64]{0:T(128)} %get-tuple-element.97.place.refs_2_, bf16[1600,768]{1,0:T(8,128)(2,1)} %get-tuple-element.99.refs_0_.refs_1_, bf16[1600,768]{1,0:T(8,128)(2,1)} %get-tuple-element.99.refs_0_.refs_1_), custom_call_target="tpu_custom_call" | custom-call | flops 1000 | bytes 1000 | tf_op jit(solution)/shard_map/attend/pallas_call | solution.py:101
  78.4 17.7 %collective-permute-done.3.refs_4_.refs_5_ = bf16[2,1600,128]{2,1,0:T(8,128)(2,1)S(1)} collective-permute-done((bf16[2,1600,128]{2,1,0:T(8,128)(2,1)}, bf16[2,1600,128]{2,1,0:T(8,128)(2,1)S(1)}, u32[]{:S(2)}, u32[]{:S(2)}) %collective-permute-start.3) | collective-permute-done | bytes 819232 | tf_op jit(solution)/shard_map/ppermute | solution.py:124
  99.4 8.0 %collective-permute-done.5.refs_7_ = bf16[1,1600,128]{2,1,0:T(8,128)(2,1)S(1)} collective-permute-done((bf16[1,1600,128]{2,1,0:T(8,128)(2,1)S(1)}, bf16[1,1600,128]{2,1,0:T(8,128)(2,1)S(1)}, u32[]{:S(2)}, u32[]{:S(2)}) %collective-permute-start.5) | collective-permute-done | bytes 409632 | tf_op jit(solution)/shard_map/ppermute | solution.py:124
  109.4 13.5 %middle.1 = (bf16[1600,1024]{1,0:T(8,128)(2,1)}, bf16[1600,128]{1,0:T(8,128)(2,1)}, s32[4,8,400]{2,1,0:T(8,128)}, f32[4,8,400]{2,1,0:T(8,128)}, f32[400,1024]{1,...) custom-call(s32[64]{0:T(128)} %get-tuple-element.97.place.refs_2_, ...), custom_call_target="tpu_custom_call" | custom-call | flops 1000 | bytes 1000 | tf_op jit(solution)/shard_map/middle/pallas_call | solution.py:101
  122.9 7.4 %dispatch.4.refs_3_ = bf16[704,1024]{1,0:T(8,128)(2,1)} custom-call(s32[64]{0:T(128)} %get-tuple-element.97.place.refs_2_, s32[16,1600]{1,0:T(8,128)} %get-tuple-element.98.refs_0_, bf16[1600,1024]{1,0:T(8,128)(2,1)} %get-tuple-element.103.refs_1_.refs_12_, bf16[1600,128]{1,0:T(8,128)(2,1)} %get-tuple-element.104.refs_2_, ...), custom_call_target="tpu_custom_call" | custom-call | flops 1000 | bytes 1000 | tf_op jit(solution)/shard_map/dispatch/pallas_call | solution.py:101
  135.7 7.4 %dispatch.5.refs_3_ = bf16[704,1024]{1,0:T(8,128)(2,1)} custom-call(s32[64]{0:T(128)} %get-tuple-element.97.place.refs_2_, s32[16,1600]{1,0:T(8,128)} %get-tuple-element.98.refs_0_, bf16[1600,1024]{1,0:T(8,128)(2,1)} %get-tuple-element.103.refs_1_.refs_12_, bf16[1600,128]{1,0:T(8,128)(2,1)} %get-tuple-element.104.refs_2_, bf16[704,1024]{1,0:T(8,128)(2,1)} %dispatch.4.refs_3_), custom_call_target="tpu_custom_call" | custom-call | flops 1000 | bytes 1000 | tf_op jit(solution)/shard_map/dispatch/pallas_call | solution.py:101
  143.2 16.0 %grad_active.1 = (bf16[640,4096]{1,0:T(8,128)(2,1)}, bf16[416,4096]{1,0:T(8,128)(2,1)}, bf16[1056,1024]{1,0:T(8,128)(2,1)}) custom-call(s32[64]{0:T(128)} %get-tuple-element.97.place.refs_2_, bf16[4,352,1024]{2,1,0:T(8,128)(2,1)} %all-to-all-done.2.refs_0_, bf16[4096,512]{1,0:T(8,128)(2,1)} %bitcast.43, ...), custom_call_target="tpu_custom_call" | custom-call | flops 1000 | bytes 1000 | tf_op jit(solution)/shard_map/grad_active/pallas_call | solution.py:101
  159.2 9.3 %all-to-all-done.1.refs_0_ = bf16[4,176,1024]{2,1,0:T(8,128)(2,1)S(1)} async-done(((bf16[4,176,1024]{2,1,0:T(8,128)(2,1)}), bf16[4,176,1024]{2,1,0:T(8,128)(2,1)S(1)}, u32[]{:S(2)}, u32[]{:S(2)}) %all-to-all-start.1) | async-done | bytes 1441824 | tf_op jit(solution)/shard_map/all_to_all | solution.py:136
  173.5 24.8 %expert.2 = (bf16[640,4096]{1,0:T(8,128)(2,1)}, bf16[640,4096]{1,0:T(8,128)(2,1)}, f32[8,4096]{1,0:T(8,128)}, bf16[640,1024]{1,0:T(8,128)(2,1)}, f32[640,128]{1,0:T(8,128)}, /*index=5*/bf16[4,176,1024]{2,1,0:T(8,128)(2,1)}) custom-call(s32[64]{0:T(128)} %get-tuple-element.97.place.refs_2_, bf16[4,176,1024]{2,1,0:T(8,128)(2,1)} %copy-done.6, ...), custom_call_target="tpu_custom_call" | custom-call | flops 1000 | bytes 1000 | tf_op jit(solution)/shard_map/expert/pallas_call | solution.py:101
  198.3 7.4 %all-to-all-done.3.refs_0_ = bf16[4,176,1024]{2,1,0:T(8,128)(2,1)S(1)} async-done(((bf16[4,176,1024]{2,1,0:T(8,128)(2,1)}), bf16[4,176,1024]{2,1,0:T(8,128)(2,1)S(1)}, u32[]{:S(2)}, u32[]{:S(2)}) %all-to-all-start.3) | async-done | bytes 1441824 | tf_op jit(solution)/shard_map/all_to_all | solution.py:136
  209.7 18.6 %expert.3 = (bf16[416,4096]{1,0:T(8,128)(2,1)}, bf16[416,4096]{1,0:T(8,128)(2,1)}, f32[8,4096]{1,0:T(8,128)}, bf16[416,1024]{1,0:T(8,128)(2,1)}, f32[416,128]{1,0:T(8,128)}, /*index=5*/bf16[4,176,1024]{2,1,0:T(8,128)(2,1)}) custom-call(s32[64]{0:T(128)} %get-tuple-element.97.place.refs_2_, bf16[4,176,1024]{2,1,0:T(8,128)(2,1)} %copy-done.7, ...), custom_call_target="tpu_custom_call" | custom-call | flops 1000 | bytes 1000 | tf_op jit(solution)/shard_map/expert/pallas_call | solution.py:101
  228.2 15.0 %all-to-all-done.4.refs_6_.refs_0_.refs_2_ = bf16[4,176,1024]{2,1,0:T(8,128)(2,1)S(1)} async-done(((bf16[4,176,1024]{2,1,0:T(8,128)(2,1)}), bf16[4,176,1024]{2,1,0:T(8,128)(2,1)S(1)}, u32[]{:S(2)}, u32[]{:S(2)}) %all-to-all-start.4) | async-done | bytes 1441824 | tf_op jit(solution)/shard_map/all_to_all | solution.py:136
  246.8 10.7 %grad_second.2.refs_4_ = bf16[4096,512]{1,0:T(8,128)(2,1)} custom-call(s32[64]{0:T(128)} %get-tuple-element.97.place.refs_2_, bf16[1056,1024]{1,0:T(8,128)(2,1)} %get-tuple-element.109.refs_5_.refs_0_, f32[640,128]{1,0:T(8,128)} %get-tuple-element.110.refs_1_.refs_0_, f32[416,128]{1,0:T(8,128)} %get-tuple-element.114.refs_2_.refs_1_, ...), custom_call_target="tpu_custom_call" | custom-call | flops 1000 | bytes 1000 | tf_op jit(solution)/shard_map/grad_second/pallas_call | solution.py:101
  257.5 10.3 %grad_first.2.refs_6_ = bf16[512,4096]{1,0:T(8,128)(2,1)} custom-call(s32[64]{0:T(128)} %get-tuple-element.97.place.refs_2_, bf16[640,1024]{1,0:T(8,128)(2,1)} %get-tuple-element.117.refs_0_, bf16[416,1024]{1,0:T(8,128)(2,1)} %get-tuple-element.118.refs_1_, bf16[640,4096]{1,0:T(8,128)(2,1)} %get-tuple-element.119.refs_2_, ...), custom_call_target="tpu_custom_call" | custom-call | flops 1000 | bytes 1000 | tf_op jit(solution)/shard_map/grad_first/pallas_call | solution.py:101
  267.8 15.6 %produce.1.refs_5_ = bf16[4,352,1024]{2,1,0:T(8,128)(2,1)} custom-call(s32[64]{0:T(128)} %get-tuple-element.97.place.refs_2_, f32[640,128]{1,0:T(8,128)} %get-tuple-element.110.refs_1_.refs_0_, f32[416,128]{1,0:T(8,128)} %get-tuple-element.114.refs_2_.refs_1_, bf16[640,4096]{1,0:T(8,128)(2,1)} %get-tuple-element.115.refs_3_.refs_2_, ...), custom_call_target="tpu_custom_call" | custom-call | flops 1000 | bytes 1000 | tf_op jit(solution)/shard_map/produce/pallas_call | solution.py:101
  291.3 12.5 %combine.2 = (bf16[2,416,512]{2,1,0:T(8,128)(2,1)}, bf16[2,416,512]{2,1,0:T(8,128)(2,1)}, bf16[2,400,512]{2,1,0:T(8,128)(2,1)}, bf16[2,400,512]{2,1,0:T(8,128)(2,1)}) custom-call(s32[64]{0:T(128)} %get-tuple-element.97.place.refs_2_, bf16[4,176,1024]{2,1,0:T(8,128)(2,1)} %copy-done, bf16[4,176,1024]{2,1,0:T(8,128)(2,1)} %copy-done.4, ...), custom_call_target="tpu_custom_call" | custom-call | flops 1000 | bytes 1000 | tf_op jit(solution)/shard_map/combine/pallas_call | solution.py:101
  305.9 12.7 %grad_second.3.refs_5_ = f32[4096,512]{1,0:T(8,128)} custom-call(s32[64]{0:T(128)} %get-tuple-element.97.place.refs_2_, bf16[1056,1024]{1,0:T(8,128)(2,1)} %get-tuple-element.109.refs_5_.refs_0_, f32[640,128]{1,0:T(8,128)} %get-tuple-element.110.refs_1_.refs_0_, f32[416,128]{1,0:T(8,128)} %get-tuple-element.114.refs_2_.refs_1_, ...), custom_call_target="tpu_custom_call" | custom-call | flops 1000 | bytes 1000 | tf_op jit(solution)/shard_map/grad_second/pallas_call | solution.py:101
  318.7 6.4 %collective-permute-done.9.refs_4_ = bf16[2,400,512]{2,1,0:T(8,128)(2,1)S(1)} collective-permute-done((bf16[2,400,512]{2,1,0:T(8,128)(2,1)}, bf16[2,400,512]{2,1,0:T(8,128)(2,1)S(1)}, u32[]{:S(2)}, u32[]{:S(2)}) %collective-permute-start.9) | collective-permute-done | bytes 819232 | tf_op jit(solution)/shard_map/ppermute | solution.py:124
  328.0 12.2 %grad_first.3.refs_14_ = f32[512,4096]{1,0:T(8,128)} custom-call(s32[64]{0:T(128)} %get-tuple-element.97.place.refs_2_, bf16[640,1024]{1,0:T(8,128)(2,1)} %get-tuple-element.117.refs_0_, bf16[416,1024]{1,0:T(8,128)(2,1)} %get-tuple-element.118.refs_1_, bf16[640,4096]{1,0:T(8,128)(2,1)} %get-tuple-element.119.refs_2_, ...), custom_call_target="tpu_custom_call" | custom-call | flops 1000 | bytes 1000 | tf_op jit(solution)/shard_map/grad_first/pallas_call | solution.py:101
  341.1 7.9 %back_two.1 = (f32[400,1024]{1,0:T(8,128)}, bf16[400,1024]{1,0:T(8,128)(2,1)}, f32[40,1024]{1,0:T(8,128)}, bf16[400,256]{1,0:T(8,128)(2,1)}, bf16[400,256]{1,0:T...) custom-call(s32[64]{0:T(128)} %get-tuple-element.97.place.refs_2_, ...), custom_call_target="tpu_custom_call" | custom-call | flops 1000 | bytes 1000 | tf_op jit(solution)/shard_map/back_two/pallas_call | solution.py:101
  355.4 10.9 %combine.3 = (bf16[2,400,512]{2,1,0:T(8,128)(2,1)}, bf16[2,400,512]{2,1,0:T(8,128)(2,1)}, bf16[2,400,512]{2,1,0:T(8,128)(2,1)}, bf16[2,400,512]{2,1,0:T(8,128)(2,1)}) custom-call(s32[64]{0:T(128)} %get-tuple-element.97.place.refs_2_, bf16[4,352,1024]{2,1,0:T(8,128)(2,1)} %all-to-all-done.6.refs_0_, s32[1600,8]{1,0:T(8,128)} %bitcast.49, ...), custom_call_target="tpu_custom_call" | custom-call | flops 11000000512 | bytes 1000 | tf_op jit(solution)/shard_map/combine/pallas_call | solution.py:101
  373.6 13.9 %attend_back.1 = (bf16[1600,768]{1,0:T(8,128)(2,1)}, f32[8,768]{1,0:T(8,128)}) custom-call(s32[64]{0:T(128)} %get-tuple-element.97.place.refs_2_, bf16[1600,768]{1,0:T(8,128)(2,1)} %get-tuple-element.99.refs_0_.refs_1_, bf16[400,256]{1,0:T(8,128)(2,1)} %get-tuple-element.139.refs_1_, bf16[400,256]{1,0:T(8,128)(2,1)} %copy-done.38, ...), custom_call_target="tpu_custom_call" | custom-call | flops 1000 | bytes 1000 | tf_op jit(solution)/shard_map/attend_back/pallas_call | solution.py:101
  391.4 8.5 %grad_one.1 = (bf16[2,416,512]{2,1,0:T(8,128)(2,1)}, bf16[2,416,512]{2,1,0:T(8,128)(2,1)}, bf16[2,416,512]{2,1,0:T(8,128)(2,1)}, bf16[2,416,512]{2,1,0:T(8,128)(2,1)}, f32[2,1024]{1,0:T(2,128)}) custom-call(s32[64]{0:T(128)} %get-tuple-element.97.place.refs_2_, bf16[1600,768]{1,0:T(8,128)(2,1)} %get-tuple-element.156.refs_0_.refs_1_, ...), custom_call_target="tpu_custom_call" | custom-call | flops 1000 | bytes 1000 | tf_op jit(solution)/shard_map/grad_one/pallas_call | solution.py:101
  408.4 7.7 %grad_qkv.1 = (bf16[3,512,256]{2,1,0:T(8,128)(2,1)}, bf16[3,512,256]{2,1,0:T(8,128)(2,1)}) custom-call(s32[64]{0:T(128)} %get-tuple-element.97.place.refs_2_, bf16[1600,1024]{1,0:T(8,128)(2,1)} %get-tuple-element.155.refs_0_, bf16[1600,768]{1,0:T(8,128)(2,1)} %get-tuple-element.156.refs_0_.refs_1_, f32[2,1024]{1,0:T(2,128)} %get-tuple-element.158.refs_2_), custom_call_target="tpu_custom_call" | custom-call | flops 1000 | bytes 1000 | tf_op jit(solution)/shard_map/grad_qkv/pallas_call | solution.py:101
  421.1 14.4 %collective-permute-done.35 = bf16[2,320,512]{2,1,0:T(8,128)(2,1)} collective-permute-done((bf16[2,320,512]{2,1,0:T(8,128)(2,1)S(1)}, bf16[2,320,512]{2,1,0:T(8,128)(2,1)}, u32[]{:S(2)}, u32[]{:S(2)}) %collective-permute-start.35) | collective-permute-done | bytes 655392 | tf_op jit(solution)/shard_map/ppermute | solution.py:124
  474.3 10.5 %collective-permute-done.26.refs_4_.refs_5_ = bf16[2,400,512]{2,1,0:T(8,128)(2,1)S(1)} collective-permute-done((bf16[2,400,512]{2,1,0:T(8,128)(2,1)S(1)}, bf16[2,400,512]{2,1,0:T(8,128)(2,1)S(1)}, u32[]{:S(2)}, u32[]{:S(2)}) %collective-permute-start.26) | collective-permute-done | bytes 819232 | tf_op jit(solution)/shard_map/ppermute | solution.py:124
  488.2 14.1 %collective-permute-done.30.refs_4_.refs_5_ = bf16[2,400,512]{2,1,0:T(8,128)(2,1)S(1)} collective-permute-done((bf16[2,400,512]{2,1,0:T(8,128)(2,1)}, bf16[2,400,512]{2,1,0:T(8,128)(2,1)S(1)}, u32[]{:S(2)}, u32[]{:S(2)}) %collective-permute-start.30) | collective-permute-done | bytes 819232 | tf_op jit(solution)/shard_map/ppermute | solution.py:124
  506.6 9.7 %all-reduce.6.cloned.1.call-done = bf16[1088,512]{1,0:T(8,128)(2,1)} async-done(((bf16[1088,512]{1,0:T(8,128)(2,1)}), bf16[1088,512]{1,0:T(8,128)(2,1)}) %all-reduce.6.cloned.1.call-update) | async-done | bytes 1114128 | tf_op jit(solution)/shard_map/psum | solution.py:1464
  (266 shorter events, 157.7 us)
Async XLA Ops:
  40.0 90.3 %all-to-all-start.2 = ((bf16[4,352,1024]{2,1,0:T(8,128)(2,1)}), bf16[4,352,1024]{2,1,0:T(8,128)(2,1)}, u32[]{:S(2)}, u32[]{:S(2)}) async-start(bf16[4,352,1024]{2,1,0:T(8,128)(2,1)} %bitcast.38), calls=%async_computation.2 | async-start | bytes 5767168 | tf_op jit(solution)/shard_map/all_to_all | solution.py:136
  45.3 63.3 %all-gather.3.cloned.1.call-start = ((), (), s32[]{:S(2)}) async-start(), calls=%async_computation.8 | async-start | bytes 2359296 | tf_op jit(solution)/shard_map/all_gather | solution.py:1354
  46.0 97.2 %collective-permute-start.7 = (bf16[4096,512]{1,0:T(8,128)(2,1)}, bf16[4096,512]{1,0:T(8,128)(2,1)}, u32[]{:S(2)}, u32[]{:S(2)}) collective-permute-start(bf16[4096,512]{1,0:T(8,128)(2,1)} %bitcast.42), channel_id=1, source_target_pairs={{0,1},{1,0},{2,3},{3,2},{4,5},{5,4},{6,7},{7,6},{8,9},{9,8},{10,11... | collective-permute-start | bytes 12582920 | tf_op jit(solution)/shard_map/ppermute | solution.py:128
  75.4 20.7 %collective-permute-start.3 = (bf16[2,1600,128]{2,1,0:T(8,128)(2,1)}, bf16[2,1600,128]{2,1,0:T(8,128)(2,1)S(1)}, u32[]{:S(2)}, u32[]{:S(2)}) collective-permute-start(bf16[2,1600,128]{2,1,0:T(8,128)(2,1)} %attend.1.refs_0_.refs_1_.refs_14_), channel_id=1, source_target_pairs={{0,4},{2,6},{4,0},{6,2},{1,5},{3,7},{5,1},{7,3},{8,12},{10,14},{12... | collective-permute-start | bytes 2457608 | tf_op jit(solution)/shard_map/ppermute | solution.py:124
  76.9 20.8 %collective-permute-start.2 = (bf16[2,1600,128]{2,1,0:T(8,128)(2,1)}, bf16[2,1600,128]{2,1,0:T(8,128)(2,1)S(1)}, u32[]{:S(2)}, u32[]{:S(2)}) collective-permute-start(bf16[2,1600,128]{2,1,0:T(8,128)(2,1)} %attend.1.refs_0_.refs_1_.refs_14_), channel_id=1, source_target_pairs={{0,2},{2,0},{4,6},{6,4},{1,3},{3,1},{5,7},{7,5},{8,10},{10,8},{12,... | collective-permute-start | bytes 2457608 | tf_op jit(solution)/shard_map/ppermute | solution.py:124
  130.3 38.2 %all-to-all-start.1 = ((bf16[4,176,1024]{2,1,0:T(8,128)(2,1)}), bf16[4,176,1024]{2,1,0:T(8,128)(2,1)S(1)}, u32[]{:S(2)}, u32[]{:S(2)}) async-start(bf16[4,176,1024]{2,1,0:T(8,128)(2,1)} %bitcast.45), calls=%async_computation.1 | async-start | bytes 2883584 | tf_op jit(solution)/shard_map/all_to_all | solution.py:136
  135.7 37.9 %collective-permute-start.6 = (bf16[512,4096]{1,0:T(8,128)(2,1)}, bf16[512,4096]{1,0:T(8,128)(2,1)}, u32[]{:S(2)}, u32[]{:S(2)}) collective-permute-start(bf16[512,4096]{1,0:T(8,128)(2,1)} %bitcast.39), channel_id=1, source_target_pairs={{0,1},{1,0},{2,3},{3,2},{4,5},{5,4},{6,7},{7,6},{8,9},{9,8},{10,11... | collective-permute-start | bytes 12582920 | tf_op jit(solution)/shard_map/ppermute | solution.py:128
  168.5 37.2 %all-to-all-start.3 = ((bf16[4,176,1024]{2,1,0:T(8,128)(2,1)}), bf16[4,176,1024]{2,1,0:T(8,128)(2,1)S(1)}, u32[]{:S(2)}, u32[]{:S(2)}) async-start(bf16[4,176,1024]{2,1,0:T(8,128)(2,1)} %bitcast.14), calls=%async_computation.3 | async-start | bytes 2883584 | tf_op jit(solution)/shard_map/all_to_all | solution.py:136
  205.7 37.6 %all-to-all-start.4 = ((bf16[4,176,1024]{2,1,0:T(8,128)(2,1)}), bf16[4,176,1024]{2,1,0:T(8,128)(2,1)S(1)}, u32[]{:S(2)}, u32[]{:S(2)}) async-start(bf16[4,176,1024]{2,1,0:T(8,128)(2,1)} %get-tuple-element.123), calls=%async_computation.4 | async-start | bytes 2883584 | tf_op jit(solution)/shard_map/all_to_all | solution.py:136
  243.3 40.2 %all-to-all-start.5 = ((bf16[4,176,1024]{2,1,0:T(8,128)(2,1)}), bf16[4,176,1024]{2,1,0:T(8,128)(2,1)S(1)}, u32[]{:S(2)}, u32[]{:S(2)}) async-start(bf16[4,176,1024]{2,1,0:T(8,128)(2,1)} %get-tuple-element.125), calls=%async_computation.5 | async-start | bytes 2883584 | tf_op jit(solution)/shard_map/all_to_all | solution.py:136
  257.5 48.4 %collective-permute-start.10 = (bf16[4096,512]{1,0:T(8,128)(2,1)}, bf16[4096,512]{1,0:T(8,128)(2,1)}, u32[]{:S(2)}, u32[]{:S(2)}) collective-permute-start(bf16[4096,512]{1,0:T(8,128)(2,1)} %grad_second.2.refs_4_), channel_id=1, source_target_pairs={{0,1},{1,0},{2,3},{3,2},{4,5},{5,4},{6,7},{7,6},{8,9},{9,8},{10,11... | collective-permute-start | bytes 12582920 | tf_op jit(solution)/shard_map/ppermute | solution.py:128
  284.5 70.9 %all-to-all-start.6 = ((bf16[4,352,1024]{2,1,0:T(8,128)(2,1)}), bf16[4,352,1024]{2,1,0:T(8,128)(2,1)}, u32[]{:S(2)}, u32[]{:S(2)}) async-start(bf16[4,352,1024]{2,1,0:T(8,128)(2,1)} %produce.1.refs_5_), calls=%async_computation.6 | async-start | bytes 5767168 | tf_op jit(solution)/shard_map/all_to_all | solution.py:136
  289.6 226.7 %all-reduce.6.cloned.1.call-start = ((), (), s32[]{:S(2)}) async-start(), calls=%async_computation.7 | async-start | bytes 2228224 | tf_op jit(solution)/shard_map/psum | solution.py:1464
  289.8 38.2 %collective-permute-start.13 = (bf16[512,4096]{1,0:T(8,128)(2,1)}, bf16[512,4096]{1,0:T(8,128)(2,1)}, u32[]{:S(2)}, u32[]{:S(2)}) collective-permute-start(bf16[512,4096]{1,0:T(8,128)(2,1)} %grad_first.2.refs_6_), channel_id=1, source_target_pairs={{0,1},{1,0},{2,3},{3,2},{4,5},{5,4},{6,7},{7,6},{8,9},{9,8},{10,11... | collective-permute-start | bytes 12582920 | tf_op jit(solution)/shard_map/ppermute | solution.py:128
  303.8 21.3 %collective-permute-start.8 = (bf16[2,416,512]{2,1,0:T(8,128)(2,1)}, bf16[2,416,512]{2,1,0:T(8,128)(2,1)S(1)}, u32[]{:S(2)}, u32[]{:S(2)}) collective-permute-start(bf16[2,416,512]{2,1,0:T(8,128)(2,1)} %get-tuple-element.129), channel_id=1, source_target_pairs={{0,2},{2,0},{4,6},{6,4},{1,3},{3,1},{5,7},{7,5},{8,10},{10,8},{12,... | collective-permute-start | bytes 2555912 | tf_op jit(solution)/shard_map/ppermute | solution.py:124
  304.9 20.2 %collective-permute-start.9 = (bf16[2,400,512]{2,1,0:T(8,128)(2,1)}, bf16[2,400,512]{2,1,0:T(8,128)(2,1)S(1)}, u32[]{:S(2)}, u32[]{:S(2)}) collective-permute-start(bf16[2,400,512]{2,1,0:T(8,128)(2,1)} %get-tuple-element.130), channel_id=1, source_target_pairs={{0,4},{2,6},{4,0},{6,2},{1,5},{3,7},{5,1},{7,3},{8,12},{10,14},{12... | collective-permute-start | bytes 2457608 | tf_op jit(solution)/shard_map/ppermute | solution.py:124
  366.4 21.2 %collective-permute-start.17 = (bf16[2,400,512]{2,1,0:T(8,128)(2,1)}, bf16[2,400,512]{2,1,0:T(8,128)(2,1)S(1)}, u32[]{:S(2)}, u32[]{:S(2)}) collective-permute-start(bf16[2,400,512]{2,1,0:T(8,128)(2,1)} %get-tuple-element.145), channel_id=1, source_target_pairs={{0,2},{2,0},{4,6},{6,4},{1,3},{3,1},{5,7},{7,5},{8,10},{10,8},{12,... | collective-permute-start | bytes 2457608 | tf_op jit(solution)/shard_map/ppermute | solution.py:124
  367.5 20.0 %collective-permute-start.18 = (bf16[2,400,512]{2,1,0:T(8,128)(2,1)}, bf16[2,400,512]{2,1,0:T(8,128)(2,1)S(1)}, u32[]{:S(2)}, u32[]{:S(2)}) collective-permute-start(bf16[2,400,512]{2,1,0:T(8,128)(2,1)} %get-tuple-element.147), channel_id=1, source_target_pairs={{0,4},{2,6},{4,0},{6,2},{1,5},{3,7},{5,1},{7,3},{8,12},{10,14},{12... | collective-permute-start | bytes 2457608 | tf_op jit(solution)/shard_map/ppermute | solution.py:124
  373.5 29.1 %collective-permute-start.34 = (bf16[4,320,512]{2,1,0:T(8,128)(2,1)}, bf16[4,320,512]{2,1,0:T(8,128)(2,1)}, u32[]{:S(2)}, u32[]{:S(2)}) collective-permute-start(bf16[4,320,512]{2,1,0:T(8,128)(2,1)} %get-tuple-element.176), channel_id=1, source_target_pairs={{0,1},{1,0},{2,3},{3,2},{4,5},{5,4},{6,7},{7,6},{8,9},{9,8},{10,11... | collective-permute-start | bytes 3932168 | tf_op jit(solution)/shard_map/ppermute | solution.py:128
  401.0 35.8 %collective-permute-start.21 = (bf16[2,416,512]{2,1,0:T(8,128)(2,1)}, bf16[2,416,512]{2,1,0:T(8,128)(2,1)}, u32[]{:S(2)}, u32[]{:S(2)}) collective-permute-start(bf16[2,416,512]{2,1,0:T(8,128)(2,1)} %get-tuple-element.163), channel_id=1, source_target_pairs={{0,2},{2,0},{4,6},{6,4},{1,3},{3,1},{5,7},{7,5},{8,10},{10,8},{12,... | collective-permute-start | bytes 2555912 | tf_op jit(solution)/shard_map/ppermute | solution.py:124
  402.0 34.8 %collective-permute-start.22 = (bf16[2,416,512]{2,1,0:T(8,128)(2,1)}, bf16[2,416,512]{2,1,0:T(8,128)(2,1)}, u32[]{:S(2)}, u32[]{:S(2)}) collective-permute-start(bf16[2,416,512]{2,1,0:T(8,128)(2,1)} %get-tuple-element.165), channel_id=1, source_target_pairs={{0,4},{2,6},{4,0},{6,2},{1,5},{3,7},{5,1},{7,3},{8,12},{10,14},{12... | collective-permute-start | bytes 2555912 | tf_op jit(solution)/shard_map/ppermute | solution.py:124
  404.3 31.2 %collective-permute-start.35 = (bf16[2,320,512]{2,1,0:T(8,128)(2,1)S(1)}, bf16[2,320,512]{2,1,0:T(8,128)(2,1)}, u32[]{:S(2)}, u32[]{:S(2)}) collective-permute-start(bf16[2,320,512]{2,1,0:T(8,128)(2,1)S(1)} %slice.169), channel_id=1, source_target_pairs={{0,2},{2,0},{4,6},{6,4},{1,3},{3,1},{5,7},{7,5},{8,10},{10,8},{12,... | collective-permute-start | bytes 1966088 | tf_op jit(solution)/shard_map/ppermute | solution.py:124
  407.1 61.3 %collective-permute-start.40 = (f32[1,2048]{1,0:T(1,128)}, f32[1,2048]{1,0:T(1,128)}, u32[]{:S(2)}, u32[]{:S(2)}) collective-permute-start(f32[1,2048]{1,0:T(1,128)} %constant_dynamic-slice_fusion), channel_id=1, source_target_pairs={{0,1},{1,0},{2,3},{3,2},{4,5},{5,4},{6,7},{7,6},{8,9},{9,8},{10,11... | collective-permute-start | bytes 24584 | tf_op jit(solution)/shard_map/ppermute | solution.py:128
  416.0 27.3 %collective-permute-start.33 = (bf16[3,512,256]{2,1,0:T(8,128)(2,1)}, bf16[3,512,256]{2,1,0:T(8,128)(2,1)S(1)}, u32[]{:S(2)}, u32[]{:S(2)}) collective-permute-start(bf16[3,512,256]{2,1,0:T(8,128)(2,1)} %get-tuple-element.174), channel_id=1, source_target_pairs={{0,1},{1,0},{2,3},{3,2},{4,5},{5,4},{6,7},{7,6},{8,9},{9,8},{10,11... | collective-permute-start | bytes 2359304 | tf_op jit(solution)/shard_map/ppermute | solution.py:128
  463.7 21.1 %collective-permute-start.26 = (bf16[2,400,512]{2,1,0:T(8,128)(2,1)S(1)}, bf16[2,400,512]{2,1,0:T(8,128)(2,1)S(1)}, u32[]{:S(2)}, u32[]{:S(2)}) collective-permute-start(bf16[2,400,512]{2,1,0:T(8,128)(2,1)S(1)} %copy-done.3), channel_id=1, source_target_pairs={{0,4},{2,6},{4,0},{6,2},{1,5},{3,7},{5,1},{7,3},{8,12},{10,14},{12... | collective-permute-start | bytes 2457608 | tf_op jit(solution)/shard_map/ppermute | solution.py:124
  464.5 21.7 %collective-permute-start.25 = (bf16[2,400,512]{2,1,0:T(8,128)(2,1)S(1)}, bf16[2,400,512]{2,1,0:T(8,128)(2,1)S(1)}, u32[]{:S(2)}, u32[]{:S(2)}) collective-permute-start(bf16[2,400,512]{2,1,0:T(8,128)(2,1)S(1)} %copy-done.3), channel_id=1, source_target_pairs={{0,2},{2,0},{4,6},{6,4},{1,3},{3,1},{5,7},{7,5},{8,10},{10,8},{12,... | collective-permute-start | bytes 2457608 | tf_op jit(solution)/shard_map/ppermute | solution.py:124
  465.5 36.8 %collective-permute-start.30 = (bf16[2,400,512]{2,1,0:T(8,128)(2,1)}, bf16[2,400,512]{2,1,0:T(8,128)(2,1)S(1)}, u32[]{:S(2)}, u32[]{:S(2)}) collective-permute-start(bf16[2,400,512]{2,1,0:T(8,128)(2,1)} %get-tuple-element.173.refs_0_.refs_1_), channel_id=1, source_target_pairs={{0,4},{2,6},{4,0},{6,2},{1,5},{3,7},{5,1},{7,3},{8,12},{10,14},{12... | collective-permute-start | bytes 2457608 | tf_op jit(solution)/shard_map/ppermute | solution.py:124
  466.4 37.4 %collective-permute-start.29 = (bf16[2,400,512]{2,1,0:T(8,128)(2,1)}, bf16[2,400,512]{2,1,0:T(8,128)(2,1)S(1)}, u32[]{:S(2)}, u32[]{:S(2)}) collective-permute-start(bf16[2,400,512]{2,1,0:T(8,128)(2,1)} %get-tuple-element.173.refs_0_.refs_1_), channel_id=1, source_target_pairs={{0,2},{2,0},{4,6},{6,4},{1,3},{3,1},{5,7},{7,5},{8,10},{10,8},{12,... | collective-permute-start | bytes 2457608 | tf_op jit(solution)/shard_map/ppermute | solution.py:124
  485.6 37.9 %collective-permute-start.28 = (bf16[1,400,512]{2,1,0:T(8,128)(2,1)}, bf16[1,400,512]{2,1,0:T(8,128)(2,1)}, u32[]{:S(2)}, u32[]{:S(2)}) collective-permute-start(bf16[1,400,512]{2,1,0:T(8,128)(2,1)} %slice.165), channel_id=1, source_target_pairs={{0,2},{2,0},{4,6},{6,4},{1,3},{3,1},{5,7},{7,5},{8,10},{10,8},{12,... | collective-permute-start | bytes 1228808 | tf_op jit(solution)/shard_map/ppermute | solution.py:124
  487.1 36.4 %collective-permute-start.27 = (bf16[1,400,512]{2,1,0:T(8,128)(2,1)}, bf16[1,400,512]{2,1,0:T(8,128)(2,1)}, u32[]{:S(2)}, u32[]{:S(2)}) collective-permute-start(bf16[1,400,512]{2,1,0:T(8,128)(2,1)} %slice.164), channel_id=1, source_target_pairs={{0,4},{2,6},{4,0},{6,2},{1,5},{3,7},{5,1},{7,3},{8,12},{10,14},{12... | collective-permute-start | bytes 1228808 | tf_op jit(solution)/shard_map/ppermute | solution.py:124
  503.2 25.1 %collective-permute-start.32 = (bf16[1,400,512]{2,1,0:T(8,128)(2,1)}, bf16[1,400,512]{2,1,0:T(8,128)(2,1)}, u32[]{:S(2)}, u32[]{:S(2)}) collective-permute-start(bf16[1,400,512]{2,1,0:T(8,128)(2,1)} %slice.167), channel_id=1, source_target_pairs={{0,2},{2,0},{4,6},{6,4},{1,3},{3,1},{5,7},{7,5},{8,10},{10,8},{12,... | collective-permute-start | bytes 1228808 | tf_op jit(solution)/shard_map/ppermute | solution.py:124
  505.5 22.8 %collective-permute-start.31 = (bf16[1,400,512]{2,1,0:T(8,128)(2,1)}, bf16[1,400,512]{2,1,0:T(8,128)(2,1)}, u32[]{:S(2)}, u32[]{:S(2)}) collective-permute-start(bf16[1,400,512]{2,1,0:T(8,128)(2,1)} %slice.166), channel_id=1, source_target_pairs={{0,4},{2,6},{4,0},{6,2},{1,5},{3,7},{5,1},{7,3},{8,12},{10,14},{12... | collective-permute-start | bytes 1228808 | tf_op jit(solution)/shard_map/ppermute | solution.py:124
  (71 other events, 633.4 us)
Sparse Core Ops, SparseCore 0:
  48.0 29.3 all-gather.2
  463.8 52.4 all-reduce.5

commit v3 on v2

--- a/solution.py
+++ b/solution.py
@@ -173,6 +173,15 @@
     return pl.BlockSpec((None,) + dims[1:], lambda i, s: (0, 0, 0))
 
 
+def same_sum(c, refs, rows):
+    parts = [ref[rows, :].astype(F32) for ref in refs]
+    if c.n == 4:
+        return (parts[0] + parts[1]).astype(BF).astype(F32) + parts[2]
+    while len(parts) > 1:
+        parts = [parts[i] + parts[i + 1] for i in range(0, len(parts), 2)]
+    return parts[0]
+
+
 def add_up(refs):
     total = refs[0][...].astype(F32)
     for ref in refs[1:]:
@@ -180,16 +189,29 @@
     return total
 
 
-def gather_mp(c, value):
+def sum_dp_start(c, value):
+    parts = trade(value.reshape((c.X, value.shape[0] // c.X) + value.shape[1:]), "dp")
+    total = jnp.sum(parts.astype(F32), axis=0).astype(BF)
+    return jnp.broadcast_to(total[None], (c.X,) + total.shape)
+
+
+def sum_dp_end(c, spread):
+    return trade(spread, "dp").reshape((-1,) + spread.shape[2:]).astype(F32)
+
+
+def gather_mp(c, value, until=None):
     if c.n != 4 or value.shape[0] != 2:
         parts = [value] + [swap_mp(c, value, k) for k in range(1, c.n)]
-        return [[(p, h) for h in range(value.shape[0])] for p in parts]
+        return [[(p, h) for h in range(value.shape[0])] for p in parts], parts[1:]
     one = swap_mp(c, value, 1)
     two = swap_mp(c, value, 2)
-    far_a = swap_mp(c, one[0:1], 2)
-    far_b = swap_mp(c, two[1:2], 1)
+    ends = one[0:1], two[1:2]
+    if until is not None:
+        ends = held(ends[0], until), held(ends[1], until)
+    far_a = swap_mp(c, ends[0], 2)
+    far_b = swap_mp(c, ends[1], 1)
     near = [[(p, 0), (p, 1)] for p in (value, one, two)]
-    return near + [[(far_a, 0), (far_b, 0)]]
+    return near + [[(far_a, 0), (far_b, 0)]], [one, two]
 
 
 def flat(pieces):
@@ -212,13 +234,6 @@
         return jnp.concatenate([cols, jnp.pad(row, ((0, 0), (0, c.half - c.W)))], axis=0)
 
     return fold(c, half_of(grid) + swap_grid(half_of(1 - grid)), (("dp", c.X),))
-
-
-def sum_proj(c, value):
-    if c.n != 4:
-        return jnp.sum(trade(value, "mp").astype(F32), axis=0).astype(BF)
-    pair = (value[:2].astype(F32) + swap_mp(c, value[2:], 1).astype(F32)).astype(BF)
-    return (pair[0].astype(F32) + swap_mp(c, pair[1], 2).astype(F32)).astype(BF)
 
 
 def expert_of(c, place, j):
@@ -559,17 +574,16 @@
     groups = groups_of(c)
     count = c.n * len(groups)
     mixes, refs = refs[:count], refs[count:]
-    w_ref, tok_ref, small_ref, off_ref, slot_ref, rt_ref = refs[:6]
-    hid_ref, weight_ref, mine_ref, keep_ref = refs[6:10]
-    after_ref, probs_ref, keep_lane_ref, weight_lane_ref, proj_ref = refs[10:]
+    own_ref, oth_ref, tok_ref, small_ref, off_ref, slot_ref, rt_ref = refs[:7]
+    hid_ref, weight_ref, mine_ref, keep_ref = refs[7:11]
+    after_ref, probs_ref, keep_lane_ref, weight_lane_ref, proj_ref = refs[11:]
     step = pl.program_id(0)
 
     @pl.when(step == 0)
     def _():
         for k in range(c.n):
-            for h in range(2):
-                cols = slice(h * c.half, (h + 1) * c.half)
-                proj_ref[k * c.W : (k + 1) * c.W, cols] = w_ref[(place[1] ^ k) * 2 + h]
+            proj_ref[k * c.W : (k + 1) * c.W, own_cols(c, place)] = own_ref[k]
+            proj_ref[k * c.W : (k + 1) * c.W, other_cols(c, place)] = oth_ref[k]
 
     branch = dot_nn(jnp.concatenate([mix[...] for mix in mixes], axis=1), proj_ref[...])
     live = live_rows(c, step * c.R, c.R)
@@ -613,13 +627,13 @@
         weight_lane_ref[...] = weight
 
 
-def middle(c, order, place, mixes, proj, tokens, small, offsets, slot, rt):
-    args = [pair[0] for pair in flat(mixes)] + [proj, tokens, small, offsets, slot, rt]
+def middle(c, order, place, mixes, own_w, oth_w, tokens, small, offsets, slot, rt):
+    args = [pair[0] for pair in flat(mixes)] + [own_w, oth_w, tokens, small, offsets, slot, rt]
     specs = [
         pl.BlockSpec((None, c.R, a.shape[2]), lambda i, s, at=at: (at, i, 0))
         for a, at in flat(mixes)
     ]
-    specs += [whole(proj), rows_of((c.R, c.D)), whole(small), whole(offsets)]
+    specs += [whole(own_w), whole(oth_w), rows_of((c.R, c.D)), whole(small), whole(offsets)]
     specs += [rows_of((1, c.E, c.R)), rows_of((1, 8, c.R))]
     outs = [
         shape_of((c.TP, c.D), BF),
@@ -911,6 +925,7 @@
 
 def combine_body(c, with_dots, place, *refs):
     refs = list(refs)
+    extra_ref = None if with_dots else refs.pop(0)
     halves = 2 if with_dots else 1
     rows, refs = refs[:halves], refs[halves:]
     tails = []
@@ -968,21 +983,28 @@
                 if side == half:
                     for at, k in enumerate(group):
                         out_ref[at, : c.R, :] = result[k * c.R : (k + 1) * c.R]
-
-
-def combine(c, order, place, rows, mine, with_dots=False, cost=0):
+                        if extra_ref is not None:
+                            more = extra_ref.shape[1] // 2
+                            out_ref[at, c.R :, :] = extra_ref[k, half * more : (half + 1) * more, :]
+
+
+def combine(c, order, place, rows, mine, extra=None, cost=0):
     pad = up(2 * c.SP, 128)
     args = list(rows)
     specs = [pl.BlockSpec((c.X, r.shape[1], c.half), lambda i, s: (0, 0, i ^ s[2])) for r in rows]
-    if with_dots:
+    if extra is None:
         args += list(rows)
         specs += [pl.BlockSpec((c.X, 16, c.half), lambda i, s: (0, c.SP // 16 - 1, 0))] * 2
+        outs = piece_outs(c, c.E)
+    else:
+        args.insert(0, extra)
+        specs.insert(0, whole(extra))
+        outs = piece_outs(c, extra.shape[1] // 2, extra.shape[1] // 2)
     args.append(mine)
     specs.append(whole(mine))
-    outs = piece_outs(c, c.E if with_dots else 0)
     result = call(
         order,
-        functools.partial(combine_body, c, with_dots),
+        functools.partial(combine_body, c, extra is None),
         place,
         args,
         specs,
@@ -998,11 +1020,13 @@
 
 def back_two_body(c, place, *refs):
     refs = list(refs)
-    count = (len(refs) - 11 - c.n) // 2
+    groups = groups_of(c)
+    heads, refs = refs[: c.n * len(groups)], refs[c.n * len(groups) :]
+    count = (len(refs) - 14 - c.n) // 2
     a, b, refs = refs[:count], refs[count : 2 * count], refs[2 * count :]
-    w_ref, after_ref, probs_ref, keep_ref, weight_ref, cot_ref, hid_ref, small_ref = refs[:8]
-    ga_ref, gb_ref, sums_ref = refs[8:11]
-    mixes = refs[11:]
+    own_ref, oth_ref, after_ref, probs_ref, keep_ref, weight_ref, cot_ref, hid_ref, small_ref = refs[:9]
+    ga_ref, proj_own_ref, proj_oth_ref = refs[9:12]
+    mixes, (gb_ref, sums_ref) = refs[12:-2], refs[-2:]
     sum_a = add_up(a)
     live = live_rows(c, place[1] * c.R, c.R)
     cot = jnp.where(live, cot_ref[...], BF(0))
@@ -1027,22 +1051,35 @@
     sums_ref[8 : 8 + c.E, :] = dot_nn(high, cot) + dot_nn(rest, cot)
     sums_ref[8 + c.E : 8 + 2 * c.E, :] = dot_nn(glog, hid)
     for k in range(c.n):
-        lane = place[1] ^ k
-        mix = dot_nt(gb_ref[:, : c.half], w_ref[2 * lane])
-        mix = mix + dot_nt(gb_ref[:, c.half :], w_ref[2 * lane + 1])
+        mix = dot_nt(gb_ref[:, own_cols(c, place)], own_ref[k])
+        mix = mix + dot_nt(gb_ref[:, other_cols(c, place)], oth_ref[k])
         mixes[k][...] = mix.astype(BF)
-
-
-def back_two(c, order, place, sums, proj, lanes, cotangent, hidden, small):
-    args = [*sums[0], *sums[1], proj, *lanes, cotangent, hidden, small]
+    height = sums_ref.shape[0]
+    for cols, out_ref in ((own_cols(c, place), proj_own_ref), (other_cols(c, place), proj_oth_ref)):
+        sums = sums_ref[:, cols].astype(BF)
+        for k in range(c.n):
+            for group, (at, lanes) in enumerate(groups):
+                part = dot_tn(heads[k * len(groups) + group][...], gb_ref[:, cols])
+                out_ref[k, at : at + lanes, :] = part.astype(BF)
+            out_ref[k, c.W : c.W + height, :] = sums
+            rest = out_ref.shape[1] - c.W - height
+            out_ref[k, c.W + height :, :] = jnp.zeros((rest, c.half), BF)
+
+
+def back_two(c, order, place, heads, sums, own_w, oth_w, lanes, cotangent, hidden, small):
+    height = 8 + 2 * c.E
+    rows = up(c.W + height, 32)
+    args = [pair[0] for pair in flat(heads)]
+    specs = [
+        pl.BlockSpec((None, c.R, a.shape[2]), lambda i, s, at=at: (at, s[1], 0))
+        for a, at in flat(heads)
+    ]
+    args += [*sums[0], *sums[1], own_w, oth_w, *lanes, cotangent, hidden, small]
     lane_rows = pl.BlockSpec((c.R, c.D), lambda i, s: (s[1], 0))
-    specs = [first_block(a) for a in [*sums[0], *sums[1]]]
-    specs += [whole(a) for a in [proj, *lanes]] + [lane_rows, lane_rows, whole(small)]
-    outs = [
-        shape_of((c.R, c.D), F32),
-        shape_of((c.R, c.D), BF),
-        shape_of((8 + 2 * c.E, c.D), F32),
-    ] + [shape_of((c.R, c.W), BF) for _ in range(c.n)]
+    specs += [first_block(a) for a in [*sums[0], *sums[1]]]
+    specs += [whole(a) for a in [own_w, oth_w, *lanes]] + [lane_rows, lane_rows, whole(small)]
+    outs = [shape_of((c.R, c.D), F32)] + [shape_of((c.n, rows, c.half), BF)] * 2
+    outs += [shape_of((c.R, c.W), BF) for _ in range(c.n)]
     result = call(
         order,
         functools.partial(back_two_body, c),
@@ -1052,6 +1089,7 @@
         outs,
         [whole(o) for o in outs],
         (1,),
+        [pltpu.VMEM((c.R, c.D), BF), pltpu.VMEM((height, c.D), F32)],
         name="back_two",
     )
     return (*result[:3], list(result[3:]))
@@ -1059,66 +1097,34 @@
 
 def block_out_body(c, place, *refs):
     refs = list(refs)
-    count = (len(refs) - 4) // 2
+    count = (len(refs) - 5) // 2
     a, b, refs = refs[:count], refs[count : 2 * count], refs[2 * count :]
-    after_ref, weight_ref, small_ref, out_ref = refs
+    after_ref, weight_ref, small_ref, out_ref, proj_ref = refs
     high, low = split_low(weight_ref[...])
     eshift = small_ref[6 : 6 + c.E, :]
     shift = dot_tn(high, eshift) + dot_tn(low, eshift)
+    more = proj_ref.shape[0] // 2
     for h, pieces in enumerate((a, b)):
         cols = slice(h * c.half, (h + 1) * c.half)
-        out_ref[h] = (after_ref[:, cols] + add_up(pieces) + shift[:, cols]).astype(BF)
+        total = add_up([ref.at[: c.R, :] for ref in pieces])
+        out_ref[h] = (after_ref[:, cols] + total + shift[:, cols]).astype(BF)
+        proj_ref[h * more : (h + 1) * more, :] = same_sum(c, pieces, slice(c.R, c.R + more)).astype(BF)
 
 
 def block_out(c, order, place, sums, after, weight, small):
     args = [*sums[0], *sums[1], after, weight, small]
-    out = shape_of((2, c.R, c.half), BF)
+    more = 2 * (sums[0][0].shape[1] - c.R)
+    outs = [shape_of((2, c.R, c.half), BF), shape_of((more, c.half), BF)]
     return call(
         order,
         functools.partial(block_out_body, c),
         place,
         args,
         [first_block(a) for a in args[:-3]] + [whole(a) for a in args[-3:]],
-        [out],
-        [whole(out)],
-        (1,),
-        name="block_out",
-    )[0]
-
-
-def grad_proj_body(c, place, *refs):
-    groups = groups_of(c)
-    count = c.n * len(groups)
-    mixes, (gb_ref, sums_ref, own_ref, oth_ref) = refs[:count], refs[count:]
-    height = sums_ref.shape[0]
-    slot = [0, 2, 1, 3] if c.n == 4 else [place[1] ^ k for k in range(c.n)]
-    for cols, out_ref in ((own_cols(c, place), own_ref), (other_cols(c, place), oth_ref)):
-        out_ref[...] = jnp.zeros_like(out_ref)
-        sums = sums_ref[:, cols].astype(BF)
-        for k in range(c.n):
-            for group, (at, lanes) in enumerate(groups):
-                part = dot_tn(mixes[k * len(groups) + group][...], gb_ref[:, cols])
-                out_ref[slot[k], at : at + lanes, :] = part.astype(BF)
-            out_ref[slot[k], c.W : c.W + height, :] = sums
-
-
-def grad_proj(c, order, place, mixes, grad_branch, sums):
-    rows = up(c.W + sums.shape[0], 16 * c.X)
-    specs = [
-        pl.BlockSpec((None, c.R, a.shape[2]), lambda i, s, at=at: (at, s[1], 0))
-        for a, at in flat(mixes)
-    ]
-    outs = [shape_of((c.n, rows, c.half), BF)] * 2
-    return call(
-        order,
-        functools.partial(grad_proj_body, c),
-        place,
-        [pair[0] for pair in flat(mixes)] + [grad_branch, sums],
-        specs + [whole(grad_branch), whole(sums)],
         outs,
         [whole(o) for o in outs],
         (1,),
-        name="grad_proj",
+        name="block_out",
     )
 
 
@@ -1317,11 +1323,6 @@
     experts = jnp.arange(E, dtype=I32)[:, None, None]
     count = jnp.sum((routes.T[None] == experts).astype(I32), axis=(1, 2))[None]
     counts = trade(jnp.broadcast_to(count, (c.X, E)), "dp")
-    slot, blocks, rt = route(c, order, here, routes, priority)
-    place, offsets = windows(c, order, here, counts)
-    grad_out = dispatch(c, order, place, slot, cotangent, (0, 1))
-    grad_in = trade(grad_out, "dp")
-
     bias_rows = F // 2 // c.half
     packed = jnp.concatenate(
         [
@@ -1346,14 +1347,22 @@
     bias = bias.transpose(1, 0, 2).reshape(1, F).astype(F32)
     qkv_own = w_qkv.transpose(1, 0, 2)
     qkv_oth = swap_grid(qkv_own)
+    slot, blocks, rt = route(c, order, here, routes, priority)
+    order.tie(packed_oth)
+    order.tie(qkv_oth)
+    proj_own = jnp.stack([w_proj] + [swap_mp(c, w_proj, k) for k in range(1, n)])
+    order.tie(proj_own)
+    place, offsets = windows(c, order, here, counts)
+    grad_out = dispatch(c, order, place, slot, cotangent, (0, 1))
+    grad_in = trade(grad_out, "dp")
+
     first_own = w_first[0]
     second_own = w_second[0]
-    proj_tied, second_tied, first_tied, _ = lax.optimization_barrier(
-        (w_proj, second_own, first_own, grad_out)
-    )
-    proj = lax.all_gather(proj_tied, ("mp", "grid"))
+    second_tied, first_tied, _ = lax.optimization_barrier((second_own, first_own, grad_out))
     second_oth = swap_grid(second_tied)
     first_oth = swap_grid(first_tied)
+
+    proj_oth = swap_grid(proj_own)
 
     outs = [shape_of((c.TP, D), BF), shape_of((c.TP, 3 * W), BF), shape_of((c.TP, D), BF)]
     hidden_one, qkv, normed_one = call(
@@ -1381,9 +1390,9 @@
         (c.images,),
         name="attend",
     )[0]
-    mixes = gather_mp(c, mix)
+    mixes, _ = gather_mp(c, mix)
     hidden_two, weight, mine, keep, after, probs, keep_lane, weight_lane = middle(
-        c, order, place, mixes, proj, tokens, small, offsets, blocks, rt
+        c, order, place, mixes, proj_own, proj_oth, tokens, small, offsets, blocks, rt
     )
     keep_mask = keep[:, :2, :].transpose(0, 2, 1).reshape(c.TP, 2)[:T].astype(I32)
     mine = mine.transpose(0, 2, 1).reshape(c.TP, 8)
@@ -1400,9 +1409,9 @@
         c, order, place, 1, rows_b, first_own, first_oth, bias, ga_b
     )
     back_b = trade(held(back_b, back_a), "dp")
-    order.tie(back_a)
     cols, acts, gps, alls = [col_a, col_b], [act_a, act_b], [gp_a, gp_b], [all_a, all_b]
     second_part = swap_grid(grad_second(c, order, place, grad_all, cols, acts))
+    order.tie(back_a)
     first_part = swap_grid(grad_first(c, order, place, alls, gps))
     prod = produce(c, order, place, cols, acts, second_own, second_oth)
     gb = (gb_a + gb_b)[0:1].reshape(2, F // 2)
@@ -1410,28 +1419,29 @@
     gb_oth = lax.dynamic_index_in_dim(gb, 1 - grid, 0, True)
     grad_fbias = gb_own + swap_grid(gb_oth)
 
-    pieces = combine(c, order, place, [back_a, back_b], mine, True)
+    pieces = combine(c, order, place, [back_a, back_b], mine)
     prod = trade(held(prod, back_b), "dp")
     two_sums = reduce_start(c, pieces)
     grad_second_out = grad_second(c, order, place, grad_all, cols, acts, second_part)
     two_sums = reduce_end(c, order, two_sums)
     grad_first_out = grad_first(c, order, place, alls, gps, first_part)
-    grad_after, grad_branch, sums_two, grad_mix = back_two(
+    grad_after, proj_a, proj_b, grad_mix = back_two(
         c,
         order,
         place,
+        mixes,
         two_sums,
-        proj,
+        proj_own,
+        proj_oth,
         [after, probs, keep_lane, weight_lane],
         cotangent,
         hidden_two,
         small,
     )
     grad_mix = [grad_mix[0]] + [swap_mp(c, grad_mix[k], k) for k in range(1, n)]
-    pieces = combine(c, order, place, [prod], mine, cost=10)
+    proj_low = (proj_a.astype(F32) + swap_grid(proj_b).astype(F32)).astype(BF)
+    pieces = combine(c, order, place, [prod], mine, proj_low, cost=10)
     out_sums = reduce_start(c, [held(p, *grad_mix) for p in pieces])
-    proj_a, proj_b = grad_proj(c, order, place, mixes, grad_branch, sums_two)
-    proj_b = swap_grid(held(proj_b, *grad_mix))
 
     outs = [shape_of((c.TP, 3 * W), BF), shape_of((8, 3 * W), F32)]
     dqkv, dqkv_sums = call(
@@ -1446,22 +1456,23 @@
         [pltpu.VMEM((c.TP, W), BF)],
         name="attend_back",
     )
+    one_pieces, one_parts = grad_one(c, order, place, dqkv, normed_one, qkv_own, qkv_oth)
+    one_sums = reduce_start(c, one_pieces)
     out_sums = reduce_end(c, order, out_sums)
-    one_pieces, one_parts = grad_one(c, order, place, dqkv, normed_one, qkv_own, qkv_oth)
-    one_sums = reduce_start(c, [held(p, out_sums[0][-1], out_sums[1][-1]) for p in one_pieces])
     qkv_a, qkv_b = grad_qkv(c, order, place, hidden_one, dqkv)
-    out_lane = block_out(c, order, place, out_sums, after, weight_lane, small)
+    out_lane, proj_sum = block_out(c, order, place, out_sums, after, weight_lane, small)
     one_sums = reduce_end(c, order, one_sums)
-    grad_low, sums_one = back_one(c, order, place, one_sums, tokens, grad_after, small)
-    out_lane = gather_mp(c, held(out_lane, one_sums[0][-1], one_sums[1][-1]))
-    grad_low = gather_mp(c, grad_low)
-
     qkv_b = swap_grid(qkv_b)
     qkv_low = (qkv_a.astype(F32) + qkv_b.astype(F32)).astype(BF)
-    proj_low = (proj_a.astype(F32) + proj_b.astype(F32)).astype(BF)
-    proj_low = sum_proj(c, proj_low)
-    shared = jnp.concatenate([qkv_low.reshape(-1, c.half), proj_low], axis=0)
-    shared = lax.psum(shared, "dp").astype(F32)
+    proj_rows = proj_sum.shape[0]
+    shared = jnp.concatenate([qkv_low.reshape(-1, c.half), proj_sum], axis=0)
+    shared = sum_dp_start(c, shared)
+    grad_low, sums_one = back_one(c, order, place, one_sums, tokens, grad_after, small)
+    grad_low, first_low = gather_mp(c, grad_low, shared)
+    out_lane, _ = gather_mp(c, held(out_lane, *first_low))
+    sums_one = held(sums_one, *[pair[0] for pair in grad_low[-1]])
+
+    shared = sum_dp_end(c, shared)
     grad_w_qkv = shared[: 3 * W].reshape(3, c.half, W)
     proj_sum = shared[3 * W :]
     rest = proj_sum[W : W + 8 + 2 * E]
@@ -1469,8 +1480,8 @@
     if n != 4:
         sums_one = fold(c, one_parts, (("mp", n),))
     sums_one = finish_sums(c, sums_one, qv_rows, grid)
+    grad_tokens = assemble(c, order, place, grad_low, F32)
     block = assemble(c, order, place, out_lane, BF)
-    grad_tokens = assemble(c, order, place, grad_low, F32)
     return (
         block,
         grad_tokens,

time: 551 us -> 531 us (0.964)
  waiting for transfers between devices: 138 us -> 118 us
  starting transfers between devices: 69.6 us -> 83.8 us
  between operations: 15.2 us -> 1.7 us
    psum x1 -> x0, waiting for transfers between devices: 9.69 us -> none  [local(): shared = lax.psum(shared, 'dp').astype(F32)]
    all_to_all x7 -> x9, starting transfers between devices: 33 us -> 41 us  [trade(): return lax.all_to_all(value, axis, split_axis=0, concat_axis=0, tiled=True)]
    ppermute x10 -> x11, waiting for transfers between devices: 6.9 us -> 0.61 us  [swap_grid(): return lax.ppermute(value, 'grid', [(0, 1), (1, 0)])]
    all_to_all x7 -> x9, waiting for transfers between devices: 34.7 us -> 28.8 us  [trade(): return lax.all_to_all(value, axis, split_axis=0, concat_axis=0, tiled=True)]
    ppermute x29 -> x30, waiting for transfers between devices: 83.8 us -> 88.9 us  [swap_mp(): return lax.ppermute(value, 'mp', [(i, i ^ mask) for i in range(c.n)])]
    ppermute x29 -> x30, starting transfers between devices: 32.5 us -> 37.5 us  [swap_mp(): return lax.ppermute(value, 'mp', [(i, i ^ mask) for i in range(c.n)])]
    pallas_call x27 -> x26, Pallas kernels: 276 us -> 274 us  [call(): pl.pallas_call(wrapped, grid_spec=pltpu.PrefetchScalarGridSpec(num_scalar...]
  transfers between devices with their start and end apart: 50 -> 52, of which waited for: 18 -> 20; matrix products, arithmetic and copies ran while one was open for 6% -> 5% of each run, Pallas kernels for 48% -> 50%
where the time goes in v3:
time: 531 us; the launch traced here: 520 us
  Pallas kernels  274 us (52%)
  waiting for transfers between devices  118 us (22%)
  starting transfers between devices  83.8 us (16%)
  local copies, waits for them, and re-layouts  24.1 us (5%)
  other arithmetic  18 us (3%)
    pallas_call x26, Pallas kernels, call(): pl.pallas_call(wrapped, grid_spec=pltpu.PrefetchScalarGridSpec(num_scalar...  274 us
    ppermute x30, waiting for transfers between devices, swap_mp(): return lax.ppermute(value, 'mp', [(i, i ^ mask) for i in range(c.n)])  88.9 us
    all_to_all x9, starting transfers between devices, trade(): return lax.all_to_all(value, axis, split_axis=0, concat_axis=0, tiled=True)  41 us
    ppermute x30, starting transfers between devices, swap_mp(): return lax.ppermute(value, 'mp', [(i, i ^ mask) for i in range(c.n)])  37.5 us
    all_to_all x9, waiting for transfers between devices, trade(): return lax.all_to_all(value, axis, split_axis=0, concat_axis=0, tiled=True)  28.8 us
  transfers between devices with their start and end apart: 52, of which 20 were waited for; matrix products, arithmetic and copies ran while one was open for 5% of the time, Pallas kernels for 50%

profile of v3, /device:TPU:0, one launch (start us, length us, event | category | flops | bytes accessed | tf_op | source)
XLA Modules:
  0.0 520.5 jit_solution(6837132318091499764)
XLA Ops:
  6.6 5.3 %all-to-all-start = ((s32[4,1,16]{2,1,0:T(1,128)}), s32[4,1,16]{2,1,0:T(1,128)S(1)}, u32[]{:S(2)}, u32[]{:S(2)}) async-start(s32[4,1,16]{2,1,0:T(1,128)} %broadcast_in_dim.10), calls=%async_computation | async-start | bytes 4096 | tf_op jit(solution)/shard_map/all_to_all | solution.py:136
  20.9 8.9 %route.1 = (s32[16,1600]{1,0:T(8,128)}, s32[4,16,400]{2,1,0:T(8,128)}, s32[4,8,400]{2,1,0:T(8,128)}) custom-call(s32[4]{0:T(128)} %pad_add_fusion.place, s32[2,1576]{1,0:T(2,128)} %bitcast_add_fusion.refs_0_, s32[1576,2]{1,0:T(8,128)} %copy.52.refs_1_, s32[2,1576]{1,0:T(2,128)} %bitcast.57), custom_call_target="tpu_custom_call" | custom-call | flops 1000 | bytes 1000 | tf_op jit(solution)/shard_map/route/pallas_call | solution.py:101
  33.9 9.6 %dispatch.3.refs_4_ = bf16[1408,1024]{1,0:T(8,128)(2,1)} custom-call(s32[64]{0:T(128)} %get-tuple-element.94.place.refs_2_, s32[16,1600]{1,0:T(8,128)} %get-tuple-element.95.refs_0_, bf16[1576,1024]{1,0:T(8,128)(2,1)} %refs_20_.1, s32[64]{0:T(128)} %get-tuple-element.94.place.refs_2_), custom_call_target="tpu_custom_call" | custom-call | flops 1000 | bytes 1000 | tf_op jit(solution)/shard_map/dispatch/pallas_call | solution.py:101
  49.4 9.2 %qkv.1 = (bf16[1600,1024]{1,0:T(8,128)(2,1)}, bf16[1600,768]{1,0:T(8,128)(2,1)}, bf16[1600,1024]{1,0:T(8,128)(2,1)}) custom-call(s32[64]{0:T(128)} %get-tuple-element.94.place.refs_2_, bf16[1576,1024]{1,0:T(8,128)(2,1)} %refs_6_.1, bf16[48,1024]{1,0:T(8,128)(2,1)} %maximum_select_fusion.refs_1_.refs_11_.refs_22_.refs_8_, bf16[3,512,256]{2,1,0:T(8,128)(2,1)} %bitcast.49, ...), custom_call_target="tpu_custom_call" | custom-call | flops 1000 | bytes 1000 | tf_op jit(solution)/shard_map/qkv/pallas_call | solution.py:101
  58.6 10.6 %attend.1.refs_0_.refs_1_.refs_15_ = bf16[2,1600,128]{2,1,0:T(8,128)(2,1)} custom-call(s32[64]{0:T(128)} %get-tuple-element.94.place.refs_2_, bf16[1600,768]{1,0:T(8,128)(2,1)} %get-tuple-element.96.refs_0_.refs_1_, bf16[1600,768]{1,0:T(8,128)(2,1)} %get-tuple-element.96.refs_0_.refs_1_), custom_call_target="tpu_custom_call" | custom-call | flops 1000 | bytes 1000 | tf_op jit(solution)/shard_map/attend/pallas_call | solution.py:101
  72.2 17.8 %collective-permute-done.6.refs_4_.refs_5_ = bf16[2,1600,128]{2,1,0:T(8,128)(2,1)S(1)} collective-permute-done((bf16[2,1600,128]{2,1,0:T(8,128)(2,1)}, bf16[2,1600,128]{2,1,0:T(8,128)(2,1)S(1)}, u32[]{:S(2)}, u32[]{:S(2)}) %collective-permute-start.6) | collective-permute-done | bytes 819232 | tf_op jit(solution)/shard_map/ppermute | solution.py:124
  93.3 8.1 %collective-permute-done.8.refs_7_ = bf16[1,1600,128]{2,1,0:T(8,128)(2,1)S(1)} collective-permute-done((bf16[1,1600,128]{2,1,0:T(8,128)(2,1)S(1)}, bf16[1,1600,128]{2,1,0:T(8,128)(2,1)S(1)}, u32[]{:S(2)}, u32[]{:S(2)}) %collective-permute-start.8) | collective-permute-done | bytes 409632 | tf_op jit(solution)/shard_map/ppermute | solution.py:124
  103.4 13.4 %middle.1 = (bf16[1600,1024]{1,0:T(8,128)(2,1)}, bf16[1600,128]{1,0:T(8,128)(2,1)}, s32[4,8,400]{2,1,0:T(8,128)}, f32[4,8,400]{2,1,0:T(8,128)}, f32[400,1024]{1,...) custom-call(s32[64]{0:T(128)} %get-tuple-element.94.place.refs_2_, ...), custom_call_target="tpu_custom_call" | custom-call | flops 1000 | bytes 1000 | tf_op jit(solution)/shard_map/middle/pallas_call | solution.py:101
  116.9 7.4 %dispatch.4.refs_3_ = bf16[704,1024]{1,0:T(8,128)(2,1)} custom-call(s32[64]{0:T(128)} %get-tuple-element.94.place.refs_2_, s32[16,1600]{1,0:T(8,128)} %get-tuple-element.95.refs_0_, bf16[1600,1024]{1,0:T(8,128)(2,1)} %get-tuple-element.99.refs_1_.refs_21_, bf16[1600,128]{1,0:T(8,128)(2,1)} %get-tuple-element.100.refs_2_, ...), custom_call_target="tpu_custom_call" | custom-call | flops 1000 | bytes 1000 | tf_op jit(solution)/shard_map/dispatch/pallas_call | solution.py:101
  129.6 7.4 %dispatch.5.refs_3_ = bf16[704,1024]{1,0:T(8,128)(2,1)} custom-call(s32[64]{0:T(128)} %get-tuple-element.94.place.refs_2_, s32[16,1600]{1,0:T(8,128)} %get-tuple-element.95.refs_0_, bf16[1600,1024]{1,0:T(8,128)(2,1)} %get-tuple-element.99.refs_1_.refs_21_, bf16[1600,128]{1,0:T(8,128)(2,1)} %get-tuple-element.100.refs_2_, bf16[704,1024]{1,0:T(8,128)(2,1)} %dispatch.4.refs_3_), custom_call_target="tpu_custom_call" | custom-call | flops 1000 | bytes 1000 | tf_op jit(solution)/shard_map/dispatch/pallas_call | solution.py:101
  137.0 16.0 %grad_active.1 = (bf16[640,4096]{1,0:T(8,128)(2,1)}, bf16[416,4096]{1,0:T(8,128)(2,1)}, bf16[1056,1024]{1,0:T(8,128)(2,1)}) custom-call(s32[64]{0:T(128)} %get-tuple-element.94.place.refs_2_, bf16[4,352,1024]{2,1,0:T(8,128)(2,1)} %all-to-all-done.2.refs_0_, bf16[4096,512]{1,0:T(8,128)(2,1)} %bitcast.43, ...), custom_call_target="tpu_custom_call" | custom-call | flops 1000 | bytes 1000 | tf_op jit(solution)/shard_map/grad_active/pallas_call | solution.py:101
  153.0 9.4 %all-to-all-done.1.refs_0_ = bf16[4,176,1024]{2,1,0:T(8,128)(2,1)S(1)} async-done(((bf16[4,176,1024]{2,1,0:T(8,128)(2,1)}), bf16[4,176,1024]{2,1,0:T(8,128)(2,1)S(1)}, u32[]{:S(2)}, u32[]{:S(2)}) %all-to-all-start.1) | async-done | bytes 1441824 | tf_op jit(solution)/shard_map/all_to_all | solution.py:136
  167.5 24.8 %expert.2 = (bf16[640,4096]{1,0:T(8,128)(2,1)}, bf16[640,4096]{1,0:T(8,128)(2,1)}, f32[8,4096]{1,0:T(8,128)}, bf16[640,1024]{1,0:T(8,128)(2,1)}, f32[640,128]{1,0:T(8,128)}, /*index=5*/bf16[4,176,1024]{2,1,0:T(8,128)(2,1)}) custom-call(s32[64]{0:T(128)} %get-tuple-element.94.place.refs_2_, bf16[4,176,1024]{2,1,0:T(8,128)(2,1)} %copy-done.7, ...), custom_call_target="tpu_custom_call" | custom-call | flops 1000 | bytes 1000 | tf_op jit(solution)/shard_map/expert/pallas_call | solution.py:101
  192.3 7.4 %all-to-all-done.3.refs_0_ = bf16[4,176,1024]{2,1,0:T(8,128)(2,1)S(1)} async-done(((bf16[4,176,1024]{2,1,0:T(8,128)(2,1)}), bf16[4,176,1024]{2,1,0:T(8,128)(2,1)S(1)}, u32[]{:S(2)}, u32[]{:S(2)}) %all-to-all-start.3) | async-done | bytes 1441824 | tf_op jit(solution)/shard_map/all_to_all | solution.py:136
  203.6 18.6 %expert.3 = (bf16[416,4096]{1,0:T(8,128)(2,1)}, bf16[416,4096]{1,0:T(8,128)(2,1)}, f32[8,4096]{1,0:T(8,128)}, bf16[416,1024]{1,0:T(8,128)(2,1)}, f32[416,128]{1,0:T(8,128)}, /*index=5*/bf16[4,176,1024]{2,1,0:T(8,128)(2,1)}) custom-call(s32[64]{0:T(128)} %get-tuple-element.94.place.refs_2_, bf16[4,176,1024]{2,1,0:T(8,128)(2,1)} %copy-done.8, ...), custom_call_target="tpu_custom_call" | custom-call | flops 1000 | bytes 1000 | tf_op jit(solution)/shard_map/expert/pallas_call | solution.py:101
  222.2 10.7 %grad_second.2.refs_4_ = bf16[4096,512]{1,0:T(8,128)(2,1)} custom-call(s32[64]{0:T(128)} %get-tuple-element.94.place.refs_2_, bf16[1056,1024]{1,0:T(8,128)(2,1)} %get-tuple-element.105.refs_5_.refs_0_, f32[640,128]{1,0:T(8,128)} %get-tuple-element.114.refs_1_.refs_0_, f32[416,128]{1,0:T(8,128)} %get-tuple-element.115.refs_2_.refs_1_, ...), custom_call_target="tpu_custom_call" | custom-call | flops 1000 | bytes 1000 | tf_op jit(solution)/shard_map/grad_second/pallas_call | solution.py:101
  240.8 10.3 %grad_first.2.refs_6_ = bf16[512,4096]{1,0:T(8,128)(2,1)} custom-call(s32[64]{0:T(128)} %get-tuple-element.94.place.refs_2_, bf16[640,1024]{1,0:T(8,128)(2,1)} %get-tuple-element.118.refs_0_, bf16[416,1024]{1,0:T(8,128)(2,1)} %get-tuple-element.119.refs_1_, bf16[640,4096]{1,0:T(8,128)(2,1)} %get-tuple-element.120.refs_2_, ...), custom_call_target="tpu_custom_call" | custom-call | flops 1000 | bytes 1000 | tf_op jit(solution)/shard_map/grad_first/pallas_call | solution.py:101
  251.0 15.6 %produce.1.refs_5_ = bf16[4,352,1024]{2,1,0:T(8,128)(2,1)} custom-call(s32[64]{0:T(128)} %get-tuple-element.94.place.refs_2_, f32[640,128]{1,0:T(8,128)} %get-tuple-element.114.refs_1_.refs_0_, f32[416,128]{1,0:T(8,128)} %get-tuple-element.115.refs_2_.refs_1_, bf16[640,4096]{1,0:T(8,128)(2,1)} %get-tuple-element.116.refs_3_.refs_2_, ...), custom_call_target="tpu_custom_call" | custom-call | flops 1000 | bytes 1000 | tf_op jit(solution)/shard_map/produce/pallas_call | solution.py:101
  266.7 7.7 %all-to-all-done.5.refs_1_.refs_3_ = bf16[4,176,1024]{2,1,0:T(8,128)(2,1)S(1)} async-done(((bf16[4,176,1024]{2,1,0:T(8,128)(2,1)}), bf16[4,176,1024]{2,1,0:T(8,128)(2,1)S(1)}, u32[]{:S(2)}, u32[]{:S(2)}) %all-to-all-start.5) | async-done | bytes 1441824 | tf_op jit(solution)/shard_map/all_to_all | solution.py:136
  281.5 12.5 %combine.2 = (bf16[2,416,512]{2,1,0:T(8,128)(2,1)}, bf16[2,416,512]{2,1,0:T(8,128)(2,1)}, bf16[2,400,512]{2,1,0:T(8,128)(2,1)}, bf16[2,400,512]{2,1,0:T(8,128)(2,1)}) custom-call(s32[64]{0:T(128)} %get-tuple-element.94.place.refs_2_, bf16[4,176,1024]{2,1,0:T(8,128)(2,1)} %copy-done, bf16[4,176,1024]{2,1,0:T(8,128)(2,1)} %copy-done.4, ...), custom_call_target="tpu_custom_call" | custom-call | flops 1000 | bytes 1000 | tf_op jit(solution)/shard_map/combine/pallas_call | solution.py:101
  296.2 12.7 %grad_second.3.refs_5_ = f32[4096,512]{1,0:T(8,128)} custom-call(s32[64]{0:T(128)} %get-tuple-element.94.place.refs_2_, bf16[1056,1024]{1,0:T(8,128)(2,1)} %get-tuple-element.105.refs_5_.refs_0_, f32[640,128]{1,0:T(8,128)} %get-tuple-element.114.refs_1_.refs_0_, f32[416,128]{1,0:T(8,128)} %get-tuple-element.115.refs_2_.refs_1_, ...), custom_call_target="tpu_custom_call" | custom-call | flops 1000 | bytes 1000 | tf_op jit(solution)/shard_map/grad_second/pallas_call | solution.py:101
  317.1 12.3 %grad_first.3.refs_23_ = f32[512,4096]{1,0:T(8,128)} custom-call(s32[64]{0:T(128)} %get-tuple-element.94.place.refs_2_, bf16[640,1024]{1,0:T(8,128)(2,1)} %get-tuple-element.118.refs_0_, bf16[416,1024]{1,0:T(8,128)(2,1)} %get-tuple-element.119.refs_1_, bf16[640,4096]{1,0:T(8,128)(2,1)} %get-tuple-element.120.refs_2_, ...), custom_call_target="tpu_custom_call" | custom-call | flops 1000 | bytes 1000 | tf_op jit(solution)/shard_map/grad_first/pallas_call | solution.py:101
  330.4 9.7 %back_two.1 = (f32[400,1024]{1,0:T(8,128)}, bf16[4,320,512]{2,1,0:T(8,128)(2,1)}, bf16[4,320,512]{2,1,0:T(8,128)(2,1)}, bf16[400,256]{1,0:T(8,128)(2,1)}, bf16[4...) custom-call(s32[64]{0:T(128)} %get-tuple-element.94.place.refs_2_, ...), custom_call_target="tpu_custom_call" | custom-call | flops 1000 | bytes 1000 | tf_op jit(solution)/shard_map/back_two/pallas_call | solution.py:101
  346.4 11.6 %combine.3 = (bf16[2,560,512]{2,1,0:T(8,128)(2,1)}, bf16[2,560,512]{2,1,0:T(8,128)(2,1)}, bf16[2,560,512]{2,1,0:T(8,128)(2,1)}, bf16[2,560,512]{2,1,0:T(8,128)(2,1)}) custom-call(s32[64]{0:T(128)} %get-tuple-element.94.place.refs_2_, bf16[4,320,512]{2,1,0:T(8,128)(2,1)} %add_convert_fusion.refs_0_, bf16[4,352,1024]{2,1,0:T(8,128)(2,1)} %all-to-all-done.6.refs_1_, ...), custom_call_target="tpu_custom_call" | custom-call | flops 11000000512 | bytes 1000 | tf_op jit(solution)/shard_map/combine/pallas_call | solution.py:101
  359.7 14.1 %attend_back.1 = (bf16[1600,768]{1,0:T(8,128)(2,1)}, f32[8,768]{1,0:T(8,128)}) custom-call(s32[64]{0:T(128)} %get-tuple-element.94.place.refs_2_, bf16[1600,768]{1,0:T(8,128)(2,1)} %get-tuple-element.96.refs_0_.refs_1_, bf16[400,256]{1,0:T(8,128)(2,1)} %get-tuple-element.135.refs_3_.refs_1_, bf16[400,256]{1,0:T(8,128)(2,1)} %copy-done.44, ...), custom_call_target="tpu_custom_call" | custom-call | flops 1000 | bytes 1000 | tf_op jit(solution)/shard_map/attend_back/pallas_call | solution.py:101
  373.8 8.6 %grad_one.1 = (bf16[2,416,512]{2,1,0:T(8,128)(2,1)}, bf16[2,416,512]{2,1,0:T(8,128)(2,1)}, bf16[2,416,512]{2,1,0:T(8,128)(2,1)}, bf16[2,416,512]{2,1,0:T(8,128)(2,1)}, f32[2,1024]{1,0:T(2,128)}) custom-call(s32[64]{0:T(128)} %get-tuple-element.94.place.refs_2_, bf16[1600,768]{1,0:T(8,128)(2,1)} %get-tuple-element.145.refs_0_.refs_1_, ...), custom_call_target="tpu_custom_call" | custom-call | flops 1000 | bytes 1000 | tf_op jit(solution)/shard_map/grad_one/pallas_call | solution.py:101
  388.8 7.6 %grad_qkv.1 = (bf16[3,512,256]{2,1,0:T(8,128)(2,1)}, bf16[3,512,256]{2,1,0:T(8,128)(2,1)}) custom-call(s32[64]{0:T(128)} %get-tuple-element.94.place.refs_2_, bf16[1600,1024]{1,0:T(8,128)(2,1)} %get-tuple-element.153.refs_0_, bf16[1600,768]{1,0:T(8,128)(2,1)} %get-tuple-element.145.refs_0_.refs_1_, f32[2,1024]{1,0:T(2,128)} %get-tuple-element.148.refs_2_, ...), custom_call_target="tpu_custom_call" | custom-call | flops 1000 | bytes 1000 | tf_op jit(solution)/shard_map/grad_qkv/pallas_call | solution.py:101
  399.0 17.1 %collective-permute-done.25.refs_5_ = bf16[1,560,512]{2,1,0:T(8,128)(2,1)S(1)} collective-permute-done((bf16[1,560,512]{2,1,0:T(8,128)(2,1)S(1)}, bf16[1,560,512]{2,1,0:T(8,128)(2,1)S(1)}, u32[]{:S(2)}, u32[]{:S(2)}) %collective-permute-start.25) | collective-permute-done | bytes 573472 | tf_op jit(solution)/shard_map/ppermute | solution.py:124
  434.2 7.7 %collective-permute-done.29.refs_5_ = bf16[1,416,512]{2,1,0:T(8,128)(2,1)S(1)} collective-permute-done((bf16[1,416,512]{2,1,0:T(8,128)(2,1)S(1)}, bf16[1,416,512]{2,1,0:T(8,128)(2,1)S(1)}, u32[]{:S(2)}, u32[]{:S(2)}) %collective-permute-start.29) | collective-permute-done | bytes 426016 | tf_op jit(solution)/shard_map/ppermute | solution.py:124
  452.4 14.4 %collective-permute-done.31.refs_4_.refs_5_ = bf16[2,400,512]{2,1,0:T(8,128)(2,1)S(1)} collective-permute-done((bf16[2,400,512]{2,1,0:T(8,128)(2,1)}, bf16[2,400,512]{2,1,0:T(8,128)(2,1)S(1)}, u32[]{:S(2)}, u32[]{:S(2)}) %collective-permute-start.31) | collective-permute-done | bytes 819232 | tf_op jit(solution)/shard_map/ppermute | solution.py:124
  486.7 10.1 %collective-permute-done.33.refs_4_.refs_5_ = bf16[2,400,512]{2,1,0:T(8,128)(2,1)S(1)} collective-permute-done((bf16[2,400,512]{2,1,0:T(8,128)(2,1)}, bf16[2,400,512]{2,1,0:T(8,128)(2,1)S(1)}, u32[]{:S(2)}, u32[]{:S(2)}) %collective-permute-start.33) | collective-permute-done | bytes 819232 | tf_op jit(solution)/shard_map/ppermute | solution.py:124
  502.9 5.6 %assemble.2.refs_8_ = f32[1576,1024]{1,0:T(8,128)} custom-call(s32[64]{0:T(128)} %get-tuple-element.94.place.refs_2_, bf16[2,400,512]{2,1,0:T(8,128)(2,1)} %get-tuple-element.164.refs_0_.refs_1_, bf16[2,400,512]{2,1,0:T(8,128)(2,1)} %get-tuple-element.164.refs_0_.refs_1_, bf16[2,400,512]{2,1,0:T(8,128)(2,1)} %copy-done.10, bf16[2,400,512]{2,1,0:T(8,128)(2,1)} %copy-done.10, ...), custom_call_target="tpu_custom_call" | custom-call | flops 1000 | bytes 1000 | tf_op jit(solution)/shard_map/assemble/pallas_call | solution.py:101
  (263 shorter events, 156.4 us)
Async XLA Ops:
  0.7 29.1 %collective-permute-start.2 = (bf16[256,512]{1,0:T(8,128)(2,1)}, bf16[256,512]{1,0:T(8,128)(2,1)S(1)}, u32[]{:S(2)}, u32[]{:S(2)}) collective-permute-start(bf16[256,512]{1,0:T(8,128)(2,1)} %param.19), channel_id=1, source_target_pairs={{0,2},{2,0},{4,6},{6,4},{1,3},{3,1},{5,7},{7,5},{8,10},{10,8},{12,... | collective-permute-start | bytes 786440 | tf_op jit(solution)/shard_map/ppermute | solution.py:124
  3.7 26.1 %collective-permute-start.4 = (bf16[256,512]{1,0:T(8,128)(2,1)}, bf16[256,512]{1,0:T(8,128)(2,1)S(1)}, u32[]{:S(2)}, u32[]{:S(2)}) collective-permute-start(bf16[256,512]{1,0:T(8,128)(2,1)} %param.19), channel_id=1, source_target_pairs={{0,6},{2,4},{4,2},{6,0},{1,7},{3,5},{5,3},{7,1},{8,14},{10,12},{12... | collective-permute-start | bytes 786440 | tf_op jit(solution)/shard_map/ppermute | solution.py:124
  5.2 24.7 %collective-permute-start.3 = (bf16[256,512]{1,0:T(8,128)(2,1)}, bf16[256,512]{1,0:T(8,128)(2,1)S(1)}, u32[]{:S(2)}, u32[]{:S(2)}) collective-permute-start(bf16[256,512]{1,0:T(8,128)(2,1)} %param.19), channel_id=1, source_target_pairs={{0,4},{2,6},{4,0},{6,2},{1,5},{3,7},{5,1},{7,3},{8,12},{10,14},{12... | collective-permute-start | bytes 786440 | tf_op jit(solution)/shard_map/ppermute | solution.py:124
  6.6 24.3 %all-to-all-start = ((s32[4,1,16]{2,1,0:T(1,128)}), s32[4,1,16]{2,1,0:T(1,128)S(1)}, u32[]{:S(2)}, u32[]{:S(2)}) async-start(s32[4,1,16]{2,1,0:T(1,128)} %broadcast_in_dim.10), calls=%async_computation | async-start | bytes 4096 | tf_op jit(solution)/shard_map/all_to_all | solution.py:136
  12.0 19.0 %collective-permute-start.1 = (bf16[3,512,256]{2,1,0:T(8,128)(2,1)}, bf16[3,512,256]{2,1,0:T(8,128)(2,1)S(1)}, u32[]{:S(2)}, u32[]{:S(2)}) collective-permute-start(bf16[3,512,256]{2,1,0:T(8,128)(2,1)} %bitcast.48), channel_id=1, source_target_pairs={{0,1},{1,0},{2,3},{3,2},{4,5},{5,4},{6,7},{7,6},{8,9},{9,8},{10,11... | collective-permute-start | bytes 2359304 | tf_op jit(solution)/shard_map/ppermute | solution.py:128
  43.5 80.8 %all-to-all-start.2 = ((bf16[4,352,1024]{2,1,0:T(8,128)(2,1)}), bf16[4,352,1024]{2,1,0:T(8,128)(2,1)}, u32[]{:S(2)}, u32[]{:S(2)}) async-start(bf16[4,352,1024]{2,1,0:T(8,128)(2,1)} %bitcast.38), calls=%async_computation.2 | async-start | bytes 5767168 | tf_op jit(solution)/shard_map/all_to_all | solution.py:136
  48.8 88.2 %collective-permute-start.11 = (bf16[4096,512]{1,0:T(8,128)(2,1)}, bf16[4096,512]{1,0:T(8,128)(2,1)}, u32[]{:S(2)}, u32[]{:S(2)}) collective-permute-start(bf16[4096,512]{1,0:T(8,128)(2,1)} %bitcast.42), channel_id=1, source_target_pairs={{0,1},{1,0},{2,3},{3,2},{4,5},{5,4},{6,7},{7,6},{8,9},{9,8},{10,11... | collective-permute-start | bytes 12582920 | tf_op jit(solution)/shard_map/ppermute | solution.py:128
  69.2 20.9 %collective-permute-start.6 = (bf16[2,1600,128]{2,1,0:T(8,128)(2,1)}, bf16[2,1600,128]{2,1,0:T(8,128)(2,1)S(1)}, u32[]{:S(2)}, u32[]{:S(2)}) collective-permute-start(bf16[2,1600,128]{2,1,0:T(8,128)(2,1)} %attend.1.refs_0_.refs_1_.refs_15_), channel_id=1, source_target_pairs={{0,4},{2,6},{4,0},{6,2},{1,5},{3,7},{5,1},{7,3},{8,12},{10,14},{12... | collective-permute-start | bytes 2457608 | tf_op jit(solution)/shard_map/ppermute | solution.py:124
  70.7 20.9 %collective-permute-start.5 = (bf16[2,1600,128]{2,1,0:T(8,128)(2,1)}, bf16[2,1600,128]{2,1,0:T(8,128)(2,1)S(1)}, u32[]{:S(2)}, u32[]{:S(2)}) collective-permute-start(bf16[2,1600,128]{2,1,0:T(8,128)(2,1)} %attend.1.refs_0_.refs_1_.refs_15_), channel_id=1, source_target_pairs={{0,2},{2,0},{4,6},{6,4},{1,3},{3,1},{5,7},{7,5},{8,10},{10,8},{12,... | collective-permute-start | bytes 2457608 | tf_op jit(solution)/shard_map/ppermute | solution.py:124
  72.2 21.1 %collective-permute-start.9 = (bf16[4,256,512]{2,1,0:T(8,128)(2,1)S(1)}, bf16[4,256,512]{2,1,0:T(8,128)(2,1)S(1)}, u32[]{:S(2)}, u32[]{:S(2)}) collective-permute-start(bf16[4,256,512]{2,1,0:T(8,128)(2,1)S(1)} %copy-done.1), channel_id=1, source_target_pairs={{0,1},{1,0},{2,3},{3,2},{4,5},{5,4},{6,7},{7,6},{8,9},{9,8},{10,11... | collective-permute-start | bytes 3145736 | tf_op jit(solution)/shard_map/ppermute | solution.py:128
  124.3 38.2 %all-to-all-start.1 = ((bf16[4,176,1024]{2,1,0:T(8,128)(2,1)}), bf16[4,176,1024]{2,1,0:T(8,128)(2,1)S(1)}, u32[]{:S(2)}, u32[]{:S(2)}) async-start(bf16[4,176,1024]{2,1,0:T(8,128)(2,1)} %bitcast.45), calls=%async_computation.1 | async-start | bytes 2883584 | tf_op jit(solution)/shard_map/all_to_all | solution.py:136
  129.5 37.9 %collective-permute-start.10 = (bf16[512,4096]{1,0:T(8,128)(2,1)}, bf16[512,4096]{1,0:T(8,128)(2,1)}, u32[]{:S(2)}, u32[]{:S(2)}) collective-permute-start(bf16[512,4096]{1,0:T(8,128)(2,1)} %bitcast.39), channel_id=1, source_target_pairs={{0,1},{1,0},{2,3},{3,2},{4,5},{5,4},{6,7},{7,6},{8,9},{9,8},{10,11... | collective-permute-start | bytes 12582920 | tf_op jit(solution)/shard_map/ppermute | solution.py:128
  162.5 37.2 %all-to-all-start.3 = ((bf16[4,176,1024]{2,1,0:T(8,128)(2,1)}), bf16[4,176,1024]{2,1,0:T(8,128)(2,1)S(1)}, u32[]{:S(2)}, u32[]{:S(2)}) async-start(bf16[4,176,1024]{2,1,0:T(8,128)(2,1)} %bitcast.17), calls=%async_computation.3 | async-start | bytes 2883584 | tf_op jit(solution)/shard_map/all_to_all | solution.py:136
  199.6 37.6 %all-to-all-start.4 = ((bf16[4,176,1024]{2,1,0:T(8,128)(2,1)}), bf16[4,176,1024]{2,1,0:T(8,128)(2,1)S(1)}, u32[]{:S(2)}, u32[]{:S(2)}) async-start(bf16[4,176,1024]{2,1,0:T(8,128)(2,1)} %get-tuple-element.108), calls=%async_computation.4 | async-start | bytes 2883584 | tf_op jit(solution)/shard_map/all_to_all | solution.py:136
  232.9 63.3 %collective-permute-start.14 = (bf16[4096,512]{1,0:T(8,128)(2,1)}, bf16[4096,512]{1,0:T(8,128)(2,1)}, u32[]{:S(2)}, u32[]{:S(2)}) collective-permute-start(bf16[4096,512]{1,0:T(8,128)(2,1)} %grad_second.2.refs_4_), channel_id=1, source_target_pairs={{0,1},{1,0},{2,3},{3,2},{4,5},{5,4},{6,7},{7,6},{8,9},{9,8},{10,11... | collective-permute-start | bytes 12582920 | tf_op jit(solution)/shard_map/ppermute | solution.py:128
  237.2 37.2 %all-to-all-start.5 = ((bf16[4,176,1024]{2,1,0:T(8,128)(2,1)}), bf16[4,176,1024]{2,1,0:T(8,128)(2,1)S(1)}, u32[]{:S(2)}, u32[]{:S(2)}) async-start(bf16[4,176,1024]{2,1,0:T(8,128)(2,1)} %get-tuple-element.112), calls=%async_computation.5 | async-start | bytes 2883584 | tf_op jit(solution)/shard_map/all_to_all | solution.py:136
  251.0 66.1 %collective-permute-start.17 = (bf16[512,4096]{1,0:T(8,128)(2,1)}, bf16[512,4096]{1,0:T(8,128)(2,1)}, u32[]{:S(2)}, u32[]{:S(2)}) collective-permute-start(bf16[512,4096]{1,0:T(8,128)(2,1)} %grad_first.2.refs_6_), channel_id=1, source_target_pairs={{0,1},{1,0},{2,3},{3,2},{4,5},{5,4},{6,7},{7,6},{8,9},{9,8},{10,11... | collective-permute-start | bytes 12582920 | tf_op jit(solution)/shard_map/ppermute | solution.py:128
  275.5 71.0 %all-to-all-start.6 = ((bf16[4,352,1024]{2,1,0:T(8,128)(2,1)}), bf16[4,352,1024]{2,1,0:T(8,128)(2,1)}, u32[]{:S(2)}, u32[]{:S(2)}) async-start(bf16[4,352,1024]{2,1,0:T(8,128)(2,1)} %produce.1.refs_5_), calls=%async_computation.6 | async-start | bytes 5767168 | tf_op jit(solution)/shard_map/all_to_all | solution.py:136
  294.0 20.2 %collective-permute-start.12 = (bf16[2,416,512]{2,1,0:T(8,128)(2,1)}, bf16[2,416,512]{2,1,0:T(8,128)(2,1)S(1)}, u32[]{:S(2)}, u32[]{:S(2)}) collective-permute-start(bf16[2,416,512]{2,1,0:T(8,128)(2,1)} %get-tuple-element.124), channel_id=1, source_target_pairs={{0,2},{2,0},{4,6},{6,4},{1,3},{3,1},{5,7},{7,5},{8,10},{10,8},{12,... | collective-permute-start | bytes 2555912 | tf_op jit(solution)/shard_map/ppermute | solution.py:124
  295.1 19.1 %collective-permute-start.13 = (bf16[2,400,512]{2,1,0:T(8,128)(2,1)}, bf16[2,400,512]{2,1,0:T(8,128)(2,1)S(1)}, u32[]{:S(2)}, u32[]{:S(2)}) collective-permute-start(bf16[2,400,512]{2,1,0:T(8,128)(2,1)} %get-tuple-element.125), channel_id=1, source_target_pairs={{0,4},{2,6},{4,0},{6,2},{1,5},{3,7},{5,1},{7,3},{8,12},{10,14},{12... | collective-permute-start | bytes 2457608 | tf_op jit(solution)/shard_map/ppermute | solution.py:124
  358.1 27.5 %collective-permute-start.23 = (bf16[2,560,512]{2,1,0:T(8,128)(2,1)}, bf16[2,560,512]{2,1,0:T(8,128)(2,1)S(1)}, u32[]{:S(2)}, u32[]{:S(2)}) collective-permute-start(bf16[2,560,512]{2,1,0:T(8,128)(2,1)} %get-tuple-element.144), channel_id=1, source_target_pairs={{0,4},{2,6},{4,0},{6,2},{1,5},{3,7},{5,1},{7,3},{8,12},{10,14},{12... | collective-permute-start | bytes 3440648 | tf_op jit(solution)/shard_map/ppermute | solution.py:124
  358.6 28.1 %collective-permute-start.22 = (bf16[2,560,512]{2,1,0:T(8,128)(2,1)}, bf16[2,560,512]{2,1,0:T(8,128)(2,1)S(1)}, u32[]{:S(2)}, u32[]{:S(2)}) collective-permute-start(bf16[2,560,512]{2,1,0:T(8,128)(2,1)} %get-tuple-element.142), channel_id=1, source_target_pairs={{0,2},{2,0},{4,6},{6,4},{1,3},{3,1},{5,7},{7,5},{8,10},{10,8},{12,... | collective-permute-start | bytes 3440648 | tf_op jit(solution)/shard_map/ppermute | solution.py:124
  382.3 39.8 %collective-permute-start.26 = (bf16[2,416,512]{2,1,0:T(8,128)(2,1)}, bf16[2,416,512]{2,1,0:T(8,128)(2,1)S(1)}, u32[]{:S(2)}, u32[]{:S(2)}) collective-permute-start(bf16[2,416,512]{2,1,0:T(8,128)(2,1)} %get-tuple-element.157), channel_id=1, source_target_pairs={{0,2},{2,0},{4,6},{6,4},{1,3},{3,1},{5,7},{7,5},{8,10},{10,8},{12,... | collective-permute-start | bytes 2555912 | tf_op jit(solution)/shard_map/ppermute | solution.py:124
  383.3 38.9 %collective-permute-start.27 = (bf16[2,416,512]{2,1,0:T(8,128)(2,1)}, bf16[2,416,512]{2,1,0:T(8,128)(2,1)S(1)}, u32[]{:S(2)}, u32[]{:S(2)}) collective-permute-start(bf16[2,416,512]{2,1,0:T(8,128)(2,1)} %get-tuple-element.158), channel_id=1, source_target_pairs={{0,4},{2,6},{4,0},{6,2},{1,5},{3,7},{5,1},{7,3},{8,12},{10,14},{12... | collective-permute-start | bytes 2555912 | tf_op jit(solution)/shard_map/ppermute | solution.py:124
  396.5 26.8 %collective-permute-start.36 = (bf16[3,512,256]{2,1,0:T(8,128)(2,1)}, bf16[3,512,256]{2,1,0:T(8,128)(2,1)S(1)}, u32[]{:S(2)}, u32[]{:S(2)}) collective-permute-start(bf16[3,512,256]{2,1,0:T(8,128)(2,1)} %get-tuple-element.166), channel_id=1, source_target_pairs={{0,1},{1,0},{2,3},{3,2},{4,5},{5,4},{6,7},{7,6},{8,9},{9,8},{10,11... | collective-permute-start | bytes 2359304 | tf_op jit(solution)/shard_map/ppermute | solution.py:128
  396.5 19.6 %collective-permute-start.25 = (bf16[1,560,512]{2,1,0:T(8,128)(2,1)S(1)}, bf16[1,560,512]{2,1,0:T(8,128)(2,1)S(1)}, u32[]{:S(2)}, u32[]{:S(2)}) collective-permute-start(bf16[1,560,512]{2,1,0:T(8,128)(2,1)S(1)} %copy-done.20), channel_id=1, source_target_pairs={{0,2},{2,0},{4,6},{6,4},{1,3},{3,1},{5,7},{7,5},{8,10},{10,8},{12,... | collective-permute-start | bytes 1720328 | tf_op jit(solution)/shard_map/ppermute | solution.py:124
  397.6 18.5 %collective-permute-start.24 = (bf16[1,560,512]{2,1,0:T(8,128)(2,1)S(1)}, bf16[1,560,512]{2,1,0:T(8,128)(2,1)S(1)}, u32[]{:S(2)}, u32[]{:S(2)}) collective-permute-start(bf16[1,560,512]{2,1,0:T(8,128)(2,1)S(1)} %copy-done.19), channel_id=1, source_target_pairs={{0,4},{2,6},{4,0},{6,2},{1,5},{3,7},{5,1},{7,3},{8,12},{10,14},{12... | collective-permute-start | bytes 1720328 | tf_op jit(solution)/shard_map/ppermute | solution.py:124
  425.2 43.6 %all-to-all-start.7 = ((bf16[4,272,512]{2,1,0:T(8,128)(2,1)}), bf16[4,272,512]{2,1,0:T(8,128)(2,1)S(1)}, u32[]{:S(2)}, u32[]{:S(2)}) async-start(bf16[4,272,512]{2,1,0:T(8,128)(2,1)} %bitcast.20), calls=%async_computation.7 | async-start | bytes 2228224 | tf_op jit(solution)/shard_map/all_to_all | solution.py:136
  473.5 23.3 %collective-permute-start.33 = (bf16[2,400,512]{2,1,0:T(8,128)(2,1)}, bf16[2,400,512]{2,1,0:T(8,128)(2,1)S(1)}, u32[]{:S(2)}, u32[]{:S(2)}) collective-permute-start(bf16[2,400,512]{2,1,0:T(8,128)(2,1)} %get-tuple-element.165.refs_0_.refs_1_), channel_id=1, source_target_pairs={{0,4},{2,6},{4,0},{6,2},{1,5},{3,7},{5,1},{7,3},{8,12},{10,14},{12... | collective-permute-start | bytes 2457608 | tf_op jit(solution)/shard_map/ppermute | solution.py:124
  475.0 22.9 %collective-permute-start.32 = (bf16[2,400,512]{2,1,0:T(8,128)(2,1)}, bf16[2,400,512]{2,1,0:T(8,128)(2,1)S(1)}, u32[]{:S(2)}, u32[]{:S(2)}) collective-permute-start(bf16[2,400,512]{2,1,0:T(8,128)(2,1)} %get-tuple-element.165.refs_0_.refs_1_), channel_id=1, source_target_pairs={{0,2},{2,0},{4,6},{6,4},{1,3},{3,1},{5,7},{7,5},{8,10},{10,8},{12,... | collective-permute-start | bytes 2457608 | tf_op jit(solution)/shard_map/ppermute | solution.py:124
  476.1 39.4 %all-to-all-start.8 = ((bf16[4,272,512]{2,1,0:T(8,128)(2,1)}), bf16[4,272,512]{2,1,0:T(8,128)(2,1)S(1)}, u32[]{:S(2)}, u32[]{:S(2)}) async-start(bf16[4,272,512]{2,1,0:T(8,128)(2,1)} %broadcast_in_dim.12), calls=%async_computation.8 | async-start | bytes 2228224 | tf_op jit(solution)/shard_map/all_to_all | solution.py:136
  483.4 18.9 %collective-permute-start.42 = (f32[1,2048]{1,0:T(1,128)S(1)}, f32[1,2048]{1,0:T(1,128)S(1)}, u32[]{:S(2)}, u32[]{:S(2)}) collective-permute-start(f32[1,2048]{1,0:T(1,128)S(1)} %constant_dynamic-slice_fusion), channel_id=1, source_target_pairs={{0,1},{1,0},{2,3},{3,2},{4,5},{5,4},{6,7},{7,6},{8,9},{9,8},{10,11... | collective-permute-start | bytes 24584 | tf_op jit(solution)/shard_map/ppermute | solution.py:128
  (72 other events, 565.9 us)

commit v4 on v3

--- a/solution.py
+++ b/solution.py
@@ -190,7 +190,10 @@
 
 
 def sum_dp_start(c, value):
-    parts = trade(value.reshape((c.X, value.shape[0] // c.X) + value.shape[1:]), "dp")
+    return trade(value.reshape((c.X, value.shape[0] // c.X) + value.shape[1:]), "dp")
+
+
+def sum_dp_turn(c, parts):
     total = jnp.sum(parts.astype(F32), axis=0).astype(BF)
     return jnp.broadcast_to(total[None], (c.X,) + total.shape)
 
@@ -207,11 +210,23 @@
     two = swap_mp(c, value, 2)
     ends = one[0:1], two[1:2]
     if until is not None:
-        ends = held(ends[0], until), held(ends[1], until)
+        ends = held(ends[0], *until), held(ends[1], *until)
     far_a = swap_mp(c, ends[0], 2)
     far_b = swap_mp(c, ends[1], 1)
     near = [[(p, 0), (p, 1)] for p in (value, one, two)]
     return near + [[(far_a, 0), (far_b, 0)]], [one, two]
+
+
+def gather_both(c, first, second, until):
+    if c.n != 4:
+        return gather_mp(c, first)[0], gather_mp(c, second)[0], first
+    one, two = swap_mp(c, first, 1), swap_mp(c, first, 2)
+    near = jnp.concatenate([one[0:1], second]), jnp.concatenate([two[1:2], second])
+    by_two, by_one = [swap_mp(c, held(x, *until), mask) for x, mask in zip(near, (2, 1))]
+    far_a, far_b = swap_mp(c, by_one[1:2], 2), swap_mp(c, by_two[2:3], 1)
+    pieces = [[(p, 0), (p, 1)] for p in (first, one, two)] + [[(by_two, 0), (by_one, 0)]]
+    others = [[(second, 0), (second, 1)], [(by_one, 1), (by_one, 2)], [(by_two, 1), (by_two, 2)]]
+    return pieces, others + [[(far_a, 0), (far_b, 0)]], one
 
 
 def flat(pieces):
@@ -227,78 +242,34 @@
     return value
 
 
-def finish_sums(c, one, parts, grid):
+def first_sums(c, sums, one_parts):
+    if c.n != 4:
+        return fold(c, one_parts, (("mp", c.n),))
+    halves = []
+    for a, b, far in sums:
+        pair = (a[0, c.R : c.R + 2].astype(F32) + b[0, c.R : c.R + 2].astype(F32)).astype(BF)
+        halves.append(pair.astype(F32) + far[0, c.R : c.R + 2].astype(F32))
+    return jnp.concatenate(halves, axis=1)
+
+
+def chip_sums(c, one, parts, grid):
     def half_of(side):
         cols = lax.dynamic_slice_in_dim(one, side * c.half, c.half, 1)
         row = lax.dynamic_index_in_dim(parts, side, 0, True)
         return jnp.concatenate([cols, jnp.pad(row, ((0, 0), (0, c.half - c.W)))], axis=0)
 
-    return fold(c, half_of(grid) + swap_grid(half_of(1 - grid)), (("dp", c.X),))
+    return half_of(grid) + swap_grid(half_of(1 - grid))
 
 
 def expert_of(c, place, j):
     return j * EXP_DEV + place[3]
 
 
-def offset_at(place, j):
-    return place[4 + j]
-
-
-def window_slot(c, place, j, slot):
-    return slot + jnp.where(slot < c.Q, place[4 + c.X + j], place[4 + 2 * c.X + j])
-
-
-def window_in(c, place, half, j):
-    return pl.multiple_of(place[4 + (3 + half) * c.X + j], 16)
-
-
-def windows_body(c, place, counts, out_ref, off_ref):
-    def window(offset, half):
-        return jnp.minimum((offset >> 4) << 4, c.CR[half] - c.SP)
-
-    def before(e, source):
-        state = (jnp.int32(0),) * 3
-        result = state
-        for b in range(c.X):
-            result = [jnp.where(source == b, new, old) for new, old in zip(state, result)]
-            number = counts[b, e]
-            kept = jnp.clip(c.cap - state[0], 0, number)
-            first = jnp.minimum(kept, c.Q)
-            state = (state[0] + number, state[1] + first, state[2] + kept - first)
-        return result
-
-    for i in range(4):
-        out_ref[i] = place[i]
-    for i in range(4 + 5 * c.X, 64):
-        out_ref[i] = jnp.int32(0)
-    here = place[0] * EXP_DEV + place[3]
-    for j in range(c.X):
-        offset, first, second = before(expert_of(c, place, j), place[0])
-        out_ref[4 + j] = offset
-        out_ref[4 + c.X + j] = first - window(first, 0)
-        out_ref[4 + 2 * c.X + j] = c.SP + second - c.Q - window(second, 1)
-        _, first, second = before(here, j)
-        out_ref[4 + 3 * c.X + j] = window(first, 0)
-        out_ref[4 + 4 * c.X + j] = window(second, 1)
-    for e in range(c.E):
-        off_ref[e : e + 1, :] = jnp.full((1, 128), before(e, place[0])[0], I32)
-
-
-def windows(c, order, place, counts):
-    return call(
-        order,
-        functools.partial(windows_body, c),
-        place,
-        [counts],
-        [pl.BlockSpec(memory_space=pltpu.SMEM)],
-        [shape_of((64,), I32), shape_of((c.E, 128), I32)],
-        [pl.BlockSpec(memory_space=pltpu.SMEM), whole(shape_of((c.E, 128), I32))],
-        (1,),
-        name="windows",
-    )
-
-
-def route_body(c, place, row_ref, col_ref, rt_ref, slot_ref, blocks_ref, rtb_ref):
+def window_slot(c, slot):
+    return jnp.where(slot < c.Q, slot, slot + (c.SP - c.Q))
+
+
+def count_places(c, row_ref, col_ref, rt_ref, slot_ref, blocks_ref, rtb_ref):
     pad = jnp.full((1, c.TP - c.T), 1 << 30, I32)
     first = jnp.broadcast_to(jnp.concatenate([row_ref[0:1, :], pad], axis=1), (8, c.TP))
     second = jnp.broadcast_to(jnp.concatenate([row_ref[1:2, :], pad], axis=1), (8, c.TP))
@@ -326,18 +297,54 @@
     pad = jnp.full((2, c.TP - c.T), -1, I32)
     rt = jnp.concatenate([rt_ref[...], pad], axis=1)
     start = jnp.zeros((1, 1), I32)
+    lane = lax.broadcasted_iota(I32, (1, c.half), 1)
+    numbers = jnp.zeros((1, c.half), I32)
     for e in range(c.E):
         in_first = rt[0:1, :] == e
         in_second = rt[1:2, :] == e
         number = jnp.sum(in_first.astype(I32) + in_second.astype(I32), axis=1, keepdims=True)
         slot_ref[e : e + 1, :] = jnp.where(in_first, a - start, jnp.where(in_second, b - start, -1))
         start = start + number
+        numbers = numbers + jnp.where(lane == e, number, 0)
     for r in range(c.n):
         blocks_ref[r] = slot_ref[:, r * c.R : (r + 1) * c.R]
         rtb_ref[r] = jnp.concatenate([rt[:, r * c.R : (r + 1) * c.R]] * 4, axis=0)
-
-
-def route(c, order, place, routes, priority):
+    return numbers
+
+
+def fill_hot(c, place, slot_ref, hot_ref, halves):
+    for j in range(c.X):
+        row = window_slot(c, slot_ref[pl.ds(expert_of(c, place, j), 1), :])
+        for index, half in enumerate(halves):
+            slots = lax.broadcasted_iota(I32, (c.SP, c.TP), 0) + half * c.SP
+            hot_ref[index, j * c.SP : (j + 1) * c.SP, :] = (slots == row).astype(BF)
+
+
+def route_body(c, place, *refs):
+    row_ref, col_ref, rt_ref, src_ref, slot_ref, blocks_ref, rtb_ref, out_ref, hot_ref, sum_ref = refs
+
+    @pl.when(pl.program_id(0) == 0)
+    def _():
+        numbers = count_places(c, row_ref, col_ref, rt_ref, slot_ref, blocks_ref, rtb_ref)
+        sum_ref[0:1, :] = (numbers >> 4).astype(F32)
+        sum_ref[1:2, :] = (numbers & 15).astype(F32)
+        fill_hot(c, place, slot_ref, hot_ref, (0, 1))
+
+    for half in range(2):
+        acc = dot_nn(hot_ref[half, :, : c.T], src_ref[...])
+        for j in range(c.X):
+            at = (2 * j + half) * c.SP
+            out_ref[at : at + c.SP, :] = acc[j * c.SP : (j + 1) * c.SP].astype(BF)
+            if half == 0:
+
+                @pl.when(pl.program_id(0) == 0)
+                def _():
+                    tile = acc[(j + 1) * c.SP - 16 : (j + 1) * c.SP]
+                    tile = last_rows(c, tile, sum_ref[0:1, :], sum_ref[1:2, :])
+                    out_ref[at + c.SP - 16 : at + c.SP, :] = tile.astype(BF)
+
+
+def route(c, order, place, routes, priority, source):
     key = routes * c.key + priority
     row = routes.T * c.key + priority.T
     rt = routes.T
@@ -345,17 +352,70 @@
         shape_of((c.E, c.TP), I32),
         shape_of((c.n, c.E, c.R), I32),
         shape_of((c.n, 8, c.R), I32),
+        shape_of((2 * c.X * c.SP, c.D), BF),
     ]
+    result = call(
+        order,
+        functools.partial(route_body, c),
+        place,
+        [row, key, rt, source],
+        [whole(row), whole(key), whole(rt)]
+        + [pl.BlockSpec((c.T, c.half), lambda i, s: (0, i ^ s[2]))],
+        outs,
+        [whole(o) for o in outs[:3]] + [cols_of((2 * c.X * c.SP, c.half))],
+        (2,),
+        [pltpu.VMEM((2, c.X * c.SP, c.TP), BF), pltpu.VMEM((8, c.half), F32)],
+        name="route",
+    )
+    return (*result[:3], result[3].reshape(c.X, 2 * c.SP, c.D))
+
+
+def keep_body(c, place, tail_ref, slot_ref, rt_ref, mine_ref, keep_ref, lane_ref):
+    earlier = jnp.zeros((1, 128), F32)
+    for b in range(c.X):
+        high, low = last_pair(c, tail_ref[b], 128)
+        earlier = earlier + jnp.where(b < place[0], high * 16.0 + low, 0.0)
+    wide = (c.E, 128)
+    eye = lax.broadcasted_iota(I32, wide, 0) == lax.broadcasted_iota(I32, wide, 1)
+    offset = jnp.sum(jnp.where(eye, earlier, 0.0), axis=1, keepdims=True).astype(I32)
+    slot = slot_ref[0]
+    kept = (slot >= 0) & (slot + offset < c.cap)
+    slots = jnp.where(kept, window_slot(c, slot), -1)
+    expert = lax.broadcasted_iota(I32, (c.E, 1), 0)
+    for j in range(8):
+        if j < c.X:
+            here = jnp.where(expert == expert_of(c, place, j), slots, -1)
+            mine_ref[0, j : j + 1, :] = jnp.max(here, axis=0, keepdims=True)
+        else:
+            mine_ref[0, j : j + 1, :] = jnp.full((1, c.R), -1, I32)
+    rows = []
+    for k in range(2):
+        picked = jnp.where((rt_ref[0, k : k + 1, :] == expert) & kept, 1.0, 0.0)
+        rows.append(jnp.sum(picked, axis=0, keepdims=True))
+    keep_ref[0] = jnp.concatenate(rows * 4, axis=0)
+
+    @pl.when(pl.program_id(0) == place[1])
+    def _():
+        lane_ref[...] = jnp.where(kept, 1.0, 0.0)
+
+
+def keep_of(c, order, place, rows, blocks, rt):
+    outs = [
+        shape_of((c.n, 8, c.R), I32),
+        shape_of((c.n, 8, c.R), F32),
+        shape_of((c.E, c.R), F32),
+    ]
+    tail = pl.BlockSpec((c.X, 16, c.half), lambda i, s: (0, c.SP // 16 - 1, 0))
     return call(
         order,
-        functools.partial(route_body, c),
-        place,
-        [row, key, rt],
-        [whole(row), whole(key), whole(rt)],
+        functools.partial(keep_body, c),
+        place,
+        [rows, blocks, rt],
+        [tail, rows_of((1, c.E, c.R)), rows_of((1, 8, c.R))],
         outs,
-        [whole(o) for o in outs],
-        (1,),
-        name="route",
+        [rows_of((1, 8, c.R)), rows_of((1, 8, c.R)), whole(outs[2])],
+        (c.n,),
+        name="keep",
     )
 
 
@@ -364,69 +424,45 @@
     return jnp.where(row == 14, high, jnp.where(row == 15, low, tile))
 
 
-def dispatch_body(c, rows_all, halves, weighted, place, *refs):
-    refs = list(refs)
-    slot_ref, src_ref = refs[:2]
-    refs = refs[2:]
-    if weighted:
-        weight_ref = refs.pop(0)
-    out_ref, hot_ref = refs
-
+def dispatch_body(c, half, place, slot_ref, src_ref, weight_ref, out_ref, hot_ref):
     @pl.when(pl.program_id(0) == 0)
     def _():
+        fill_hot(c, place, slot_ref, hot_ref, (half,))
+
+    acc = dot_nn(hot_ref[0], src_ref[...])
+    out_ref[...] = acc.astype(BF)
+
+    @pl.when(pl.program_id(0) == 0)
+    def _():
+        gates = dot_nn(hot_ref[0], weight_ref[...])
+        lane = lax.broadcasted_iota(I32, (1, 128), 1)
+        wide = (c.SP, c.half)
+        eye = lax.broadcasted_iota(I32, wide, 0) == lax.broadcasted_iota(I32, wide, 1)
         for j in range(c.X):
-            slot = slot_ref[pl.ds(expert_of(c, place, j), 1), :]
-            kept = (slot >= 0) & (slot + offset_at(place, j) < c.cap)
-            row = jnp.where(kept, window_slot(c, place, j, slot), -1)
-            for index, half in enumerate(halves):
-                slots = lax.broadcasted_iota(I32, (c.SP, c.TP), 0) + half * c.SP
-                hot_ref[index, j * c.SP : (j + 1) * c.SP, :] = (slots == row).astype(BF)
-
-    for index in range(len(halves)):
-        acc = dot_nn(hot_ref[index, :, :rows_all], src_ref[...])
-        for j in range(c.X):
-            at = (len(halves) * j + index) * c.SP
-            out_ref[at : at + c.SP, :] = acc[j * c.SP : (j + 1) * c.SP].astype(BF)
-        if weighted:
-
-            @pl.when(pl.program_id(0) == 0)
-            def _():
-                gates = dot_nn(hot_ref[index], weight_ref[...])
-                lane = lax.broadcasted_iota(I32, (1, 128), 1)
-                wide = (c.SP, c.half)
-                eye = lax.broadcasted_iota(I32, wide, 0) == lax.broadcasted_iota(I32, wide, 1)
-                for j in range(c.X):
-                    e = expert_of(c, place, j)
-                    mine = gates[j * c.SP : (j + 1) * c.SP]
-                    rows = []
-                    for at in (e, e + 64):
-                        col = jnp.sum(jnp.where(lane == at, mine, 0.0), axis=1, keepdims=True)
-                        rows.append(jnp.sum(jnp.where(eye, col, 0.0), axis=0, keepdims=True))
-                    end = (j + 1) * c.SP
-                    tile = last_rows(c, acc[end - 16 : end], rows[0], rows[1])
-                    out_ref[end - 16 : end, :] = tile.astype(BF)
-
-
-def dispatch(c, order, place, slot, source, halves, weight=None):
-    rows_all = source.shape[0]
-    args = [slot, source]
-    specs = [whole(slot), pl.BlockSpec((rows_all, c.half), lambda i, s: (0, i ^ s[2]))]
-    if weight is not None:
-        args.append(weight)
-        specs.append(whole(weight))
-    size = len(halves) * c.SP
+            e = expert_of(c, place, j)
+            mine = gates[j * c.SP : (j + 1) * c.SP]
+            rows = []
+            for at in (e, e + 64):
+                col = jnp.sum(jnp.where(lane == at, mine, 0.0), axis=1, keepdims=True)
+                rows.append(jnp.sum(jnp.where(eye, col, 0.0), axis=0, keepdims=True))
+            end = (j + 1) * c.SP
+            tile = last_rows(c, acc[end - 16 : end], rows[0], rows[1])
+            out_ref[end - 16 : end, :] = tile.astype(BF)
+
+
+def dispatch(c, order, place, slot, source, weight, half):
     return call(
         order,
-        functools.partial(dispatch_body, c, rows_all, halves, weight is not None),
-        place,
-        args,
-        specs,
-        [shape_of((c.X * size, c.D), BF)],
-        [cols_of((c.X * size, c.half))],
+        functools.partial(dispatch_body, c, half),
+        place,
+        [slot, source, weight],
+        [whole(slot), pl.BlockSpec((c.TP, c.half), lambda i, s: (0, i ^ s[2])), whole(weight)],
+        [shape_of((c.X * c.SP, c.D), BF)],
+        [cols_of((c.X * c.SP, c.half))],
         (2,),
-        [pltpu.VMEM((len(halves), c.X * c.SP, c.TP), BF)],
+        [pltpu.VMEM((1, c.X * c.SP, c.TP), BF)],
         name="dispatch",
-    )[0].reshape(c.X, size, c.D)
+    )[0].reshape(c.X, c.SP, c.D)
 
 
 def norm_rows(values):
@@ -574,16 +610,16 @@
     groups = groups_of(c)
     count = c.n * len(groups)
     mixes, refs = refs[:count], refs[count:]
-    own_ref, oth_ref, tok_ref, small_ref, off_ref, slot_ref, rt_ref = refs[:7]
-    hid_ref, weight_ref, mine_ref, keep_ref = refs[7:11]
-    after_ref, probs_ref, keep_lane_ref, weight_lane_ref, proj_ref = refs[11:]
+    w_ref, tok_ref, small_ref, table_ref, slot_ref = refs[:5]
+    hid_ref, weight_ref, after_ref, probs_ref, proj_ref = refs[5:]
     step = pl.program_id(0)
 
     @pl.when(step == 0)
     def _():
         for k in range(c.n):
-            proj_ref[k * c.W : (k + 1) * c.W, own_cols(c, place)] = own_ref[k]
-            proj_ref[k * c.W : (k + 1) * c.W, other_cols(c, place)] = oth_ref[k]
+            for h in range(2):
+                cols = slice(h * c.half, (h + 1) * c.half)
+                proj_ref[k * c.W : (k + 1) * c.W, cols] = w_ref[(place[1] ^ k) * 2 + h]
 
     branch = dot_nn(jnp.concatenate([mix[...] for mix in mixes], axis=1), proj_ref[...])
     live = live_rows(c, step * c.R, c.R)
@@ -592,65 +628,36 @@
     normed, _ = norm_rows(after)
     hidden = (normed * small_row(c, small_ref, 1) + small_row(c, small_ref, 3)).astype(BF)
     hid_ref[...] = hidden
-    router = small_ref[6 + c.E : 6 + 2 * c.E, :]
+    router = table_ref[c.E : 2 * c.E, :]
     logits = dot_nt(router, hidden)
     exps = jnp.exp(logits - jnp.max(logits, axis=0, keepdims=True))
     probs = exps / jnp.sum(exps, axis=0, keepdims=True)
-    slot = slot_ref[0]
-    kept = (slot >= 0) & (slot + off_ref[:, 0:1] < c.cap)
-    weight = jnp.where(kept, probs, 0.0)
+    weight = jnp.where(slot_ref[0] >= 0, probs, 0.0)
     high, rest = split_low(weight)
     lane = lax.broadcasted_iota(I32, (c.E, 128), 1)
     index = lax.broadcasted_iota(I32, (c.E, 128), 0)
     both = dot_tn(high, (lane == index).astype(BF)) + dot_tn(rest, (lane == index + 64).astype(BF))
     weight_ref[...] = both.astype(BF)
-    for j in range(c.X):
-        e = expert_of(c, place, j)
-        slot_j = slot_ref[0, pl.ds(e, 1), :]
-        kept_j = (slot_j >= 0) & (slot_j + offset_at(place, j) < c.cap)
-        row = jnp.where(kept_j, window_slot(c, place, j, slot_j), -1)
-        mine_ref[0, j : j + 1, :] = row
-    for j in range(c.X, 8):
-        mine_ref[0, j : j + 1, :] = jnp.full((1, c.R), -1, I32)
-    expert = lax.broadcasted_iota(I32, (c.E, c.R), 0)
-    rows = []
-    for k in range(2):
-        picked = jnp.where((rt_ref[0, k : k + 1, :] == expert) & kept, 1.0, 0.0)
-        rows.append(jnp.sum(picked, axis=0, keepdims=True))
-    keep_ref[0] = jnp.concatenate(rows * 4, axis=0)
-
     @pl.when(step == place[1])
     def _():
         after_ref[...] = after
         probs_ref[...] = probs
-        keep_lane_ref[...] = jnp.where(kept, 1.0, 0.0)
-        weight_lane_ref[...] = weight
-
-
-def middle(c, order, place, mixes, own_w, oth_w, tokens, small, offsets, slot, rt):
-    args = [pair[0] for pair in flat(mixes)] + [own_w, oth_w, tokens, small, offsets, slot, rt]
+
+
+def middle(c, order, place, mixes, proj, tokens, small, table, blocks):
+    args = [pair[0] for pair in flat(mixes)] + [proj, tokens, small, table, blocks]
     specs = [
         pl.BlockSpec((None, c.R, a.shape[2]), lambda i, s, at=at: (at, i, 0))
         for a, at in flat(mixes)
     ]
-    specs += [whole(own_w), whole(oth_w), rows_of((c.R, c.D)), whole(small), whole(offsets)]
-    specs += [rows_of((1, c.E, c.R)), rows_of((1, 8, c.R))]
+    specs += [whole(proj), rows_of((c.R, c.D)), whole(small), whole(table)]
+    specs += [rows_of((1, c.E, c.R))]
     outs = [
         shape_of((c.TP, c.D), BF),
         shape_of((c.TP, 128), BF),
-        shape_of((c.n, 8, c.R), I32),
-        shape_of((c.n, 8, c.R), F32),
         shape_of((c.R, c.D), F32),
         shape_of((c.E, c.R), F32),
-        shape_of((c.E, c.R), F32),
-        shape_of((c.E, c.R), F32),
     ]
-    out_specs = [
-        rows_of((c.R, c.D)),
-        rows_of((c.R, 128)),
-        rows_of((1, 8, c.R)),
-        rows_of((1, 8, c.R)),
-    ] + [whole(o) for o in outs[4:]]
     return call(
         order,
         functools.partial(middle_body, c),
@@ -658,22 +665,30 @@
         args,
         specs,
         outs,
-        out_specs,
+        [rows_of((c.R, c.D)), rows_of((c.R, 128)), whole(outs[2]), whole(outs[3])],
         (c.n,),
         [pltpu.VMEM((c.D, c.D), BF)],
         name="middle",
     )
 
 
-def pack_rows(c, place, half, rows, out_ref, base=0, start=0):
-    main = c.SP - 16
-    used = lax.broadcasted_iota(I32, (16, 1), 0) < 14
-    out_ref[base : base + c.CR[half], :] = jnp.zeros((c.CR[half], c.D), BF)
+def fill_packs(c, place, tails, packs):
+    lane = lax.broadcasted_iota(I32, (1, 128), 1)
+    here = place[0] * EXP_DEV + place[3]
+    state = [jnp.zeros((1, 1), F32)] * 3
     for j in range(c.X):
-        at = pl.multiple_of(window_in(c, place, half, j) + base, 16)
-        out_ref[pl.ds(at, main), :] += rows[j, start : start + main, :]
-        tail = jnp.where(used, rows[j, start + main : start + c.SP, :], BF(0))
-        out_ref[pl.ds(pl.multiple_of(at + main, 16), 16), :] += tail
+        high, low = last_pair(c, tails[j], 128)
+        number = jnp.sum(jnp.where(lane == here, high * 16.0 + low, 0.0), axis=1, keepdims=True)
+        kept = jnp.clip(c.cap - state[0], 0.0, number)
+        first = jnp.minimum(kept, float(c.Q))
+        sizes = first, kept - first
+        for half in range(2):
+            wide = (c.CR[half], c.SP)
+            slot = lax.broadcasted_iota(I32, wide, 1)
+            at = lax.broadcasted_iota(I32, wide, 0) - state[1 + half].astype(I32)
+            hot = (at == slot) & (slot < sizes[half].astype(I32))
+            packs[half][:, j * c.SP : (j + 1) * c.SP] = hot.astype(BF)
+        state = [state[0] + number, state[1] + sizes[0], state[2] + sizes[1]]
 
 
 def last_pair(c, tile, lanes):
@@ -685,23 +700,28 @@
     return [slice(at, min(at + size, rows)) for at in range(0, rows, size)]
 
 
-def grad_active_body(c, place, *refs):
-    rows, own_ref, oth_ref, *outs, all_ref = refs
+def grad_active_body(c, place, rows_ref, own_ref, oth_ref, *outs):
+    gas, all_ref, packs = outs[:2], outs[2], outs[3:]
 
     @pl.when(pl.program_id(0) == 0)
     def _():
-        pack_rows(c, place, 0, rows, all_ref)
-        pack_rows(c, place, 1, rows, all_ref, c.CR[0], c.SP)
+        tails = [rows_ref[j, c.SP - 16 : c.SP, :] for j in range(c.X)]
+        fill_packs(c, place, tails, packs)
+        for half, base in enumerate((0, c.CR[0])):
+            rows = [rows_ref[j, half * c.SP : (half + 1) * c.SP, :] for j in range(c.X)]
+            got = dot_nn(packs[half][...], jnp.concatenate(rows, axis=0))
+            all_ref[base : base + c.CR[half], :] = got.astype(BF)
 
     weights = jnp.concatenate([own_ref[...], oth_ref[...]], axis=1)
     for half, base in enumerate((0, c.CR[0])):
         for at in row_chunks(c.CR[half], 320):
             values = all_ref[base + at.start : base + at.stop, :]
-            outs[half][at, :] = dot_nt(values, weights).astype(BF)
+            gas[half][at, :] = dot_nt(values, weights).astype(BF)
 
 
 def grad_active(c, order, place, rows, own_w, oth_w):
-    outs = [shape_of((rows, c.F), BF) for rows in c.CR] + [shape_of((sum(c.CR), c.D), BF)]
+    outs = [shape_of((count, c.F), BF) for count in c.CR] + [shape_of((sum(c.CR), c.D), BF)]
+    outs += [shape_of((count, c.X * c.SP), BF) for count in c.CR]
     return call(
         order,
         functools.partial(grad_active_body, c),
@@ -709,29 +729,34 @@
         [rows, own_w, oth_w],
         [whole(rows, 1)] + [rows_of((c.fblk, c.half))] * 2,
         outs,
-        [cols_of((rows, c.fblk)) for rows in c.CR] + [whole(outs[2])],
+        [cols_of((count, c.fblk)) for count in c.CR] + [whole(o) for o in outs[2:]],
         (c.F // c.fblk,),
         name="grad_active",
     )
 
 
 def expert_body(c, half, place, *refs):
-    rows, own_ref, oth_ref, bias_ref, ga_ref = refs[:5]
-    act_ref, gp_ref, gb_ref, all_ref, col_ref, back_ref = refs[5:11]
-    acc_ref, dot_ref, row_ref = refs[11:]
+    rows_ref, pack_ref, own_ref, oth_ref, bias_ref, ga_ref = refs[:6]
+    act_ref, gp_ref, gb_ref, all_ref, col_ref, back_ref = refs[6:12]
+    acc_ref, dot_ref, row_ref, wide_ref = refs[12:]
     step = pl.program_id(0)
 
     @pl.when(step == 0)
     def _():
         acc_ref[...] = jnp.zeros_like(acc_ref)
         dot_ref[...] = jnp.zeros_like(dot_ref)
-        pack_rows(c, place, half, rows, all_ref)
-        col_ref[...] = jnp.zeros_like(col_ref)
+        all_ref[...] = dot_nn(pack_ref[...], rows_ref[...]).astype(BF)
         eye = lax.broadcasted_iota(I32, (c.SP, c.SP), 0) == lax.broadcasted_iota(I32, (c.SP, c.SP), 1)
+        lane = lax.broadcasted_iota(I32, (1, 128), 1)
         for j in range(c.X):
-            high, low = last_pair(c, rows[j, c.SP - 16 :, :], c.SP)
-            col = jnp.sum(jnp.where(eye, high + low, 0.0), axis=1, keepdims=True)
-            col_ref[pl.ds(window_in(c, place, half, j), c.SP), :] += jnp.broadcast_to(col, (c.SP, 128))
+            end = (j + 1) * c.SP
+            high, low = last_pair(c, rows_ref[end - 16 : end, :], c.SP)
+            high = jnp.sum(jnp.where(eye, high, 0.0), axis=1, keepdims=True)
+            low = jnp.sum(jnp.where(eye, low, 0.0), axis=1, keepdims=True)
+            both = jnp.where(lane == 0, high, jnp.where(lane == 1, low, 0.0))
+            wide_ref[j * c.SP : end, :] = both.astype(BF)
+        both = dot_nn(pack_ref[...], wide_ref[...])
+        col_ref[...] = jnp.broadcast_to(both[:, 0:1] + both[:, 1:2], (c.CR[half], 128))
 
     bias = bias_ref[...]
     weights = jnp.concatenate([own_ref[...], oth_ref[...]], axis=0)
@@ -767,23 +792,26 @@
     def _():
         ones = jnp.ones((8, 128), BF)
         row_ref[...] = jnp.zeros_like(row_ref)
+        back_ref[...] = dot_tn(pack_ref[...], acc_ref[...].astype(BF)).astype(BF)
+        a, rest = split_low(dot_ref[...])
+        total = dot_nt(ones, a) + dot_nt(ones, rest)
+        high, low = split_low(total)
+        high = dot_nn(high, pack_ref[...])
+        low = dot_nn(low, pack_ref[...])
         for j in range(c.X):
-            at = window_in(c, place, half, j)
-            back_ref[j] = acc_ref[pl.ds(at, c.SP), :].astype(BF)
-            a, rest = split_low(dot_ref[pl.ds(at, c.SP), :])
-            total = dot_nt(ones, a) + dot_nt(ones, rest)
-            high = total.astype(BF).astype(F32)
-            row_ref[0:8, : c.SP] = high
-            row_ref[8:16, : c.SP] = total - high
-            tile = back_ref[j, c.SP - 16 :, : c.half].astype(F32)
+            end = (j + 1) * c.SP
+            row_ref[0:8, : c.SP] = high[:, j * c.SP : end]
+            row_ref[8:16, : c.SP] = low[:, j * c.SP : end]
+            tile = back_ref[end - 16 : end, : c.half].astype(F32)
             tile = last_rows(c, tile, row_ref[0:1, :], row_ref[8:9, :])
-            back_ref[j, c.SP - 16 :, : c.half] = tile.astype(BF)
-
-
-def expert(c, order, place, half, rows, own_w, oth_w, bias, ga):
-    args = [rows, own_w, oth_w, bias, ga]
+            back_ref[end - 16 : end, : c.half] = tile.astype(BF)
+
+
+def expert(c, order, place, half, rows, pack, own_w, oth_w, bias, ga):
+    rows = rows.reshape(c.X * c.SP, c.D)
+    args = [rows, pack, own_w, oth_w, bias, ga]
     count = c.CR[half]
-    specs = [whole(rows, 1)]
+    specs = [whole(rows, 1), whole(pack, 1)]
     specs += [cols_of((c.half, c.fblk))] * 2
     specs += [cols_of((1, c.fblk)), cols_of((count, c.fblk))]
     outs = [
@@ -793,8 +821,8 @@
     ]
     out_specs = [cols_of((count, c.fblk))] * 2 + [cols_of((8, c.fblk))]
     late = [shape_of((count, c.D), BF), shape_of((count, 128), F32)]
-    late.append(shape_of((c.X, c.SP, c.D), BF))
-    return call(
+    late.append(shape_of((c.X * c.SP, c.D), BF))
+    result = call(
         order,
         functools.partial(expert_body, c, half),
         place,
@@ -807,13 +835,16 @@
             pltpu.VMEM((count, c.D), F32),
             pltpu.VMEM((count, 128), F32),
             pltpu.VMEM((16, c.half), F32),
+            pltpu.VMEM((c.X * c.SP, 128), BF),
         ],
         name="expert",
     )
+    return (*result[:5], result[5].reshape(c.X, c.SP, c.D))
 
 
 def produce_body(c, place, *refs):
-    cols, acts, own_ref, oth_ref, out_ref, accs = refs[:2], refs[2:4], refs[4], refs[5], refs[6], refs[7:]
+    cols, acts, packs, own_ref, oth_ref, out_ref = refs[:2], refs[2:4], refs[4:6], *refs[6:9]
+    accs = refs[9:]
     step = pl.program_id(0)
 
     @pl.when(step == 0)
@@ -829,21 +860,23 @@
     @pl.when(step == pl.num_programs(0) - 1)
     def _():
         for half in range(2):
+            values = (accs[half][...] * cols[half][:, 0:1]).astype(BF)
+            values = dot_tn(packs[half][...], values).astype(BF)
             for j in range(c.X):
-                rows_at = pl.ds(window_in(c, place, half, j), c.SP)
-                col = cols[half][rows_at, 0:1]
-                out_ref[j, half * c.SP : (half + 1) * c.SP, :] = (accs[half][rows_at, :] * col).astype(BF)
-
-
-def produce(c, order, place, cols, acts, own_w, oth_w):
+                rows = values[j * c.SP : (j + 1) * c.SP]
+                out_ref[j, half * c.SP : (half + 1) * c.SP, :] = rows
+
+
+def produce(c, order, place, cols, acts, packs, own_w, oth_w):
     out = shape_of((c.X, 2 * c.SP, c.D), BF)
     return call(
         order,
         functools.partial(produce_body, c),
         place,
-        [*cols, *acts, own_w, oth_w],
+        [*cols, *acts, *packs, own_w, oth_w],
         [whole(col) for col in cols]
         + [cols_of((rows, c.fblk)) for rows in c.CR]
+        + [whole(pack) for pack in packs]
         + [rows_of((c.fblk, c.half))] * 2,
         [out],
         [whole(out, 1)],
@@ -1022,16 +1055,16 @@
     refs = list(refs)
     groups = groups_of(c)
     heads, refs = refs[: c.n * len(groups)], refs[c.n * len(groups) :]
-    count = (len(refs) - 14 - c.n) // 2
+    count = (len(refs) - 13 - c.n) // 2
     a, b, refs = refs[:count], refs[count : 2 * count], refs[2 * count :]
-    own_ref, oth_ref, after_ref, probs_ref, keep_ref, weight_ref, cot_ref, hid_ref, small_ref = refs[:9]
-    ga_ref, proj_own_ref, proj_oth_ref = refs[9:12]
-    mixes, (gb_ref, sums_ref) = refs[12:-2], refs[-2:]
+    w_ref, after_ref, probs_ref, keep_ref = refs[:4]
+    cot_ref, hid_ref, small_ref, table_ref, ga_ref, proj_own_ref, proj_oth_ref = refs[4:11]
+    mixes, (gb_ref, sums_ref) = refs[11:-2], refs[-2:]
     sum_a = add_up(a)
     live = live_rows(c, place[1] * c.R, c.R)
     cot = jnp.where(live, cot_ref[...], BF(0))
-    eshift = small_ref[6 : 6 + c.E, :]
-    router = small_ref[6 + c.E : 6 + 2 * c.E, :]
+    eshift = table_ref[: c.E, :]
+    router = table_ref[c.E : 2 * c.E, :]
     kept = keep_ref[...] > 0
     pulls = jnp.where(kept, sum_a[c.R :, : c.R] + dot_nt(eshift, cot), 0.0)
     probs = probs_ref[...]
@@ -1042,7 +1075,7 @@
     ga_ref[...] = grad_after
     low = grad_after.astype(BF)
     gb_ref[...] = low
-    high, rest = split_low(weight_ref[...])
+    high, rest = split_low(probs * keep_ref[...])
     hid = jnp.where(live, hid_ref[...], BF(0))
     sums_ref[0:1, :] = jnp.sum(two * normed, axis=0, keepdims=True)
     sums_ref[1:2, :] = jnp.sum(two, axis=0, keepdims=True)
@@ -1051,8 +1084,9 @@
     sums_ref[8 : 8 + c.E, :] = dot_nn(high, cot) + dot_nn(rest, cot)
     sums_ref[8 + c.E : 8 + 2 * c.E, :] = dot_nn(glog, hid)
     for k in range(c.n):
-        mix = dot_nt(gb_ref[:, own_cols(c, place)], own_ref[k])
-        mix = mix + dot_nt(gb_ref[:, other_cols(c, place)], oth_ref[k])
+        lane = place[1] ^ k
+        mix = dot_nt(gb_ref[:, : c.half], w_ref[2 * lane])
+        mix = mix + dot_nt(gb_ref[:, c.half :], w_ref[2 * lane + 1])
         mixes[k][...] = mix.astype(BF)
     height = sums_ref.shape[0]
     for cols, out_ref in ((own_cols(c, place), proj_own_ref), (other_cols(c, place), proj_oth_ref)):
@@ -1066,7 +1100,7 @@
             out_ref[k, c.W + height :, :] = jnp.zeros((rest, c.half), BF)
 
 
-def back_two(c, order, place, heads, sums, own_w, oth_w, lanes, cotangent, hidden, small):
+def back_two(c, order, place, heads, sums, proj, lanes, cotangent, hidden, small, table):
     height = 8 + 2 * c.E
     rows = up(c.W + height, 32)
     args = [pair[0] for pair in flat(heads)]
@@ -1074,10 +1108,11 @@
         pl.BlockSpec((None, c.R, a.shape[2]), lambda i, s, at=at: (at, s[1], 0))
         for a, at in flat(heads)
     ]
-    args += [*sums[0], *sums[1], own_w, oth_w, *lanes, cotangent, hidden, small]
+    args += [*sums[0], *sums[1], proj, *lanes, cotangent, hidden, small, table]
     lane_rows = pl.BlockSpec((c.R, c.D), lambda i, s: (s[1], 0))
     specs += [first_block(a) for a in [*sums[0], *sums[1]]]
-    specs += [whole(a) for a in [own_w, oth_w, *lanes]] + [lane_rows, lane_rows, whole(small)]
+    specs += [whole(a) for a in [proj, *lanes]] + [lane_rows, lane_rows]
+    specs += [whole(small), whole(table)]
     outs = [shape_of((c.R, c.D), F32)] + [shape_of((c.n, rows, c.half), BF)] * 2
     outs += [shape_of((c.R, c.W), BF) for _ in range(c.n)]
     result = call(
@@ -1097,11 +1132,11 @@
 
 def block_out_body(c, place, *refs):
     refs = list(refs)
-    count = (len(refs) - 5) // 2
+    count = (len(refs) - 6) // 2
     a, b, refs = refs[:count], refs[count : 2 * count], refs[2 * count :]
-    after_ref, weight_ref, small_ref, out_ref, proj_ref = refs
-    high, low = split_low(weight_ref[...])
-    eshift = small_ref[6 : 6 + c.E, :]
+    after_ref, probs_ref, keep_ref, table_ref, out_ref, proj_ref = refs
+    high, low = split_low(probs_ref[...] * keep_ref[...])
+    eshift = table_ref[: c.E, :]
     shift = dot_tn(high, eshift) + dot_tn(low, eshift)
     more = proj_ref.shape[0] // 2
     for h, pieces in enumerate((a, b)):
@@ -1111,8 +1146,8 @@
         proj_ref[h * more : (h + 1) * more, :] = same_sum(c, pieces, slice(c.R, c.R + more)).astype(BF)
 
 
-def block_out(c, order, place, sums, after, weight, small):
-    args = [*sums[0], *sums[1], after, weight, small]
+def block_out(c, order, place, sums, after, probs, keep, table):
+    args = [*sums[0], *sums[1], after, probs, keep, table]
     more = 2 * (sums[0][0].shape[1] - c.R)
     outs = [shape_of((2, c.R, c.half), BF), shape_of((more, c.half), BF)]
     return call(
@@ -1120,7 +1155,7 @@
         functools.partial(block_out_body, c),
         place,
         args,
-        [first_block(a) for a in args[:-3]] + [whole(a) for a in args[-3:]],
+        [first_block(a) for a in args[:-4]] + [whole(a) for a in args[-4:]],
         outs,
         [whole(o) for o in outs],
         (1,),
@@ -1201,39 +1236,33 @@
 
 def back_one_body(c, place, *refs):
     refs = list(refs)
-    count = (len(refs) - 5) // 2
+    count = (len(refs) - 4) // 2
     a, b, refs = refs[:count], refs[count : 2 * count], refs[2 * count :]
-    tok_ref, after_ref, small_ref, out_ref, sums_ref = refs
+    tok_ref, after_ref, small_ref, out_ref = refs
     live = live_rows(c, place[1] * c.R, c.R)
     normed, inv_std = norm_rows(jnp.where(live, tok_ref[...].astype(F32), 0.0))
     one = jnp.concatenate([add_up(a)[: c.R], add_up(b)[: c.R]], axis=1)
     grad = after_ref[...] + norm_back(one, small_row(c, small_ref, 0), normed, inv_std)
     for h in range(2):
         out_ref[h] = grad[:, h * c.half : (h + 1) * c.half].astype(BF)
-    for h, refs in enumerate((a, b)):
-        tiles = [ref[c.R :, :].astype(F32) for ref in refs]
-        pair = (tiles[0] + tiles[1]).astype(BF).astype(F32)
-        for tile in tiles[2:]:
-            pair = pair + tile
-        sums_ref[:, h * c.half : (h + 1) * c.half] = pair[0:2]
 
 
 def back_one(c, order, place, sums, tokens, after, small):
     args = [*sums[0], *sums[1], tokens, after, small]
     lane_rows = pl.BlockSpec((c.R, c.D), lambda i, s: (s[1], 0))
     specs = [first_block(a) for a in args[:-3]] + [lane_rows, whole(after), whole(small)]
-    outs = [shape_of((2, c.R, c.half), BF), shape_of((2, c.D), F32)]
+    out = shape_of((2, c.R, c.half), BF)
     return call(
         order,
         functools.partial(back_one_body, c),
         place,
         args,
         specs,
-        outs,
-        [whole(o) for o in outs],
+        [out],
+        [whole(out)],
         (1,),
         name="back_one",
-    )
+    )[0]
 
 
 def assemble_body(c, place, *refs):
@@ -1303,7 +1332,7 @@
         E=E,
         S=S,
         Q=Q,
-        SP=up(Q + 17, 16),
+        SP=up(Q + 2, 16),
         CR=(up(min(cap, X * Q), 16), up(full * (S - Q) + max(0, cap - full * S - Q), 16)),
         R=R,
         TP=n * R,
@@ -1318,51 +1347,30 @@
     )
     order = Order()
     dp, mp, grid = lax.axis_index("dp"), lax.axis_index("mp"), lax.axis_index("grid")
-    here = jnp.stack([dp, mp, grid, mp // c.quarters]).astype(I32)
-
-    experts = jnp.arange(E, dtype=I32)[:, None, None]
-    count = jnp.sum((routes.T[None] == experts).astype(I32), axis=(1, 2))[None]
-    counts = trade(jnp.broadcast_to(count, (c.X, E)), "dp")
-    bias_rows = F // 2 // c.half
-    packed = jnp.concatenate(
-        [
-            norm_gains,
-            norm_shifts,
-            proj_bias[None],
-            jnp.pad(qv_bias, ((0, 0), (0, c.half - W))),
-            expert_shift,
-            w_router.T,
-            first_bias.reshape(bias_rows, c.half),
-        ],
-        axis=0,
-    )
-    packed = jnp.pad(packed, ((0, up(packed.shape[0], 16) - packed.shape[0]), (0, 0)))
-    packed_oth = swap_grid(packed)
-    small = jnp.where(
-        grid == 0,
-        jnp.concatenate([packed, packed_oth], axis=1),
-        jnp.concatenate([packed_oth, packed], axis=1),
-    )
-    bias = small[6 + 2 * E : 6 + 2 * E + bias_rows].reshape(bias_rows, 2, c.half)
-    bias = bias.transpose(1, 0, 2).reshape(1, F).astype(F32)
+    place = jnp.stack([dp, mp, grid, mp // c.quarters]).astype(I32)
+
+    slot, blocks, rt, grad_out = route(c, order, place, routes, priority, cotangent)
+    grad_in = trade(grad_out, "dp")
+
+    def both_halves(rows):
+        rows = jnp.pad(rows, ((0, up(rows.shape[0], 16) - rows.shape[0]), (0, 0)))
+        other = swap_grid(rows)
+        return jnp.where(
+            grid == 0,
+            jnp.concatenate([rows, other], axis=1),
+            jnp.concatenate([other, rows], axis=1),
+        )
+
+    wide_bias = jnp.pad(qv_bias, ((0, 0), (0, c.half - W)))
+    small = both_halves(
+        jnp.concatenate([norm_gains, norm_shifts, proj_bias[None], wide_bias], axis=0)
+    )
     qkv_own = w_qkv.transpose(1, 0, 2)
     qkv_oth = swap_grid(qkv_own)
-    slot, blocks, rt = route(c, order, here, routes, priority)
-    order.tie(packed_oth)
-    order.tie(qkv_oth)
-    proj_own = jnp.stack([w_proj] + [swap_mp(c, w_proj, k) for k in range(1, n)])
-    order.tie(proj_own)
-    place, offsets = windows(c, order, here, counts)
-    grad_out = dispatch(c, order, place, slot, cotangent, (0, 1))
-    grad_in = trade(grad_out, "dp")
 
     first_own = w_first[0]
     second_own = w_second[0]
-    second_tied, first_tied, _ = lax.optimization_barrier((second_own, first_own, grad_out))
-    second_oth = swap_grid(second_tied)
-    first_oth = swap_grid(first_tied)
-
-    proj_oth = swap_grid(proj_own)
+    proj = lax.all_gather(w_proj, ("mp", "grid"))
 
     outs = [shape_of((c.TP, D), BF), shape_of((c.TP, 3 * W), BF), shape_of((c.TP, D), BF)]
     hidden_one, qkv, normed_one = call(
@@ -1377,6 +1385,14 @@
         [pltpu.VMEM((D, 3 * W), BF)],
         name="qkv",
     )
+    bias_rows = F // 2 // c.half
+    tied = held(jnp.concatenate([expert_shift, w_router.T]), qkv)
+    table = both_halves(tied)
+    bias = both_halves(held(first_bias.reshape(bias_rows, c.half), qkv))[:bias_rows]
+    bias = bias.reshape(bias_rows, 2, c.half).transpose(1, 0, 2).reshape(1, F).astype(F32)
+    order.tie(proj)
+    second_oth = swap_grid(held(second_own, qkv))
+    first_oth = swap_grid(held(first_own, qkv))
     groups = groups_of(c)
     out = shape_of((len(groups), c.TP, groups[0][1]), BF)
     mix = call(
@@ -1391,29 +1407,33 @@
         name="attend",
     )[0]
     mixes, _ = gather_mp(c, mix)
-    hidden_two, weight, mine, keep, after, probs, keep_lane, weight_lane = middle(
-        c, order, place, mixes, proj_own, proj_oth, tokens, small, offsets, blocks, rt
-    )
+    hidden_two, weight, after, probs = middle(
+        c, order, place, mixes, proj, tokens, small, table, blocks
+    )
+
+    rows_a = trade(dispatch(c, order, place, slot, hidden_two, weight, 0), "dp")
+    rows_b = dispatch(c, order, place, slot, hidden_two, weight, 1)
+    ga_a, ga_b, grad_all, pack_a, pack_b = grad_active(
+        c, order, place, grad_in, second_own, second_oth
+    )
+    mine, keep, keep_lane = keep_of(c, order, place, grad_in, blocks, rt)
     keep_mask = keep[:, :2, :].transpose(0, 2, 1).reshape(c.TP, 2)[:T].astype(I32)
     mine = mine.transpose(0, 2, 1).reshape(c.TP, 8)
-
-    rows_a = trade(dispatch(c, order, place, slot, hidden_two, (0,), weight), "dp")
-    rows_b = dispatch(c, order, place, slot, hidden_two, (1,), weight)
-    ga_a, ga_b, grad_all = grad_active(c, order, place, grad_in, second_own, second_oth)
     rows_b = trade(held(rows_b, rows_a, grad_all), "dp")
     act_a, gp_a, gb_a, all_a, col_a, back_a = expert(
-        c, order, place, 0, rows_a, first_own, first_oth, bias, ga_a
+        c, order, place, 0, rows_a, pack_a, first_own, first_oth, bias, ga_a
     )
     back_a = trade(held(back_a, rows_b), "dp")
     act_b, gp_b, gb_b, all_b, col_b, back_b = expert(
-        c, order, place, 1, rows_b, first_own, first_oth, bias, ga_b
+        c, order, place, 1, rows_b, pack_b, first_own, first_oth, bias, ga_b
     )
     back_b = trade(held(back_b, back_a), "dp")
     cols, acts, gps, alls = [col_a, col_b], [act_a, act_b], [gp_a, gp_b], [all_a, all_b]
     second_part = swap_grid(grad_second(c, order, place, grad_all, cols, acts))
     order.tie(back_a)
     first_part = swap_grid(grad_first(c, order, place, alls, gps))
-    prod = produce(c, order, place, cols, acts, second_own, second_oth)
+    packs = [pack_a, pack_b]
+    prod = produce(c, order, place, cols, acts, packs, second_own, second_oth)
     gb = (gb_a + gb_b)[0:1].reshape(2, F // 2)
     gb_own = lax.dynamic_index_in_dim(gb, grid, 0, True)
     gb_oth = lax.dynamic_index_in_dim(gb, 1 - grid, 0, True)
@@ -1431,12 +1451,12 @@
         place,
         mixes,
         two_sums,
-        proj_own,
-        proj_oth,
-        [after, probs, keep_lane, weight_lane],
+        proj,
+        [after, probs, keep_lane],
         cotangent,
         hidden_two,
         small,
+        table,
     )
     grad_mix = [grad_mix[0]] + [swap_mp(c, grad_mix[k], k) for k in range(1, n)]
     proj_low = (proj_a.astype(F32) + swap_grid(proj_b).astype(F32)).astype(BF)
@@ -1460,26 +1480,24 @@
     one_sums = reduce_start(c, one_pieces)
     out_sums = reduce_end(c, order, out_sums)
     qkv_a, qkv_b = grad_qkv(c, order, place, hidden_one, dqkv)
-    out_lane, proj_sum = block_out(c, order, place, out_sums, after, weight_lane, small)
     one_sums = reduce_end(c, order, one_sums)
+    out_lane, proj_sum = block_out(c, order, place, out_sums, after, probs, keep_lane, table)
+
     qkv_b = swap_grid(qkv_b)
     qkv_low = (qkv_a.astype(F32) + qkv_b.astype(F32)).astype(BF)
-    proj_rows = proj_sum.shape[0]
+    proj_end = 3 * W + proj_sum.shape[0]
     shared = jnp.concatenate([qkv_low.reshape(-1, c.half), proj_sum], axis=0)
+    shared = jnp.pad(shared, ((0, up(shared.shape[0], 16 * c.X) - shared.shape[0]), (0, 0)))
     shared = sum_dp_start(c, shared)
-    grad_low, sums_one = back_one(c, order, place, one_sums, tokens, grad_after, small)
-    grad_low, first_low = gather_mp(c, grad_low, shared)
-    out_lane, _ = gather_mp(c, held(out_lane, *first_low))
-    sums_one = held(sums_one, *[pair[0] for pair in grad_low[-1]])
-
-    shared = sum_dp_end(c, shared)
+    grad_low = back_one(c, order, place, one_sums, tokens, grad_after, small)
+    qv_rows = jnp.concatenate([dqkv_sums[0:1, :W], dqkv_sums[0:1, 2 * W :]], axis=0)
+    sums_one = held(first_sums(c, one_sums, one_parts), grad_low)
+    sums_one = chip_sums(c, sums_one, qv_rows, grid)
+    sums_one = fold(c, sums_one, (("dp", c.X),))
+    grad_low, out_lane, one = gather_both(c, grad_low, out_lane, (sums_one,))
+    shared = sum_dp_end(c, sum_dp_turn(c, held(shared, one)))
     grad_w_qkv = shared[: 3 * W].reshape(3, c.half, W)
-    proj_sum = shared[3 * W :]
-    rest = proj_sum[W : W + 8 + 2 * E]
-    qv_rows = jnp.concatenate([dqkv_sums[0:1, :W], dqkv_sums[0:1, 2 * W :]], axis=0)
-    if n != 4:
-        sums_one = fold(c, one_parts, (("mp", n),))
-    sums_one = finish_sums(c, sums_one, qv_rows, grid)
+    rest = shared[4 * W : 4 * W + 8 + 2 * E]
     grad_tokens = assemble(c, order, place, grad_low, F32)
     block = assemble(c, order, place, out_lane, BF)
     return (
@@ -1487,7 +1505,7 @@
         grad_tokens,
         grad_w_qkv.transpose(1, 0, 2),
         sums_one[2:3, :W],
-        proj_sum[:W],
+        shared[3 * W : 4 * W],
         rest[2],
         jnp.stack([sums_one[0], rest[0]]),
         jnp.stack([sums_one[1], rest[1]]),

time: 531 us -> 514 us (0.968)
  waiting for transfers between devices: 118 us -> 88.1 us
  between operations: 1.7 us -> 15.2 us
  starting transfers between devices: 83.8 us -> 75.4 us
  Pallas kernels: 274 us -> 281 us
  other arithmetic: 18 us -> 23.4 us
    ppermute x30 -> x25, waiting for transfers between devices: 88.9 us -> 60.4 us  [swap_mp(): return lax.ppermute(value, 'mp', [(i, i ^ mask) for i in range(c.n)])]
    all_to_all x9 -> x8, waiting for transfers between devices: 28.8 us -> 10.4 us  [trade(): return lax.all_to_all(value, axis, split_axis=0, concat_axis=0, tiled=True)]
    ppermute x11 -> x12, waiting for transfers between devices: 0.61 us -> 10.2 us  [swap_grid(): return lax.ppermute(value, 'grid', [(0, 1), (1, 0)])]
    ppermute x30 -> x25, starting transfers between devices: 37.5 us -> 28.1 us  [swap_mp(): return lax.ppermute(value, 'mp', [(i, i ^ mask) for i in range(c.n)])]
    ppermute x2, waiting for transfers between devices: 0.01 us -> 6.44 us  [fold(): lax.ppermute(value, axis, [(i, i ^ mask) for i in range(size)])]
    pallas_call x26 -> x25, Pallas kernels: 274 us -> 281 us  [call(): pl.pallas_call(wrapped, grid_spec=pltpu.PrefetchScalarGridSpec(num_scalar...]
    all_to_all x9 -> x8, starting transfers between devices: 41 us -> 38.8 us  [trade(): return lax.all_to_all(value, axis, split_axis=0, concat_axis=0, tiled=True)]
  transfers between devices with their start and end apart: 52 -> 48, of which waited for: 20 -> 23; matrix products, arithmetic and copies ran while one was open for 5% -> 6% of each run, Pallas kernels for 50% -> 56%
where the time goes in v4:
time: 514 us; the launch traced here: 504 us
  Pallas kernels  281 us (55%)
  waiting for transfers between devices  88.1 us (17%)
  starting transfers between devices  75.4 us (15%)
  other arithmetic  23.4 us (5%)
  local copies, waits for them, and re-layouts  21 us (4%)
  between operations  15.2 us (3%)
    pallas_call x25, Pallas kernels, call(): pl.pallas_call(wrapped, grid_spec=pltpu.PrefetchScalarGridSpec(num_scalar...  281 us
    ppermute x25, waiting for transfers between devices, swap_mp(): return lax.ppermute(value, 'mp', [(i, i ^ mask) for i in range(c.n)])  60.4 us
    all_to_all x8, starting transfers between devices, trade(): return lax.all_to_all(value, axis, split_axis=0, concat_axis=0, tiled=True)  38.8 us
    ppermute x25, starting transfers between devices, swap_mp(): return lax.ppermute(value, 'mp', [(i, i ^ mask) for i in range(c.n)])  28.1 us
    unnamed x96, local copies, waits for them, and re-layouts  10.6 us
    all_to_all x8, waiting for transfers between devices, trade(): return lax.all_to_all(value, axis, split_axis=0, concat_axis=0, tiled=True)  10.4 us
  transfers between devices with their start and end apart: 48, of which 23 were waited for; matrix products, arithmetic and copies ran while one was open for 6% of the time, Pallas kernels for 56%

profile of v4, /device:TPU:0, one launch (start us, length us, event | category | flops | bytes accessed | tf_op | source)
XLA Modules:
  0.0 503.6 jit_solution(8973984079708408485)
XLA Ops:
  11.8 16.6 %route.1 = (s32[16,1600]{1,0:T(8,128)}, s32[4,16,400]{2,1,0:T(8,128)}, s32[4,8,400]{2,1,0:T(8,128)}, bf16[1280,1024]{1,0:T(8,128)(2,1)}) custom-call(s32[4]{0:T(128)} %pad_add_fusion.place, s32[2,1576]{1,0:T(2,128)} %bitcast_add_fusion.refs_0_, s32[1576,2]{1,0:T(8,128)} %copy.40.refs_1_, s32[2,1576]{1,0:T(2,128)} %bitcast.56, bf16[1576,1024]{1,0:T(8,128)(2,1)} %refs_18_.1), custom_call_target="tpu_custom_call" | custom-call | flops 1000 | bytes 1000 | tf_op jit(solution)/shard_map/route/pallas_call | solution.py:101
  28.4 6.5 %all-to-all-start.1 = ((bf16[4,320,1024]{2,1,0:T(8,128)(2,1)}), bf16[4,320,1024]{2,1,0:T(8,128)(2,1)S(1)}, u32[]{:S(2)}, u32[]{:S(2)}) async-start(bf16[4,320,1024]{2,1,0:T(8,128)(2,1)} %bitcast.52), calls=%async_computation.1 | async-start | bytes 5242880 | tf_op jit(solution)/shard_map/all_to_all | solution.py:136
  37.9 9.2 %qkv.1 = (bf16[1600,1024]{1,0:T(8,128)(2,1)}, bf16[1600,768]{1,0:T(8,128)(2,1)}, bf16[1600,1024]{1,0:T(8,128)(2,1)}) custom-call(s32[4]{0:T(128)} %pad_add_fusion.place, bf16[1576,1024]{1,0:T(8,128)(2,1)} %refs_6_.1, bf16[16,1024]{1,0:T(8,128)(2,1)} %maximum_select_fusion.1.refs_1_.refs_10_.refs_20_.refs_8_, bf16[3,512,256]{2,1,0:T(8,128)(2,1)} %bitcast.49, ...), custom_call_target="tpu_custom_call" | custom-call | flops 1000 | bytes 1000 | tf_op jit(solution)/shard_map/qkv/pallas_call | solution.py:101
  47.2 10.4 %attend.1.refs_0_.refs_1_.refs_13_ = bf16[2,1600,128]{2,1,0:T(8,128)(2,1)} custom-call(s32[4]{0:T(128)} %pad_add_fusion.place, bf16[1600,768]{1,0:T(8,128)(2,1)} %get-tuple-element.94.refs_0_.refs_1_, bf16[1600,768]{1,0:T(8,128)(2,1)} %get-tuple-element.94.refs_0_.refs_1_, bf16[8,256,512]{2,1,0:T(8,128)(2,1)} %bitcast.42), custom_call_target="tpu_custom_call" | custom-call | flops 1000 | bytes 1000 | tf_op jit(solution)/shard_map/attend/pallas_call | solution.py:101
  60.5 17.9 %collective-permute-done.3.refs_4_.refs_5_ = bf16[2,1600,128]{2,1,0:T(8,128)(2,1)S(1)} collective-permute-done((bf16[2,1600,128]{2,1,0:T(8,128)(2,1)}, bf16[2,1600,128]{2,1,0:T(8,128)(2,1)S(1)}, u32[]{:S(2)}, u32[]{:S(2)}) %collective-permute-start.3) | collective-permute-done | bytes 819232 | tf_op jit(solution)/shard_map/ppermute | solution.py:124
  81.8 6.1 %collective-permute-done.6 = bf16[32,512]{1,0:T(8,128)(2,1)S(1)} collective-permute-done((bf16[32,512]{1,0:T(8,128)(2,1)S(1)}, bf16[32,512]{1,0:T(8,128)(2,1)S(1)}, u32[]{:S(2)}, u32[]{:S(2)}) %collective-permute-start.6) | collective-permute-done | bytes 32800 | tf_op jit(solution)/shard_map/ppermute | solution.py:128
  91.5 13.4 %middle.1 = (bf16[1600,1024]{1,0:T(8,128)(2,1)}, bf16[1600,128]{1,0:T(8,128)(2,1)}, f32[400,1024]{1,0:T(8,128)}, f32[16,400]{1,0:T(8,128)}) custom-call(s32[4]{0:T(128)} %pad_add_fusion.place, bf16[2,1600,128]{2,1,0:T(8,128)(2,1)} %attend.1.refs_0_.refs_1_.refs_13_, bf16[2,1600,128]{2,1,0:T(8,128)(2,1)} %attend.1.refs_0_.refs_1_.refs_13_, ...), custom_call_target="tpu_custom_call" | custom-call | flops 1000 | bytes 1000 | tf_op jit(solution)/shard_map/middle/pallas_call | solution.py:101
  104.9 7.0 %dispatch.2.refs_3_ = bf16[640,1024]{1,0:T(8,128)(2,1)} custom-call(s32[4]{0:T(128)} %pad_add_fusion.place, s32[16,1600]{1,0:T(8,128)} %get-tuple-element.95.refs_0_, bf16[1600,1024]{1,0:T(8,128)(2,1)} %get-tuple-element.98.refs_1_.refs_19_, bf16[1600,128]{1,0:T(8,128)(2,1)} %get-tuple-element.99.refs_2_, f32[16,400]{1,0:T(8,128)} %get-tuple-element.100.refs_3_.refs_16_.refs_7_), custom_call_target="tpu_custom_call" | custom-call | flops 1000 | bytes 1000 | tf_op jit(solution)/shard_map/dispatch/pallas_call | solution.py:101
  113.4 5.3 %all-to-all-start = ((bf16[4,160,1024]{2,1,0:T(8,128)(2,1)}), bf16[4,160,1024]{2,1,0:T(8,128)(2,1)}, u32[]{:S(2)}, u32[]{:S(2)}) async-start(bf16[4,160,1024]{2,1,0:T(8,128)(2,1)} %bitcast.45), calls=%async_computation | async-start | bytes 2621440 | tf_op jit(solution)/shard_map/all_to_all | solution.py:136
  118.8 7.1 %dispatch.3.refs_3_ = bf16[640,1024]{1,0:T(8,128)(2,1)} custom-call(s32[4]{0:T(128)} %pad_add_fusion.place, s32[16,1600]{1,0:T(8,128)} %get-tuple-element.95.refs_0_, bf16[1600,1024]{1,0:T(8,128)(2,1)} %get-tuple-element.98.refs_1_.refs_19_, bf16[1600,128]{1,0:T(8,128)(2,1)} %get-tuple-element.99.refs_2_, bf16[640,1024]{1,0:T(8,128)(2,1)} %dispatch.2.refs_3_), custom_call_target="tpu_custom_call" | custom-call | flops 1000 | bytes 1000 | tf_op jit(solution)/shard_map/dispatch/pallas_call | solution.py:101
  125.9 17.8 %grad_active.1 = (bf16[640,4096]{1,0:T(8,128)(2,1)}, bf16[416,4096]{1,0:T(8,128)(2,1)}, bf16[1056,1024]{1,0:T(8,128)(2,1)}, bf16[640,640]{1,0:T(8,128)(2,1)}, bf16[416,640]{1,0:T(8,128)(2,1)}) custom-call(s32[4]{0:T(128)} %pad_add_fusion.place, bf16[4,320,1024]{2,1,0:T(8,128)(2,1)} %copy-done, bf16[4096,512]{1,0:T(8,128)(2,1)} %bitcast.11.refs_1_.refs_6_, ...), custom_call_target="tpu_custom_call" | custom-call | flops 1000 | bytes 1000 | tf_op jit(solution)/shard_map/grad_active/pallas_call | solution.py:101
  143.7 5.5 %all-to-all-done = bf16[4,160,1024]{2,1,0:T(8,128)(2,1)} async-done(((bf16[4,160,1024]{2,1,0:T(8,128)(2,1)}), bf16[4,160,1024]{2,1,0:T(8,128)(2,1)}, u32[]{:S(2)}, u32[]{:S(2)}) %all-to-all-start) | async-done | bytes 1310752 | tf_op jit(solution)/shard_map/all_to_all | solution.py:136
  158.7 27.0 %expert.2 = (bf16[640,4096]{1,0:T(8,128)(2,1)}, bf16[640,4096]{1,0:T(8,128)(2,1)}, f32[8,4096]{1,0:T(8,128)}, bf16[640,1024]{1,0:T(8,128)(2,1)}, f32[640,128]{1,0:T(8,128)}, /*index=5*/bf16[640,1024]{1,0:T(8,128)(2,1)}) custom-call(s32[4]{0:T(128)} %pad_add_fusion.place, bf16[640,1024]{1,0:T(8,128)(2,1)} %bitcast.9.refs_0_, ...), custom_call_target="tpu_custom_call" | custom-call | flops 1000 | bytes 1000 | tf_op jit(solution)/shard_map/expert/pallas_call | solution.py:101
  186.8 5.4 %all-to-all-start.3 = ((bf16[4,160,1024]{2,1,0:T(8,128)(2,1)}), bf16[4,160,1024]{2,1,0:T(8,128)(2,1)S(1)}, u32[]{:S(2)}, u32[]{:S(2)}) async-start(bf16[4,160,1024]{2,1,0:T(8,128)(2,1)} %bitcast.54), calls=%async_computation.3 | async-start | bytes 2621440 | tf_op jit(solution)/shard_map/all_to_all | solution.py:136
  192.3 20.0 %expert.3 = (bf16[416,4096]{1,0:T(8,128)(2,1)}, bf16[416,4096]{1,0:T(8,128)(2,1)}, f32[8,4096]{1,0:T(8,128)}, bf16[416,1024]{1,0:T(8,128)(2,1)}, f32[416,128]{1,0:T(8,128)}, /*index=5*/bf16[640,1024]{1,0:T(8,128)(2,1)}) custom-call(s32[4]{0:T(128)} %pad_add_fusion.place, bf16[640,1024]{1,0:T(8,128)(2,1)} %bitcast.46, ...), custom_call_target="tpu_custom_call" | custom-call | flops 1000 | bytes 1000 | tf_op jit(solution)/shard_map/expert/pallas_call | solution.py:101
  212.2 10.7 %grad_second.2.refs_4_ = bf16[4096,512]{1,0:T(8,128)(2,1)} custom-call(s32[4]{0:T(128)} %pad_add_fusion.place, bf16[1056,1024]{1,0:T(8,128)(2,1)} %get-tuple-element.110.refs_0_, f32[640,128]{1,0:T(8,128)} %get-tuple-element.118.refs_1_.refs_0_, f32[416,128]{1,0:T(8,128)} %get-tuple-element.119.refs_2_.refs_1_, ...), custom_call_target="tpu_custom_call" | custom-call | flops 1000 | bytes 1000 | tf_op jit(solution)/shard_map/grad_second/pallas_call | solution.py:101
  229.1 10.2 %grad_first.2.refs_8_ = bf16[512,4096]{1,0:T(8,128)(2,1)} custom-call(s32[4]{0:T(128)} %pad_add_fusion.place, bf16[640,1024]{1,0:T(8,128)(2,1)} %get-tuple-element.122.refs_0_, bf16[416,1024]{1,0:T(8,128)(2,1)} %get-tuple-element.123.refs_1_, bf16[640,4096]{1,0:T(8,128)(2,1)} %get-tuple-element.124.refs_2_, bf16[416,4096]{1,0:T(8,128)(2,1)} %get-tuple-element.125.refs_3_, ...), custom_call_target="tpu_custom_call" | custom-call | flops 1000 | bytes 1000 | tf_op jit(solution)/shard_map/grad_first/pallas_call | solution.py:101
  239.6 17.6 %produce.1.refs_5_ = bf16[4,320,1024]{2,1,0:T(8,128)(2,1)} custom-call(s32[4]{0:T(128)} %pad_add_fusion.place, f32[640,128]{1,0:T(8,128)} %get-tuple-element.118.refs_1_.refs_0_, f32[416,128]{1,0:T(8,128)} %get-tuple-element.119.refs_2_.refs_1_, bf16[640,4096]{1,0:T(8,128)(2,1)} %get-tuple-element.120.refs_3_.refs_2_, ...), custom_call_target="tpu_custom_call" | custom-call | flops 1000 | bytes 1000 | tf_op jit(solution)/shard_map/produce/pallas_call | solution.py:101
  268.1 12.4 %combine.2 = (bf16[2,416,512]{2,1,0:T(8,128)(2,1)}, bf16[2,416,512]{2,1,0:T(8,128)(2,1)}, bf16[2,400,512]{2,1,0:T(8,128)(2,1)}, bf16[2,400,512]{2,1,0:T(8,128)(2,1)}) custom-call(s32[4]{0:T(128)} %pad_add_fusion.place, bf16[4,160,1024]{2,1,0:T(8,128)(2,1)} %copy-done.1, bf16[4,160,1024]{2,1,0:T(8,128)(2,1)} %copy-done.6, bf16[4,160,1024]{2,1,0:T(8,128)(2,1)} %copy-done.1, ...), custom_call_target="tpu_custom_call" | custom-call | flops 1000 | bytes 1000 | tf_op jit(solution)/shard_map/combine/pallas_call | solution.py:101
  282.2 12.7 %grad_second.3.refs_5_ = f32[4096,512]{1,0:T(8,128)} custom-call(s32[4]{0:T(128)} %pad_add_fusion.place, bf16[1056,1024]{1,0:T(8,128)(2,1)} %get-tuple-element.110.refs_0_, f32[640,128]{1,0:T(8,128)} %get-tuple-element.118.refs_1_.refs_0_, f32[416,128]{1,0:T(8,128)} %get-tuple-element.119.refs_2_.refs_1_, ...), custom_call_target="tpu_custom_call" | custom-call | flops 1000 | bytes 1000 | tf_op jit(solution)/shard_map/grad_second/pallas_call | solution.py:101
  294.9 5.7 %collective-permute-done.11.refs_12_ = bf16[2,400,512]{2,1,0:T(8,128)(2,1)S(1)} collective-permute-done((bf16[2,400,512]{2,1,0:T(8,128)(2,1)}, bf16[2,400,512]{2,1,0:T(8,128)(2,1)S(1)}, u32[]{:S(2)}, u32[]{:S(2)}) %collective-permute-start.11) | collective-permute-done | bytes 819232 | tf_op jit(solution)/shard_map/ppermute | solution.py:124
  303.5 12.3 %grad_first.3.refs_22_ = f32[512,4096]{1,0:T(8,128)} custom-call(s32[4]{0:T(128)} %pad_add_fusion.place, bf16[640,1024]{1,0:T(8,128)(2,1)} %get-tuple-element.122.refs_0_, bf16[416,1024]{1,0:T(8,128)(2,1)} %get-tuple-element.123.refs_1_, bf16[640,4096]{1,0:T(8,128)(2,1)} %get-tuple-element.124.refs_2_, bf16[416,4096]{1,0:T(8,128)(2,1)} %get-tuple-element.125.refs_3_, ...), custom_call_target="tpu_custom_call" | custom-call | flops 1000 | bytes 1000 | tf_op jit(solution)/shard_map/grad_first/pallas_call | solution.py:101
  316.7 9.7 %back_two.1 = (f32[400,1024]{1,0:T(8,128)}, bf16[4,320,512]{2,1,0:T(8,128)(2,1)}, bf16[4,320,512]{2,1,0:T(8,128)(2,1)}, bf16[400,256]{1,0:T(8,128)(2,1)}, bf16[4...) custom-call(s32[4]{0:T(128)} %pad_add_fusion.place, ...), custom_call_target="tpu_custom_call" | custom-call | flops 1000 | bytes 1000 | tf_op jit(solution)/shard_map/back_two/pallas_call | solution.py:101
  332.8 11.5 %combine.3 = (bf16[2,560,512]{2,1,0:T(8,128)(2,1)}, bf16[2,560,512]{2,1,0:T(8,128)(2,1)}, bf16[2,560,512]{2,1,0:T(8,128)(2,1)}, bf16[2,560,512]{2,1,0:T(8,128)(2,1)}) custom-call(s32[4]{0:T(128)} %pad_add_fusion.place, bf16[4,320,512]{2,1,0:T(8,128)(2,1)} %add_convert_fusion.refs_0_, bf16[4,320,1024]{2,1,0:T(8,128)(2,1)} %all-to-all-done.5.refs_1_, ...), custom_call_target="tpu_custom_call" | custom-call | flops 11000000512 | bytes 1000 | tf_op jit(solution)/shard_map/combine/pallas_call | solution.py:101
  346.4 14.0 %attend_back.1 = (bf16[1600,768]{1,0:T(8,128)(2,1)}, f32[8,768]{1,0:T(8,128)}) custom-call(s32[4]{0:T(128)} %pad_add_fusion.place, bf16[1600,768]{1,0:T(8,128)(2,1)} %get-tuple-element.94.refs_0_.refs_1_, bf16[400,256]{1,0:T(8,128)(2,1)} %get-tuple-element.137.refs_3_.refs_1_, bf16[400,256]{1,0:T(8,128)(2,1)} %copy-done.37, bf16[400,256]{1,0:T(8,128)(2,1)} %copy-done.38, ...), custom_call_target="tpu_custom_call" | custom-call | flops 1000 | bytes 1000 | tf_op jit(solution)/shard_map/attend_back/pallas_call | solution.py:101
  360.4 8.5 %grad_one.1 = (bf16[2,416,512]{2,1,0:T(8,128)(2,1)}, bf16[2,416,512]{2,1,0:T(8,128)(2,1)}, bf16[2,416,512]{2,1,0:T(8,128)(2,1)}, bf16[2,416,512]{2,1,0:T(8,128)(2,1)}, f32[2,1024]{1,0:T(2,128)}) custom-call(s32[4]{0:T(128)} %pad_add_fusion.place, bf16[1600,768]{1,0:T(8,128)(2,1)} %get-tuple-element.147.refs_0_.refs_1_, ...), custom_call_target="tpu_custom_call" | custom-call | flops 1000 | bytes 1000 | tf_op jit(solution)/shard_map/grad_one/pallas_call | solution.py:101
  375.7 7.6 %grad_qkv.1 = (bf16[3,512,256]{2,1,0:T(8,128)(2,1)}, bf16[3,512,256]{2,1,0:T(8,128)(2,1)}) custom-call(s32[4]{0:T(128)} %pad_add_fusion.place, bf16[1600,1024]{1,0:T(8,128)(2,1)} %get-tuple-element.155.refs_0_, bf16[1600,768]{1,0:T(8,128)(2,1)} %get-tuple-element.147.refs_0_.refs_1_, f32[2,1024]{1,0:T(2,128)} %get-tuple-element.150.refs_2_, ...), custom_call_target="tpu_custom_call" | custom-call | flops 1000 | bytes 1000 | tf_op jit(solution)/shard_map/grad_qkv/pallas_call | solution.py:101
  385.4 6.6 %collective-permute-done.24.refs_1_ = bf16[2,416,512]{2,1,0:T(8,128)(2,1)} collective-permute-done((bf16[2,416,512]{2,1,0:T(8,128)(2,1)}, bf16[2,416,512]{2,1,0:T(8,128)(2,1)}, u32[]{:S(2)}, u32[]{:S(2)}) %collective-permute-start.24) | collective-permute-done | bytes 852000 | tf_op jit(solution)/shard_map/ppermute | solution.py:124
  397.4 6.9 %collective-permute-done.23.refs_5_ = bf16[1,560,512]{2,1,0:T(8,128)(2,1)} collective-permute-done((bf16[1,560,512]{2,1,0:T(8,128)(2,1)S(1)}, bf16[1,560,512]{2,1,0:T(8,128)(2,1)}, u32[]{:S(2)}, u32[]{:S(2)}) %collective-permute-start.23) | collective-permute-done | bytes 573472 | tf_op jit(solution)/shard_map/ppermute | solution.py:124
  419.2 5.3 %back_one.1.refs_0_.refs_1_.refs_8_ = bf16[2,400,512]{2,1,0:T(8,128)(2,1)} custom-call(s32[4]{0:T(128)} %pad_add_fusion.place, bf16[2,416,512]{2,1,0:T(8,128)(2,1)} %get-tuple-element.157.refs_0_, bf16[2,416,512]{2,1,0:T(8,128)(2,1)} %collective-permute-done.24.refs_1_, bf16[1,416,512]{2,1,0:T(8,128)(2,1)} %copy-done.32, ...), custom_call_target="tpu_custom_call" | custom-call | flops 1000 | bytes 1000 | tf_op jit(solution)/shard_map/back_one/pallas_call | solution.py:101
  457.8 16.6 %collective-permute-done.32.refs_7_.refs_2_.refs_3_ = bf16[3,400,512]{2,1,0:T(8,128)(2,1)S(1)} collective-permute-done((bf16[3,400,512]{2,1,0:T(8,128)(2,1)}, bf16[3,400,512]{2,1,0:T(8,128)(2,1)S(1)}, u32[]{:S(2)}, u32[]{:S(2)}) %collective-permute-start.32) | collective-permute-done | bytes 1228832 | tf_op jit(solution)/shard_map/ppermute | solution.py:124
  478.0 5.7 %assemble.2.refs_8_ = f32[1576,1024]{1,0:T(8,128)} custom-call(s32[4]{0:T(128)} %pad_add_fusion.place, bf16[2,400,512]{2,1,0:T(8,128)(2,1)} %back_one.1.refs_0_.refs_1_.refs_8_, bf16[2,400,512]{2,1,0:T(8,128)(2,1)} %back_one.1.refs_0_.refs_1_.refs_8_, bf16[2,400,512]{2,1,0:T(8,128)(2,1)} %copy-done.10, bf16[2,400,512]{2,1,0:T(8,128)(2,1)} %copy-done.10, ...), custom_call_target="tpu_custom_call" | custom-call | flops 1000 | bytes 1000 | tf_op jit(solution)/shard_map/assemble/pallas_call | solution.py:101
  (250 shorter events, 139.1 us)
Async XLA Ops:
  7.2 40.1 %all-gather.3.cloned.1.call-start = ((), (), s32[]{:S(2)}) async-start(), calls=%async_computation.8 | async-start | bytes 2359296 | tf_op jit(solution)/shard_map/all_gather | solution.py:1373
  28.4 83.5 %all-to-all-start.1 = ((bf16[4,320,1024]{2,1,0:T(8,128)(2,1)}), bf16[4,320,1024]{2,1,0:T(8,128)(2,1)S(1)}, u32[]{:S(2)}, u32[]{:S(2)}) async-start(bf16[4,320,1024]{2,1,0:T(8,128)(2,1)} %bitcast.52), calls=%async_computation.1 | async-start | bytes 5242880 | tf_op jit(solution)/shard_map/all_to_all | solution.py:136
  47.1 78.8 %collective-permute-start.7 = (bf16[4096,512]{1,0:T(8,128)(2,1)}, bf16[4096,512]{1,0:T(8,128)(2,1)}, u32[]{:S(2)}, u32[]{:S(2)}) collective-permute-start(bf16[4096,512]{1,0:T(8,128)(2,1)} %bitcast.11.refs_1_.refs_6_), channel_id=1, source_target_pairs={{0,1},{1,0},{2,3},{3,2},{4,5},{5,4},{6,7},{7,6},{8,9},{9,8},{10,11... | collective-permute-start | bytes 12582920 | tf_op jit(solution)/shard_map/ppermute | solution.py:128
  57.7 20.7 %collective-permute-start.3 = (bf16[2,1600,128]{2,1,0:T(8,128)(2,1)}, bf16[2,1600,128]{2,1,0:T(8,128)(2,1)S(1)}, u32[]{:S(2)}, u32[]{:S(2)}) collective-permute-start(bf16[2,1600,128]{2,1,0:T(8,128)(2,1)} %attend.1.refs_0_.refs_1_.refs_13_), channel_id=1, source_target_pairs={{0,4},{2,6},{4,0},{6,2},{1,5},{3,7},{5,1},{7,3},{8,12},{10,14},{12... | collective-permute-start | bytes 2457608 | tf_op jit(solution)/shard_map/ppermute | solution.py:124
  59.2 20.8 %collective-permute-start.2 = (bf16[2,1600,128]{2,1,0:T(8,128)(2,1)}, bf16[2,1600,128]{2,1,0:T(8,128)(2,1)S(1)}, u32[]{:S(2)}, u32[]{:S(2)}) collective-permute-start(bf16[2,1600,128]{2,1,0:T(8,128)(2,1)} %attend.1.refs_0_.refs_1_.refs_13_), channel_id=1, source_target_pairs={{0,2},{2,0},{4,6},{6,4},{1,3},{3,1},{5,7},{7,5},{8,10},{10,8},{12,... | collective-permute-start | bytes 2457608 | tf_op jit(solution)/shard_map/ppermute | solution.py:124
  81.3 77.4 %collective-permute-start.8 = (bf16[512,4096]{1,0:T(8,128)(2,1)}, bf16[512,4096]{1,0:T(8,128)(2,1)}, u32[]{:S(2)}, u32[]{:S(2)}) collective-permute-start(bf16[512,4096]{1,0:T(8,128)(2,1)} %bitcast.12.refs_2_), channel_id=1, source_target_pairs={{0,1},{1,0},{2,3},{3,2},{4,5},{5,4},{6,7},{7,6},{8,9},{9,8},{10,11... | collective-permute-start | bytes 12582920 | tf_op jit(solution)/shard_map/ppermute | solution.py:128
  113.4 35.7 %all-to-all-start = ((bf16[4,160,1024]{2,1,0:T(8,128)(2,1)}), bf16[4,160,1024]{2,1,0:T(8,128)(2,1)}, u32[]{:S(2)}, u32[]{:S(2)}) async-start(bf16[4,160,1024]{2,1,0:T(8,128)(2,1)} %bitcast.45), calls=%async_computation | async-start | bytes 2621440 | tf_op jit(solution)/shard_map/all_to_all | solution.py:136
  149.1 36.6 %all-to-all-start.2 = ((bf16[4,160,1024]{2,1,0:T(8,128)(2,1)}), bf16[4,160,1024]{2,1,0:T(8,128)(2,1)S(1)}, u32[]{:S(2)}, u32[]{:S(2)}) async-start(bf16[4,160,1024]{2,1,0:T(8,128)(2,1)} %bitcast.15), calls=%async_computation.2 | async-start | bytes 2621440 | tf_op jit(solution)/shard_map/all_to_all | solution.py:136
  186.8 37.1 %all-to-all-start.3 = ((bf16[4,160,1024]{2,1,0:T(8,128)(2,1)}), bf16[4,160,1024]{2,1,0:T(8,128)(2,1)S(1)}, u32[]{:S(2)}, u32[]{:S(2)}) async-start(bf16[4,160,1024]{2,1,0:T(8,128)(2,1)} %bitcast.54), calls=%async_computation.3 | async-start | bytes 2621440 | tf_op jit(solution)/shard_map/all_to_all | solution.py:136
  222.9 59.3 %collective-permute-start.12 = (bf16[4096,512]{1,0:T(8,128)(2,1)}, bf16[4096,512]{1,0:T(8,128)(2,1)}, u32[]{:S(2)}, u32[]{:S(2)}) collective-permute-start(bf16[4096,512]{1,0:T(8,128)(2,1)} %grad_second.2.refs_4_), channel_id=1, source_target_pairs={{0,1},{1,0},{2,3},{3,2},{4,5},{5,4},{6,7},{7,6},{8,9},{9,8},{10,11... | collective-permute-start | bytes 12582920 | tf_op jit(solution)/shard_map/ppermute | solution.py:128
  225.0 36.1 %all-to-all-start.4 = ((bf16[4,160,1024]{2,1,0:T(8,128)(2,1)}), bf16[4,160,1024]{2,1,0:T(8,128)(2,1)S(1)}, u32[]{:S(2)}, u32[]{:S(2)}) async-start(bf16[4,160,1024]{2,1,0:T(8,128)(2,1)} %bitcast.55), calls=%async_computation.4 | async-start | bytes 2621440 | tf_op jit(solution)/shard_map/all_to_all | solution.py:136
  239.3 64.1 %collective-permute-start.15 = (bf16[512,4096]{1,0:T(8,128)(2,1)}, bf16[512,4096]{1,0:T(8,128)(2,1)}, u32[]{:S(2)}, u32[]{:S(2)}) collective-permute-start(bf16[512,4096]{1,0:T(8,128)(2,1)} %grad_first.2.refs_8_), channel_id=1, source_target_pairs={{0,1},{1,0},{2,3},{3,2},{4,5},{5,4},{6,7},{7,6},{8,9},{9,8},{10,11... | collective-permute-start | bytes 12582920 | tf_op jit(solution)/shard_map/ppermute | solution.py:128
  262.2 70.7 %all-to-all-start.5 = ((bf16[4,320,1024]{2,1,0:T(8,128)(2,1)}), bf16[4,320,1024]{2,1,0:T(8,128)(2,1)}, u32[]{:S(2)}, u32[]{:S(2)}) async-start(bf16[4,320,1024]{2,1,0:T(8,128)(2,1)} %produce.1.refs_5_), calls=%async_computation.5 | async-start | bytes 5242880 | tf_op jit(solution)/shard_map/all_to_all | solution.py:136
  280.5 20.5 %collective-permute-start.10 = (bf16[2,416,512]{2,1,0:T(8,128)(2,1)}, bf16[2,416,512]{2,1,0:T(8,128)(2,1)S(1)}, u32[]{:S(2)}, u32[]{:S(2)}) collective-permute-start(bf16[2,416,512]{2,1,0:T(8,128)(2,1)} %get-tuple-element.128), channel_id=1, source_target_pairs={{0,2},{2,0},{4,6},{6,4},{1,3},{3,1},{5,7},{7,5},{8,10},{10,8},{12,... | collective-permute-start | bytes 2555912 | tf_op jit(solution)/shard_map/ppermute | solution.py:124
  281.1 19.5 %collective-permute-start.11 = (bf16[2,400,512]{2,1,0:T(8,128)(2,1)}, bf16[2,400,512]{2,1,0:T(8,128)(2,1)S(1)}, u32[]{:S(2)}, u32[]{:S(2)}) collective-permute-start(bf16[2,400,512]{2,1,0:T(8,128)(2,1)} %get-tuple-element.129), channel_id=1, source_target_pairs={{0,4},{2,6},{4,0},{6,2},{1,5},{3,7},{5,1},{7,3},{8,12},{10,14},{12... | collective-permute-start | bytes 2457608 | tf_op jit(solution)/shard_map/ppermute | solution.py:124
  326.5 17.8 %collective-permute-start.17 = (bf16[400,256]{1,0:T(8,128)(2,1)}, bf16[400,256]{1,0:T(8,128)(2,1)S(1)}, u32[]{:S(2)}, u32[]{:S(2)}) collective-permute-start(bf16[400,256]{1,0:T(8,128)(2,1)} %get-tuple-element.139), channel_id=1, source_target_pairs={{0,2},{2,0},{4,6},{6,4},{1,3},{3,1},{5,7},{7,5},{8,10},{10,8},{12,... | collective-permute-start | bytes 614408 | tf_op jit(solution)/shard_map/ppermute | solution.py:124
  344.4 27.3 %collective-permute-start.21 = (bf16[2,560,512]{2,1,0:T(8,128)(2,1)}, bf16[2,560,512]{2,1,0:T(8,128)(2,1)S(1)}, u32[]{:S(2)}, u32[]{:S(2)}) collective-permute-start(bf16[2,560,512]{2,1,0:T(8,128)(2,1)} %get-tuple-element.146), channel_id=1, source_target_pairs={{0,4},{2,6},{4,0},{6,2},{1,5},{3,7},{5,1},{7,3},{8,12},{10,14},{12... | collective-permute-start | bytes 3440648 | tf_op jit(solution)/shard_map/ppermute | solution.py:124
  345.4 28.2 %collective-permute-start.20 = (bf16[2,560,512]{2,1,0:T(8,128)(2,1)}, bf16[2,560,512]{2,1,0:T(8,128)(2,1)S(1)}, u32[]{:S(2)}, u32[]{:S(2)}) collective-permute-start(bf16[2,560,512]{2,1,0:T(8,128)(2,1)} %get-tuple-element.144), channel_id=1, source_target_pairs={{0,2},{2,0},{4,6},{6,4},{1,3},{3,1},{5,7},{7,5},{8,10},{10,8},{12,... | collective-permute-start | bytes 3440648 | tf_op jit(solution)/shard_map/ppermute | solution.py:124
  368.9 23.0 %collective-permute-start.24 = (bf16[2,416,512]{2,1,0:T(8,128)(2,1)}, bf16[2,416,512]{2,1,0:T(8,128)(2,1)}, u32[]{:S(2)}, u32[]{:S(2)}) collective-permute-start(bf16[2,416,512]{2,1,0:T(8,128)(2,1)} %get-tuple-element.158), channel_id=1, source_target_pairs={{0,2},{2,0},{4,6},{6,4},{1,3},{3,1},{5,7},{7,5},{8,10},{10,8},{12,... | collective-permute-start | bytes 2555912 | tf_op jit(solution)/shard_map/ppermute | solution.py:124
  370.0 22.2 %collective-permute-start.25 = (bf16[2,416,512]{2,1,0:T(8,128)(2,1)}, bf16[2,416,512]{2,1,0:T(8,128)(2,1)}, u32[]{:S(2)}, u32[]{:S(2)}) collective-permute-start(bf16[2,416,512]{2,1,0:T(8,128)(2,1)} %get-tuple-element.159), channel_id=1, source_target_pairs={{0,4},{2,6},{4,0},{6,2},{1,5},{3,7},{5,1},{7,3},{8,12},{10,14},{12... | collective-permute-start | bytes 2555912 | tf_op jit(solution)/shard_map/ppermute | solution.py:124
  383.3 26.1 %collective-permute-start.37 = (bf16[3,512,256]{2,1,0:T(8,128)(2,1)}, bf16[3,512,256]{2,1,0:T(8,128)(2,1)}, u32[]{:S(2)}, u32[]{:S(2)}) collective-permute-start(bf16[3,512,256]{2,1,0:T(8,128)(2,1)} %get-tuple-element.169), channel_id=1, source_target_pairs={{0,1},{1,0},{2,3},{3,2},{4,5},{5,4},{6,7},{7,6},{8,9},{9,8},{10,11... | collective-permute-start | bytes 2359304 | tf_op jit(solution)/shard_map/ppermute | solution.py:128
  383.3 20.9 %collective-permute-start.23 = (bf16[1,560,512]{2,1,0:T(8,128)(2,1)S(1)}, bf16[1,560,512]{2,1,0:T(8,128)(2,1)}, u32[]{:S(2)}, u32[]{:S(2)}) collective-permute-start(bf16[1,560,512]{2,1,0:T(8,128)(2,1)S(1)} %copy-done.19), channel_id=1, source_target_pairs={{0,2},{2,0},{4,6},{6,4},{1,3},{3,1},{5,7},{7,5},{8,10},{10,8},{12,... | collective-permute-start | bytes 1720328 | tf_op jit(solution)/shard_map/ppermute | solution.py:124
  384.3 20.2 %collective-permute-start.22 = (bf16[1,560,512]{2,1,0:T(8,128)(2,1)S(1)}, bf16[1,560,512]{2,1,0:T(8,128)(2,1)}, u32[]{:S(2)}, u32[]{:S(2)}) collective-permute-start(bf16[1,560,512]{2,1,0:T(8,128)(2,1)S(1)} %copy-done.18), channel_id=1, source_target_pairs={{0,4},{2,6},{4,0},{6,2},{1,5},{3,7},{5,1},{7,3},{8,12},{10,14},{12... | collective-permute-start | bytes 1720328 | tf_op jit(solution)/shard_map/ppermute | solution.py:124
  394.1 24.3 %collective-permute-start.27 = (bf16[1,416,512]{2,1,0:T(8,128)(2,1)}, bf16[1,416,512]{2,1,0:T(8,128)(2,1)S(1)}, u32[]{:S(2)}, u32[]{:S(2)}) collective-permute-start(bf16[1,416,512]{2,1,0:T(8,128)(2,1)} %add_convert_fusion.4.refs_12_), channel_id=1, source_target_pairs={{0,2},{2,0},{4,6},{6,4},{1,3},{3,1},{5,7},{7,5},{8,10},{10,8},{12,... | collective-permute-start | bytes 1277960 | tf_op jit(solution)/shard_map/ppermute | solution.py:124
  396.2 22.2 %collective-permute-start.26 = (bf16[1,416,512]{2,1,0:T(8,128)(2,1)S(1)}, bf16[1,416,512]{2,1,0:T(8,128)(2,1)S(1)}, u32[]{:S(2)}, u32[]{:S(2)}) collective-permute-start(bf16[1,416,512]{2,1,0:T(8,128)(2,1)S(1)} %add_convert_fusion.5.refs_11_), channel_id=1, source_target_pairs={{0,4},{2,6},{4,0},{6,2},{1,5},{3,7},{5,1},{7,3},{8,12},{10,14},{12... | collective-permute-start | bytes 1277960 | tf_op jit(solution)/shard_map/ppermute | solution.py:124
  412.8 35.5 %all-to-all-start.6 = ((bf16[4,272,512]{2,1,0:T(8,128)(2,1)}), bf16[4,272,512]{2,1,0:T(8,128)(2,1)}, u32[]{:S(2)}, u32[]{:S(2)}) async-start(bf16[4,272,512]{2,1,0:T(8,128)(2,1)} %bitcast.22), calls=%async_computation.6 | async-start | bytes 2228224 | tf_op jit(solution)/shard_map/all_to_all | solution.py:136
  424.6 18.0 %collective-permute-start.33 = (bf16[2,400,512]{2,1,0:T(8,128)(2,1)}, bf16[2,400,512]{2,1,0:T(8,128)(2,1)S(1)}, u32[]{:S(2)}, u32[]{:S(2)}) collective-permute-start(bf16[2,400,512]{2,1,0:T(8,128)(2,1)} %back_one.1.refs_0_.refs_1_.refs_8_), channel_id=1, source_target_pairs={{0,2},{2,0},{4,6},{6,4},{1,3},{3,1},{5,7},{7,5},{8,10},{10,8},{12,... | collective-permute-start | bytes 2457608 | tf_op jit(solution)/shard_map/ppermute | solution.py:124
  425.5 18.0 %collective-permute-start.28 = (bf16[2,400,512]{2,1,0:T(8,128)(2,1)}, bf16[2,400,512]{2,1,0:T(8,128)(2,1)S(1)}, u32[]{:S(2)}, u32[]{:S(2)}) collective-permute-start(bf16[2,400,512]{2,1,0:T(8,128)(2,1)} %back_one.1.refs_0_.refs_1_.refs_8_), channel_id=1, source_target_pairs={{0,4},{2,6},{4,0},{6,2},{1,5},{3,7},{5,1},{7,3},{8,12},{10,14},{12... | collective-permute-start | bytes 2457608 | tf_op jit(solution)/shard_map/ppermute | solution.py:124
  446.1 28.3 %collective-permute-start.32 = (bf16[3,400,512]{2,1,0:T(8,128)(2,1)}, bf16[3,400,512]{2,1,0:T(8,128)(2,1)S(1)}, u32[]{:S(2)}, u32[]{:S(2)}) collective-permute-start(bf16[3,400,512]{2,1,0:T(8,128)(2,1)} %get-tuple-element.167), channel_id=1, source_target_pairs={{0,2},{2,0},{4,6},{6,4},{1,3},{3,1},{5,7},{7,5},{8,10},{10,8},{12,... | collective-permute-start | bytes 3686408 | tf_op jit(solution)/shard_map/ppermute | solution.py:124
  447.2 28.4 %collective-permute-start.34 = (bf16[3,400,512]{2,1,0:T(8,128)(2,1)}, bf16[3,400,512]{2,1,0:T(8,128)(2,1)S(1)}, u32[]{:S(2)}, u32[]{:S(2)}) collective-permute-start(bf16[3,400,512]{2,1,0:T(8,128)(2,1)} %get-tuple-element.168), channel_id=1, source_target_pairs={{0,4},{2,6},{4,0},{6,2},{1,5},{3,7},{5,1},{7,3},{8,12},{10,14},{12... | collective-permute-start | bytes 3686408 | tf_op jit(solution)/shard_map/ppermute | solution.py:124
  450.9 39.7 %all-to-all-start.7 = ((bf16[4,272,512]{2,1,0:T(8,128)(2,1)}), bf16[4,272,512]{2,1,0:T(8,128)(2,1)}, u32[]{:S(2)}, u32[]{:S(2)}) async-start(bf16[4,272,512]{2,1,0:T(8,128)(2,1)} %broadcast_in_dim.16), calls=%async_computation.7 | async-start | bytes 2228224 | tf_op jit(solution)/shard_map/all_to_all | solution.py:136
  457.2 19.6 %collective-permute-start.38 = (f32[1,2048]{1,0:T(1,128)S(1)}, f32[1,2048]{1,0:T(1,128)S(1)}, u32[]{:S(2)}, u32[]{:S(2)}) collective-permute-start(f32[1,2048]{1,0:T(1,128)S(1)} %constant_dynamic-slice_fusion), channel_id=1, source_target_pairs={{0,1},{1,0},{2,3},{3,2},{4,5},{5,4},{6,7},{7,6},{8,9},{9,8},{10,11... | collective-permute-start | bytes 24584 | tf_op jit(solution)/shard_map/ppermute | solution.py:128
  (64 other events, 446.5 us)
Sparse Core Ops, SparseCore 0:
  9.9 30.6 all-gather.2
